TPU v7x, 32 devices: a whole 2x2x4 slice. The times are simulated.
32 devices in a mesh: replica: 4 (over x, core), group: 8 (over z, y).
Axes of the slice: x: 2, y: 2, z: 4, core: 2. Of those that a mesh axis runs over, the one named last changes fastest.
Arguments:
- tokens: bfloat16 [32768, 1024], P(('replica', 'group')), may hold values from -6 to 6
- segment_ids: int32 [64, 512], P(('replica', 'group')), may hold values from 0 to 7, never falling along the last dimension, each value on 1 to 256 neighbouring positions
- w_query: bfloat16 [1024, 1024], P(('replica', 'group')), may hold values from -0.1875 to 0.1875
- b_query: bfloat16 [1024], P(('replica', 'group')), may hold values from -3 to 3
- w_key: bfloat16 [1024, 1024], P(('replica', 'group')), may hold values from -0.1875 to 0.1875
- w_value: bfloat16 [1024, 1024], P(('replica', 'group')), may hold values from -0.1875 to 0.1875
- b_value: bfloat16 [1024], P(('replica', 'group')), may hold values from -3 to 3
- w_out: bfloat16 [1024, 1024], P(('replica', 'group')), may hold values from -0.75 to 0.75
- b_out: bfloat16 [1024], P(('replica', 'group')), may hold values from -3 to 3
- gain_first: bfloat16 [1024], P(('replica', 'group')), may hold values from 0.099609375 to 1.8984375
- shift_first: bfloat16 [1024], P(('replica', 'group')), may hold values from -3 to 3
- w_inner: bfloat16 [1024, 4096], P(('replica', 'group')), may hold values from -0.1875 to 0.1875
- b_inner: bfloat16 [4096], P(('replica', 'group')), may hold values from -3 to 3
- w_outer: bfloat16 [4096, 1024], P(('replica', 'group')), may hold values from -0.1875 to 0.1875
- b_outer: bfloat16 [1024], P(('replica', 'group')), may hold values from -3 to 3
- gain_second: bfloat16 [1024], P(('replica', 'group')), may hold values from 0.099609375 to 1.8984375
- shift_second: bfloat16 [1024], P(('replica', 'group')), may hold values from -3 to 3
- cotangent: bfloat16 [32768, 1024], P(('replica', 'group')), may hold values from -6 to 6
Outputs:
- output: bfloat16 [32768, 1024], P(('replica', 'group'))
- grad_tokens: bfloat16 [32768, 1024], P(('replica', 'group'))
- grad_wquery: float32 [1024, 1024], P('group')
- grad_bquery: float32 [1024], P('group')
- grad_wkey: float32 [1024, 1024], P('group')
- grad_wvalue: float32 [1024, 1024], P('group')
- grad_bvalue: float32 [1024], P('group')
- grad_wout: float32 [1024, 1024], P('group')
- grad_bout: float32 [1024], P('group')
- grad_gainfirst: float32 [1024], P('group')
- grad_shiftfirst: float32 [1024], P('group')
- grad_winner: float32 [1024, 4096], P('group')
- grad_binner: float32 [4096], P('group')
- grad_wouter: float32 [4096, 1024], P('group')
- grad_bouter: float32 [1024], P('group')
- grad_gainsecond: float32 [1024], P('group')
- grad_shiftsecond: float32 [1024], P('group')
Inputs may be any that keep to these rules, and one draw needn't show every extreme that they name: `segment_ids`: along each row of 512 positions the ids never fall; each of the 8 ids covers 1 to 256 consecutive positions, and some id exactly 256.
All inputs are finite; a program needn't handle non-finite values.
Results may differ from a plain program's by a relative error of at most 0.018.
Values may be sent and summed in bfloat16 or wider, within the bound.
No kernel may reach another device: no remote copies, remote signals or barrier semaphores. Data moves between devices by JAX's collectives and lax.ppermute only.
A program may use at most 256 MiB of HBM per device.

v0:
```python
import math

import jax
import jax.numpy as jnp
from jax import lax
from jax.sharding import PartitionSpec as P

H = 16


def layer_norm(value, gain, shift):
    center = value - jnp.mean(value, axis=-1, keepdims=True)
    scale = lax.rsqrt(jnp.mean(center * center, axis=-1, keepdims=True) + 1e-06)
    return center * scale * gain + shift


def gelu_exact(value):
    return 0.5 * value * (1.0 + lax.erf(value * (1.0 / math.sqrt(2.0))))


def matmul(left, right):
    return jnp.dot(left, right, preferred_element_type=jnp.float32)


def left_product(left, right):
    return lax.dot_general(
        left, right, (((0,), (0,)), ((), ())), preferred_element_type=jnp.float32
    )


def right_product(left, right):
    return lax.dot_general(
        left, right, (((1,), (1,)), ((), ())), preferred_element_type=jnp.float32
    )


def column_sum(value):
    return jnp.sum(value, axis=0, dtype=jnp.float32)


def masked_scores(query, keys, segment):
    same = (segment[:, None] == segment[None, :])[None]
    scores = jnp.einsum("qhd,khd->hqk", query, keys, preferred_element_type=jnp.float32) * 0.125
    return jnp.where(same, scores, -1000000000.0)


def attend_forward(item):
    query, keys, values, segment = item
    masked = masked_scores(query, keys, segment)
    top = jnp.max(masked, axis=-1, keepdims=True)
    expo = jnp.exp(masked - top)
    total = jnp.sum(expo, axis=-1, keepdims=True)
    probs = expo / total
    mixed = jnp.einsum(
        "hqk,khd->qhd", probs.astype(jnp.bfloat16), values, preferred_element_type=jnp.float32
    ).astype(jnp.bfloat16)
    return (mixed, top + jnp.log(total))


def attend_backward(item):
    query, keys, values, segment, log_total, mixed_grad = item
    probs = jnp.exp(masked_scores(query, keys, segment) - log_total)
    probs_grad = jnp.einsum("qhd,khd->hqk", mixed_grad, values, preferred_element_type=jnp.float32)
    value_grad = jnp.einsum(
        "hqk,qhd->khd", probs.astype(jnp.bfloat16), mixed_grad, preferred_element_type=jnp.float32
    ).astype(jnp.bfloat16)
    delta = jnp.sum(probs * probs_grad, axis=-1, keepdims=True)
    score_grad = (probs * (probs_grad - delta)).astype(jnp.bfloat16)
    query_grad = (
        jnp.einsum("hqk,khd->qhd", score_grad, keys, preferred_element_type=jnp.float32) * 0.125
    ).astype(jnp.bfloat16)
    key_grad = (
        jnp.einsum("hqk,qhd->khd", score_grad, query, preferred_element_type=jnp.float32) * 0.125
    ).astype(jnp.bfloat16)
    return (query_grad, key_grad, value_grad)


def local(
    tokens,
    segment_ids,
    w_query,
    b_query,
    w_key,
    w_value,
    b_value,
    w_out,
    b_out,
    gain_first,
    shift_first,
    w_inner,
    b_inner,
    w_outer,
    b_outer,
    gain_second,
    shift_second,
    cotangent,
):
    (
        whole_wquery,
        whole_bquery,
        whole_wkey,
        whole_wvalue,
        whole_bvalue,
        whole_wout,
        whole_bout,
        whole_gainf,
        whole_shiftf,
        whole_winner,
        whole_binner,
        whole_wouter,
        whole_bouter,
        whole_gains,
        whole_shifts,
    ) = (
        lax.all_gather(w_query, ("replica", "group"), axis=0, tiled=True),
        lax.all_gather(b_query, ("replica", "group"), axis=0, tiled=True),
        lax.all_gather(w_key, ("replica", "group"), axis=0, tiled=True),
        lax.all_gather(w_value, ("replica", "group"), axis=0, tiled=True),
        lax.all_gather(b_value, ("replica", "group"), axis=0, tiled=True),
        lax.all_gather(w_out, ("replica", "group"), axis=0, tiled=True),
        lax.all_gather(b_out, ("replica", "group"), axis=0, tiled=True),
        lax.all_gather(gain_first, ("replica", "group"), axis=0, tiled=True),
        lax.all_gather(shift_first, ("replica", "group"), axis=0, tiled=True),
        lax.all_gather(w_inner, ("replica", "group"), axis=0, tiled=True),
        lax.all_gather(b_inner, ("replica", "group"), axis=0, tiled=True),
        lax.all_gather(w_outer, ("replica", "group"), axis=0, tiled=True),
        lax.all_gather(b_outer, ("replica", "group"), axis=0, tiled=True),
        lax.all_gather(gain_second, ("replica", "group"), axis=0, tiled=True),
        lax.all_gather(shift_second, ("replica", "group"), axis=0, tiled=True),
    )
    seqs, length = segment_ids.shape
    width = tokens.shape[1]
    shape4 = (seqs, length, H, width // H)
    query = (matmul(tokens, whole_wquery) + whole_bquery.astype(jnp.float32)).astype(jnp.bfloat16)
    keys = matmul(tokens, whole_wkey).astype(jnp.bfloat16)
    values = (matmul(tokens, whole_wvalue) + whole_bvalue.astype(jnp.float32)).astype(jnp.bfloat16)
    query4 = query.reshape(shape4)
    keys4 = keys.reshape(shape4)
    values4 = values.reshape(shape4)
    mixed4, log_total = lax.map(attend_forward, (query4, keys4, values4, segment_ids))
    mixed = mixed4.reshape(-1, width)
    attended = matmul(mixed, whole_wout) + whole_bout.astype(jnp.float32)
    hidden, first_back = jax.vjp(
        layer_norm,
        tokens.astype(jnp.float32) + attended,
        whole_gainf.astype(jnp.float32),
        whole_shiftf.astype(jnp.float32),
    )
    hidden_low = hidden.astype(jnp.bfloat16)
    inner = matmul(hidden_low, whole_winner) + whole_binner.astype(jnp.float32)
    active, gelu_back = jax.vjp(gelu_exact, inner)
    active_low = active.astype(jnp.bfloat16)
    outer = matmul(active_low, whole_wouter) + whole_bouter.astype(jnp.float32)
    result, second_back = jax.vjp(
        layer_norm,
        hidden + outer,
        whole_gains.astype(jnp.float32),
        whole_shifts.astype(jnp.float32),
    )
    (
        whole_wquery,
        whole_bquery,
        whole_wkey,
        whole_wvalue,
        whole_bvalue,
        whole_wout,
        whole_bout,
        whole_gainf,
        whole_shiftf,
        whole_winner,
        whole_binner,
        whole_wouter,
        whole_bouter,
        whole_gains,
        whole_shifts,
    ) = (
        lax.all_gather(w_query, ("replica", "group"), axis=0, tiled=True),
        lax.all_gather(b_query, ("replica", "group"), axis=0, tiled=True),
        lax.all_gather(w_key, ("replica", "group"), axis=0, tiled=True),
        lax.all_gather(w_value, ("replica", "group"), axis=0, tiled=True),
        lax.all_gather(b_value, ("replica", "group"), axis=0, tiled=True),
        lax.all_gather(w_out, ("replica", "group"), axis=0, tiled=True),
        lax.all_gather(b_out, ("replica", "group"), axis=0, tiled=True),
        lax.all_gather(gain_first, ("replica", "group"), axis=0, tiled=True),
        lax.all_gather(shift_first, ("replica", "group"), axis=0, tiled=True),
        lax.all_gather(w_inner, ("replica", "group"), axis=0, tiled=True),
        lax.all_gather(b_inner, ("replica", "group"), axis=0, tiled=True),
        lax.all_gather(w_outer, ("replica", "group"), axis=0, tiled=True),
        lax.all_gather(b_outer, ("replica", "group"), axis=0, tiled=True),
        lax.all_gather(gain_second, ("replica", "group"), axis=0, tiled=True),
        lax.all_gather(shift_second, ("replica", "group"), axis=0, tiled=True),
    )
    resid_second, grad_gains, grad_shifts = second_back(cotangent.astype(jnp.float32))
    outer_grad = resid_second.astype(jnp.bfloat16)
    grad_bouter = column_sum(outer_grad)
    grad_wouter = left_product(active_low, outer_grad)
    inner_grad = gelu_back(right_product(outer_grad, whole_wouter))[0].astype(jnp.bfloat16)
    grad_binner = column_sum(inner_grad)
    grad_winner = left_product(hidden_low, inner_grad)
    hidden_grad = resid_second + right_product(inner_grad, whole_winner)
    resid_first, grad_gainf, grad_shiftf = first_back(hidden_grad)
    attend_grad = resid_first.astype(jnp.bfloat16)
    grad_bout = column_sum(attend_grad)
    grad_wout = left_product(mixed, attend_grad)
    mixed_grad = right_product(attend_grad, whole_wout).astype(jnp.bfloat16).reshape(shape4)
    query_grad4, key_grad4, value_grad4 = lax.map(
        attend_backward, (query4, keys4, values4, segment_ids, log_total, mixed_grad)
    )
    query_grad = query_grad4.reshape(-1, width)
    key_grad = key_grad4.reshape(-1, width)
    value_grad = value_grad4.reshape(-1, width)
    grad_bquery = column_sum(query_grad)
    grad_bvalue = column_sum(value_grad)
    grad_wquery = left_product(tokens, query_grad)
    grad_wkey = left_product(tokens, key_grad)
    grad_wvalue = left_product(tokens, value_grad)
    grad_tokens = (
        resid_first
        + right_product(query_grad, whole_wquery)
        + right_product(key_grad, whole_wkey)
        + right_product(value_grad, whole_wvalue)
    ).astype(jnp.bfloat16)
    (
        part_wquery,
        part_bquery,
        part_wkey,
        part_wvalue,
        part_bvalue,
        part_wout,
        part_bout,
        part_gainf,
        part_shiftf,
        part_winner,
        part_binner,
        part_wouter,
        part_bouter,
        part_gains,
        part_shifts,
    ) = (
        lax.psum_scatter(grad_wquery, "group", scatter_dimension=0, tiled=True),
        lax.psum_scatter(grad_bquery, "group", scatter_dimension=0, tiled=True),
        lax.psum_scatter(grad_wkey, "group", scatter_dimension=0, tiled=True),
        lax.psum_scatter(grad_wvalue, "group", scatter_dimension=0, tiled=True),
        lax.psum_scatter(grad_bvalue, "group", scatter_dimension=0, tiled=True),
        lax.psum_scatter(grad_wout, "group", scatter_dimension=0, tiled=True),
        lax.psum_scatter(grad_bout, "group", scatter_dimension=0, tiled=True),
        lax.psum_scatter(grad_gainf, "group", scatter_dimension=0, tiled=True),
        lax.psum_scatter(grad_shiftf, "group", scatter_dimension=0, tiled=True),
        lax.psum_scatter(grad_winner, "group", scatter_dimension=0, tiled=True),
        lax.psum_scatter(grad_binner, "group", scatter_dimension=0, tiled=True),
        lax.psum_scatter(grad_wouter, "group", scatter_dimension=0, tiled=True),
        lax.psum_scatter(grad_bouter, "group", scatter_dimension=0, tiled=True),
        lax.psum_scatter(grad_gains, "group", scatter_dimension=0, tiled=True),
        lax.psum_scatter(grad_shifts, "group", scatter_dimension=0, tiled=True),
    )
    shares = (
        lax.psum(part_wquery.astype(jnp.bfloat16), "replica").astype(jnp.float32),
        lax.psum(part_bquery.astype(jnp.bfloat16), "replica").astype(jnp.float32),
        lax.psum(part_wkey.astype(jnp.bfloat16), "replica").astype(jnp.float32),
        lax.psum(part_wvalue.astype(jnp.bfloat16), "replica").astype(jnp.float32),
        lax.psum(part_bvalue.astype(jnp.bfloat16), "replica").astype(jnp.float32),
        lax.psum(part_wout.astype(jnp.bfloat16), "replica").astype(jnp.float32),
        lax.psum(part_bout.astype(jnp.bfloat16), "replica").astype(jnp.float32),
        lax.psum(part_gainf.astype(jnp.bfloat16), "replica").astype(jnp.float32),
        lax.psum(part_shiftf.astype(jnp.bfloat16), "replica").astype(jnp.float32),
        lax.psum(part_winner.astype(jnp.bfloat16), "replica").astype(jnp.float32),
        lax.psum(part_binner.astype(jnp.bfloat16), "replica").astype(jnp.float32),
        lax.psum(part_wouter.astype(jnp.bfloat16), "replica").astype(jnp.float32),
        lax.psum(part_bouter.astype(jnp.bfloat16), "replica").astype(jnp.float32),
        lax.psum(part_gains.astype(jnp.bfloat16), "replica").astype(jnp.float32),
        lax.psum(part_shifts.astype(jnp.bfloat16), "replica").astype(jnp.float32),
    )
    return (result.astype(jnp.bfloat16), grad_tokens) + tuple(shares)


def solution(mesh):
    in_specs = (
        P(("replica", "group"), None),
        P(("replica", "group"), None),
        P(("replica", "group"), None),
        P(("replica", "group")),
        P(("replica", "group"), None),
        P(("replica", "group"), None),
        P(("replica", "group")),
        P(("replica", "group"), None),
        P(("replica", "group")),
        P(("replica", "group")),
        P(("replica", "group")),
        P(("replica", "group"), None),
        P(("replica", "group")),
        P(("replica", "group"), None),
        P(("replica", "group")),
        P(("replica", "group")),
        P(("replica", "group")),
        P(("replica", "group"), None),
    )
    out_specs = (
        P(("replica", "group"), None),
        P(("replica", "group"), None),
        P("group", None),
        P("group"),
        P("group", None),
        P("group", None),
        P("group"),
        P("group", None),
        P("group"),
        P("group"),
        P("group"),
        P("group", None),
        P("group"),
        P("group", None),
        P("group"),
        P("group"),
        P("group"),
    )
    return jax.shard_map(local, mesh=mesh, in_specs=in_specs, out_specs=out_specs, check_vma=False)
```

profile of v0, /device:TPU:9, one launch (start us, length us, event | category | flops | bytes accessed | tf_op | source)
XLA Modules:
  0.0 1541.9 jit_solution(8781443514886243452)
XLA Ops:
  17.9 40.9 %all-reduce.18 = (bf16[1024]{0:T(1024)(128)(2,1)S(1)}, bf16[1024]{0:T(1024)(128)(2,1)S(1)}, bf16[1024]{0:T(1024)(128)(2,1)S(1)}, bf16[1024]{0:T(1024)(128)(2,1)S...) all-reduce(bf16[1024]{0:T(1024)(128)(2,1)S(1)} %dynamic-update-slic, ...), channel_id=1, replica_groups=mesh['replica'=4,'group'=8] {'replica','group'}, use_global_device_ids=true, to_apply=%add.1 | all-reduce | flops 8192 | bytes 32768
  64.6 56.9 %all-gather = bf16[32,1,128]{2,1,0:T(2,128)(2,1)S(1)} all-gather(bf16[1,1,128]{2,1,0:T(2,128)(2,1)S(1)} %bitcast.186), channel_id=1, replica_groups=mesh['replica'=4,'group'=8] {'replica','group'}, dimensions={0}, use_global_device_ids=true | all-gather | bytes 8448 | tf_op jit(solution)/shard_map/all_gather | solution.py:125
  126.4 4.5 add_convert_fusion.4
  134.9 5.5 copy.95
  140.4 4.6 add_convert_fusion.3
  148.9 5.4 copy.96
  154.3 30.9 %all-gather.12.cloned.1.call-done = bf16[1024,1024]{1,0:T(8,128)(2,1)} async-done(((bf16[32,1024]{1,0:T(8,128)(2,1)}), bf16[1024,1024]{1,0:T(8,128)(2,1)}) %all-gather.12.cloned.1.call-update) | async-done | bytes 2097168 | tf_op jit(solution)/shard_map/all_gather | solution.py:117
  185.2 4.5 convolution_convert_fusion.1
  193.7 4.5 copy.97
  199.8 55.1 %while.26 = (s32[]{:T(128)}, bf16[2,512,16,64]{1,3,2,0:T(8,128)(2,1)}, f32[2,16,512,1]{2,1,3,0:T(8,128)S(1)}, bf16[2,512,16,64]{1,3,2,0:T(8,128)(2,1)}, s32[2,51...) while((s32[]{:T(128)}, ...), condition=%wide.region_3.4_spmd, body=%wide.region_0.3_spmd.sunk | while | flops 1124851712 | bytes 55844956 | solution.py:140
  200.2 8.5 fusion.124
  208.7 9.2 fusion.125
  217.9 9.2 fusion.126
  227.4 8.6 fusion.124
  235.9 9.4 fusion.125
  245.3 9.2 fusion.126
  260.6 5.7 fusion.65
  268.8 54.7 %all-gather.16.cloned.1.call-done = bf16[1024,4096]{1,0:T(8,128)(2,1)} async-done(((bf16[32,4096]{1,0:T(8,128)(2,1)}), bf16[1024,4096]{1,0:T(8,128)(2,1)}) %all-gather.16.cloned.1.call-update) | async-done | bytes 8388624 | tf_op jit(solution)/shard_map/all_gather | solution.py:124
  323.5 19.9 %multiply_convert_fusion.3 = (bf16[1024,4096]{1,0:T(8,128)(2,1)}, f32[1024,4096]{1,0:T(8,128)}) fusion(f32[4096]{0:T(1024)S(1)} %bitcast.184, bf16[1024,4096]{1,0:T(8,128)(2,1)} %all-gather.16.cloned.1.call-done, f32[1024,1024]{0,1:T(8,128)} %copy-done.9, f32[1024]{0:T(1024)S(1)} %copy-done.51, f32[1024]{0:T(1024)S(1)} %copy-done.41, f32[1024]{0:T(1024)S(1)} %fusion.57, ...), kind=kOutput, calls=%fused_computation.62 | convolution fusion | flops 8620343296 | bytes 37781504 | tf_op jit(solution)/shard_map/dot_general | solution.py:22
  343.4 58.9 %all-gather.18.cloned.1.call-done = bf16[4096,1024]{1,0:T(8,128)(2,1)} async-done(((bf16[128,1024]{1,0:T(8,128)(2,1)}), bf16[4096,1024]{1,0:T(8,128)(2,1)}) %all-gather.18.cloned.1.call-update) | async-done | bytes 8388624 | tf_op jit(solution)/shard_map/all_gather | solution.py:126
  402.4 16.4 %fusion.66 = (f32[1024]{0:T(1024)S(1)}, f32[1024,1024]{0,1:T(8,128)}) fusion(f32[1024]{0:T(1024)S(1)} %copy-done.53, bf16[1024,4096]{1,0:T(8,128)(2,1)} %get-tuple-element.307, bf16[4096,1024]{1,0:T(8,128)(2,1)} %all-gather.18.cloned.1.call-done, f32[1024]{0:T(1024)S(1)} %copy-done.51, f32[1024]{0:T(1024)S(1)} %copy-done.41, f32[1024]{0:T(1024)S(1)} %fusion.57, ...), kind=kOutput, calls=%fused_computation.121 | convolution fusion | flops 8597273600 | bytes 25190400 | tf_op jit(solution)/shard_map/dot_general | solution.py:22
  418.8 5.0 fusion.54
  430.9 21.2 %convert_reduce_fusion = (f32[4096]{0:T(1024)}, bf16[1024,4096]{1,0:T(8,128)(2,1)}) fusion(f32[1024,4096]{1,0:T(8,128)} %get-tuple-element.308, f32[4096]{0:T(1024)S(1)} %bitcast.185, bf16[1024,1024]{0,1:T(8,128)(2,1)S(1)} %get-tuple-element.291, bf16[4096,1024]{1,0:T(8,128)(2,1)S(1)} %bitcast.188), kind=kOutput, calls=%fused_computation.60 | convolution fusion | flops 8657039360 | bytes 35684352 | tf_op jit(solution)/shard_map/dot_general | solution.py:32
  452.1 16.8 %multiply_reduce_fusion.1 = (f32[1024]{0:T(1024)}, f32[1024]{0:T(1024)S(1)}, f32[1024]{0:T(1024)}, f32[1024,1024]{0,1:T(8,128)S(1)}) fusion(f32[1024,1024]{0,1:T(8,128)S(1)} %copy-done.10, f32[1024]{0:T(1024)S(1)} %fusion.57, f32[1024]{0:T(1024)S(1)} %broadcast_multiply_fusion.1, f32[1024]{0:T(1024)S(1)} %copy-done.41, ...), kind=kOutput, calls=%fused_computation.74 | convolution fusion | flops 8607757312 | bytes 31502336 | tf_op jit(solution)/shard_map/dot_general | solution.py:32
  478.9 5.9 convolution_convert_fusion
  484.8 6.8 reshape.242
  491.6 5.5 copy.104
  501.9 98.7 %while.27 = (s32[]{:T(128)}, bf16[2,512,16,64]{1,3,2,0:T(8,128)(2,1)}, bf16[2,512,16,64]{1,3,2,0:T(8,128)(2,1)}, bf16[2,512,16,64]{1,3,2,0:T(8,128)(2,1)}, bf16[...) while((s32[]{:T(128)}, ...), condition=%wide.region_14.15_spmd, body=%wide.region_12.14_spmd.sunk | while | flops 2724978688 | bytes 187346224 | solution.py:206
  501.9 9.8 fusion.135
  511.9 12.2 multiply_reduce_fusion.6
  524.1 12.1 multiply_convert_fusion.5
  541.7 9.8 fusion.138
  551.5 9.8 fusion.135
  561.6 12.1 multiply_reduce_fusion.6
  573.7 11.7 multiply_convert_fusion.5
  590.9 9.5 fusion.138
  616.3 4.3 convolution_bitcast_fusion.1
  626.8 4.3 convolution_bitcast_fusion
  631.8 16.9 %fusion.59 = f32[1024,4096]{1,0:T(8,128)} fusion(bf16[1024,4096]{1,0:T(8,128)(2,1)} %get-tuple-element.293, f32[1024,1024]{0,1:T(8,128)} %copy-done.9, f32[1024]{0:T(1024)S(1)} %copy-done.52, f32[1024]{0:T(1024)S(1)} %copy-done.42, f32[1024]{0:T(1024)S(1)} %copy-done.44, f32[1024]{0:T(1024)S(1)} %copy-done.35), kind=kOutput, calls=%fused_computation.116 | convolution fusion | flops 8595177472 | bytes 29376512 | tf_op jit(solution)/shard_map/dot_general | solution.py:26
  650.4 14.7 fusion.68
  670.0 28.0 %all-reduce.17 = (bf16[1024]{0:T(1024)(128)(2,1)S(1)}, bf16[1024]{0:T(1024)(128)(2,1)S(1)}, bf16[1024]{0:T(1024)(128)(2,1)S(1)}, bf16[1024]{0:T(1024)(128)(2,1)S...) all-reduce(f32[1024]{0:T(1024)S(1)} %reduce_sum.216, ...), channel_id=3, replica_groups=mesh['replica'=4,'group'=8] {'group'}, use_global_device_ids=true, to_apply=%region_18.19.clone | all-reduce | flops 12288 | bytes 73728
  698.7 12.5 all-reduce.19
  715.9 6.6 fusion.69
  726.1 64.0 %reduce-scatter.9.cloned.1.call-done = f32[128,1024]{0,1:T(8,128)} async-done(((f32[1024,1024]{0,1:T(8,128)}), f32[128,1024]{0,1:T(8,128)}) %reduce-scatter.9.cloned.1.call-update) | async-done | bytes 524304 | tf_op jit(solution)/shard_map/reduce_scatter | solution.py:242
  791.8 90.2 %reduce-scatter.11.cloned.1.call-done = f32[128,1024]{0,1:T(8,128)} async-done(((f32[1024,1024]{0,1:T(8,128)}), f32[128,1024]{0,1:T(8,128)}) %reduce-scatter.11.cloned.1.call-update) | async-done | bytes 524304 | tf_op jit(solution)/shard_map/reduce_scatter | solution.py:243
  883.8 283.2 %reduce-scatter.15.cloned.1.call-done = f32[128,4096]{1,0:T(8,128)} async-done(((f32[1024,4096]{1,0:T(8,128)}), f32[128,4096]{1,0:T(8,128)}) %reduce-scatter.15.cloned.1.call-update) | async-done | bytes 2097168 | tf_op jit(solution)/shard_map/reduce_scatter | solution.py:249
  1169.7 283.1 %reduce-scatter.17.cloned.1.call-done = f32[512,1024]{1,0:T(8,128)} async-done(((f32[4096,1024]{1,0:T(8,128)}), f32[512,1024]{1,0:T(8,128)}) %reduce-scatter.17.cloned.1.call-update) | async-done | bytes 2097168 | tf_op jit(solution)/shard_map/reduce_scatter | solution.py:251
  1471.7 54.1 %all-reduce.23.cloned.1.call-done = (bf16[128,1024]{0,1:T(8,128)(2,1)}, bf16[128,1024]{0,1:T(8,128)(2,1)}, bf16[128,1024]{0,1:T(8,128)(2,1)}, bf16[128,1024]{1,0...) async-done(((bf16[128,1024]{0,1:T(8,128)(2,1)}, bf16[128,1024]{0,1:T(8,128)(2,1)}, bf16[128,1024]{0,1:T(8,128)(2,1)}, bf16[128,1024]{1,0:T(8,128)(2,1)}, ...) | async-done | bytes 3145744 | tf_op jit(solution)/shard_map/psum | solution.py:257
  (277 shorter events, 147.4 us)
Async XLA Ops:
  7.2 57.4 %copy-start.55 = (bf16[128]{0:T(256)(128)(2,1)S(1)}, bf16[128]{0:T(256)(128)(2,1)}, u32[]{:S(2)}) copy-start(bf16[128]{0:T(256)(128)(2,1)} %param.34) | copy-start | bytes 772
  7.2 116.1 %copy-start.15 = (bf16[1024,1024]{1,0:T(8,128)(2,1)S(1)}, bf16[1024,1024]{1,0:T(8,128)(2,1)}, u32[]{:S(2)}) copy-start(bf16[1024,1024]{1,0:T(8,128)(2,1)} %param.39) | copy-start | bytes 6291460
  7.2 119.2 %all-gather.8.cloned.1.call-start = ((), (), s32[]{:S(2)}) async-start(), calls=%async_computation.6 | async-start | bytes 2162688 | tf_op jit(solution)/shard_map/all_gather | solution.py:118
  7.9 132.4 %all-gather.10.cloned.1.call-start = ((), (), s32[]{:S(2)}) async-start(), calls=%async_computation.7 | async-start | bytes 2162688 | tf_op jit(solution)/shard_map/all_gather | solution.py:115
  8.7 176.5 %all-gather.12.cloned.1.call-start = ((), (), s32[]{:S(2)}) async-start(), calls=%async_computation.8 | async-start | bytes 2162688 | tf_op jit(solution)/shard_map/all_gather | solution.py:117
  9.4 251.2 %all-gather.14.cloned.1.call-start = ((), (), s32[]{:S(2)}) async-start(), calls=%async_computation.9 | async-start | bytes 2162688 | tf_op jit(solution)/shard_map/all_gather | solution.py:120
  10.0 313.5 %all-gather.16.cloned.1.call-start = ((), (), s32[]{:S(2)}) async-start(), calls=%async_computation.10 | async-start | bytes 8650752 | tf_op jit(solution)/shard_map/all_gather | solution.py:124
  10.6 391.8 %all-gather.18.cloned.1.call-start = ((), (), s32[]{:S(2)}) async-start(), calls=%async_computation.11 | async-start | bytes 8650752 | tf_op jit(solution)/shard_map/all_gather | solution.py:126
  11.2 711.3 %reduce-scatter.13.cloned.1.call-start = ((), (), s32[]{:S(2)}) async-start(), calls=%async_computation.15 | async-start | bytes 4718592 | tf_op jit(solution)/shard_map/reduce_scatter | solution.py:245
  193.7 6.1 copy-start.32
  254.9 5.7 copy-start.54
  266.3 57.2 %copy-start.41 = (f32[1024]{0:T(1024)S(1)}, f32[1024]{0:T(1024)}, u32[]{:S(2)}) copy-start(f32[1024]{0:T(1024)} %convert_element_type.213) | copy-start | bytes 12292
  266.3 57.2 %copy-start.47 = (f32[32,1,128]{2,1,0:T(1,128)S(1)}, f32[32,1,128]{2,1,0:T(1,128)}, u32[]{:S(2)}) copy-start(f32[32,1,128]{2,1,0:T(1,128)} %convert_element_type.263) | copy-start | bytes 49156
  266.3 57.2 %copy-start.51 = (f32[1024]{0:T(1024)S(1)}, f32[1024]{0:T(1024)}, u32[]{:S(2)}) copy-start(f32[1024]{0:T(1024)} %convert_element_type.214) | copy-start | bytes 12292
  266.4 202.6 %copy-start.34 = (f32[1024]{0:T(1024)}, f32[1024]{0:T(1024)S(1)}, u32[]{:S(2)}) copy-start(f32[1024]{0:T(1024)S(1)} %broadcast_multiply_fusion.1) | copy-start | bytes 12292
  268.8 200.2 %copy-start.43 = (f32[1024]{0:T(1024)}, f32[1024]{0:T(1024)S(1)}, u32[]{:S(2)}) copy-start(f32[1024]{0:T(1024)S(1)} %fusion.57) | copy-start | bytes 12292
  323.5 78.9 %copy-start.53 = (f32[1024]{0:T(1024)S(1)}, f32[1024]{0:T(1024)}, u32[]{:S(2)}) copy-start(f32[1024]{0:T(1024)} %convert_element_type.218) | copy-start | bytes 12292
  402.4 16.5 %copy-start.33 = (f32[1024]{0:T(1024)S(1)}, f32[1024]{0:T(1024)}, u32[]{:S(2)}) copy-start(f32[1024]{0:T(1024)} %convert_element_type.219) | copy-start | bytes 12292
  418.8 5.0 copy-start.2
  418.8 5.0 copy-start.3
  423.9 7.1 slice-start
  430.9 21.2 %copy-start.26 = (bf16[1024,1024]{0,1:T(8,128)(2,1)}, bf16[1024,1024]{0,1:T(8,128)(2,1)S(1)}, u32[]{:S(2)}) copy-start(bf16[1024,1024]{0,1:T(8,128)(2,1)S(1)} %get-tuple-element.291) | copy-start | bytes 6291460
  430.9 21.2 %copy-start.10 = (f32[1024,1024]{0,1:T(8,128)S(1)}, f32[1024,1024]{0,1:T(8,128)}, u32[]{:S(2)}) copy-start(f32[1024,1024]{0,1:T(8,128)} %copy-done.9) | copy-start | bytes 12582916
  470.1 8.8 copy-start.39
  478.9 245.4 %reduce-scatter.7.cloned.1.call-start = ((), (), s32[]{:S(2)}) async-start(), calls=%async_computation.12 | async-start | bytes 4718592 | tf_op jit(solution)/shard_map/reduce_scatter | solution.py:240
  501.9 10.1 copy-start
  524.1 12.1 copy-start.11
  551.5 10.1 copy-start
  573.7 11.7 copy-start.11
  600.5 5.8 copy-start.16
  610.7 179.4 %reduce-scatter.9.cloned.1.call-start = ((), (), s32[]{:S(2)}) async-start(), calls=%async_computation.13 | async-start | bytes 4718592 | tf_op jit(solution)/shard_map/reduce_scatter | solution.py:242
  620.6 261.4 %reduce-scatter.11.cloned.1.call-start = ((), (), s32[]{:S(2)}) async-start(), calls=%async_computation.14 | async-start | bytes 4718592 | tf_op jit(solution)/shard_map/reduce_scatter | solution.py:243
  620.9 5.9 copy-start.18
  631.1 535.8 %reduce-scatter.15.cloned.1.call-start = ((), (), s32[]{:S(2)}) async-start(), calls=%async_computation.16 | async-start | bytes 18874368 | tf_op jit(solution)/shard_map/reduce_scatter | solution.py:249
  648.8 804.0 %reduce-scatter.17.cloned.1.call-start = ((), (), s32[]{:S(2)}) async-start(), calls=%async_computation.17 | async-start | bytes 18874368 | tf_op jit(solution)/shard_map/reduce_scatter | solution.py:251
  665.1 4.9 copy-start.36
  665.1 4.9 copy-start.37
  665.1 4.9 copy-start.38
  665.2 4.9 copy-start.46
  665.2 4.8 copy-start.48
  665.2 4.8 copy-start.49
  665.2 860.6 %all-reduce.23.cloned.1.call-start = ((), (), s32[]{:S(2)}) async-start(), calls=%async_computation.18 | async-start | bytes 6291456 | tf_op jit(solution)/shard_map/psum | solution.py:257
  883.8 571.9 %copy-start.20 = (bf16[128,8,2,512]{3,1,2,0:T(8,128)(2,1)S(1)}, bf16[128,8,2,512]{3,1,2,0:T(8,128)(2,1)}, u32[]{:S(2)}) copy-start(bf16[128,8,2,512]{3,1,2,0:T(8,128)(2,1)} %copy-done.19) | copy-start | bytes 6291460
  1455.7 5.3 copy-start.58
  1525.8 5.6 copy-start.31
  1525.8 6.5 copy-start.30
  1525.8 7.4 copy-start.29
  1525.8 8.4 copy-start.28
  (32 other events, 76.4 us)
Sparse Core Ops, SparseCore 0:
  11.0 57.5 all-gather.7
  71.6 55.2 all-gather.9
  129.9 55.3 all-gather.11
  188.1 55.3 all-gather.13
  246.3 77.1 all-gather.15
  326.3 75.9 all-gather.17
  479.0 86.2 reduce-scatter.12
  610.8 87.2 reduce-scatter.6
  701.7 88.2 reduce-scatter.8
  794.0 88.0 reduce-scatter.10
  885.8 281.1 reduce-scatter.14
  1171.1 281.6 reduce-scatter.16
  1456.2 69.5 all-reduce.22
where the time goes:
time: 1550 us; the launch traced here: 1540 us
  waiting for transfers between devices  923 us (60%)
  matrix products  270 us (17%)
  blocking collectives  138 us (9%)
  local copies, waits for them, and re-layouts  105 us (7%)
  other arithmetic  88.1 us (6%)
  between operations  16.2 us (1%)
    reduce_scatter x1, waiting for transfers between devices, local(): lax.psum_scatter(grad_winner, 'group', scatter_dimension=0, tiled=True)  283 us
    reduce_scatter x1, waiting for transfers between devices, local(): lax.psum_scatter(grad_wouter, 'group', scatter_dimension=0, tiled=True)  283 us
    reduce_scatter x1, waiting for transfers between devices, local(): lax.psum_scatter(grad_wvalue, 'group', scatter_dimension=0, tiled=True)  90.2 us
    unnamed x2, blocking collectives  68.9 us
    reduce_scatter x1, waiting for transfers between devices, local(): lax.psum_scatter(grad_wkey, 'group', scatter_dimension=0, tiled=True)  64 us
    all_gather x1, waiting for transfers between devices, local(): lax.all_gather(w_outer, ('replica', 'group'), axis=0, tiled=True)  58.9 us
    dot_general x6, matrix products, right_product(): lax.dot_general(left, right, (((1,), (1,)), ((), ())), preferred_element_...  58.7 us
    all_gather x1, blocking collectives, local(): lax.all_gather(b_inner, ('replica', 'group'), axis=0, tiled=True)  56.9 us
  transfers between devices with their start and end apart: 13, of which 8 were waited for; matrix products, arithmetic and copies ran while one was open for 23% of the time, Pallas kernels for 0%

commit v1 on v0

v1 whole, which is shorter than its diff:
```python
import functools
import math

import jax
import jax.numpy as jnp
from jax import lax
from jax.experimental import pallas as pl
from jax.experimental.pallas import tpu as pltpu
from jax.sharding import PartitionSpec as P

F32 = jnp.float32
BF16 = jnp.bfloat16
VMEM_LIMIT = 56 * 1024 * 1024


def params(*semantics):
    return pltpu.CompilerParams(dimension_semantics=semantics, vmem_limit_bytes=VMEM_LIMIT)


def cost(flops, bytes_accessed, transcendentals=0):
    return pl.CostEstimate(flops=int(flops), bytes_accessed=int(bytes_accessed), transcendentals=int(transcendentals))


def dot(left, right):
    return lax.dot_general(left, right, (((1,), (0,)), ((), ())), preferred_element_type=F32)


def dot_nt(left, right):
    return lax.dot_general(left, right, (((1,), (1,)), ((), ())), preferred_element_type=F32)


def whole(shape):
    return pl.BlockSpec(shape, lambda *i: (0,) * len(shape))


def transpose_kernel(x_ref, out_ref):
    out_ref[...] = x_ref[...].T


def transposed(x, tile=256):
    rows, cols = x.shape
    return pl.pallas_call(
        transpose_kernel,
        out_shape=jax.ShapeDtypeStruct((cols, rows), x.dtype),
        grid=(rows // tile,),
        in_specs=[pl.BlockSpec((tile, cols), lambda i: (i, 0))],
        out_specs=pl.BlockSpec((cols, tile), lambda i: (0, i)),
        compiler_params=params("arbitrary"),
        cost_estimate=cost(0, 4 * rows * cols),
        name="transposed",
    )(x)


def project_kernel(order_ref, x_ref, w_ref, b_ref, out_ref, whole_ref, held, arrived, left, *, tile):
    step = pl.program_id(0)
    pieces, rows, _ = w_ref.shape
    cols = held.shape[1]
    write = pltpu.make_async_copy(held, whole_ref, left)

    @pl.when(step == 0)
    def _():
        def fetch(j):
            start = pl.multiple_of(order_ref[j] * rows, rows)
            return pltpu.make_async_copy(w_ref.at[j, :, pl.ds(0, cols)], held.at[pl.ds(start, rows)], arrived.at[j])

        for j in range(pieces):
            fetch(j).start()
        for j in range(pieces):
            fetch(j).wait()
        write.start()

    part = held[:, pl.ds(pl.multiple_of(step * tile, tile), tile)]
    out_ref[...] = (dot(x_ref[...], part) + b_ref[...]).astype(BF16)

    @pl.when(step == pl.num_programs(0) - 1)
    def _():
        write.wait()


def project(order, x, w, bias, tile=512):
    rows, depth = x.shape
    cols = bias.shape[1]
    return pl.pallas_call(
        functools.partial(project_kernel, tile=tile),
        out_shape=(jax.ShapeDtypeStruct((rows, cols), BF16), jax.ShapeDtypeStruct((depth, cols), BF16)),
        grid_spec=pltpu.PrefetchScalarGridSpec(
            num_scalar_prefetch=1,
            grid=(cols // tile,),
            in_specs=[
                pl.BlockSpec((rows, depth), lambda i, order: (0, 0)),
                pl.BlockSpec(memory_space=pl.ANY),
                pl.BlockSpec((1, tile), lambda i, order: (0, i)),
            ],
            out_specs=(pl.BlockSpec((rows, tile), lambda i, order: (0, i)), pl.BlockSpec(memory_space=pl.ANY)),
            scratch_shapes=[pltpu.VMEM((depth, cols), BF16), pltpu.SemaphoreType.DMA((w.shape[0],)), pltpu.SemaphoreType.DMA],
        ),
        compiler_params=params("arbitrary"),
        cost_estimate=cost(2 * rows * depth * cols, 2 * (rows * depth + depth * cols + rows * cols)),
        name="project",
    )(order, x, w, bias)


def attend_kernel(q_ref, k_ref, v_ref, row_ref, col_ref, o_ref, ot_ref, p_ref, bias_ref):
    @pl.when(pl.program_id(1) == 0)
    def _():
        bias_ref[...] = jnp.where(col_ref[0] == row_ref[0], 0.0, -1e9).astype(F32)

    qt = q_ref[...].T
    keys = k_ref[...]
    vt = v_ref[...].T
    half = qt.shape[0] // 2
    zero = jnp.zeros((half, qt.shape[1]), BF16)
    for head in range(2):
        own = qt[head * half : (head + 1) * half]
        qh = jnp.concatenate([own, zero] if head == 0 else [zero, own], axis=0)
        scores = dot(keys, qh) * 0.125 + bias_ref[...]
        top = jnp.max(scores, axis=0, keepdims=True)
        expo = jnp.exp(scores - top)
        total = jnp.sum(expo, axis=0, keepdims=True)
        probs = (expo * (1.0 / total)).astype(BF16)
        p_ref[0, head] = probs
        ot_ref[pl.ds(head * half, half), :] = dot(vt[head * half : (head + 1) * half], probs).astype(BF16)
    o_ref[...] = ot_ref[...].T


def attend(qkv, segment, pair=128):
    seqs, length = segment.shape
    width = qkv.shape[1] // 3
    pairs = width // pair
    row = segment.reshape(seqs, 1, length)
    col = segment.reshape(seqs, length, 1)
    spec = lambda part: pl.BlockSpec((length, pair), lambda s, p: (s, part * pairs + p))
    return pl.pallas_call(
        attend_kernel,
        out_shape=(
            jax.ShapeDtypeStruct((seqs * length, width), BF16),
            jax.ShapeDtypeStruct((width, seqs * length), BF16),
            jax.ShapeDtypeStruct((seqs, 2 * pairs, length, length), BF16),
        ),
        grid=(seqs, pairs),
        in_specs=[
            spec(0),
            spec(1),
            spec(2),
            pl.BlockSpec((1, 1, length), lambda s, p: (s, 0, 0)),
            pl.BlockSpec((1, length, 1), lambda s, p: (s, 0, 0)),
        ],
        out_specs=(
            pl.BlockSpec((length, pair), lambda s, p: (s, p)),
            pl.BlockSpec((pair, length), lambda s, p: (p, s)),
            pl.BlockSpec((1, 2, length, length), lambda s, p: (s, p, 0, 0)),
        ),
        scratch_shapes=[pltpu.VMEM((length, length), F32)],
        compiler_params=params("arbitrary", "arbitrary"),
        cost_estimate=cost(8 * seqs * length * length * width, 20e6, seqs * length * length * 16),
        name="attend",
    )(qkv, qkv, qkv, row, col)


def attend_back_kernel(q_ref, k_ref, v_ref, ot_ref, p_ref, do_ref, d_ref, bq_ref, bv_ref):
    pair = q_ref.shape[1]
    half = pair // 2
    length = q_ref.shape[0]
    do = do_ref[...]
    dot_t = do.T
    q = q_ref[...]
    kt = k_ref[...].T
    v = v_ref[...]
    product = dot_t.astype(F32) * ot_ref[...].astype(F32)
    zero = jnp.zeros((half, length), BF16)
    first = lax.broadcasted_iota(jnp.int32, (1, pair), 1) < half
    dk, dv, dqt = [], [], []
    for head in range(2):
        here = slice(head * half, (head + 1) * half)
        delta = jnp.sum(product[here], axis=0, keepdims=True)
        own = dot_t[here]
        dh = jnp.concatenate([own, zero] if head == 0 else [zero, own], axis=0)
        probs = p_ref[0, head]
        ds = (probs.astype(F32) * (dot(v, dh) - delta)).astype(BF16)
        dv.append(dot(probs, do))
        dk.append(dot(ds, q))
        dqt.append(dot(kt[here], ds))
    dv = jnp.where(first, dv[0], dv[1]).astype(BF16)
    dk = (jnp.where(first, dk[0], dk[1]) * 0.125).astype(BF16)
    dq = (jnp.concatenate(dqt, axis=0) * 0.125).astype(BF16).T
    d_ref[0] = dq
    d_ref[1] = dk
    d_ref[2] = dv
    sum_q = jnp.sum(dq.astype(F32), axis=0, keepdims=True)
    sum_v = jnp.sum(dv.astype(F32), axis=0, keepdims=True)
    bq_ref[0] = sum_q
    bv_ref[0] = sum_v


def attend_back(qkv, ot, probs, do, seqs, part, pair=128):
    tokens, width = do.shape[0], qkv.shape[1] // 3
    length = tokens // seqs
    pairs = width // pair
    spec = lambda part: pl.BlockSpec((length, pair), lambda s, p: (s, part * pairs + p))
    sums = pl.BlockSpec((1, 1, pair), lambda s, p: (s, 0, p))
    return pl.pallas_call(
        attend_back_kernel,
        out_shape=(jax.ShapeDtypeStruct((3, tokens, width), BF16),)
        + (jax.ShapeDtypeStruct((seqs, 1, width), F32),) * 2,
        grid=(seqs, pairs),
        in_specs=[
            spec(0),
            spec(1),
            spec(2),
            pl.BlockSpec((pair, length), lambda s, p: (p, s)),
            pl.BlockSpec((1, 2, length, length), lambda s, p: (s, p, 0, 0)),
            pl.BlockSpec((length, pair), lambda s, p: (s, part * pairs + p)),
        ],
        out_specs=(pl.BlockSpec((3, length, pair), lambda s, p: (0, s, p)), sums, sums),
        compiler_params=params("arbitrary", "arbitrary"),
        cost_estimate=cost(16 * seqs * length * length * width, 30e6),
        name="attend_back",
    )(qkv, qkv, qkv, ot, probs, do)


def normed(z):
    center = z - jnp.mean(z, axis=-1, keepdims=True)
    rstd = lax.rsqrt(jnp.mean(center * center, axis=-1, keepdims=True) + 1e-06)
    return center * rstd, rstd


def norm_back(dn, n, rstd):
    return rstd * (dn - jnp.mean(dn, axis=-1, keepdims=True) - n * jnp.mean(dn * n, axis=-1, keepdims=True))


def join_kernel(o0_ref, o1_ref, w_ref, x_ref, b_ref, g_ref, s_ref, n_ref, r_ref, h_ref, ht_ref):
    half = o0_ref.shape[1]
    mixed = dot(o0_ref[...], w_ref[:half]) + dot(o1_ref[...], w_ref[half:])
    z = x_ref[...].astype(F32) + (mixed + b_ref[...])
    n, rstd = normed(z)
    n_ref[...] = n
    r_ref[...] = rstd
    h = (n * g_ref[...] + s_ref[...]).astype(BF16)
    h_ref[...] = h
    ht_ref[...] = h.T


def join(o0, o1, w, x, bias, gain, shift, tile=256):
    rows, width = x.shape
    tok = pl.BlockSpec((tile, width), lambda i: (i, 0))
    half = pl.BlockSpec((tile, width // 2), lambda i: (i, 0))
    vec = whole((1, width))
    return pl.pallas_call(
        join_kernel,
        out_shape=(
            jax.ShapeDtypeStruct((rows, width), F32),
            jax.ShapeDtypeStruct((rows, 1), F32),
            jax.ShapeDtypeStruct((rows, width), BF16),
            jax.ShapeDtypeStruct((width, rows), BF16),
        ),
        grid=(rows // tile,),
        in_specs=[half, half, whole((width, width)), tok, vec, vec, vec],
        out_specs=(tok, pl.BlockSpec((tile, 1), lambda i: (i, 0)), tok, pl.BlockSpec((width, tile), lambda i: (0, i))),
        compiler_params=params("arbitrary"),
        cost_estimate=cost(2 * rows * width * width, 16 * rows * width),
        name="join",
    )(o0, o1, w, x, bias, gain, shift)


def gelu_pair(f):
    size = jnp.abs(f)
    t = 1.0 / (1.0 + (0.3275911 / math.sqrt(2.0)) * size)
    bell = jnp.exp(-0.5 * (f * f))
    poly = t * (0.127414796 + t * (-0.142248368 + t * (0.7107068705 + t * (-0.7265760135 + t * 0.5307027145))))
    tail = poly * bell
    weight = jnp.where(f < 0, tail, 1.0 - tail)
    return f * weight, weight + f * (bell * (1.0 / math.sqrt(2.0 * math.pi)))


def inner_kernel(h_ref, w_ref, b_ref, u_ref, g_ref):
    f = dot(h_ref[...], w_ref[...]) + b_ref[...]
    u, slope = gelu_pair(f)
    u_ref[...] = u.astype(BF16)
    g_ref[...] = slope.astype(BF16)


def inner(h, w, bias, tile=512):
    rows, depth = h.shape
    cols = w.shape[1]
    out = pl.BlockSpec((rows, tile), lambda i: (0, i))
    return pl.pallas_call(
        inner_kernel,
        out_shape=(jax.ShapeDtypeStruct((rows, cols), BF16),) * 2,
        grid=(cols // tile,),
        in_specs=[whole((rows, depth)), pl.BlockSpec((depth, tile), lambda i: (0, i)), pl.BlockSpec((1, tile), lambda i: (0, i))],
        out_specs=(out, out),
        compiler_params=params("arbitrary"),
        cost_estimate=cost(2 * rows * depth * cols, 2 * (depth * cols + 2 * rows * cols), 2 * rows * cols),
        name="inner",
    )(h, w, bias)


def outer_kernel(u_ref, w_ref, n_ref, c_ref, b_ref, g1_ref, s1_ref, g2_ref, s2_ref, out_ref, dz_ref, dm_ref, dmt_ref, sums_ref):
    @pl.when(pl.program_id(0) == 0)
    def _():
        sums_ref[...] = jnp.zeros_like(sums_ref)

    z = (n_ref[...] * g1_ref[...] + s1_ref[...]) + (dot(u_ref[...], w_ref[...]) + b_ref[...])
    n, rstd = normed(z)
    out_ref[...] = (n * g2_ref[...] + s2_ref[...]).astype(BF16)
    c = c_ref[...].astype(F32)
    dz = norm_back(c * g2_ref[...], n, rstd)
    dz_ref[...] = dz
    dm = dz.astype(BF16)
    dm_ref[...] = dm
    dmt_ref[...] = dm.T
    sums_ref[0:1, :] += jnp.sum(c * n, axis=0, keepdims=True)
    sums_ref[1:2, :] += jnp.sum(c, axis=0, keepdims=True)
    sums_ref[2:3, :] += jnp.sum(dm.astype(F32), axis=0, keepdims=True)


def outer(u, w, n1, cot, bias, gain1, shift1, gain2, shift2, tile=256):
    rows, depth = u.shape
    width = w.shape[1]
    tok = pl.BlockSpec((tile, width), lambda i: (i, 0))
    vec = whole((1, width))
    return pl.pallas_call(
        outer_kernel,
        out_shape=(
            jax.ShapeDtypeStruct((rows, width), BF16),
            jax.ShapeDtypeStruct((rows, width), F32),
            jax.ShapeDtypeStruct((rows, width), BF16),
            jax.ShapeDtypeStruct((width, rows), BF16),
            jax.ShapeDtypeStruct((8, width), F32),
        ),
        grid=(rows // tile,),
        in_specs=[pl.BlockSpec((tile, depth), lambda i: (i, 0)), whole((depth, width)), tok, tok, vec, vec, vec, vec, vec],
        out_specs=(tok, tok, tok, pl.BlockSpec((width, tile), lambda i: (0, i)), whole((8, width))),
        compiler_params=params("arbitrary"),
        cost_estimate=cost(2 * rows * depth * width, 2 * (rows * depth + depth * width) + 20 * rows * width),
        name="outer",
    )(u, w, n1, cot, bias, gain1, shift1, gain2, shift2)


def outer_grad_kernel(half_ref, left_ref, right_ref, out_ref):
    made = dot(left_ref[...], right_ref[...]).astype(BF16)
    halves, blocks, rows, part = out_ref.shape
    for i in range(blocks):
        out_ref[:, i] = made[:, i * part : (i + 1) * part].reshape(halves, rows, part)


def outer_grad(half, dmt, u, groups):
    width, rows = dmt.shape
    cols = u.shape[1]
    part = cols // groups
    blocks = max(1, 512 // part)
    return pl.pallas_call(
        outer_grad_kernel,
        out_shape=jax.ShapeDtypeStruct((2, groups, width // 4, part), BF16),
        grid_spec=pltpu.PrefetchScalarGridSpec(
            num_scalar_prefetch=1,
            grid=(groups // blocks,),
            in_specs=[
                pl.BlockSpec((width // 2, rows), lambda i, half: (half[0], 0)),
                pl.BlockSpec((rows, blocks * part), lambda i, half: (0, i)),
            ],
            out_specs=pl.BlockSpec((2, blocks, width // 4, part), lambda i, half: (0, i, 0, 0)),
        ),
        compiler_params=params("arbitrary"),
        cost_estimate=cost(rows * width * cols, 2 * rows * (width + cols) + width * cols),
        name="outer_grad",
    )(half, dmt, u)


def inner_back_kernel(half_ref, dm_ref, w2_ref, g_ref, ht_ref, w1_ref, dh0_ref, dw_ref, dh_ref, sum_ref):
    @pl.when(pl.program_id(0) == 0)
    def _():
        dh_ref[...] = dh0_ref[...]

    df = (dot_nt(dm_ref[...], w2_ref[...]) * g_ref[...].astype(F32)).astype(BF16)
    sum_ref[...] = jnp.sum(df.astype(F32), axis=0, keepdims=True)
    dw_ref[...] = dot(ht_ref[...], df).astype(BF16).reshape(dw_ref.shape)
    dh_ref[...] += dot_nt(df, w1_ref[...])


def inner_back(half, dm, w2, slope, ht, w1, dh, groups, tile=512):
    rows, width = dm.shape
    cols = slope.shape[1]
    steps = cols // 2 // tile
    per = steps // 2
    at = lambda i, half: half[0] * steps + i
    return pl.pallas_call(
        inner_back_kernel,
        out_shape=(
            jax.ShapeDtypeStruct((2, groups, width // groups, cols // 4), BF16),
            jax.ShapeDtypeStruct((rows, width), F32),
            jax.ShapeDtypeStruct((1, cols // 2), F32),
        ),
        grid_spec=pltpu.PrefetchScalarGridSpec(
            num_scalar_prefetch=1,
            grid=(steps,),
            in_specs=[
                pl.BlockSpec((rows, width), lambda i, half: (0, 0)),
                pl.BlockSpec((tile, width), lambda i, half: (at(i, half), 0)),
                pl.BlockSpec((rows, tile), lambda i, half: (0, at(i, half))),
                pl.BlockSpec((width, rows), lambda i, half: (0, 0)),
                pl.BlockSpec((width, tile), lambda i, half: (0, at(i, half))),
                pl.BlockSpec((rows, width), lambda i, half: (0, 0)),
            ],
            out_specs=(
                pl.BlockSpec((1, groups, width // groups, tile), lambda i, half: (i // per, 0, 0, i % per)),
                pl.BlockSpec((rows, width), lambda i, half: (0, 0)),
                pl.BlockSpec((1, tile), lambda i, half: (0, i)),
            ),
        ),
        compiler_params=params("arbitrary"),
        cost_estimate=cost(3 * rows * width * cols, 3 * width * cols + rows * cols + 12 * rows * width),
        name="inner_back",
    )(half, dm, w2, slope, ht, w1, dh)


def mix_grad_kernel(half_ref, left0_ref, left1_ref, right_ref, out_ref):
    for i, left_ref in enumerate((left0_ref, left1_ref)):
        made = dot(left_ref[...], right_ref[...]).astype(BF16)
        groups = out_ref.shape[1] // 2
        shape = (groups,) + out_ref.shape[2:]
        for x in range(2):
            cols = out_ref.shape[3]
            out_ref[x, i * groups : (i + 1) * groups] = made[:, x * cols : (x + 1) * cols].reshape(shape)


def mix_grad(half, ot0, ot1, da, groups):
    rows, width = da.shape
    left = pl.BlockSpec((width // 2, rows), lambda i, half: (0, 0))
    return pl.pallas_call(
        mix_grad_kernel,
        out_shape=jax.ShapeDtypeStruct((2, groups, width // groups, width // 4), BF16),
        grid_spec=pltpu.PrefetchScalarGridSpec(
            num_scalar_prefetch=1,
            grid=(1,),
            in_specs=[left, left, pl.BlockSpec((rows, width // 2), lambda i, half: (0, half[0]))],
            out_specs=pl.BlockSpec((2, groups, width // groups, width // 4), lambda i, half: (0, 0, 0, 0)),
        ),
        compiler_params=params("arbitrary"),
        cost_estimate=cost(rows * width * width, 5 * width * width),
        name="mix_grad",
    )(half, ot0, ot1, da)


def token_weights_grad_kernel(half_ref, left_ref, right_ref, *refs):
    out_ref = refs[-1]
    rows = left_ref.shape[0] // out_ref.shape[1]
    cols = right_ref.shape[2] // 2
    shape = (out_ref.shape[1], rows, cols)
    for which in range(3):
        made = dot(left_ref[...], right_ref[which]).astype(BF16)
        for x in range(2):
            out_ref[x, :, :rows, which * cols : (which + 1) * cols] = made[:, x * cols : (x + 1) * cols].reshape(shape)
    for extra_ref in refs[:-1]:
        for x in range(2):
            out_ref[x, :, rows:, :] = extra_ref[...]


def token_weights_grad(half, xt, d, groups, *extra):
    width, rows = xt.shape
    part = d.shape[2] // 2
    cols = 3 * part // 2
    more = sum(e.shape[1] for e in extra)
    return pl.pallas_call(
        token_weights_grad_kernel,
        out_shape=jax.ShapeDtypeStruct((2, groups, width // groups + more, cols), BF16),
        grid_spec=pltpu.PrefetchScalarGridSpec(
            num_scalar_prefetch=1,
            grid=(1,),
            in_specs=[
                pl.BlockSpec((width, rows), lambda i, half: (0, 0)),
                pl.BlockSpec((3, rows, part), lambda i, half: (0, 0, half[0])),
            ]
            + [pl.BlockSpec(e.shape, lambda i, half: (0, 0, 0)) for e in extra],
            out_specs=pl.BlockSpec((2, groups, width // groups + more, cols), lambda i, half: (0, 0, 0, 0)),
        ),
        compiler_params=params("arbitrary"),
        cost_estimate=cost(6 * rows * width * part, 2 * width * rows + 12 * rows * part),
        name="token_weights_grad",
    )(half, xt, d, *extra)


def join_back_kernel(dz2_ref, dh_ref, n_ref, r_ref, g_ref, w_ref, dz_ref, da_ref, do_ref, sums_ref):
    @pl.when(pl.program_id(0) == 0)
    def _():
        sums_ref[...] = jnp.zeros_like(sums_ref)

    dh = dz2_ref[...] + dh_ref[...]
    n = n_ref[...]
    dz = norm_back(dh * g_ref[...], n, r_ref[...])
    dz_ref[...] = dz
    da = dz.astype(BF16)
    da_ref[...] = da
    do_ref[...] = dot_nt(da, w_ref[...]).astype(BF16)
    sums_ref[0:1, :] += jnp.sum(dh * n, axis=0, keepdims=True)
    sums_ref[1:2, :] += jnp.sum(dh, axis=0, keepdims=True)
    sums_ref[2:3, :] += jnp.sum(da.astype(F32), axis=0, keepdims=True)


def join_back(dz2, dh, n1, rstd, gain, w, tile=256):
    rows, width = dz2.shape
    tok = pl.BlockSpec((tile, width), lambda i: (i, 0))
    return pl.pallas_call(
        join_back_kernel,
        out_shape=(
            jax.ShapeDtypeStruct((rows, width), F32),
            jax.ShapeDtypeStruct((rows, width), BF16),
            jax.ShapeDtypeStruct((rows, width), BF16),
            jax.ShapeDtypeStruct((8, width), F32),
        ),
        grid=(rows // tile,),
        in_specs=[tok, tok, tok, pl.BlockSpec((tile, 1), lambda i: (i, 0)), whole((1, width)), whole((width, width))],
        out_specs=(tok, tok, tok, whole((8, width))),
        compiler_params=params("arbitrary"),
        cost_estimate=cost(2 * rows * width * width, 22 * rows * width),
        name="join_back",
    )(dz2, dh, n1, rstd, gain, w)


def token_grad_kernel(dz_ref, d0_ref, d1_ref, w0_ref, w1_ref, out_ref):
    width = d0_ref.shape[2]
    total = dz_ref[...]
    for d_ref, w_ref in ((d0_ref, w0_ref), (d1_ref, w1_ref)):
        for i in range(3):
            total = total + dot_nt(d_ref[i], w_ref[:, i * width : (i + 1) * width])
    out_ref[...] = total.astype(BF16)


def token_grad(dz, d0, d1, w0, w1, tile=256):
    rows, width = dz.shape
    tok = pl.BlockSpec((tile, width), lambda i: (i, 0))
    part = pl.BlockSpec((3, tile, width // 2), lambda i: (0, i, 0))
    weight = whole((width, 3 * width // 2))
    return pl.pallas_call(
        token_grad_kernel,
        out_shape=jax.ShapeDtypeStruct((rows, width), BF16),
        grid=(rows // tile,),
        in_specs=[tok, part, part, weight, weight],
        out_specs=tok,
        compiler_params=params("arbitrary"),
        cost_estimate=cost(6 * rows * width * width, 18 * rows * width),
        name="token_grad",
    )(dz, d0, d1, w0, w1)


def digits_of(axis, total, base):
    digits, stride = [], total
    while stride > 1:
        size = base if stride % base == 0 else 2
        stride //= size
        digits.append((axis, stride, size))
    return digits


class Layout:
    def __init__(self, mesh):
        self.replicas, self.groups = mesh.shape["replica"], mesh.shape["group"]
        self.group = digits_of("group", self.groups, 4)
        replica = digits_of("replica", self.replicas, 2)
        self.core, self.over = replica[-1], replica[:-1]
        self.sizes = {"replica": self.replicas, "group": self.groups}
        self.devices = self.replicas * self.groups

    def place(self, digit):
        axis, stride, size = digit
        return (lax.axis_index(axis) // stride) % size

    def send(self, value, digit, shift):
        axis, stride, size = digit
        pairs = []
        for i in range(self.sizes[axis]):
            own = (i // stride) % size
            pairs.append((i, i + ((own + shift) % size - own) * stride))
        return lax.ppermute(value, axis, pairs)

    def gather(self, value, order):
        value = value[None]
        for digit in order:
            value = jnp.concatenate([value] + [self.send(value, digit, k) for k in range(1, digit[2])], axis=0)
        return value

    def places(self, order):
        total = jnp.zeros((1,), jnp.int32)
        for axis, stride, size in order:
            own = self.place((axis, stride, size))
            weight = stride * (self.groups if axis == "replica" else 1)
            source = (own - jnp.arange(size, dtype=jnp.int32) + size) % size
            total = (source[:, None] * weight + total[None, :]).reshape(-1)
        return total

    def scatter(self, terms, order):
        dims = self.over + self.group
        for digit in order:
            axis = dims.index(digit)
            dims = dims[:axis] + dims[axis + 1 :]
            size, own = digit[2], self.place(digit)
            pick = lambda at: [lax.dynamic_index_in_dim(t, at, axis, keepdims=False) for t in terms]
            came = [self.send(total_of(pick((own + k) % size)), digit, k) for k in range(1, size)]
            terms = pick(own) + came
        return total_of(terms)

    def spread(self, block):
        for digit in self.over[::-1] + [self.core]:
            came = self.send(block, digit, 1)
            own = self.place(digit)
            block = jnp.where(own == 0, jnp.stack([block, came]), jnp.stack([came, block]))
        return block


def total_of(terms):
    total = terms[0].astype(F32)
    for term in terms[1:]:
        total = total + term.astype(F32)
    return total.astype(BF16)


def local(layout, tokens, segment_ids, w_query, b_query, w_key, w_value, b_value, w_out, b_out, gain_first, shift_first, w_inner, b_inner, w_outer, b_outer, gain_second, shift_second, cotangent):
    groups, devices = layout.groups, layout.devices
    seqs = segment_ids.shape[0]
    width = tokens.shape[1]
    rows = w_query.shape[0]
    each = b_query.shape[0]
    lanes = 128
    half_width = width // 2
    core = layout.place(layout.core).astype(jnp.int32)
    mine, theirs = core.reshape(1), (1 - core).reshape(1)

    both = ("replica", "group")
    whole_wouter = lax.all_gather(w_outer, both, axis=0, tiled=True)
    whole_rest = lax.all_gather(jnp.concatenate([w_inner, w_out], axis=1), both, axis=0, tiled=True)
    whole_winner, whole_wout = whole_rest[:, : w_inner.shape[1]], whole_rest[:, w_inner.shape[1] :]
    vectors = (b_query, b_value, b_out, gain_first, shift_first, b_outer, gain_second, shift_second)
    small = jnp.concatenate(vectors + (b_inner,))
    small = jnp.pad(small, (0, rows * lanes - small.shape[0])).reshape(rows, lanes)
    parts = [jnp.concatenate([w[:, i * half_width : (i + 1) * half_width] for w in (w_query, w_key, w_value)], axis=1) for i in range(2)]
    z_first = layout.group[:1] + layout.over + layout.group[1:] + [layout.core]
    z_last = layout.group[:1] + layout.group[1:] + layout.over + [layout.core]
    came0 = layout.gather(jnp.concatenate([parts[0], small], axis=1), z_first)
    came1 = layout.gather(parts[1], z_last)
    place0, place1 = layout.places(z_first), layout.places(z_last)
    count = sum(v.shape[0] for v in vectors) + b_inner.shape[0]
    chosen = (place0[None, :] == jnp.arange(devices, dtype=jnp.int32)[:, None]).astype(BF16)
    small = dot(chosen, came0[:, :, 3 * half_width :].reshape(devices, -1)[:, :count])
    vec = small[:, : 8 * each].reshape(devices, 8, each).transpose(1, 0, 2).reshape(8, 1, width)
    whole_binner = small[:, 8 * each :].reshape(1, -1)
    bias = [jnp.concatenate([vec[0, :, at], jnp.zeros((1, half_width), F32), vec[1, :, at]], axis=1) for at in (slice(0, half_width), slice(half_width, None))]
    if rows % 16:
        came0, came1 = came0[jnp.argsort(place0)].reshape(1, width, -1), came1[jnp.argsort(place1)].reshape(1, width, -1)
        place0 = place1 = jnp.zeros((1,), jnp.int32)

    xt = transposed(tokens)
    qkv0, wqkv0 = project(place0, tokens, came0, bias[0])
    o0, ot0, probs0 = attend(qkv0, segment_ids)
    qkv1, wqkv1 = project(place1, tokens, came1, bias[1])
    o1, ot1, probs1 = attend(qkv1, segment_ids)
    n1, rstd1, h, ht = join(o0, o1, whole_wout, tokens, vec[2], vec[3], vec[4])
    u, slope = inner(h, whole_winner, whole_binner)
    out, dz2, dm, dmt, sums2 = outer(u, whole_wouter, n1, cotangent, vec[5], vec[3], vec[4], vec[6], vec[7])

    digits = tuple(d[2] for d in layout.group)
    unfold = lambda a: a.reshape((2,) * len(layout.over) + digits + a.shape[2:])

    def reduced(own, other, order):
        came = layout.send(other, layout.core, 1)
        return layout.spread(layout.scatter([unfold(own), unfold(came)], order))

    x_first = layout.over + layout.group[1:] + layout.group[:1]
    y_first = layout.group[1:] + layout.over + layout.group[:1]
    other = outer_grad(theirs, dmt, u, groups)
    own = outer_grad(mine, dmt, u, groups)
    got_wouter = reduced(own, other, x_first)
    other, dh, sum_other = inner_back(theirs, dm, whole_wouter, slope, ht, whole_winner, jnp.zeros_like(dz2), groups)
    own, dh, sum_own = inner_back(mine, dm, whole_wouter, slope, ht, whole_winner, dh, groups)
    got_winner = reduced(own, other, y_first)
    sum_inner = jnp.where(core == 0, jnp.concatenate([sum_own, sum_other], axis=1), jnp.concatenate([sum_other, sum_own], axis=1))
    dz1, da, do, sums1 = join_back(dz2, dh, n1, rstd1, vec[3], whole_wout)
    other = mix_grad(theirs, ot0, ot1, da, groups)
    own = mix_grad(mine, ot0, ot1, da, groups)
    got_wout = reduced(own, other, x_first)
    d0, sq0, sv0 = attend_back(qkv0, ot0, probs0, do, seqs, 0)
    other = token_weights_grad(theirs, xt, d0, groups)
    own = token_weights_grad(mine, xt, d0, groups)
    got_first = reduced(own, other, x_first)
    d1, sq1, sv1 = attend_back(qkv1, ot1, probs1, do, seqs, 1)
    bq = jnp.concatenate([jnp.sum(s, axis=0) for s in (sq0, sq1)], axis=1)
    bv = jnp.concatenate([jnp.sum(s, axis=0) for s in (sv0, sv1)], axis=1)
    sums = jnp.concatenate([bq, bv, sums1[2:3], sums1[0:1], sums1[1:2], sums2[2:3], sums2[0:1], sums2[1:2]], axis=0)
    sums = sums.reshape(8, groups, -1).transpose(1, 0, 2).reshape(groups, -1)
    sums = jnp.concatenate([sums, sum_inner.reshape(groups, -1)], axis=1)
    used = sums.shape[1]
    cols = 3 * width // 8
    extra = jnp.pad(sums.astype(BF16), ((0, 0), (0, 16 * cols - used))).reshape(groups, 16, cols)
    other = token_weights_grad(theirs, xt, d1, groups, extra)
    own = token_weights_grad(mine, xt, d1, groups, extra)
    got_second = reduced(own, other, y_first)
    grad_tokens = token_grad(dz1, d0, d1, wqkv0, wqkv1)

    joined = lambda got: jnp.moveaxis(got, -2, 0).reshape(got.shape[-2], -1).astype(F32)
    grad_wouter = got_wouter.reshape(width, -1).T.astype(F32)
    grad_winner, grad_wout = joined(got_winner), joined(got_wout)
    keep = width // groups
    quarter = half_width // 4
    both_parts = [got_first, got_second[..., :keep, :]]
    wqkv = [jnp.concatenate([joined(g[..., i * quarter : (i + 1) * quarter]) for g in both_parts], axis=1) for i in range(3)]
    sums = got_second[(0,) * (got_second.ndim - 2)][keep:].reshape(-1)[:used].astype(F32)
    bq, bv, bout, gain1, shift1, bouter, gain2, shift2 = (sums[i * keep : (i + 1) * keep] for i in range(8))
    binner = sums[8 * keep :]
    return (out, grad_tokens, wqkv[0], bq, wqkv[1], wqkv[2], bv, grad_wout, bout, gain1, shift1, grad_winner, binner, grad_wouter, bouter, gain2, shift2)


def solution(mesh):
    layout = Layout(mesh)
    both = ("replica", "group")
    rows, vector = P(both, None), P(both)
    in_specs = (rows, rows, rows, vector, rows, rows, vector, rows, vector, vector, vector, rows, vector, rows, vector, vector, vector, rows)
    kept, kept_vector = P("group", None), P("group")
    out_specs = (rows, rows, kept, kept_vector, kept, kept, kept_vector, kept, kept_vector, kept_vector, kept_vector, kept, kept_vector, kept, kept_vector, kept_vector, kept_vector)
    return jax.shard_map(functools.partial(local, layout), mesh=mesh, in_specs=in_specs, out_specs=out_specs, check_vma=False)
```

time: 1550 us -> 570 us (0.37)
  waiting for transfers between devices: 923 us -> 136 us
  matrix products: 270 us -> 0.13 us
  Pallas kernels: 0 us -> 247 us
  blocking collectives: 138 us -> 0 us
  starting transfers between devices: 0.98 us -> 58.1 us
  local copies, waits for them, and re-layouts: 105 us -> 52.3 us
  other arithmetic: 88.1 us -> 49.9 us
    reduce_scatter x6 -> x0, waiting for transfers between devices: 720 us -> none  [the longest x1 283 us: local(): lax.psum_scatter(grad_winner, 'group', scatter_dimension=0, tiled=True)]
    dot_general x32 -> x1, matrix products: 270 us -> 0.13 us  [dot(): lax.dot_general(left, right, (((1,), (0,)), ((), ())), preferred_element_...]
    pallas_call x0 -> x22, Pallas kernels: none -> 247 us  [the longest x2 42.3 us: inner_back(): pl.pallas_call(inner_back_kernel, out_shape=(jax.ShapeDtypeStruct((2, gro...]
    all_gather x6 -> x2, waiting for transfers between devices: 145 us -> 1.3 us  [the longest x1 1.29 us: local(): whole_wouter = lax.all_gather(w_outer, both, axis=0, tiled=True)]
    ppermute x0 -> x52, waiting for transfers between devices: none -> 134 us  [send(): return lax.ppermute(value, axis, pairs)]
    unnamed x2 -> x0, blocking collectives: 68.9 us -> none
    ppermute x0 -> x52, starting transfers between devices: none -> 58.1 us  [send(): return lax.ppermute(value, axis, pairs)]
    all_gather x1 -> x0, blocking collectives: 56.9 us -> none  [local(): lax.all_gather(b_inner, ('replica', 'group'), axis=0, tiled=True)]
  transfers between devices with their start and end apart: 13 -> 54, of which waited for: 8 -> 18; matrix products, arithmetic and copies ran while one was open for 23% -> 16% of each run, Pallas kernels for 0% -> 39%
where the time goes in v1:
time: 570 us; the launch traced here: 559 us
  Pallas kernels  247 us (43%)
  waiting for transfers between devices  136 us (24%)
  starting transfers between devices  58.1 us (10%)
  local copies, waits for them, and re-layouts  52.3 us (9%)
  other arithmetic  49.9 us (9%)
  between operations  15.2 us (3%)
    ppermute x52, waiting for transfers between devices, send(): return lax.ppermute(value, axis, pairs)  134 us
    ppermute x52, starting transfers between devices, send(): return lax.ppermute(value, axis, pairs)  58.1 us
    pallas_call x2, Pallas kernels, inner_back(): pl.pallas_call(inner_back_kernel, out_shape=(jax.ShapeDtypeStruct((2, gro...  42.3 us
    convert_element_type x20, other arithmetic, total_of(): return total.astype(BF16)  38.3 us
    pallas_call x2, Pallas kernels, attend(): pl.pallas_call(attend_kernel, out_shape=(jax.ShapeDtypeStruct((seqs * len...  28.8 us
    pallas_call x2, Pallas kernels, attend_back(): pl.pallas_call(attend_back_kernel, out_shape=(jax.ShapeDtypeStruct((3, to...  27 us
    pallas_call x1, Pallas kernels, inner(): pl.pallas_call(inner_kernel, out_shape=(jax.ShapeDtypeStruct((rows, cols)...  26.1 us
    pallas_call x2, Pallas kernels, outer_grad(): pl.pallas_call(outer_grad_kernel, out_shape=jax.ShapeDtypeStruct((2, grou...  20.9 us
  transfers between devices with their start and end apart: 54, of which 18 were waited for; matrix products, arithmetic and copies ran while one was open for 16% of the time, Pallas kernels for 39%

profile of v1, /device:TPU:9, one launch (start us, length us, event | category | flops | bytes accessed | tf_op | source)
XLA Modules:
  0.0 559.2 jit_solution(12650375242526377147)
XLA Ops:
  15.2 6.1 %concatenate.163 = bf16[384]{0:T(512)(128)(2,1)S(1)} concatenate(bf16[32]{0:T(256)(128)(2,1)} %param.21, bf16[32]{0:T(256)(128)(2,1)} %param.24, bf16[32]{0:T(256)(128)(2,1)} %param.26, bf16[32]{0:T(256)(128)(2,1)} %param.27, bf16[32]{0:T(256)(128)(2,1)} %param.28, bf16[32]{0:T(256)(128)(2,1)} %param.32, bf16[32]{0:T(256)(128)(2,1)} %param.33, bf16[32]{0:T(256)(128)(2,1)} %param.34, ...), dimensions={0} | concatenate | bytes 1536 | tf_op jit(solution)/shard_map/concatenate | solution.py:633
  21.4 3.1 collective-permute-start.1
  29.2 7.2 %collective-permute-done.1 = bf16[1,32,1664]{2,1,0:T(8,128)(2,1)S(1)} collective-permute-done((bf16[1,32,1664]{2,1,0:T(8,128)(2,1)S(1)}, bf16[1,32,1664]{2,1,0:T(8,128)(2,1)S(1)}, u32[]{:S(2)}, u32[]{:S(2)}) %collective-permute-start.1) | collective-permute-done | bytes 106528 | tf_op jit(solution)/shard_map/ppermute | solution.py:574
  36.4 3.9 collective-permute-done.2
  44.7 9.3 %collective-permute-done.3 = bf16[4,32,1664]{2,1,0:T(8,128)(2,1)S(1)} collective-permute-done((bf16[4,32,1664]{2,1,0:T(8,128)(2,1)S(1)}, bf16[4,32,1664]{2,1,0:T(8,128)(2,1)S(1)}, u32[]{:S(2)}, u32[]{:S(2)}) %collective-permute-start.3) | collective-permute-done | bytes 426016 | tf_op jit(solution)/shard_map/ppermute | solution.py:574
  56.0 21.1 %collective-permute-done.10 = bf16[8,32,1536]{2,1,0:T(8,128)(2,1)S(1)} collective-permute-done((bf16[8,32,1536]{2,1,0:T(8,128)(2,1)S(1)}, bf16[8,32,1536]{2,1,0:T(8,128)(2,1)S(1)}, u32[]{:S(2)}, u32[]{:S(2)}) %collective-permute-start.10) | collective-permute-done | bytes 786464 | tf_op jit(solution)/shard_map/ppermute | solution.py:574
  86.1 4.4 transposed.1.left_ref
  99.4 9.6 %project.3 = (bf16[1024,1536]{1,0:T(8,128)(2,1)}, bf16[1024,1536]{1,0:T(8,128)(2,1)}) custom-call(s32[32]{0:T(128)} %add.1237.order_ref, bf16[1024,1024]{1,0:T(8,128)(2,1)} %x_ref.7, bf16[32,32,1536]{2,1,0:T(8,128)(2,1)} %constant_dynamic-update-slice_fusion.29.w_ref, f32[1,1536]{1,0:T(1,128)} %get-tuple-element.170.b_ref), custom_call_target="tpu_custom_call" | custom-call | flops 3221225472 | bytes 8388608 | tf_op jit(solution)/shard_map/project/pallas_call | solution.py:83
  108.9 14.5 %attend.3 = (bf16[1024,512]{1,0:T(8,128)(2,1)}, bf16[512,1024]{1,0:T(8,128)(2,1)}, bf16[2,8,512,512]{3,2,1,0:T(8,128)(2,1)}) custom-call(bf16[1024,1536]{1,0:T(8,128)(2,1)} %get-tuple-element.56.q_ref.k_ref.v_ref, bf16[1024,1536]{1,0:T(8,128)(2,1)} %get-tuple-element.56.q_ref.k_ref.v_ref, bf16[1024,1536]{1,0:T(8,128)(2,1)} %get-tuple-element.56.q_ref.k_ref.v_ref, ...), custom_call_target="tpu_custom_call" | custom-call | flops 2147483648 | bytes 20000000 | tf_op jit(solution)/shard_map/attend/pallas_call | solution.py:133
  123.4 9.5 %project.2 = (bf16[1024,1536]{1,0:T(8,128)(2,1)}, bf16[1024,1536]{1,0:T(8,128)(2,1)}) custom-call(s32[32]{0:T(128)} %copy-done.17, bf16[1024,1024]{1,0:T(8,128)(2,1)} %x_ref.7, bf16[32,32,1664]{2,1,0:T(8,128)(2,1)} %copy-done.8, f32[1,1536]{1,0:T(1,128)} %get-tuple-element.171.b_ref), custom_call_target="tpu_custom_call" | custom-call | flops 3221225472 | bytes 8388608 | tf_op jit(solution)/shard_map/project/pallas_call | solution.py:83
  132.9 14.3 %attend.2 = (bf16[1024,512]{1,0:T(8,128)(2,1)}, bf16[512,1024]{1,0:T(8,128)(2,1)}, bf16[2,8,512,512]{3,2,1,0:T(8,128)(2,1)}) custom-call(bf16[1024,1536]{1,0:T(8,128)(2,1)} %get-tuple-element.54.q_ref.k_ref.v_ref, bf16[1024,1536]{1,0:T(8,128)(2,1)} %get-tuple-element.54.q_ref.k_ref.v_ref, bf16[1024,1536]{1,0:T(8,128)(2,1)} %get-tuple-element.54.q_ref.k_ref.v_ref, ...), custom_call_target="tpu_custom_call" | custom-call | flops 2147483648 | bytes 20000000 | tf_op jit(solution)/shard_map/attend/pallas_call | solution.py:133
  147.2 3.1 slice.202.w_ref
  150.3 7.8 %slice.206.w_ref.w1_ref = bf16[1024,4096]{1,0:T(8,128)(2,1)} slice(bf16[1024,5120]{1,0:T(8,128)(2,1)} %all-gather.3.cloned.1.call-done), slice={[0:1024], [0:4096]} | slice | bytes 16777216 | tf_op jit(solution)/shard_map/slice | solution.py:631
  158.1 8.6 %join.1 = (f32[1024,1024]{1,0:T(8,128)}, f32[1024,1]{1,0:T(8,128)}, bf16[1024,1024]{1,0:T(8,128)(2,1)}, bf16[1024,1024]{1,0:T(8,128)(2,1)}) custom-call(bf16[1024,512]{1,0:T(8,128)(2,1)} %get-tuple-element.55.o0_ref, bf16[1024,512]{1,0:T(8,128)(2,1)} %get-tuple-element.57.o1_ref, bf16[1024,1024]{1,0:T(8,128)(2,1)} %slice.202.w_ref, ...), custom_call_target="tpu_custom_call" | custom-call | flops 2147483648 | bytes 16777216 | tf_op jit(solution)/shard_map/join/pallas_call | solution.py:248
  166.7 26.1 %inner.1 = (bf16[1024,4096]{1,0:T(8,128)(2,1)}, bf16[1024,4096]{1,0:T(8,128)(2,1)}) custom-call(bf16[1024,1024]{1,0:T(8,128)(2,1)} %get-tuple-element.58.h_ref, bf16[1024,4096]{1,0:T(8,128)(2,1)} %slice.206.w_ref.w1_ref, f32[1,4096]{1,0:T(1,128)} %bitcast.367), custom_call_target="tpu_custom_call" | custom-call | flops 8589934592 | bytes 25165824 | tf_op jit(solution)/shard_map/inner/pallas_call | solution.py:286
  194.1 19.5 %outer.1 = (bf16[1024,1024]{1,0:T(8,128)(2,1)}, f32[1024,1024]{1,0:T(8,128)}, bf16[1024,1024]{1,0:T(8,128)(2,1)}, bf16[1024,1024]{1,0:T(8,128)(2,1)}, f32[8,1024]{1,0:T(8,128)}) custom-call(bf16[1024,4096]{1,0:T(8,128)(2,1)} %get-tuple-element.59.u_ref.right_ref, bf16[4096,1024]{1,0:T(8,128)(2,1)} %all-gather.5.cloned.1.call-done.w_ref.w2_ref, ...), custom_call_target="tpu_custom_call" | custom-call | flops 8589934592 | bytes 37748736 | tf_op jit(solution)/shard_map/outer/pallas_call | solution.py:322
  213.6 10.4 %outer_grad.3 = bf16[2,8,256,512]{3,2,1,0:T(8,128)(2,1)} custom-call(s32[1]{0:T(128)} %bitcast.11.half_ref, bf16[1024,1024]{1,0:T(8,128)(2,1)} %get-tuple-element.90.left_ref, bf16[1024,4096]{1,0:T(8,128)(2,1)} %get-tuple-element.59.u_ref.right_ref), custom_call_target="tpu_custom_call" | custom-call | flops 4294967296 | bytes 14680064 | tf_op jit(solution)/shard_map/outer_grad/pallas_call | solution.py:352
  226.7 21.2 %inner_back.2 = (bf16[2,8,128,1024]{3,2,1,0:T(8,128)(2,1)}, f32[1024,1024]{1,0:T(8,128)}, f32[1,2048]{1,0:T(1,128)}) custom-call(s32[1]{0:T(128)} %bitcast.11.half_ref, bf16[1024,1024]{1,0:T(8,128)(2,1)} %get-tuple-element.63.dm_ref, bf16[4096,1024]{1,0:T(8,128)(2,1)} %all-gather.5.cloned.1.call-done.w_ref.w2_ref, ...), custom_call_target="tpu_custom_call" | custom-call | flops 12884901888 | bytes 29360128 | tf_op jit(solution)/shard_map/inner_back/pallas_call | solution.py:387
  248.2 21.1 %inner_back.3 = (bf16[2,8,128,1024]{3,2,1,0:T(8,128)(2,1)}, f32[1024,1024]{1,0:T(8,128)}, f32[1,2048]{1,0:T(1,128)}) custom-call(s32[1]{0:T(128)} %bitcast.10.half_ref, bf16[1024,1024]{1,0:T(8,128)(2,1)} %get-tuple-element.63.dm_ref, bf16[4096,1024]{1,0:T(8,128)(2,1)} %all-gather.5.cloned.1.call-done.w_ref.w2_ref, ...), custom_call_target="tpu_custom_call" | custom-call | flops 12884901888 | bytes 29360128 | tf_op jit(solution)/shard_map/inner_back/pallas_call | solution.py:387
  269.4 10.3 %join_back.1 = (f32[1024,1024]{1,0:T(8,128)}, bf16[1024,1024]{1,0:T(8,128)(2,1)}, bf16[1024,1024]{1,0:T(8,128)(2,1)}, f32[8,1024]{1,0:T(8,128)}) custom-call(f32[1024,1024]{1,0:T(8,128)} %get-tuple-element.62.dz2_ref, f32[1024,1024]{1,0:T(8,128)} %get-tuple-element.67.dh_ref, f32[1024,1024]{1,0:T(8,128)} %get-tuple-element.60.n_ref, ...), custom_call_target="tpu_custom_call" | custom-call | flops 2147483648 | bytes 23068672 | tf_op jit(solution)/shard_map/join_back/pallas_call | solution.py:503
  279.7 4.1 mix_grad.3
  284.0 13.5 %attend_back.2 = (bf16[3,1024,512]{2,1,0:T(8,128)(2,1)}, f32[2,1,512]{2,1,0:T(1,128)}, f32[2,1,512]{2,1,0:T(1,128)}) custom-call(bf16[1024,1536]{1,0:T(8,128)(2,1)} %get-tuple-element.54.q_ref.k_ref.v_ref, bf16[1024,1536]{1,0:T(8,128)(2,1)} %get-tuple-element.54.q_ref.k_ref.v_ref, bf16[1024,1536]{1,0:T(8,128)(2,1)} %get-tuple-element.54.q_ref.k_ref.v_ref, ...), custom_call_target="tpu_custom_call" | custom-call | flops 4294967296 | bytes 30000000 | tf_op jit(solution)/shard_map/attend_back/pallas_call | solution.py:201
  297.6 5.0 token_weights_grad.5
  302.8 13.4 %attend_back.3 = (bf16[3,1024,512]{2,1,0:T(8,128)(2,1)}, f32[2,1,512]{2,1,0:T(1,128)}, f32[2,1,512]{2,1,0:T(1,128)}) custom-call(bf16[1024,1536]{1,0:T(8,128)(2,1)} %get-tuple-element.56.q_ref.k_ref.v_ref, bf16[1024,1536]{1,0:T(8,128)(2,1)} %get-tuple-element.56.q_ref.k_ref.v_ref, bf16[1024,1536]{1,0:T(8,128)(2,1)} %get-tuple-element.56.q_ref.k_ref.v_ref, ...), custom_call_target="tpu_custom_call" | custom-call | flops 4294967296 | bytes 30000000 | tf_op jit(solution)/shard_map/attend_back/pallas_call | solution.py:201
  318.7 5.1 token_weights_grad.7
  324.1 4.1 mix_grad.2
  331.3 5.1 token_weights_grad.4
  336.3 7.4 %collective-permute-done.29 = bf16[4,2,128,256]{3,2,1,0:T(8,128)(2,1)} collective-permute-done((bf16[4,2,128,256]{3,2,1,0:T(8,128)(2,1)}, bf16[4,2,128,256]{3,2,1,0:T(8,128)(2,1)}, u32[]{:S(2)}, u32[]{:S(2)}) %collective-permute-start.29) | collective-permute-done | bytes 524320 | tf_op jit(solution)/shard_map/ppermute | solution.py:574
  346.0 2.8 fusion.6
  349.1 10.4 %outer_grad.2 = bf16[2,8,256,512]{3,2,1,0:T(8,128)(2,1)} custom-call(s32[1]{0:T(128)} %bitcast.10.half_ref, bf16[1024,1024]{1,0:T(8,128)(2,1)} %get-tuple-element.90.left_ref, bf16[1024,4096]{1,0:T(8,128)(2,1)} %get-tuple-element.59.u_ref.right_ref), custom_call_target="tpu_custom_call" | custom-call | flops 4294967296 | bytes 14680064 | tf_op jit(solution)/shard_map/outer_grad/pallas_call | solution.py:352
  361.9 5.2 token_weights_grad.6
  368.9 2.6 fusion.4
  376.5 3.7 fusion.1
  380.8 3.9 fusion
  385.5 11.8 %token_grad.1 = bf16[1024,1024]{1,0:T(8,128)(2,1)} custom-call(f32[1024,1024]{1,0:T(8,128)} %get-tuple-element.69.dz_ref, bf16[3,1024,512]{2,1,0:T(8,128)(2,1)} %get-tuple-element.73.d0_ref.right_ref, bf16[3,1024,512]{2,1,0:T(8,128)(2,1)} %get-tuple-element.76.d1_ref.right_ref, bf16[1024,1536]{1,0:T(8,128)(2,1)} %get-tuple-element.77.w0_ref, ...), custom_call_target="tpu_custom_call" | custom-call | flops 6442450944 | bytes 18874368 | tf_op jit(solution)/shard_map/token_grad/pallas_call | solution.py:534
  401.7 2.6 collective-permute-start.16
  405.6 7.3 %collective-permute-start.35 = (bf16[2,128,256]{2,1,0:T(8,128)(2,1)S(1)}, bf16[2,128,256]{2,1,0:T(8,128)(2,1)S(1)}, u32[]{:S(2)}, u32[]{:S(2)}) collective-permute-start(bf16[2,128,256]{2,1,0:T(8,128)(2,1)S(1)} %maximum_select_fusion.14), channel_id=1, source_target_pairs={{0,8},{8,0},{16,24},{24,16},{1,9},{9,1},{17,25},{25,17},{2,10},{10... | collective-permute-start | bytes 393224 | tf_op jit(solution)/shard_map/ppermute | solution.py:574
  417.2 18.5 %collective-permute-done.18 = bf16[128,384]{1,0:T(8,128)(2,1)S(1)} collective-permute-done((bf16[128,384]{1,0:T(8,128)(2,1)S(1)}, bf16[128,384]{1,0:T(8,128)(2,1)S(1)}, u32[]{:S(2)}, u32[]{:S(2)}) %collective-permute-start.18) | collective-permute-done | bytes 98336 | tf_op jit(solution)/shard_map/ppermute | solution.py:574
  435.7 4.4 collective-permute-start.19
  443.1 2.5 collective-permute-start.24
  447.0 6.0 %collective-permute-done.24 = bf16[144,384]{1,0:T(8,128)(2,1)S(1)} collective-permute-done((bf16[144,384]{1,0:T(8,128)(2,1)S(1)}, bf16[144,384]{1,0:T(8,128)(2,1)S(1)}, u32[]{:S(2)}, u32[]{:S(2)}) %collective-permute-start.24) | collective-permute-done | bytes 110624 | tf_op jit(solution)/shard_map/ppermute | solution.py:574
  466.2 17.1 %collective-permute-done.46 = bf16[4,256,512]{2,1,0:T(8,128)(2,1)} collective-permute-done((bf16[4,256,512]{2,1,0:T(8,128)(2,1)S(1)}, bf16[4,256,512]{2,1,0:T(8,128)(2,1)}, u32[]{:S(2)}, u32[]{:S(2)}) %collective-permute-start.46) | collective-permute-done | bytes 1048608 | tf_op jit(solution)/shard_map/ppermute | solution.py:574
  494.6 11.0 %collective-permute-done.48 = bf16[256,512]{1,0:T(8,128)(2,1)S(1)} collective-permute-done((bf16[256,512]{1,0:T(8,128)(2,1)S(1)}, bf16[256,512]{1,0:T(8,128)(2,1)S(1)}, u32[]{:S(2)}, u32[]{:S(2)}) %collective-permute-start.48) | collective-permute-done | bytes 262176 | tf_op jit(solution)/shard_map/ppermute | solution.py:574
  505.6 15.3 %collective-permute-done.49 = bf16[256,512]{1,0:T(8,128)(2,1)S(1)} collective-permute-done((bf16[256,512]{1,0:T(8,128)(2,1)S(1)}, bf16[256,512]{1,0:T(8,128)(2,1)S(1)}, u32[]{:S(2)}, u32[]{:S(2)}) %collective-permute-start.49) | collective-permute-done | bytes 262176 | tf_op jit(solution)/shard_map/ppermute | solution.py:574
  524.7 4.1 collective-permute-done.40
  528.8 3.5 collective-permute-done.41
  538.5 2.8 collective-permute-done.42
  549.1 2.8 reshape.1028
  (264 shorter events, 116.8 us)
Async XLA Ops:
  7.2 140.0 %all-gather.3.cloned.1.call-start = ((), (), s32[]{:S(2)}) async-start(), calls=%async_computation | async-start | bytes 10813440 | tf_op jit(solution)/shard_map/all_gather | solution.py:630
  9.0 185.1 %all-gather.5.cloned.1.call-start = ((), (), s32[]{:S(2)}) async-start(), calls=%async_computation.1 | async-start | bytes 8650752 | tf_op jit(solution)/shard_map/all_gather | solution.py:629
  11.4 14.5 %collective-permute-start.6 = (bf16[1,32,1536]{2,1,0:T(8,128)(2,1)S(1)}, bf16[1,32,1536]{2,1,0:T(8,128)(2,1)S(1)}, u32[]{:S(2)}, u32[]{:S(2)}) collective-permute-start(bf16[1,32,1536]{2,1,0:T(8,128)(2,1)S(1)} %maximum_bitcast_fusion.1), channel_id=1, source_target_pairs={{0,2},{1,3},{2,4},{3,5},{4,6},{5,7},{6,0},{7,1},{8,10},{9,11},{10,... | collective-permute-start | bytes 294920 | tf_op jit(solution)/shard_map/ppermute | solution.py:574
  12.7 13.1 %collective-permute-start.7 = (bf16[1,32,1536]{2,1,0:T(8,128)(2,1)S(1)}, bf16[1,32,1536]{2,1,0:T(8,128)(2,1)S(1)}, u32[]{:S(2)}, u32[]{:S(2)}) collective-permute-start(bf16[1,32,1536]{2,1,0:T(8,128)(2,1)S(1)} %maximum_bitcast_fusion.1), channel_id=1, source_target_pairs={{0,4},{1,5},{2,6},{3,7},{4,0},{5,1},{6,2},{7,3},{8,12},{9,13},{10,... | collective-permute-start | bytes 294920 | tf_op jit(solution)/shard_map/ppermute | solution.py:574
  13.8 12.1 %collective-permute-start.8 = (bf16[1,32,1536]{2,1,0:T(8,128)(2,1)S(1)}, bf16[1,32,1536]{2,1,0:T(8,128)(2,1)S(1)}, u32[]{:S(2)}, u32[]{:S(2)}) collective-permute-start(bf16[1,32,1536]{2,1,0:T(8,128)(2,1)S(1)} %maximum_bitcast_fusion.1), channel_id=1, source_target_pairs={{0,6},{1,7},{2,0},{3,1},{4,2},{5,3},{6,4},{7,5},{8,14},{9,15},{10,... | collective-permute-start | bytes 294920 | tf_op jit(solution)/shard_map/ppermute | solution.py:574
  21.3 7.9 %collective-permute-start = (bf16[1,32,1664]{2,1,0:T(8,128)(2,1)S(1)}, bf16[1,32,1664]{2,1,0:T(8,128)(2,1)S(1)}, u32[]{:S(2)}, u32[]{:S(2)}) collective-permute-start(bf16[1,32,1664]{2,1,0:T(8,128)(2,1)S(1)} %maximum_bitcast_fusion), channel_id=1, source_target_pairs={{0,2},{1,3},{2,4},{3,5},{4,6},{5,7},{6,0},{7,1},{8,10},{9,11},{10,... | collective-permute-start | bytes 319496 | tf_op jit(solution)/shard_map/ppermute | solution.py:574
  21.4 15.0 %collective-permute-start.1 = (bf16[1,32,1664]{2,1,0:T(8,128)(2,1)S(1)}, bf16[1,32,1664]{2,1,0:T(8,128)(2,1)S(1)}, u32[]{:S(2)}, u32[]{:S(2)}) collective-permute-start(bf16[1,32,1664]{2,1,0:T(8,128)(2,1)S(1)} %maximum_bitcast_fusion), channel_id=1, source_target_pairs={{0,4},{1,5},{2,6},{3,7},{4,0},{5,1},{6,2},{7,3},{8,12},{9,13},{10,... | collective-permute-start | bytes 319496 | tf_op jit(solution)/shard_map/ppermute | solution.py:574
  25.9 14.5 %collective-permute-start.2 = (bf16[1,32,1664]{2,1,0:T(8,128)(2,1)S(1)}, bf16[1,32,1664]{2,1,0:T(8,128)(2,1)S(1)}, u32[]{:S(2)}, u32[]{:S(2)}) collective-permute-start(bf16[1,32,1664]{2,1,0:T(8,128)(2,1)S(1)} %maximum_bitcast_fusion), channel_id=1, source_target_pairs={{0,6},{1,7},{2,0},{3,1},{4,2},{5,3},{6,4},{7,5},{8,14},{9,15},{10,... | collective-permute-start | bytes 319496 | tf_op jit(solution)/shard_map/ppermute | solution.py:574
  25.9 17.7 %collective-permute-start.9 = (bf16[4,32,1536]{2,1,0:T(8,128)(2,1)S(1)}, bf16[4,32,1536]{2,1,0:T(8,128)(2,1)S(1)}, u32[]{:S(2)}, u32[]{:S(2)}) collective-permute-start(bf16[4,32,1536]{2,1,0:T(8,128)(2,1)S(1)} %pad_maximum_fusion.1), channel_id=1, source_target_pairs={{0,1},{1,0},{2,3},{3,2},{4,5},{5,4},{6,7},{7,6},{8,9},{9,8},{10,11... | collective-permute-start | bytes 1179656 | tf_op jit(solution)/shard_map/ppermute | solution.py:574
  40.4 13.7 %collective-permute-start.3 = (bf16[4,32,1664]{2,1,0:T(8,128)(2,1)S(1)}, bf16[4,32,1664]{2,1,0:T(8,128)(2,1)S(1)}, u32[]{:S(2)}, u32[]{:S(2)}) collective-permute-start(bf16[4,32,1664]{2,1,0:T(8,128)(2,1)S(1)} %pad_maximum_fusion), channel_id=1, source_target_pairs={{0,16},{8,24},{16,0},{24,8},{1,17},{9,25},{17,1},{25,9},{2,18},{10... | collective-permute-start | bytes 1277960 | tf_op jit(solution)/shard_map/ppermute | solution.py:574
  44.4 32.7 %collective-permute-start.10 = (bf16[8,32,1536]{2,1,0:T(8,128)(2,1)S(1)}, bf16[8,32,1536]{2,1,0:T(8,128)(2,1)S(1)}, u32[]{:S(2)}, u32[]{:S(2)}) collective-permute-start(bf16[8,32,1536]{2,1,0:T(8,128)(2,1)S(1)} %get-tuple-element.121), channel_id=1, source_target_pairs={{0,16},{8,24},{16,0},{24,8},{1,17},{9,25},{17,1},{25,9},{2,18},{10... | collective-permute-start | bytes 2359304 | tf_op jit(solution)/shard_map/ppermute | solution.py:574
  54.9 24.9 %collective-permute-start.4 = (bf16[8,32,1664]{2,1,0:T(8,128)(2,1)S(1)}, bf16[8,32,1664]{2,1,0:T(8,128)(2,1)S(1)}, u32[]{:S(2)}, u32[]{:S(2)}) collective-permute-start(bf16[8,32,1664]{2,1,0:T(8,128)(2,1)S(1)} %get-tuple-element.115), channel_id=1, source_target_pairs={{0,1},{1,0},{2,3},{3,2},{4,5},{5,4},{6,7},{7,6},{8,9},{9,8},{10,11... | collective-permute-start | bytes 2555912 | tf_op jit(solution)/shard_map/ppermute | solution.py:574
  78.1 12.4 %collective-permute-start.11 = (bf16[16,32,1536]{2,1,0:T(8,128)(2,1)}, bf16[16,32,1536]{2,1,0:T(8,128)(2,1)S(1)}, u32[]{:S(2)}, u32[]{:S(2)}) collective-permute-start(bf16[16,32,1536]{2,1,0:T(8,128)(2,1)} %get-tuple-element.108), channel_id=1, source_target_pairs={{0,8},{8,0},{16,24},{24,16},{1,9},{9,1},{17,25},{25,17},{2,10},{10... | collective-permute-start | bytes 4718600 | tf_op jit(solution)/shard_map/ppermute | solution.py:574
  82.6 9.2 %collective-permute-start.5 = (bf16[16,32,1664]{2,1,0:T(8,128)(2,1)}, bf16[16,32,1664]{2,1,0:T(8,128)(2,1)S(1)}, u32[]{:S(2)}, u32[]{:S(2)}) collective-permute-start(bf16[16,32,1664]{2,1,0:T(8,128)(2,1)} %get-tuple-element.106), channel_id=1, source_target_pairs={{0,8},{8,0},{16,24},{24,16},{1,9},{9,1},{17,25},{25,17},{2,10},{10... | collective-permute-start | bytes 5111816 | tf_op jit(solution)/shard_map/ppermute | solution.py:574
  224.0 152.5 %collective-permute-start.44 = (bf16[2,8,256,512]{3,2,1,0:T(8,128)(2,1)}, bf16[2,8,256,512]{3,2,1,0:T(8,128)(2,1)}, u32[]{:S(2)}, u32[]{:S(2)}) collective-permute-start(bf16[2,8,256,512]{3,2,1,0:T(8,128)(2,1)} %outer_grad.3), channel_id=1, source_target_pairs={{0,8},{8,0},{16,24},{24,16},{1,9},{9,1},{17,25},{25,17},{2,10},{10... | collective-permute-start | bytes 12582920 | tf_op jit(solution)/shard_map/ppermute | solution.py:574
  247.9 132.9 %collective-permute-start.36 = (bf16[2,8,128,1024]{3,2,1,0:T(8,128)(2,1)}, bf16[2,8,128,1024]{3,2,1,0:T(8,128)(2,1)}, u32[]{:S(2)}, u32[]{:S(2)}) collective-permute-start(bf16[2,8,128,1024]{3,2,1,0:T(8,128)(2,1)} %get-tuple-element.89), channel_id=1, source_target_pairs={{0,8},{8,0},{16,24},{24,16},{1,9},{9,1},{17,25},{25,17},{2,10},{10... | collective-permute-start | bytes 12582920 | tf_op jit(solution)/shard_map/ppermute | solution.py:574
  283.8 44.4 %collective-permute-start.28 = (bf16[2,8,128,256]{3,2,1,0:T(8,128)(2,1)}, bf16[2,8,128,256]{3,2,1,0:T(8,128)(2,1)S(1)}, u32[]{:S(2)}, u32[]{:S(2)}) collective-permute-start(bf16[2,8,128,256]{3,2,1,0:T(8,128)(2,1)} %mix_grad.3), channel_id=1, source_target_pairs={{0,8},{8,0},{16,24},{24,16},{1,9},{9,1},{17,25},{25,17},{2,10},{10... | collective-permute-start | bytes 3145736 | tf_op jit(solution)/shard_map/ppermute | solution.py:574
  302.5 43.5 %collective-permute-start.12 = (bf16[2,8,128,384]{3,2,1,0:T(8,128)(2,1)}, bf16[2,8,128,384]{3,2,1,0:T(8,128)(2,1)S(1)}, u32[]{:S(2)}, u32[]{:S(2)}) collective-permute-start(bf16[2,8,128,384]{3,2,1,0:T(8,128)(2,1)} %token_weights_grad.5), channel_id=1, source_target_pairs={{0,8},{8,0},{16,24},{24,16},{1,9},{9,1},{17,25},{25,17},{2,10},{10... | collective-permute-start | bytes 4718600 | tf_op jit(solution)/shard_map/ppermute | solution.py:574
  323.8 43.3 %collective-permute-start.20 = (bf16[2,8,144,384]{3,2,1,0:T(8,128)(2,1)}, bf16[2,8,144,384]{3,2,1,0:T(8,128)(2,1)}, u32[]{:S(2)}, u32[]{:S(2)}) collective-permute-start(bf16[2,8,144,384]{3,2,1,0:T(8,128)(2,1)} %token_weights_grad.7), channel_id=1, source_target_pairs={{0,8},{8,0},{16,24},{24,16},{1,9},{9,1},{17,25},{25,17},{2,10},{10... | collective-permute-start | bytes 5308424 | tf_op jit(solution)/shard_map/ppermute | solution.py:574
  330.1 13.6 %collective-permute-start.29 = (bf16[4,2,128,256]{3,2,1,0:T(8,128)(2,1)}, bf16[4,2,128,256]{3,2,1,0:T(8,128)(2,1)}, u32[]{:S(2)}, u32[]{:S(2)}) collective-permute-start(bf16[4,2,128,256]{3,2,1,0:T(8,128)(2,1)} %fusion.8), channel_id=1, source_target_pairs={{0,16},{8,24},{16,0},{24,8},{1,17},{9,25},{17,1},{25,9},{2,18},{10... | collective-permute-start | bytes 1572872 | tf_op jit(solution)/shard_map/ppermute | solution.py:574
  344.8 14.7 %collective-permute-start.30 = (bf16[4,128,256]{2,1,0:T(8,128)(2,1)S(1)}, bf16[4,128,256]{2,1,0:T(8,128)(2,1)S(1)}, u32[]{:S(2)}, u32[]{:S(2)}) collective-permute-start(bf16[4,128,256]{2,1,0:T(8,128)(2,1)S(1)} %fusion.23), channel_id=1, source_target_pairs={{0,1},{1,0},{2,3},{3,2},{4,5},{5,4},{6,7},{7,6},{8,9},{9,8},{10,11... | collective-permute-start | bytes 786440 | tf_op jit(solution)/shard_map/ppermute | solution.py:574
  348.8 25.5 %collective-permute-start.13 = (bf16[4,2,128,384]{3,2,1,0:T(8,128)(2,1)}, bf16[4,2,128,384]{3,2,1,0:T(8,128)(2,1)}, u32[]{:S(2)}, u32[]{:S(2)}) collective-permute-start(bf16[4,2,128,384]{3,2,1,0:T(8,128)(2,1)} %fusion.6), channel_id=1, source_target_pairs={{0,16},{8,24},{16,0},{24,8},{1,17},{9,25},{17,1},{25,9},{2,18},{10... | collective-permute-start | bytes 2359304 | tf_op jit(solution)/shard_map/ppermute | solution.py:574
  361.2 7.5 %collective-permute-start.31 = (bf16[128,256]{1,0:T(8,128)(2,1)}, bf16[128,256]{1,0:T(8,128)(2,1)S(1)}, u32[]{:S(2)}, u32[]{:S(2)}) collective-permute-start(bf16[128,256]{1,0:T(8,128)(2,1)} %get-tuple-element.103), channel_id=1, source_target_pairs={{0,2},{1,3},{2,4},{3,5},{4,6},{5,7},{6,0},{7,1},{8,10},{9,11},{10,... | collective-permute-start | bytes 196616 | tf_op jit(solution)/shard_map/ppermute | solution.py:574
  371.5 32.8 %collective-permute-start.21 = (bf16[2,4,144,384]{3,2,1,0:T(8,128)(2,1)}, bf16[2,4,144,384]{3,2,1,0:T(8,128)(2,1)}, u32[]{:S(2)}, u32[]{:S(2)}) collective-permute-start(bf16[2,4,144,384]{3,2,1,0:T(8,128)(2,1)} %fusion.4), channel_id=1, source_target_pairs={{0,1},{1,0},{2,3},{3,2},{4,5},{5,4},{6,7},{7,6},{8,9},{9,8},{10,11... | collective-permute-start | bytes 2654216 | tf_op jit(solution)/shard_map/ppermute | solution.py:574
  373.6 23.8 %collective-permute-start.34 = (bf16[128,256]{1,0:T(8,128)(2,1)S(1)}, bf16[128,256]{1,0:T(8,128)(2,1)S(1)}, u32[]{:S(2)}, u32[]{:S(2)}) collective-permute-start(bf16[128,256]{1,0:T(8,128)(2,1)S(1)} %fusion.46), channel_id=1, source_target_pairs={{0,16},{8,24},{16,0},{24,8},{1,17},{9,25},{17,1},{25,9},{2,18},{10... | collective-permute-start | bytes 196616 | tf_op jit(solution)/shard_map/ppermute | solution.py:574
  375.6 23.1 %collective-permute-start.14 = (bf16[4,128,384]{2,1,0:T(8,128)(2,1)S(1)}, bf16[4,128,384]{2,1,0:T(8,128)(2,1)S(1)}, u32[]{:S(2)}, u32[]{:S(2)}) collective-permute-start(bf16[4,128,384]{2,1,0:T(8,128)(2,1)S(1)} %fusion.7), channel_id=1, source_target_pairs={{0,1},{1,0},{2,3},{3,2},{4,5},{5,4},{6,7},{7,6},{8,9},{9,8},{10,11... | collective-permute-start | bytes 1179656 | tf_op jit(solution)/shard_map/ppermute | solution.py:574
  380.2 76.9 %collective-permute-start.45 = (bf16[4,2,256,512]{3,2,1,0:T(8,128)(2,1)}, bf16[4,2,256,512]{3,2,1,0:T(8,128)(2,1)}, u32[]{:S(2)}, u32[]{:S(2)}) collective-permute-start(bf16[4,2,256,512]{3,2,1,0:T(8,128)(2,1)} %fusion.1), channel_id=1, source_target_pairs={{0,16},{8,24},{16,0},{24,8},{1,17},{9,25},{17,1},{25,9},{2,18},{10... | collective-permute-start | bytes 6291464 | tf_op jit(solution)/shard_map/ppermute | solution.py:574
  384.6 77.6 %collective-permute-start.37 = (bf16[2,4,128,1024]{3,2,1,0:T(8,128)(2,1)}, bf16[2,4,128,1024]{3,2,1,0:T(8,128)(2,1)}, u32[]{:S(2)}, u32[]{:S(2)}) collective-permute-start(bf16[2,4,128,1024]{3,2,1,0:T(8,128)(2,1)} %fusion), channel_id=1, source_target_pairs={{0,1},{1,0},{2,3},{3,2},{4,5},{5,4},{6,7},{7,6},{8,9},{9,8},{10,11... | collective-permute-start | bytes 6291464 | tf_op jit(solution)/shard_map/ppermute | solution.py:574
  400.0 5.6 %collective-permute-start.15 = (bf16[128,384]{1,0:T(8,128)(2,1)S(1)}, bf16[128,384]{1,0:T(8,128)(2,1)S(1)}, u32[]{:S(2)}, u32[]{:S(2)}) collective-permute-start(bf16[128,384]{1,0:T(8,128)(2,1)S(1)} %get-tuple-element.100), channel_id=1, source_target_pairs={{0,2},{1,3},{2,4},{3,5},{4,6},{5,7},{6,0},{7,1},{8,10},{9,11},{10,... | collective-permute-start | bytes 294920 | tf_op jit(solution)/shard_map/ppermute | solution.py:574
  401.7 11.2 %collective-permute-start.16 = (bf16[128,384]{1,0:T(8,128)(2,1)S(1)}, bf16[128,384]{1,0:T(8,128)(2,1)S(1)}, u32[]{:S(2)}, u32[]{:S(2)}) collective-permute-start(bf16[128,384]{1,0:T(8,128)(2,1)S(1)} %get-tuple-element.102), channel_id=1, source_target_pairs={{0,4},{1,5},{2,6},{3,7},{4,0},{5,1},{6,2},{7,3},{8,12},{9,13},{10,... | collective-permute-start | bytes 294920 | tf_op jit(solution)/shard_map/ppermute | solution.py:574
  404.3 9.8 %collective-permute-start.17 = (bf16[128,384]{1,0:T(8,128)(2,1)S(1)}, bf16[128,384]{1,0:T(8,128)(2,1)S(1)}, u32[]{:S(2)}, u32[]{:S(2)}) collective-permute-start(bf16[128,384]{1,0:T(8,128)(2,1)S(1)} %get-tuple-element.101), channel_id=1, source_target_pairs={{0,6},{1,7},{2,0},{3,1},{4,2},{5,3},{6,4},{7,5},{8,14},{9,15},{10,... | collective-permute-start | bytes 294920 | tf_op jit(solution)/shard_map/ppermute | solution.py:574
  405.6 9.9 %collective-permute-start.35 = (bf16[2,128,256]{2,1,0:T(8,128)(2,1)S(1)}, bf16[2,128,256]{2,1,0:T(8,128)(2,1)S(1)}, u32[]{:S(2)}, u32[]{:S(2)}) collective-permute-start(bf16[2,128,256]{2,1,0:T(8,128)(2,1)S(1)} %maximum_select_fusion.14), channel_id=1, source_target_pairs={{0,8},{8,0},{16,24},{24,16},{1,9},{9,1},{17,25},{25,17},{2,10},{10... | collective-permute-start | bytes 393224 | tf_op jit(solution)/shard_map/ppermute | solution.py:574
  412.9 27.3 %collective-permute-start.22 = (bf16[4,144,384]{2,1,0:T(8,128)(2,1)S(1)}, bf16[4,144,384]{2,1,0:T(8,128)(2,1)S(1)}, u32[]{:S(2)}, u32[]{:S(2)}) collective-permute-start(bf16[4,144,384]{2,1,0:T(8,128)(2,1)S(1)} %fusion.5), channel_id=1, source_target_pairs={{0,16},{8,24},{16,0},{24,8},{1,17},{9,25},{17,1},{25,9},{2,18},{10... | collective-permute-start | bytes 1327112 | tf_op jit(solution)/shard_map/ppermute | solution.py:574
  415.2 20.5 %collective-permute-start.18 = (bf16[128,384]{1,0:T(8,128)(2,1)S(1)}, bf16[128,384]{1,0:T(8,128)(2,1)S(1)}, u32[]{:S(2)}, u32[]{:S(2)}) collective-permute-start(bf16[128,384]{1,0:T(8,128)(2,1)S(1)} %fusion.39), channel_id=1, source_target_pairs={{0,16},{8,24},{16,0},{24,8},{1,17},{9,25},{17,1},{25,9},{2,18},{10... | collective-permute-start | bytes 294920 | tf_op jit(solution)/shard_map/ppermute | solution.py:574
  435.7 9.9 %collective-permute-start.19 = (bf16[2,128,384]{2,1,0:T(8,128)(2,1)S(1)}, bf16[2,128,384]{2,1,0:T(8,128)(2,1)S(1)}, u32[]{:S(2)}, u32[]{:S(2)}) collective-permute-start(bf16[2,128,384]{2,1,0:T(8,128)(2,1)S(1)} %maximum_select_fusion.12), channel_id=1, source_target_pairs={{0,8},{8,0},{16,24},{24,16},{1,9},{9,1},{17,25},{25,17},{2,10},{10... | collective-permute-start | bytes 589832 | tf_op jit(solution)/shard_map/ppermute | solution.py:574
  443.1 9.9 %collective-permute-start.24 = (bf16[144,384]{1,0:T(8,128)(2,1)S(1)}, bf16[144,384]{1,0:T(8,128)(2,1)S(1)}, u32[]{:S(2)}, u32[]{:S(2)}) collective-permute-start(bf16[144,384]{1,0:T(8,128)(2,1)S(1)} %get-tuple-element.99), channel_id=1, source_target_pairs={{0,4},{1,5},{2,6},{3,7},{4,0},{5,1},{6,2},{7,3},{8,12},{9,13},{10,... | collective-permute-start | bytes 331784 | tf_op jit(solution)/shard_map/ppermute | solution.py:574
  445.6 9.5 %collective-permute-start.25 = (bf16[144,384]{1,0:T(8,128)(2,1)S(1)}, bf16[144,384]{1,0:T(8,128)(2,1)S(1)}, u32[]{:S(2)}, u32[]{:S(2)}) collective-permute-start(bf16[144,384]{1,0:T(8,128)(2,1)S(1)} %get-tuple-element.98), channel_id=1, source_target_pairs={{0,6},{1,7},{2,0},{3,1},{4,2},{5,3},{6,4},{7,5},{8,14},{9,15},{10,... | collective-permute-start | bytes 331784 | tf_op jit(solution)/shard_map/ppermute | solution.py:574
  459.4 23.8 %collective-permute-start.46 = (bf16[4,256,512]{2,1,0:T(8,128)(2,1)S(1)}, bf16[4,256,512]{2,1,0:T(8,128)(2,1)}, u32[]{:S(2)}, u32[]{:S(2)}) collective-permute-start(bf16[4,256,512]{2,1,0:T(8,128)(2,1)S(1)} %fusion.2), channel_id=1, source_target_pairs={{0,1},{1,0},{2,3},{3,2},{4,5},{5,4},{6,7},{7,6},{8,9},{9,8},{10,11... | collective-permute-start | bytes 3145736 | tf_op jit(solution)/shard_map/ppermute | solution.py:574
  464.7 24.9 %collective-permute-start.38 = (bf16[4,128,1024]{2,1,0:T(8,128)(2,1)S(1)}, bf16[4,128,1024]{2,1,0:T(8,128)(2,1)}, u32[]{:S(2)}, u32[]{:S(2)}) collective-permute-start(bf16[4,128,1024]{2,1,0:T(8,128)(2,1)S(1)} %fusion.3), channel_id=1, source_target_pairs={{0,16},{8,24},{16,0},{24,8},{1,17},{9,25},{17,1},{25,9},{2,18},{10... | collective-permute-start | bytes 3145736 | tf_op jit(solution)/shard_map/ppermute | solution.py:574
  485.5 8.9 %collective-permute-start.47 = (bf16[256,512]{1,0:T(8,128)(2,1)S(1)}, bf16[256,512]{1,0:T(8,128)(2,1)S(1)}, u32[]{:S(2)}, u32[]{:S(2)}) collective-permute-start(bf16[256,512]{1,0:T(8,128)(2,1)S(1)} %get-tuple-element.91), channel_id=1, source_target_pairs={{0,2},{1,3},{2,4},{3,5},{4,6},{5,7},{6,0},{7,1},{8,10},{9,11},{10,... | collective-permute-start | bytes 786440 | tf_op jit(solution)/shard_map/ppermute | solution.py:574
  485.6 20.1 %collective-permute-start.48 = (bf16[256,512]{1,0:T(8,128)(2,1)S(1)}, bf16[256,512]{1,0:T(8,128)(2,1)S(1)}, u32[]{:S(2)}, u32[]{:S(2)}) collective-permute-start(bf16[256,512]{1,0:T(8,128)(2,1)S(1)} %get-tuple-element.93), channel_id=1, source_target_pairs={{0,4},{1,5},{2,6},{3,7},{4,0},{5,1},{6,2},{7,3},{8,12},{9,13},{10,... | collective-permute-start | bytes 786440 | tf_op jit(solution)/shard_map/ppermute | solution.py:574
  486.1 34.9 %collective-permute-start.49 = (bf16[256,512]{1,0:T(8,128)(2,1)S(1)}, bf16[256,512]{1,0:T(8,128)(2,1)S(1)}, u32[]{:S(2)}, u32[]{:S(2)}) collective-permute-start(bf16[256,512]{1,0:T(8,128)(2,1)S(1)} %get-tuple-element.92), channel_id=1, source_target_pairs={{0,6},{1,7},{2,0},{3,1},{4,2},{5,3},{6,4},{7,5},{8,14},{9,15},{10,... | collective-permute-start | bytes 786440 | tf_op jit(solution)/shard_map/ppermute | solution.py:574
  492.1 32.5 %collective-permute-start.39 = (bf16[128,1024]{1,0:T(8,128)(2,1)S(1)}, bf16[128,1024]{1,0:T(8,128)(2,1)S(1)}, u32[]{:S(2)}, u32[]{:S(2)}) collective-permute-start(bf16[128,1024]{1,0:T(8,128)(2,1)S(1)} %get-tuple-element.94), channel_id=1, source_target_pairs={{0,2},{1,3},{2,4},{3,5},{4,6},{5,7},{6,0},{7,1},{8,10},{9,11},{10,... | collective-permute-start | bytes 786440 | tf_op jit(solution)/shard_map/ppermute | solution.py:574
  492.2 36.6 %collective-permute-start.40 = (bf16[128,1024]{1,0:T(8,128)(2,1)S(1)}, bf16[128,1024]{1,0:T(8,128)(2,1)S(1)}, u32[]{:S(2)}, u32[]{:S(2)}) collective-permute-start(bf16[128,1024]{1,0:T(8,128)(2,1)S(1)} %get-tuple-element.96), channel_id=1, source_target_pairs={{0,4},{1,5},{2,6},{3,7},{4,0},{5,1},{6,2},{7,3},{8,12},{9,13},{10,... | collective-permute-start | bytes 786440 | tf_op jit(solution)/shard_map/ppermute | solution.py:574
  494.3 38.0 %collective-permute-start.41 = (bf16[128,1024]{1,0:T(8,128)(2,1)S(1)}, bf16[128,1024]{1,0:T(8,128)(2,1)}, u32[]{:S(2)}, u32[]{:S(2)}) collective-permute-start(bf16[128,1024]{1,0:T(8,128)(2,1)S(1)} %get-tuple-element.95), channel_id=1, source_target_pairs={{0,6},{1,7},{2,0},{3,1},{4,2},{5,3},{6,4},{7,5},{8,14},{9,15},{10,... | collective-permute-start | bytes 786440 | tf_op jit(solution)/shard_map/ppermute | solution.py:574
  522.4 12.7 %collective-permute-start.50 = (bf16[256,512]{1,0:T(8,128)(2,1)S(1)}, bf16[256,512]{1,0:T(8,128)(2,1)S(1)}, u32[]{:S(2)}, u32[]{:S(2)}) collective-permute-start(bf16[256,512]{1,0:T(8,128)(2,1)S(1)} %fusion.15), channel_id=1, source_target_pairs={{0,16},{8,24},{16,0},{24,8},{1,17},{9,25},{17,1},{25,9},{2,18},{10... | collective-permute-start | bytes 786440 | tf_op jit(solution)/shard_map/ppermute | solution.py:574
  533.9 7.4 %collective-permute-start.42 = (bf16[128,1024]{1,0:T(8,128)(2,1)S(1)}, bf16[128,1024]{1,0:T(8,128)(2,1)S(1)}, u32[]{:S(2)}, u32[]{:S(2)}) collective-permute-start(bf16[128,1024]{1,0:T(8,128)(2,1)S(1)} %fusion.22), channel_id=1, source_target_pairs={{0,16},{8,24},{16,0},{24,8},{1,17},{9,25},{17,1},{25,9},{2,18},{10... | collective-permute-start | bytes 786440 | tf_op jit(solution)/shard_map/ppermute | solution.py:574
  535.2 8.5 %collective-permute-start.51 = (bf16[2,256,512]{2,1,0:T(8,128)(2,1)S(1)}, bf16[2,256,512]{2,1,0:T(8,128)(2,1)S(1)}, u32[]{:S(2)}, u32[]{:S(2)}) collective-permute-start(bf16[2,256,512]{2,1,0:T(8,128)(2,1)S(1)} %maximum_select_fusion.5), channel_id=1, source_target_pairs={{0,8},{8,0},{16,24},{24,16},{1,9},{9,1},{17,25},{25,17},{2,10},{10... | collective-permute-start | bytes 1572872 | tf_op jit(solution)/shard_map/ppermute | solution.py:574
  (24 other events, 205.3 us)
Sparse Core Ops, SparseCore 0:
  11.5 103.3 all-gather.2
  117.9 76.1 all-gather.4

commit v2 on v0

v2 whole, which is shorter than its diff:
```python
import functools
import math

import jax
import jax.numpy as jnp
from jax import lax
from jax.experimental import pallas as pl
from jax.experimental.pallas import tpu as pltpu
from jax.sharding import PartitionSpec as P

F32 = jnp.float32
BF16 = jnp.bfloat16
VMEM_LIMIT = 56 * 1024 * 1024
ANY = pl.BlockSpec(memory_space=pl.ANY)
BQ, BV, BOUT, GAIN1, SHIFT1, BOUTER, GAIN2, SHIFT2 = range(8)


LAST = []


def call(kernel, name, operands, in_specs, out_shape, out_specs, *, grid=(1,), scalars=(), after=(), carry=(), scratch=(), room=None):
    single = not isinstance(out_shape, (tuple, list))
    shapes, specs = ([out_shape], [out_specs]) if single else (list(out_shape), list(out_specs))
    first, made = len(scalars) + len(operands), len(shapes)
    unread = list(carry) + list(after) + LAST

    limit = VMEM_LIMIT
    if room is not None:
        pairs = list(zip(specs, shapes)) + list(zip(in_specs, operands))
        blocks = [math.prod(spec.block_shape) * array.dtype.itemsize for spec, array in pairs if spec.block_shape is not None]
        limit = min(VMEM_LIMIT, 2 * sum(blocks) + room)

    def body(*refs):
        outs = first + len(unread)
        kernel(*refs[:first], *refs[outs : outs + made], *refs[outs + made + len(carry) :])

    outs = pl.pallas_call(
        body,
        out_shape=shapes + [jax.ShapeDtypeStruct(c.shape, c.dtype) for c in carry],
        grid_spec=pltpu.PrefetchScalarGridSpec(
            num_scalar_prefetch=len(scalars),
            grid=grid,
            in_specs=list(in_specs) + [ANY] * len(unread),
            out_specs=specs + [ANY] * len(carry),
            scratch_shapes=list(scratch),
        ),
        input_output_aliases={first + i: made + i for i in range(len(carry))},
        compiler_params=pltpu.CompilerParams(dimension_semantics=("arbitrary",) * len(grid), vmem_limit_bytes=limit),
        cost_estimate=pl.CostEstimate(flops=1, bytes_accessed=1, transcendentals=0),
        name=name,
    )(*scalars, *operands, *unread)
    LAST[:] = outs[made - 1 : made]
    result = outs[0] if single else tuple(outs[:made])
    return (result, outs[made:]) if carry else result


def like(shape, dtype=BF16):
    return jax.ShapeDtypeStruct(shape, dtype)


def dot(left, right):
    return lax.dot_general(left, right, (((1,), (0,)), ((), ())), preferred_element_type=F32)


def dot_nt(left, right):
    return lax.dot_general(left, right, (((1,), (1,)), ((), ())), preferred_element_type=F32)


def whole(shape):
    return pl.BlockSpec(shape, lambda *i: (0,) * len(shape))


def column_sum(value):
    return jnp.sum(value.astype(F32), axis=0, keepdims=True)


def pack(operands, makes, vectors=()):
    lanes = 128 if vectors else 0

    def kernel(*refs):
        outs = refs[len(operands) + len(vectors) :]
        for out_ref, pieces in zip(outs, makes):
            at = 0
            for which, start, size in pieces:
                out_ref[:, at : at + size] = refs[which][:, start : start + size]
                at += size
        if vectors:
            rows, cols = outs[0].shape
            outs[0][:, cols - lanes :] = jnp.zeros((rows, lanes), BF16)
            for ref, (row, lane) in zip(refs[len(operands) :], vector_places(vectors, rows)):
                size = ref.shape[0]
                start = cols - lanes + lane
                outs[0][row : row + 1, start : start + size] = ref[...].astype(F32).reshape(1, size).astype(BF16)

    shapes = [(operands[pieces[0][0]].shape[0], sum(p[2] for p in pieces)) for pieces in makes]
    if vectors:
        shapes[0] = (shapes[0][0], shapes[0][1] + lanes)
    everything = list(operands) + list(vectors)
    return call(kernel, "pack", everything, [whole(o.shape) for o in everything], [like(s) for s in shapes], [whole(s) for s in shapes], room=4 << 20)


def vector_places(vectors, rows):
    size = vectors[0].shape[0]
    places = [(i % rows, i // rows * size) for i in range(len(vectors) - 1)]
    return places + [(8, 0) if rows > 8 else (0, 64)]


def stack(jobs, carry=()):
    flat = [array for arrays, *_ in jobs for array in arrays]
    shapes = []
    for arrays, _, axis, _, cols in jobs:
        shape = arrays[0].shape
        shapes.append(shape[:axis] + (len(arrays),) + shape[axis:-1] + (cols,))

    def kernel(*refs):
        place_refs, refs = refs[: len(jobs)], refs[len(jobs) :]
        ins, outs, arrived = refs[: len(flat)], refs[len(flat) : -1], refs[-1]
        copies = []
        for (arrays, _, axis, first, cols), place_ref, out_ref in zip(jobs, place_refs, outs):
            count = len(arrays)
            for k in range(count):
                ref = ins[len(copies)]
                source = ref.at[(slice(None),) * (len(ref.shape) - 1) + (pl.ds(first, cols),)]
                target = out_ref.at[(slice(None),) * axis + (lax.rem(place_ref[0] + count - k, count),)]
                copies.append(pltpu.make_async_copy(source, target, arrived.at[len(copies)]))
        for copy in copies:
            copy.start()
        for copy in copies:
            copy.wait()

    return call(
        kernel,
        "stack",
        flat,
        [ANY] * len(flat),
        [like(shape) for shape in shapes],
        [whole(shape) for shape in shapes],
        scalars=[job[1] for job in jobs],
        carry=carry,
        scratch=[pltpu.SemaphoreType.DMA((len(flat),))],
        room=4 << 20,
    )


def combine(jobs, carry=(), after=()):
    n = jobs[0][1][0][0].shape[1]
    sizes = []
    for _, terms in jobs:
        before, _, behind, _, _ = terms[0][0].shape
        sizes.append((before, behind) + terms[0][2])
    flat = [t for _, terms in jobs for t in terms]

    def kernel(*refs):
        refs = refs[len(jobs) :]
        outs = refs[len(flat) :]
        i = 0
        for job, (_, terms) in enumerate(jobs):
            total = refs[i][:, 0].astype(F32)
            for ref in refs[i + 1 : i + len(terms)]:
                total = total + ref[:, 0].astype(F32)
            total = total.astype(BF16)
            i += len(terms)
            for j, out_ref in enumerate(outs[job * n : (job + 1) * n]):

                @pl.when(pl.program_id(0) == j)
                def _():
                    out_ref[...] = total

    def at(job, block):
        before, behind, rows, cols = sizes[job]
        return pl.BlockSpec((before, 1, behind, rows, cols), lambda i, *own: (0, lax.rem(own[job][0] + i + 1, n), 0) + block)

    made = call(
        kernel,
        "combine",
        [t[0] for t in flat],
        [at(job, t[1]) for job, (_, terms) in enumerate(jobs) for t in terms],
        [like(size) for size in sizes for _ in range(n)],
        [whole(size) for size in sizes for _ in range(n)],
        grid=(n,),
        scalars=[own for own, _ in jobs],
        carry=carry,
        after=after,
        room=12 << 20,
    )
    made, carried = made if carry else (made, ())
    return [made[job * n : (job + 1) * n] for job in range(len(jobs))], carried


def gather_sums(own, lists):
    flat = [t for terms in lists for t in terms]
    n = flat[0].shape[0]
    rows = max(t.shape[1] for t in flat)
    cols = sum(terms[0].shape[2] for terms in lists)

    def kernel(own_ref, *refs):
        outs = refs[len(flat) :]
        parts, i = [], 0
        for terms in lists:
            total = refs[i][0].astype(F32)
            for ref in refs[i + 1 : i + len(terms)]:
                total = total + ref[0].astype(F32)
            parts.append(total.astype(BF16))
            i += len(terms)
        for j, out_ref in enumerate(outs):

            @pl.when(pl.program_id(0) == j)
            def _():
                at = 0
                for part in parts:
                    high, wide = part.shape
                    out_ref[:high, at : at + wide] = part
                    if high < rows:
                        out_ref[high:, at : at + wide] = jnp.zeros((rows - high, wide), BF16)
                    at += wide

    return call(
        kernel,
        "gather_sums",
        flat,
        [pl.BlockSpec((1,) + t.shape[1:], lambda i, own: (lax.rem(own[0] + i + 1, n), 0, 0)) for t in flat],
        [like((rows, cols))] * n,
        [whole((rows, cols))] * n,
        grid=(n,),
        scalars=[own],
        room=6 << 20,
    )


def add_up(lists, after=()):
    flat = [a for arrays in lists for a in arrays]

    def kernel(*refs):
        at, i = 0, 0
        for arrays in lists:
            total = refs[i][...].astype(F32)
            for ref in refs[i + 1 : i + len(arrays)]:
                total = total + ref[...].astype(F32)
            rows, cols = total.shape
            refs[-1][:rows, at : at + cols] = total.astype(BF16)
            if rows < refs[-1].shape[0]:
                refs[-1][rows:, at : at + cols] = jnp.zeros((refs[-1].shape[0] - rows, cols), BF16)
            at += cols
            i += len(arrays)

    shape = (max(a.shape[0] for a in flat), sum(arrays[0].shape[1] for arrays in lists))
    return call(kernel, "add_up", flat, [whole(a.shape) for a in flat], like(shape), whole(shape), after=after, room=12 << 20)


def outer_result(got, order, runs=2):
    count, cols, rows = got.shape
    rows //= runs

    def kernel(got_ref, out_ref):
        for i, j in enumerate(order):
            for run in range(runs):
                at = (j * runs + run) * cols
                out_ref[:, at : at + cols] = got_ref[i, :, run * rows : (run + 1) * rows].astype(F32).T

    shape = (rows, count * runs * cols)
    return call(kernel, "outer_result", [got], [whole(got.shape)], like(shape, F32), whole(shape), room=8 << 20)


def inner_result(got, order):
    count, rows, cols = got.shape

    def kernel(got_ref, out_ref):
        for i, j in enumerate(order):
            out_ref[:, j * cols : (j + 1) * cols] = got_ref[i].astype(F32)

    shape = (rows, count * cols)
    return call(kernel, "inner_result", [got], [whole(got.shape)], like(shape, F32), whole(shape), room=8 << 20)


def token_weights_result(pieces, places, keep, size, last):
    count = len(pieces)
    rows = pieces[0].shape[0]
    second = 3 * size + last

    def kernel(place_ref, *refs):
        outs = refs[count:]
        for i in range(count):
            at = lambda j, wide: pl.ds(pl.multiple_of(j * wide, wide), wide)
            piece = refs[i][:keep].astype(F32)
            for which in range(3):
                outs[which][:, at(place_ref[i], size)] = piece[:, which * size : (which + 1) * size]
                outs[which][:, at(count + place_ref[i], size)] = piece[:, second + which * size : second + (which + 1) * size]
            outs[3][:, at(place_ref[i], last)] = piece[:, 3 * size : second]
        outs[4][...] = refs[0][keep:, second:].astype(F32)

    shapes = [(keep, 2 * count * size)] * 3 + [(keep, count * last), (rows - keep, 3 * size)]
    return call(
        kernel,
        "token_weights_result",
        pieces,
        [whole(p.shape) for p in pieces],
        [like(s, F32) for s in shapes],
        [whole(s) for s in shapes],
        scalars=[places],
        room=8 << 20,
    )


def transposed(x, tile=256):
    rows, cols = x.shape

    def kernel(x_ref, out_ref):
        out_ref[...] = x_ref[...].T

    return call(
        kernel,
        "transposed",
        [x],
        [pl.BlockSpec((tile, cols), lambda i: (i, 0))],
        like((cols, rows)),
        pl.BlockSpec((cols, tile), lambda i: (0, i)),
        grid=(rows // tile,),
    )


class Pieces:
    def __init__(self, cores, buffers, spans, shape):
        self.cores, self.buffers, self.spans, self.shape = cores, buffers, spans, shape
        self.count = sum(b.shape[0] for b in buffers)

    def part(self, start, cols):
        kept = []
        for buffer, (first, size, to) in zip(self.buffers, self.spans):
            low, high = max(to, start), min(to + size, start + cols)
            kept.append((buffer, (first + low - to, high - low, low - start)))
        buffers, spans = zip(*(k for k in kept if k[1][1] > 0))
        return Pieces(self.cores, list(buffers), list(spans), (self.shape[0], cols))

    def scratch(self):
        return [pltpu.VMEM(self.shape, BF16), pltpu.SemaphoreType.DMA((self.count,)), pltpu.SemaphoreType.DMA]

    def fetch(self, cores_ref, refs, held, arrived):
        copies = []
        for i, (ref, (first, cols, to)) in enumerate(zip(refs, self.spans)):
            blocks, rows, _ = ref.shape
            for j in range(blocks):
                target = held.at[pl.ds(pl.multiple_of((2 * j + cores_ref[i % 2]) * rows, rows), rows), pl.ds(to, cols)]
                copies.append(pltpu.make_async_copy(ref.at[j, :, pl.ds(first, cols)], target, arrived.at[len(copies)]))
        for copy in copies:
            copy.start()
        for copy in copies:
            copy.wait()


def project(pieces, x, vec, half, after=()):
    rows, depth = x.shape
    cols = pieces.shape[1]
    tile = cols // 3
    count = len(pieces.buffers)

    def kernel(*refs):
        (cores_ref,), (x_ref, vec_ref), refs = refs[:1], refs[1 : 3], refs[3:]
        buffer_refs, (out_ref, whole_ref, held, arrived, left) = refs[:count], refs[count:]
        step = pl.program_id(0)
        write = pltpu.make_async_copy(held, whole_ref, left)

        @pl.when(step == 0)
        def _():
            pieces.fetch(cores_ref, buffer_refs, held, arrived)
            write.start()

        at = slice(half * tile, (half + 1) * tile)
        for i, row in enumerate((BQ, None, BV)):

            @pl.when(step == i)
            def _():
                made = dot(x_ref[...], held[:, i * tile : (i + 1) * tile])
                out_ref[...] = (made if row is None else made + vec_ref[row : row + 1, at]).astype(BF16)

        @pl.when(step == 2)
        def _():
            write.wait()

    return call(
        kernel,
        "project",
        [x, vec] + list(pieces.buffers),
        [whole(x.shape), whole(vec.shape)] + [ANY] * count,
        (like((rows, cols)), like((depth, cols))),
        (pl.BlockSpec((rows, tile), lambda i, *_: (0, i)), ANY),
        grid=(3,),
        scalars=[pieces.cores],
        scratch=pieces.scratch(),
        after=after,
    )


def attend(qkv, row, col, heads=4, size=64, after=()):
    seqs, _, length = row.shape
    width = qkv.shape[1] // 3
    block = heads * size
    blocks = width // block

    def kernel(q_ref, k_ref, v_ref, row_ref, col_ref, o_ref, ot_ref, p_ref, r_ref, bias_ref):
        @pl.when(pl.program_id(1) == 0)
        def _():
            bias_ref[...] = jnp.where(col_ref[0] == row_ref[0], 0.0, -1e9).astype(F32)

        qt = (q_ref[...] * jnp.asarray(0.125, BF16)).T
        vt = v_ref[...].T
        zero = jnp.zeros((size, length), BF16)
        for head in range(heads):
            here = slice(head * size, (head + 1) * size)
            pair = slice(head // 2 * 2 * size, (head // 2 + 1) * 2 * size)
            own = [qt[here], zero] if head % 2 == 0 else [zero, qt[here]]
            scores = dot(k_ref[:, pair], jnp.concatenate(own, axis=0)) + bias_ref[...]
            expo = jnp.exp(scores - jnp.max(scores, axis=0, keepdims=True))
            share = 1.0 / jnp.sum(expo, axis=0, keepdims=True)
            expo = expo.astype(BF16)
            p_ref[0, head] = expo
            r_ref[0, 0, head : head + 1] = share
            ot_ref[here, :] = (dot(vt[here], expo) * share).astype(BF16)
        o_ref[...] = ot_ref[...].T

    spec = lambda part: pl.BlockSpec((length, block), lambda s, p: (s, part * blocks + p))
    return call(
        kernel,
        "attend",
        [qkv, qkv, qkv, row, col],
        [spec(0), spec(1), spec(2), pl.BlockSpec((1, 1, length), lambda s, p: (s, 0, 0)), pl.BlockSpec((1, length, 1), lambda s, p: (s, 0, 0))],
        (like((seqs * length, width)), like((width, seqs * length)), like((seqs, heads * blocks, length, length)), like((seqs, blocks, heads, length), F32)),
        (
            pl.BlockSpec((length, block), lambda s, p: (s, p)),
            pl.BlockSpec((block, length), lambda s, p: (p, s)),
            pl.BlockSpec((1, heads, length, length), lambda s, p: (s, p, 0, 0)),
            pl.BlockSpec((1, 1, heads, length), lambda s, p: (s, p, 0, 0)),
        ),
        grid=(seqs, blocks),
        scratch=[pltpu.VMEM((length, length), F32)],
        after=after,
    )


def attend_back(qkv, ot, probs, share, do, part, after=()):
    seqs, blocks, heads, length = share.shape
    tokens, width = ot.shape[1], ot.shape[0]
    block = width // blocks
    size = block // heads

    def kernel(q_ref, k_ref, v_ref, ot_ref, p_ref, r_ref, do_ref, d_ref, bq_ref, bv_ref):
        dot_t = do_ref[...].T.astype(F32)
        shares = jnp.concatenate([jnp.broadcast_to(r_ref[0, 0, h : h + 1], (size, length)) for h in range(heads)], axis=0)
        dot_t = (dot_t * shares).astype(BF16)
        do = dot_t.T
        kt = k_ref[...].T
        product = dot_t.astype(F32) * ot_ref[...].astype(F32)
        zero = jnp.zeros((size, length), BF16)
        first = lax.broadcasted_iota(jnp.int32, (1, 2 * size), 1) < size
        dk, dv, dqt = [], [], []
        for head in range(heads):
            here = slice(head * size, (head + 1) * size)
            pair = slice(head // 2 * 2 * size, (head // 2 + 1) * 2 * size)
            delta = jnp.sum(product[here], axis=0, keepdims=True)
            own = [dot_t[here], zero] if head % 2 == 0 else [zero, dot_t[here]]
            expo = p_ref[0, head]
            ds = (expo.astype(F32) * (dot(v_ref[:, pair], jnp.concatenate(own, axis=0)) - delta)).astype(BF16)
            dv.append(dot(expo, do[:, pair]))
            dk.append(dot(ds, q_ref[:, pair]))
            dqt.append(dot(kt[here], ds))
        paired = lambda parts: jnp.concatenate([jnp.where(first, parts[i], parts[i + 1]) for i in range(0, heads, 2)], axis=1)
        dq = (jnp.concatenate(dqt, axis=0) * 0.125).astype(BF16).T
        dv = paired(dv).astype(BF16)
        d_ref[0] = dq
        d_ref[1] = (paired(dk) * 0.125).astype(BF16)
        d_ref[2] = dv
        bq_ref[0] = column_sum(dq)
        bv_ref[0] = column_sum(dv)

    spec = lambda which: pl.BlockSpec((length, block), lambda s, p: (s, which * blocks + p))
    sums = pl.BlockSpec((1, 1, block), lambda s, p: (s, 0, p))
    return call(
        kernel,
        "attend_back",
        [qkv, qkv, qkv, ot, probs, share, do],
        [
            spec(0),
            spec(1),
            spec(2),
            pl.BlockSpec((block, length), lambda s, p: (p, s)),
            pl.BlockSpec((1, heads, length, length), lambda s, p: (s, p, 0, 0)),
            pl.BlockSpec((1, 1, heads, length), lambda s, p: (s, p, 0, 0)),
            spec(part),
        ],
        (like((3, tokens, width)), like((seqs, 1, width), F32), like((seqs, 1, width), F32)),
        (pl.BlockSpec((3, length, block), lambda s, p: (0, s, p)), sums, sums),
        grid=(seqs, blocks),
        after=after,
    )


def normed(z):
    center = z - jnp.mean(z, axis=-1, keepdims=True)
    rstd = lax.rsqrt(jnp.mean(center * center, axis=-1, keepdims=True) + 1e-06)
    return center * rstd, rstd


def norm_back(dn, n, rstd):
    return rstd * (dn - jnp.mean(dn, axis=-1, keepdims=True) - n * jnp.mean(dn * n, axis=-1, keepdims=True))


def join(pieces, o0, o1, x, vec, tile=256, after=()):
    rows, width = x.shape
    count = len(pieces.buffers)

    def kernel(*refs):
        (cores_ref,), (o0_ref, o1_ref, x_ref, vec_ref), refs = refs[:1], refs[1 : 5], refs[5:]
        buffer_refs, (n_ref, r_ref, h_ref, ht_ref, whole_ref, held, arrived, left) = refs[:count], refs[count:]
        write = pltpu.make_async_copy(held, whole_ref, left)

        @pl.when(pl.program_id(0) == 0)
        def _():
            pieces.fetch(cores_ref, buffer_refs, held, arrived)
            write.start()

        half = o0_ref.shape[1]
        mixed = dot(o0_ref[...], held[:half]) + dot(o1_ref[...], held[half:])
        z = x_ref[...].astype(F32) + (mixed + vec_ref[BOUT : BOUT + 1])
        n, rstd = normed(z)
        n_ref[...] = n
        r_ref[...] = rstd
        h = (n * vec_ref[GAIN1 : GAIN1 + 1] + vec_ref[SHIFT1 : SHIFT1 + 1]).astype(BF16)
        h_ref[...] = h
        ht_ref[...] = h.T

        @pl.when(pl.program_id(0) == pl.num_programs(0) - 1)
        def _():
            write.wait()

    tok = pl.BlockSpec((tile, width), lambda i, *_: (i, 0))
    half = pl.BlockSpec((tile, width // 2), lambda i, *_: (i, 0))
    return call(
        kernel,
        "join",
        [o0, o1, x, vec] + list(pieces.buffers),
        [half, half, tok, whole(vec.shape)] + [ANY] * count,
        (like((rows, width), F32), like((rows, 1), F32), like((rows, width)), like((width, rows)), like((width, width))),
        (tok, pl.BlockSpec((tile, 1), lambda i, *_: (i, 0)), tok, pl.BlockSpec((width, tile), lambda i, *_: (0, i)), ANY),
        grid=(rows // tile,),
        scalars=[pieces.cores],
        scratch=pieces.scratch(),
        after=after,
    )


def inner(h, rest, bias, tile=512, after=()):
    rows, depth = h.shape
    cols = bias.shape[1]

    def kernel(h_ref, w_ref, b_ref, u_ref, g_ref):
        f = dot(h_ref[...], w_ref[...]) + b_ref[...]
        weight = 0.5 + 0.5 * lax.erf(f * math.sqrt(0.5))
        u_ref[...] = (f * weight).astype(BF16)
        bell = jnp.exp2((f * f) * (-0.5 * math.log2(math.e)))
        g_ref[...] = (weight + (f * (1.0 / math.sqrt(2.0 * math.pi))) * bell).astype(BF16)

    out = pl.BlockSpec((rows, tile), lambda i: (0, i))
    return call(
        kernel,
        "inner",
        [h, rest, bias],
        [whole(h.shape), pl.BlockSpec((depth, tile), lambda i: (0, i)), pl.BlockSpec((1, tile), lambda i: (0, i))],
        (like((rows, cols)), like((rows, cols))),
        (out, out),
        grid=(cols // tile,),
        after=after,
    )


def outer(pieces, u, n1, cot, vec, tile=256, after=()):
    rows, depth = u.shape
    width = n1.shape[1]
    count = len(pieces.buffers)

    def kernel(*refs):
        (cores_ref,), (u_ref, n_ref, c_ref, vec_ref), refs = refs[:1], refs[1 : 5], refs[5:]
        buffer_refs, (out_ref, dz_ref, dm_ref, dmt_ref, sums_ref, whole_ref, held, arrived, left) = refs[:count], refs[count:]
        write = pltpu.make_async_copy(held, whole_ref, left)

        @pl.when(pl.program_id(0) == 0)
        def _():
            sums_ref[...] = jnp.zeros_like(sums_ref)
            pieces.fetch(cores_ref, buffer_refs, held, arrived)
            write.start()

        row = lambda i: vec_ref[i : i + 1]
        z = (n_ref[...] * row(GAIN1) + row(SHIFT1)) + (dot(u_ref[...], held[...]) + row(BOUTER))
        n, rstd = normed(z)
        out_ref[...] = (n * row(GAIN2) + row(SHIFT2)).astype(BF16)
        c = c_ref[...].astype(F32)
        dz = norm_back(c * row(GAIN2), n, rstd)
        dz_ref[...] = dz
        dm = dz.astype(BF16)
        dm_ref[...] = dm
        dmt_ref[...] = dm.T
        sums_ref[0:1, :] += column_sum(dm)
        sums_ref[1:2, :] += column_sum(c * n)
        sums_ref[2:3, :] += column_sum(c)

        @pl.when(pl.program_id(0) == pl.num_programs(0) - 1)
        def _():
            write.wait()

    tok = pl.BlockSpec((tile, width), lambda i, *_: (i, 0))
    return call(
        kernel,
        "outer",
        [u, n1, cot, vec] + list(pieces.buffers),
        [pl.BlockSpec((tile, depth), lambda i, *_: (i, 0)), tok, tok, whole(vec.shape)] + [ANY] * count,
        (like((rows, width)), like((rows, width), F32), like((rows, width)), like((width, rows)), like((8, width), F32), like((depth, width))),
        (tok, tok, tok, pl.BlockSpec((width, tile), lambda i, *_: (0, i)), whole((8, width)), ANY),
        grid=(rows // tile,),
        scalars=[pieces.cores],
        scratch=pieces.scratch(),
        after=after,
    )


def outer_grad(half, dmt, u, groups, after=()):
    width, rows = dmt.shape
    cols = u.shape[1]
    part = cols // groups
    blocks = 2048 // part

    def kernel(half_ref, left_ref, right_ref, out_ref):
        made = dot(left_ref[...], right_ref[...]).astype(BF16)
        for i in range(blocks):
            out_ref[:, i] = made[:, i * part : (i + 1) * part].reshape(2, width // 4, part)

    return call(
        kernel,
        "outer_grad",
        [dmt, u],
        [pl.BlockSpec((width // 2, rows), lambda i, half: (half[0], 0)), pl.BlockSpec((rows, blocks * part), lambda i, half: (0, i))],
        like((2, groups, width // 4, part)),
        pl.BlockSpec((2, blocks, width // 4, part), lambda i, half: (0, i, 0, 0)),
        grid=(groups // blocks,),
        scalars=[half],
        after=after,
    )


def inner_back(halves, dm, w2, slope, ht, w1, groups, tile=512, after=()):
    rows, width = dm.shape
    cols = slope.shape[1]
    steps = cols // 2 // tile
    per = steps // 2

    def kernel(halves_ref, dm_ref, w2_ref, g_ref, ht_ref, w1_ref, first_ref, second_ref, dh_ref, sum_ref):
        step = pl.program_id(0)

        @pl.when(step == 0)
        def _():
            dh_ref[...] = jnp.zeros_like(dh_ref)

        df = (dot_nt(dm_ref[...], w2_ref[...]) * g_ref[...].astype(F32)).astype(BF16)
        sum_ref[...] = column_sum(df)
        made = dot(ht_ref[...], df).astype(BF16).reshape(first_ref.shape)

        @pl.when(step < steps)
        def _():
            first_ref[...] = made

        @pl.when(step >= steps)
        def _():
            second_ref[...] = made

        dh_ref[...] += dot_nt(df, w1_ref[...])

    at = lambda i, halves: halves[i // steps] * steps + i % steps
    grad = like((2, groups, width // groups, cols // 4))
    block = (1, groups, width // groups, tile)
    kept = lambda step: (step // per, 0, 0, step % per)
    return call(
        kernel,
        "inner_back",
        [dm, w2, slope, ht, w1],
        [
            whole(dm.shape),
            pl.BlockSpec((tile, width), lambda i, halves: (at(i, halves), 0)),
            pl.BlockSpec((rows, tile), lambda i, halves: (0, at(i, halves))),
            whole(ht.shape),
            pl.BlockSpec((width, tile), lambda i, halves: (0, at(i, halves))),
        ],
        (grad, grad, like((rows, width), F32), like((1, cols), F32)),
        (
            pl.BlockSpec(block, lambda i, halves: kept(jnp.minimum(i, steps - 1))),
            pl.BlockSpec(block, lambda i, halves: kept(jnp.maximum(i - steps, 0))),
            whole((rows, width)),
            pl.BlockSpec((1, tile), lambda i, halves: (0, at(i, halves))),
        ),
        grid=(2 * steps,),
        scalars=[halves],
        after=after,
    )


def join_back(dz2, dh, n1, rstd, vec, w, tile=256, after=()):
    rows, width = dz2.shape

    def kernel(dz2_ref, dh_ref, n_ref, r_ref, vec_ref, w_ref, dz_ref, da_ref, do_ref, sums_ref):
        @pl.when(pl.program_id(0) == 0)
        def _():
            sums_ref[...] = jnp.zeros_like(sums_ref)

        dh = dz2_ref[...] + dh_ref[...]
        n = n_ref[...]
        dz = norm_back(dh * vec_ref[GAIN1 : GAIN1 + 1], n, r_ref[...])
        dz_ref[...] = dz
        da = dz.astype(BF16)
        da_ref[...] = da
        do_ref[...] = dot_nt(da, w_ref[...]).astype(BF16)
        sums_ref[0:1, :] += column_sum(da)
        sums_ref[1:2, :] += column_sum(dh * n)
        sums_ref[2:3, :] += column_sum(dh)

    tok = pl.BlockSpec((tile, width), lambda i: (i, 0))
    return call(
        kernel,
        "join_back",
        [dz2, dh, n1, rstd, vec, w],
        [tok, tok, tok, pl.BlockSpec((tile, 1), lambda i: (i, 0)), whole(vec.shape), whole(w.shape)],
        (like((rows, width), F32), like((rows, width)), like((rows, width)), like((8, width), F32)),
        (tok, tok, tok, whole((8, width))),
        grid=(rows // tile,),
        after=after,
    )


def token_weights_grad(halves, xt, d, groups, mixed=None, extra=None, after=()):
    width, rows = xt.shape
    part = d.shape[2] // 2
    last = width // 4
    mixed_at = -(-3 * part // (2 * last)) * last
    cols = mixed_at + last if mixed else 3 * part // 2
    more = 0 if extra is None else extra.shape[1]
    keep = width // groups

    def kernel(halves_ref, left_ref, d_ref, *refs):
        refs, first_ref, second_ref = refs[:-2], refs[-2], refs[-1]

        def fill(out_ref):
            def store(made, start, group, blocks):
                size = made.shape[1] // 2
                for x in range(2):
                    piece = made[:, x * size : (x + 1) * size].reshape(blocks, keep, size)
                    out_ref[x, group : group + blocks, :keep, start : start + size] = piece

            for which in range(3):
                store(dot(left_ref[...], d_ref[which]).astype(BF16), which * (part // 2), 0, groups)
            if mixed:
                for i in range(2):
                    store(dot(refs[i][...], refs[2][...]).astype(BF16), mixed_at, i * groups // 2, groups // 2)
                if mixed_at > 3 * part // 2:
                    out_ref[:, :, :, 3 * part // 2 : mixed_at] = jnp.zeros((2, groups, keep, mixed_at - 3 * part // 2), BF16)
            if more:
                for x in range(2):
                    out_ref[x, :, keep:, :] = refs[-1][...]

        @pl.when(pl.program_id(0) == 0)
        def _():
            fill(first_ref)

        @pl.when(pl.program_id(0) == 1)
        def _():
            fill(second_ref)

    operands = [xt, d]
    specs = [whole(xt.shape), pl.BlockSpec((3, rows, part), lambda i, halves: (0, 0, halves[i]))]
    if mixed:
        operands += mixed
        specs += [whole(mixed[0].shape), whole(mixed[1].shape), pl.BlockSpec((rows, width // 2), lambda i, halves: (0, halves[i]))]
    if more:
        operands.append(extra)
        specs.append(whole(extra.shape))
    shape = (2, groups, keep + more, cols)
    return call(
        kernel,
        "token_weights_grad",
        operands,
        specs,
        (like(shape), like(shape)),
        (whole(shape), whole(shape)),
        grid=(2,),
        scalars=[halves],
        after=after,
    )


def token_grad(base, d, w, dtype, tile=256, after=()):
    rows, width = base.shape
    part = d.shape[2]

    def kernel(base_ref, d_ref, w_ref, out_ref):
        total = base_ref[...]
        for i in range(3):
            total = total + dot_nt(d_ref[i], w_ref[:, i * part : (i + 1) * part])
        out_ref[...] = total.astype(dtype)

    tok = pl.BlockSpec((tile, width), lambda i: (i, 0))
    return call(
        kernel,
        "token_grad",
        [base, d, w],
        [tok, pl.BlockSpec((3, tile, part), lambda i: (0, i, 0)), whole(w.shape)],
        like((rows, width), dtype),
        tok,
        grid=(rows // tile,),
        after=after,
    )


def digits_of(axis, total, base):
    digits, stride = [], total
    while stride > 1:
        size = base if stride % base == 0 else 2
        stride //= size
        digits.append((axis, stride, size))
    return digits


def total_of(terms):
    total = terms[0].astype(F32)
    for term in terms[1:]:
        total = total + term.astype(F32)
    return total.astype(BF16)


class Layout:
    def __init__(self, mesh):
        self.replicas, self.groups = mesh.shape["replica"], mesh.shape["group"]
        self.group = digits_of("group", self.groups, 4)
        replica = digits_of("replica", self.replicas, 2)
        self.core, self.over = replica[-1], replica[:-1]
        self.sizes = {"replica": self.replicas, "group": self.groups}
        self.devices = self.replicas * self.groups
        cores = self.core[2]
        self.same_core = [
            [r * self.groups + g for r in range(c, self.replicas, cores) for g in range(self.groups)] for c in range(cores)
        ]

    def place(self, digit):
        axis, stride, size = digit
        return (lax.axis_index(axis) // stride) % size

    def send(self, value, digit, shift=1):
        axis, stride, size = digit
        pairs = []
        for i in range(self.sizes[axis]):
            own = (i // stride) % size
            pairs.append((i, i + ((own + shift) % size - own) * stride))
        return lax.ppermute(value, axis, pairs)

    def sends(self, value, digit):
        return [self.send(value, digit, k) for k in range(1, digit[2])]

    def pieces(self, parts, shape):
        core = self.place(self.core).astype(jnp.int32)
        cores = jnp.stack([core, 1 - core])
        buffers, spans, start = [], [], 0
        for chain, cols in parts:
            came = self.send(chain.value, self.core)
            blocks = math.prod(d[2] for d in self.over)
            for buffer in (chain.value, came):
                buffers.append(buffer.reshape(blocks, -1, buffer.shape[-1]))
                spans.append((0, cols, start))
            start += cols
        return Pieces(cores, buffers, spans, shape)

    def along(self, digit):
        axis, stride, size = digit
        stride *= self.groups if axis == "replica" else 1
        starts = [d for d in range(self.devices) if d // stride % size == 0]
        return [[d + k * stride for k in range(size)] for d in starts]


class Chain:
    def __init__(self, layout, value, order, done=()):
        self.layout, self.value, self.order, self.done = layout, value, list(order), list(done)
        self.came = layout.sends(value, self.order[0]) if self.order else []

    def job(self, first=0, cols=None):
        digits = self.layout.over + self.layout.group
        axis = sum(digits.index(d) < digits.index(self.order[0]) for d in self.done)
        place = self.layout.place(self.order[0]).astype(jnp.int32).reshape(1)
        return [self.value] + self.came, place, axis, first, self.value.shape[-1] if cols is None else cols

    def after(self, value, order=None):
        return Chain(self.layout, value, (self.order if order is None else order)[1:], self.done + self.order[:1])


def move(*chains, carry=()):
    values = stack([c.job() for c in chains], carry)
    values, carried = values if carry else (values, ())
    moved = [c.after(v) for c, v in zip(chains, values)]
    return moved + list(carried)


class Reduction:
    def __init__(self, layout, terms, order):
        self.layout, self.dims, self.terms, self.order = layout, layout.over + layout.group, terms, list(order)

    def job(self):
        digit = self.digit = self.order.pop(0)
        axis = self.dims.index(digit)
        count = lambda dims: math.prod(d[2] for d in dims)
        shape = (count(self.dims[:axis]), digit[2], count(self.dims[axis + 1 :]))
        self.dims = self.dims[:axis] + self.dims[axis + 1 :]
        terms = [(t.reshape(shape + t.shape[-2:]), block, cols) for t, block, cols in self.terms]
        return self.layout.place(digit).astype(jnp.int32).reshape(1), terms

    def take(self, made):
        came = [self.layout.send(s, self.digit, k + 1) for k, s in enumerate(made[:-1])]
        self.terms = [(t, (0, 0), t.shape[-2:]) for t in [made[-1]] + came]

    def came(self):
        return [t for t, _, _ in self.terms[1:]]

    def last(self):
        return [t.reshape((-1,) + t.shape[-2:]) for t, _, _ in self.terms]


def step(*reductions, carry=(), after=()):
    jobs = [r.job() for r in reductions]
    if len({r.digit[2] for r in reductions}) == 1:
        made, carry = combine(jobs, carry, after)
    else:
        made = []
        for job in jobs:
            one, carry = combine([job], carry, after)
            made += one
    for reduction, one in zip(reductions, made):
        reduction.take(one)
    return carry


def local(layout, tokens, segment_ids, w_query, b_query, w_key, w_value, b_value, w_out, b_out, gain_first, shift_first, w_inner, b_inner, w_outer, b_outer, gain_second, shift_second, cotangent):
    LAST.clear()
    groups, devices = layout.groups, layout.devices
    seqs, length = segment_ids.shape
    width = tokens.shape[1]
    hidden = w_inner.shape[1]
    each = b_query.shape[0]
    half = width // 2
    core = layout.place(layout.core).astype(jnp.int32)
    mine, theirs = core.reshape(1), (1 - core).reshape(1)
    halves = jnp.concatenate([theirs, mine])
    z_digit, y_digits = layout.group[:1], layout.group[1:]
    zxy, zyx = z_digit + layout.over + y_digits, z_digit + y_digits + layout.over
    xyz, yxz = layout.over + y_digits + z_digit, y_digits + layout.over + z_digit

    vectors = (b_query, b_value, b_out, gain_first, shift_first, b_outer, gain_second, shift_second, b_inner)
    lanes, cut, wide = 128, 3 * half // 2, (3 * half + width) // 2
    (first,) = pack([w_query, w_key, w_value], [[(0, 0, half), (1, 0, half), (2, 0, half)]], vectors)
    high = first.shape[0]
    first = Chain(layout, first, zxy)
    xt = transposed(tokens)
    a, b = stack([first.job(0, cut), first.job(cut, cut + lanes)])
    a, b = first.after(a), first.after(b, zyx)
    second, last, inner_rows = pack(
        [w_query, w_key, w_value, w_out, w_outer, w_inner],
        [[(0, half, half), (1, half, half), (2, half, half), (3, 0, width)], [(4, 0, width)], [(5, 0, hidden)]],
    )
    second = Chain(layout, second, zxy)
    (va, vb, vc, vd), (inner_rows,) = stack([a.job(), b.job(), second.job(0, wide), second.job(wide, wide)], carry=[inner_rows])
    a, b, c, d = a.after(va), b.after(vb), second.after(vc), second.after(vd, zyx)
    whole_winner = lax.all_gather(inner_rows, ("replica", "group"), axis=0, tiled=True)
    while a.order:
        a, b, c, d = move(a, b, c, d)
    pieces0 = layout.pieces([(a, cut), (b, cut)], (width, 3 * half))
    spots = vector_places(vectors, high)
    used = max(r for r, _ in spots) + 1
    both = [v.reshape(-1, groups, high, v.shape[-1])[:, :, :used, cut:].astype(F32) for v in pieces0.buffers[-2:]]
    small = jnp.stack([jnp.where(core == k, both[0], both[1]) for k in range(2)], axis=1).reshape(devices, used, lanes)
    vec = jnp.stack([small[:, r, l : l + each].reshape(width) for r, l in spots[:-1]])
    r, l = spots[-1]
    whole_binner = small[:, r, l : l + b_inner.shape[0]].reshape(1, -1)
    row, col = segment_ids.reshape(seqs, 1, length), segment_ids.reshape(seqs, length, 1)

    qkv0, wqkv0 = project(pieces0, tokens, vec, 0)
    while c.order:
        c, d, last = move(c, d, carry=[last])
    pieces1 = layout.pieces([(c, wide), (d, wide)], (width, 3 * half + width))
    last = Chain(layout, last, zxy)
    o0, ot0, probs0, share0 = attend(qkv0, row, col)
    qkv1, wqkv1 = project(pieces1.part(0, 3 * half), tokens, vec, 1)
    e, f = stack([last.job(0, half), last.job(half, half)])
    e, f = last.after(e), last.after(f, zyx)
    o1, ot1, probs1, share1 = attend(qkv1, row, col)
    while len(e.order) > 1:
        e, f = move(e, f)
    n1, rstd1, h, ht, whole_wout = join(pieces1.part(3 * half, width), o0, o1, tokens, vec)
    u, slope = inner(h, whole_winner, whole_binner)
    e, f = move(e, f)
    pieces2 = layout.pieces([(e, half), (f, half)], (w_outer.shape[0] * devices, width))
    out, dz2, dm, dmt, sums2, whole_wouter = outer(pieces2, u, n1, cotangent, vec)

    def reduction(other, own, *orders, by_rows=False, runs=None):
        came = layout.send(other, layout.core)
        rows, cols = own.shape[2:]
        if by_rows:
            parts = [((i, 0), (rows // len(orders), cols)) for i in range(len(orders))]
        else:
            runs = runs or [(i * cols // len(orders), cols // len(orders)) for i in range(len(orders))]
            parts = [((0, start // size), (rows, size)) for start, size in runs]
        return [Reduction(layout, [(own,) + part, (came,) + part], order) for part, order in zip(parts, orders)]

    def along_z(reductions):
        sums = add_up([[t.reshape(-1, t.shape[-1]) for t in r.last()] for r in reductions])
        return lax.psum_scatter(sums, ("replica", "group"), scatter_dimension=0, axis_index_groups=layout.along(z_digit[0]), tiled=True)

    def across_z(reductions):
        made = gather_sums(layout.place(z_digit[0]).astype(jnp.int32).reshape(1), [r.last() for r in reductions])
        return [made[-1]] + [layout.send(s, z_digit[0], k + 1) for k, s in enumerate(made[:-1])]

    spread = lambda block: lax.all_gather(block, "replica", axis=0, tiled=False)
    other = outer_grad(theirs, dmt, u, groups)
    own = outer_grad(mine, dmt, u, groups)
    outers = reduction(other, own, xyz, yxz, by_rows=True)
    step(*outers)
    other, own, dh, sum_inner = inner_back(halves, dm, whole_wouter, slope, ht, whole_winner, groups)
    for _ in range(len(xyz) - 2):
        (other,) = step(*outers, carry=[other])
    inners = reduction(other, own, xyz, yxz)
    dz1, da, do, sums1 = join_back(dz2, dh, n1, rstd1, vec, whole_wout)
    got_wouter = along_z(outers)
    step(*inners)
    d0, sq0, sv0 = attend_back(qkv0, ot0, probs0, share0, do, 0)
    other, own = token_weights_grad(halves, xt, d0, groups, mixed=[ot0, ot1, da])
    for _ in range(len(xyz) - 2):
        (other,) = step(*inners, carry=[other])
    runs = ((0, 3 * half // 4), (other.shape[3] - width // 4, width // 4))
    firsts = reduction(other, own, xyz, yxz, runs=runs)
    d1, sq1, sv1 = attend_back(qkv1, ot1, probs1, share1, do, 1)
    bq = jnp.concatenate([jnp.sum(s, axis=0) for s in (sq0, sq1)], axis=1)
    bv = jnp.concatenate([jnp.sum(s, axis=0) for s in (sv0, sv1)], axis=1)
    sums = jnp.concatenate([bq, bv, sums1[:3], sums2[:3]], axis=0)
    sums = sums.reshape(8, groups, -1).transpose(1, 0, 2).reshape(groups, -1)
    sums = jnp.concatenate([sums, sum_inner.reshape(groups, -1)], axis=1)
    used, cols = sums.shape[1], 3 * half // 4
    extra = jnp.pad(sums.astype(BF16), ((0, 0), (0, 16 * cols - used))).reshape(groups, 16, cols)
    got_winner = along_z(inners)
    step(*firsts)
    partial = token_grad(dz1, d0, wqkv0, F32)
    other, own = token_weights_grad(halves, xt, d1, groups, extra=extra)
    for _ in range(len(xyz) - 2):
        (other,) = step(*firsts, carry=[other])
    seconds = reduction(other, own, xyz, yxz, runs=((0, 2 * cols // 3), (2 * cols // 3, cols // 3)))
    grad_tokens = token_grad(partial, d1, wqkv1, BF16)
    step(*seconds, after=[t for r in firsts for t in r.came()])
    first_sums = across_z(firsts)
    for _ in range(len(xyz) - 2):
        step(*seconds, after=first_sums[1:])
    second_sums = across_z(seconds)
    got_wouter, got_winner = spread(got_wouter), spread(got_winner)
    cores = layout.core[2]
    order = [r % cores * (layout.replicas // cores) + r // cores for r in range(layout.replicas)]
    grad_wouter = outer_result(got_wouter, order)
    grad_winner = inner_result(got_winner, order)
    got = [add_up([first_sums, second_sums])]
    places = jnp.zeros((1,), jnp.int32)
    weight = 1
    for digit in layout.over[::-1] + [layout.core]:
        own = layout.place(digit).astype(jnp.int32)
        places = jnp.concatenate([places + own * weight, places + (1 - own) * weight])
        got = got + [layout.send(g, digit) for g in got]
        weight *= digit[2]
    keep = width // groups
    wq, wk, wv, grad_wout, sums = token_weights_result(got, places, keep, half // 4, width // 4)
    sums = sums.reshape(-1)[:used]
    bq, bv, bout, gain1, shift1, bouter, gain2, shift2 = (sums[i * keep : (i + 1) * keep] for i in range(8))
    binner = sums[8 * keep :]
    return (out, grad_tokens, wq, bq, wk, wv, bv, grad_wout, bout, gain1, shift1, grad_winner, binner, grad_wouter, bouter, gain2, shift2)


def solution(mesh):
    layout = Layout(mesh)
    both = ("replica", "group")
    rows, vector = P(both, None), P(both)
    in_specs = (rows, rows, rows, vector, rows, rows, vector, rows, vector, vector, vector, rows, vector, rows, vector, vector, vector, rows)
    kept, kept_vector = P("group", None), P("group")
    out_specs = (rows, rows, kept, kept_vector, kept, kept, kept_vector, kept, kept_vector, kept_vector, kept_vector, kept, kept_vector, kept, kept_vector, kept_vector, kept_vector)
    return jax.shard_map(functools.partial(local, layout), mesh=mesh, in_specs=in_specs, out_specs=out_specs, check_vma=False)
```

time: 1550 us -> 496 us (0.32)
  waiting for transfers between devices: 923 us -> 104 us
  matrix products: 270 us -> 0 us
  Pallas kernels: 0 us -> 254 us
  blocking collectives: 138 us -> 0 us
  other arithmetic: 88.1 us -> 2.38 us
  starting transfers between devices: 0.98 us -> 48 us
  local copies, waits for them, and re-layouts: 105 us -> 63.8 us
    reduce_scatter x6 -> x2, waiting for transfers between devices: 720 us -> 0.01 us  [along_z(): lax.psum_scatter(sums, ('replica', 'group'), scatter_dimension=0, axis_in...]
    dot_general x32 -> x0, matrix products: 270 us -> none  [the longest x6 58.7 us: right_product(): lax.dot_general(left, right, (((1,), (1,)), ((), ())), preferred_element_...]
    pallas_call x0 -> x43, Pallas kernels: none -> 254 us  [call(): pl.pallas_call(body, out_shape=shapes + [jax.ShapeDtypeStruct(c.shape, c....]
    all_gather x6 -> x3, waiting for transfers between devices: 145 us -> 0.02 us  [the longest x1 0.02 us: local(): lax.all_gather(inner_rows, ('replica', 'group'), axis=0, tiled=True)]
    ppermute x0 -> x56, waiting for transfers between devices: none -> 104 us  [send(): return lax.ppermute(value, axis, pairs)]
    unnamed x2 -> x0, blocking collectives: 68.9 us -> none
    all_gather x1 -> x0, blocking collectives: 56.9 us -> none  [local(): lax.all_gather(b_inner, ('replica', 'group'), axis=0, tiled=True)]
    psum x1 -> x0, waiting for transfers between devices: 54.1 us -> none  [local(): lax.psum(part_wquery.astype(jnp.bfloat16), 'replica').astype(jnp.float32)]
  transfers between devices with their start and end apart: 13 -> 61, of which waited for: 8 -> 27; matrix products, arithmetic and copies ran while one was open for 23% -> 2% of each run, Pallas kernels for 0% -> 44%
where the time goes in v2:
time: 496 us; the launch traced here: 488 us
  Pallas kernels  254 us (51%)
  waiting for transfers between devices  104 us (21%)
  local copies, waits for them, and re-layouts  63.8 us (13%)
  starting transfers between devices  48 us (10%)
  between operations  15.1 us (3%)
    pallas_call x43, Pallas kernels, call(): pl.pallas_call(body, out_shape=shapes + [jax.ShapeDtypeStruct(c.shape, c....  254 us
    ppermute x56, waiting for transfers between devices, send(): return lax.ppermute(value, axis, pairs)  104 us
    unnamed x171, local copies, waits for them, and re-layouts  56.8 us
    ppermute x56, starting transfers between devices, send(): return lax.ppermute(value, axis, pairs)  47.8 us
  transfers between devices with their start and end apart: 61, of which 27 were waited for; matrix products, arithmetic and copies ran while one was open for 2% of the time, Pallas kernels for 44%

profile of v2, /device:TPU:9, one launch (start us, length us, event | category | flops | bytes accessed | tf_op | source)
XLA Modules:
  0.0 487.8 jit_solution(16487176056864204069)
XLA Ops:
  19.6 4.1 transposed.1.refs_10_.refs_1_
  23.7 1.9 collective-permute-done.1.refs_4_.refs_8_
  25.6 2.8 collective-permute-done.2.refs_5_.refs_9_
  36.0 2.5 collective-permute-done.5.refs_9_.refs_13_
  38.5 8.7 %collective-permute-done.6.refs_10_.refs_14_ = bf16[32,2560]{1,0:T(8,128)(2,1)S(1)} collective-permute-done((bf16[32,2560]{1,0:T(8,128)(2,1)S(1)}, bf16[32,2560]{1,0:T(8,128)(2,1)S(1)}, u32[]{:S(2)}, u32[]{:S(2)}) %collective-permute-start.6) | collective-permute-done | bytes 163872 | tf_op jit(solution)/shard_map/ppermute | solution.py:856
  47.1 2.9 collective-permute-done.7.refs_11_.refs_15_
  57.3 16.2 %collective-permute-done.10.refs_9_ = bf16[4,32,1280]{2,1,0:T(8,128)(2,1)S(1)} collective-permute-done((bf16[4,32,1280]{2,1,0:T(8,128)(2,1)S(1)}, bf16[4,32,1280]{2,1,0:T(8,128)(2,1)S(1)}, u32[]{:S(2)}, u32[]{:S(2)}) %collective-permute-start.10) | collective-permute-done | bytes 327712 | tf_op jit(solution)/shard_map/ppermute | solution.py:856
  83.1 9.0 %project.2 = (bf16[1024,1536]{1,0:T(8,128)(2,1)}, bf16[1024,1536]{1,0:T(8,128)(2,1)}) custom-call(s32[2]{0:T(128)} %pad_add_fusion.refs_0_, bf16[1024,1024]{1,0:T(8,128)(2,1)} %refs_3_.6, f32[8,1024]{1,0:T(8,128)} %stack.40.refs_2_.refs_4_, bf16[2,256,768]{2,1,0:T(8,128)(2,1)} %bitcast.145, bf16[2,256,768]{2,1,0:T(8,128)(2,1)} %bitcast.11.refs_4_, ...), custom_call_target="tpu_custom_call" | custom-call | flops 1 | bytes 1 | tf_op jit(solution)/shard_map/project/pallas_call | solution.py:37
  92.1 7.2 %collective-permute-done.14.refs_3_ = bf16[2,4,32,1280]{3,2,1,0:T(8,128)(2,1)} collective-permute-done((bf16[2,4,32,1280]{3,2,1,0:T(8,128)(2,1)}, bf16[2,4,32,1280]{3,2,1,0:T(8,128)(2,1)}, u32[]{:S(2)}, u32[]{:S(2)}) %collective-permute-start.14) | collective-permute-done | bytes 655392 | tf_op jit(solution)/shard_map/ppermute | solution.py:856
  99.3 3.6 collective-permute-done.15.refs_5_
  103.0 1.9 copy-done.9
  109.4 1.9 collective-permute-start.20
  113.0 12.6 %attend.2 = (bf16[1024,512]{1,0:T(8,128)(2,1)}, bf16[512,1024]{1,0:T(8,128)(2,1)}, bf16[2,8,512,512]{3,2,1,0:T(8,128)(2,1)}, f32[2,2,4,512]{3,2,1,0:T(4,128)}) custom-call(bf16[1024,1536]{1,0:T(8,128)(2,1)} %get-tuple-element.142.refs_0_.refs_1_.refs_2_, bf16[1024,1536]{1,0:T(8,128)(2,1)} %get-tuple-element.142.refs_0_.refs_1_.refs_2_, ...), custom_call_target="tpu_custom_call" | custom-call | flops 1 | bytes 1 | tf_op jit(solution)/shard_map/attend/pallas_call | solution.py:37
  125.6 9.1 %project.3 = (bf16[1024,1536]{1,0:T(8,128)(2,1)}, bf16[1024,1536]{1,0:T(8,128)(2,1)}) custom-call(s32[2]{0:T(128)} %pad_add_fusion.refs_0_, bf16[1024,1024]{1,0:T(8,128)(2,1)} %refs_3_.6, f32[8,1024]{1,0:T(8,128)} %stack.40.refs_2_.refs_4_, bf16[2,256,1280]{2,1,0:T(8,128)(2,1)} %bitcast.131, bf16[2,256,1280]{2,1,0:T(8,128)(2,1)} %bitcast.16.refs_4_, ...), custom_call_target="tpu_custom_call" | custom-call | flops 1 | bytes 1 | tf_op jit(solution)/shard_map/project/pallas_call | solution.py:37
  134.7 18.2 %collective-permute-done.19.refs_4_.refs_8_ = bf16[128,1024]{1,0:T(8,128)(2,1)S(1)} collective-permute-done((bf16[128,1024]{1,0:T(8,128)(2,1)S(1)}, bf16[128,1024]{1,0:T(8,128)(2,1)S(1)}, u32[]{:S(2)}, u32[]{:S(2)}) %collective-permute-start.19) | collective-permute-done | bytes 262176 | tf_op jit(solution)/shard_map/ppermute | solution.py:856
  161.4 12.6 %attend.3 = (bf16[1024,512]{1,0:T(8,128)(2,1)}, bf16[512,1024]{1,0:T(8,128)(2,1)}, bf16[2,8,512,512]{3,2,1,0:T(8,128)(2,1)}, f32[2,2,4,512]{3,2,1,0:T(4,128)}) custom-call(bf16[1024,1536]{1,0:T(8,128)(2,1)} %get-tuple-element.150.refs_0_.refs_1_.refs_2_, bf16[1024,1536]{1,0:T(8,128)(2,1)} %get-tuple-element.150.refs_0_.refs_1_.refs_2_, ...), custom_call_target="tpu_custom_call" | custom-call | flops 1 | bytes 1 | tf_op jit(solution)/shard_map/attend/pallas_call | solution.py:37
  178.1 10.4 %join.1 = (f32[1024,1024]{1,0:T(8,128)}, f32[1024,1]{1,0:T(8,128)}, bf16[1024,1024]{1,0:T(8,128)(2,1)}, bf16[1024,1024]{1,0:T(8,128)(2,1)}, bf16[1024,1024]{1,0:T(8,128)(2,1)}) custom-call(s32[2]{0:T(128)} %pad_add_fusion.refs_0_, bf16[1024,512]{1,0:T(8,128)(2,1)} %get-tuple-element.147.refs_1_, bf16[1024,512]{1,0:T(8,128)(2,1)} %get-tuple-element.154.refs_2_, ...), custom_call_target="tpu_custom_call" | custom-call | flops 1 | bytes 1 | tf_op jit(solution)/shard_map/join/pallas_call | solution.py:37
  188.5 18.9 %inner.1 = (bf16[1024,4096]{1,0:T(8,128)(2,1)}, bf16[1024,4096]{1,0:T(8,128)(2,1)}) custom-call(bf16[1024,1024]{1,0:T(8,128)(2,1)} %get-tuple-element.158.refs_0_, bf16[1024,4096]{1,0:T(8,128)(2,1)} %all-gather.6.cloned.1.call-done.refs_1_.refs_5_, f32[1,4096]{1,0:T(1,128)} %bitcast.171, bf16[1024,1024]{1,0:T(8,128)(2,1)} %get-tuple-element.160.refs_3_.refs_5_), custom_call_target="tpu_custom_call" | custom-call | flops 1 | bytes 1 | tf_op jit(solution)/shard_map/inner/pallas_call | solution.py:37
  207.5 3.4 copy-done.2
  212.3 2.1 collective-permute-start.25
  214.5 3.7 collective-permute-done.25
  218.2 3.0 collective-permute-done.26
  222.6 21.1 %outer.1 = (bf16[1024,1024]{1,0:T(8,128)(2,1)}, f32[1024,1024]{1,0:T(8,128)}, bf16[1024,1024]{1,0:T(8,128)(2,1)}, bf16[1024,1024]{1,0:T(8,128)(2,1)}, f32[8,1024]{1,0:T(8,128)}, /*index=5*/bf16[4096,1024]{1,0:T(8,128)(2,1)}) custom-call(s32[2]{0:T(128)} %pad_add_fusion.refs_0_, bf16[1024,4096]{1,0:T(8,128)(2,1)} %get-tuple-element.161.refs_1_.refs_2_, ...), custom_call_target="tpu_custom_call" | custom-call | flops 1 | bytes 1 | tf_op jit(solution)/shard_map/outer/pallas_call | solution.py:37
  243.7 8.5 %outer_grad.2.refs_3_ = bf16[2,8,256,512]{3,2,1,0:T(8,128)(2,1)} custom-call(s32[1]{0:T(128)} %bitcast.1.refs_0_, bf16[1024,1024]{1,0:T(8,128)(2,1)} %get-tuple-element.172.refs_1_, bf16[1024,4096]{1,0:T(8,128)(2,1)} %get-tuple-element.161.refs_1_.refs_2_, bf16[4096,1024]{1,0:T(8,128)(2,1)} %get-tuple-element.170.refs_3_.refs_2_), custom_call_target="tpu_custom_call" | custom-call | flops 1 | bytes 1 | tf_op jit(solution)/shard_map/outer_grad/pallas_call | solution.py:37
  252.6 8.5 %outer_grad.3.refs_6_ = bf16[2,8,256,512]{3,2,1,0:T(8,128)(2,1)} custom-call(s32[1]{0:T(128)} %bitcast.refs_0_, bf16[1024,1024]{1,0:T(8,128)(2,1)} %get-tuple-element.172.refs_1_, bf16[1024,4096]{1,0:T(8,128)(2,1)} %get-tuple-element.161.refs_1_.refs_2_, bf16[2,8,256,512]{3,2,1,0:T(8,128)(2,1)} %outer_grad.2.refs_3_), custom_call_target="tpu_custom_call" | custom-call | flops 1 | bytes 1 | tf_op jit(solution)/shard_map/outer_grad/pallas_call | solution.py:37
  261.1 2.2 copy-done
  263.3 2.9 combine.8
  269.5 37.8 %inner_back.1 = (bf16[2,8,128,1024]{3,2,1,0:T(8,128)(2,1)}, bf16[2,8,128,1024]{3,2,1,0:T(8,128)(2,1)}, f32[1024,1024]{1,0:T(8,128)}, f32[1,4096]{1,0:T(1,128)}) custom-call(s32[2]{0:T(128)} %pad_add_fusion.1.refs_0_, bf16[1024,1024]{1,0:T(8,128)(2,1)} %get-tuple-element.169.refs_1_, bf16[4096,1024]{1,0:T(8,128)(2,1)} %get-tuple-element.170.refs_3_.refs_2_, ...), custom_call_target="tpu_custom_call" | custom-call | flops 1 | bytes 1 | tf_op jit(solution)/shard_map/inner_back/pallas_call | solution.py:37
  312.0 10.5 %join_back.1 = (f32[1024,1024]{1,0:T(8,128)}, bf16[1024,1024]{1,0:T(8,128)(2,1)}, bf16[1024,1024]{1,0:T(8,128)(2,1)}, f32[8,1024]{1,0:T(8,128)}) custom-call(f32[1024,1024]{1,0:T(8,128)} %get-tuple-element.168.refs_0_, f32[1024,1024]{1,0:T(8,128)} %get-tuple-element.174.refs_1_, f32[1024,1024]{1,0:T(8,128)} %get-tuple-element.162.refs_2_, ...), custom_call_target="tpu_custom_call" | custom-call | flops 1 | bytes 1 | tf_op jit(solution)/shard_map/join_back/pallas_call | solution.py:37
  326.9 2.2 copy-done.5
  329.1 3.9 combine.10
  335.3 11.8 %attend_back.2 = (bf16[3,1024,512]{2,1,0:T(8,128)(2,1)}, f32[2,1,512]{2,1,0:T(1,128)}, f32[2,1,512]{2,1,0:T(1,128)}) custom-call(bf16[1024,1536]{1,0:T(8,128)(2,1)} %get-tuple-element.142.refs_0_.refs_1_.refs_2_, bf16[1024,1536]{1,0:T(8,128)(2,1)} %get-tuple-element.142.refs_0_.refs_1_.refs_2_, ...), custom_call_target="tpu_custom_call" | custom-call | flops 1 | bytes 1 | tf_op jit(solution)/shard_map/attend_back/pallas_call | solution.py:37
  347.1 12.5 %token_weights_grad.2 = (bf16[2,8,128,768]{3,2,1,0:T(8,128)(2,1)}, bf16[2,8,128,768]{3,2,1,0:T(8,128)(2,1)}) custom-call(s32[2]{0:T(128)} %pad_add_fusion.1.refs_0_, bf16[1024,1024]{1,0:T(8,128)(2,1)} %transposed.1.refs_10_.refs_1_, bf16[3,1024,512]{2,1,0:T(8,128)(2,1)} %get-tuple-element.193.refs_2_.refs_1_, bf16[512,1024]{1,0:T(8,128)(2,1)} %get-tuple-element.183.refs_3_, ...), custom_call_target="tpu_custom_call" | custom-call | flops 1 | bytes 1 | tf_op jit(solution)/shard_map/token_weights_grad/pallas_call | solution.py:37
  361.5 2.2 combine.11
  367.8 11.8 %attend_back.3 = (bf16[3,1024,512]{2,1,0:T(8,128)(2,1)}, f32[2,1,512]{2,1,0:T(1,128)}, f32[2,1,512]{2,1,0:T(1,128)}) custom-call(bf16[1024,1536]{1,0:T(8,128)(2,1)} %get-tuple-element.150.refs_0_.refs_1_.refs_2_, bf16[1024,1536]{1,0:T(8,128)(2,1)} %get-tuple-element.150.refs_0_.refs_1_.refs_2_, ...), custom_call_target="tpu_custom_call" | custom-call | flops 1 | bytes 1 | tf_op jit(solution)/shard_map/attend_back/pallas_call | solution.py:37
  385.6 3.0 combine.12
  391.6 8.5 %token_grad.2.refs_4_.refs_0_ = f32[1024,1024]{1,0:T(8,128)} custom-call(f32[1024,1024]{1,0:T(8,128)} %get-tuple-element.182.refs_0_, bf16[3,1024,512]{2,1,0:T(8,128)(2,1)} %get-tuple-element.193.refs_2_.refs_1_, bf16[1024,1536]{1,0:T(8,128)(2,1)} %get-tuple-element.145.refs_7_.refs_2_, bf16[8,1,128,256]{3,2,1,0:T(8,128)(2,1)} %copy-done.30), custom_call_target="tpu_custom_call" | custom-call | flops 1 | bytes 1 | tf_op jit(solution)/shard_map/token_grad/pallas_call | solution.py:37
  400.1 8.4 %token_weights_grad.3 = (bf16[2,8,144,384]{3,2,1,0:T(8,128)(2,1)}, bf16[2,8,144,384]{3,2,1,0:T(8,128)(2,1)}) custom-call(s32[2]{0:T(128)} %pad_add_fusion.1.refs_0_, bf16[1024,1024]{1,0:T(8,128)(2,1)} %transposed.1.refs_10_.refs_1_, bf16[3,1024,512]{2,1,0:T(8,128)(2,1)} %get-tuple-element.210.refs_2_.refs_1_, bf16[8,16,384]{2,1,0:T(8,128)(2,1)} %bitcast.169, ...), custom_call_target="tpu_custom_call" | custom-call | flops 1 | bytes 1 | tf_op jit(solution)/shard_map/token_weights_grad/pallas_call | solution.py:37
  414.4 8.3 %token_grad.3.refs_8_ = bf16[1024,1024]{1,0:T(8,128)(2,1)} custom-call(f32[1024,1024]{1,0:T(8,128)} %token_grad.2.refs_4_.refs_0_, bf16[3,1024,512]{2,1,0:T(8,128)(2,1)} %get-tuple-element.210.refs_2_.refs_1_, bf16[1024,1536]{1,0:T(8,128)(2,1)} %get-tuple-element.152.refs_10_.refs_2_, bf16[1,4,128,256]{3,2,1,0:T(8,128)(2,1)} %copy-done.42), custom_call_target="tpu_custom_call" | custom-call | flops 1 | bytes 1 | tf_op jit(solution)/shard_map/token_grad/pallas_call | solution.py:37
  428.8 2.0 collective-permute-start.44
  433.2 8.3 %collective-permute-done.44.refs_7_.refs_2_ = bf16[128,640]{1,0:T(8,128)(2,1)S(1)} collective-permute-done((bf16[128,640]{1,0:T(8,128)(2,1)S(1)}, bf16[128,640]{1,0:T(8,128)(2,1)S(1)}, u32[]{:S(2)}, u32[]{:S(2)}) %collective-permute-start.44) | collective-permute-done | bytes 163872 | tf_op jit(solution)/shard_map/ppermute | solution.py:856
  441.5 4.5 collective-permute-done.45.refs_8_.refs_3_
  448.4 3.4 collective-permute-done.49
  451.8 1.9 collective-permute-done.48
  462.8 2.5 collective-permute-done.52.refs_7_
  469.7 4.3 collective-permute-done.53.refs_2_
  474.0 2.5 collective-permute-start.55
  477.7 2.1 token_weights_result.1
  (331 shorter events, 120.7 us)
Async XLA Ops:
  7.2 181.3 %all-gather.6.cloned.1.call-start = ((), (), s32[]{:S(2)}) async-start(), calls=%async_computation.2 | async-start | bytes 8650752 | tf_op jit(solution)/shard_map/all_gather | solution.py:971
  18.2 10.2 %collective-permute-start.2 = (bf16[32,1664]{1,0:T(8,128)(2,1)S(1)}, bf16[32,1664]{1,0:T(8,128)(2,1)S(1)}, u32[]{:S(2)}, u32[]{:S(2)}) collective-permute-start(bf16[32,1664]{1,0:T(8,128)(2,1)S(1)} %pack.2.refs_1_.refs_2_.refs_6_), channel_id=1, source_target_pairs={{0,6},{1,7},{2,0},{3,1},{4,2},{5,3},{6,4},{7,5},{8,14},{9,15},{10,... | collective-permute-start | bytes 319496 | tf_op jit(solution)/shard_map/ppermute | solution.py:856
  31.2 19.5 %collective-permute-start.4 = (bf16[4,32,896]{2,1,0:T(8,128)(2,1)S(1)}, bf16[4,32,896]{2,1,0:T(8,128)(2,1)S(1)}, u32[]{:S(2)}, u32[]{:S(2)}) collective-permute-start(bf16[4,32,896]{2,1,0:T(8,128)(2,1)S(1)} %get-tuple-element.132.refs_6_), channel_id=1, source_target_pairs={{0,1},{1,0},{2,3},{3,2},{4,5},{5,4},{6,7},{7,6},{8,9},{9,8},{10,11... | collective-permute-start | bytes 688136 | tf_op jit(solution)/shard_map/ppermute | solution.py:856
  32.5 17.5 %collective-permute-start.3 = (bf16[4,32,768]{2,1,0:T(8,128)(2,1)S(1)}, bf16[4,32,768]{2,1,0:T(8,128)(2,1)S(1)}, u32[]{:S(2)}, u32[]{:S(2)}) collective-permute-start(bf16[4,32,768]{2,1,0:T(8,128)(2,1)S(1)} %get-tuple-element.131.refs_4_), channel_id=1, source_target_pairs={{0,16},{8,24},{16,0},{24,8},{1,17},{9,25},{17,1},{25,9},{2,18},{10... | collective-permute-start | bytes 589832 | tf_op jit(solution)/shard_map/ppermute | solution.py:856
  33.8 13.3 %collective-permute-start.6 = (bf16[32,2560]{1,0:T(8,128)(2,1)S(1)}, bf16[32,2560]{1,0:T(8,128)(2,1)S(1)}, u32[]{:S(2)}, u32[]{:S(2)}) collective-permute-start(bf16[32,2560]{1,0:T(8,128)(2,1)S(1)} %get-tuple-element.133.refs_8_.refs_12_), channel_id=1, source_target_pairs={{0,4},{1,5},{2,6},{3,7},{4,0},{5,1},{6,2},{7,3},{8,12},{9,13},{10,... | collective-permute-start | bytes 491528 | tf_op jit(solution)/shard_map/ppermute | solution.py:856
  34.8 15.2 %collective-permute-start.7 = (bf16[32,2560]{1,0:T(8,128)(2,1)S(1)}, bf16[32,2560]{1,0:T(8,128)(2,1)S(1)}, u32[]{:S(2)}, u32[]{:S(2)}) collective-permute-start(bf16[32,2560]{1,0:T(8,128)(2,1)S(1)} %get-tuple-element.133.refs_8_.refs_12_), channel_id=1, source_target_pairs={{0,6},{1,7},{2,0},{3,1},{4,2},{5,3},{6,4},{7,5},{8,14},{9,15},{10,... | collective-permute-start | bytes 491528 | tf_op jit(solution)/shard_map/ppermute | solution.py:856
  52.8 331.3 %reduce-scatter.5.cloned.1.call-start = ((), (), s32[]{:S(2)}) async-start(), calls=%async_computation.4 | async-start | bytes 1310720 | tf_op jit(solution)/shard_map/reduce_scatter | solution.py:1014
  52.8 20.7 %collective-permute-start.9 = (bf16[4,2,32,896]{3,2,1,0:T(8,128)(2,1)S(1)}, bf16[4,2,32,896]{3,2,1,0:T(8,128)(2,1)S(1)}, u32[]{:S(2)}, u32[]{:S(2)}) collective-permute-start(bf16[4,2,32,896]{3,2,1,0:T(8,128)(2,1)S(1)} %get-tuple-element.136.refs_6_), channel_id=1, source_target_pairs={{0,16},{8,24},{16,0},{24,8},{1,17},{9,25},{17,1},{25,9},{2,18},{10... | collective-permute-start | bytes 1376264 | tf_op jit(solution)/shard_map/ppermute | solution.py:856
  53.1 20.4 %collective-permute-start.8 = (bf16[2,4,32,768]{3,2,1,0:T(8,128)(2,1)S(1)}, bf16[2,4,32,768]{3,2,1,0:T(8,128)(2,1)S(1)}, u32[]{:S(2)}, u32[]{:S(2)}) collective-permute-start(bf16[2,4,32,768]{3,2,1,0:T(8,128)(2,1)S(1)} %get-tuple-element.135.refs_4_), channel_id=1, source_target_pairs={{0,1},{1,0},{2,3},{3,2},{4,5},{5,4},{6,7},{7,6},{8,9},{9,8},{10,11... | collective-permute-start | bytes 1179656 | tf_op jit(solution)/shard_map/ppermute | solution.py:856
  54.1 19.4 %collective-permute-start.10 = (bf16[4,32,1280]{2,1,0:T(8,128)(2,1)S(1)}, bf16[4,32,1280]{2,1,0:T(8,128)(2,1)S(1)}, u32[]{:S(2)}, u32[]{:S(2)}) collective-permute-start(bf16[4,32,1280]{2,1,0:T(8,128)(2,1)S(1)} %get-tuple-element.137.refs_8_), channel_id=1, source_target_pairs={{0,16},{8,24},{16,0},{24,8},{1,17},{9,25},{17,1},{25,9},{2,18},{10... | collective-permute-start | bytes 983048 | tf_op jit(solution)/shard_map/ppermute | solution.py:856
  56.0 17.4 %collective-permute-start.11 = (bf16[4,32,1280]{2,1,0:T(8,128)(2,1)S(1)}, bf16[4,32,1280]{2,1,0:T(8,128)(2,1)S(1)}, u32[]{:S(2)}, u32[]{:S(2)}) collective-permute-start(bf16[4,32,1280]{2,1,0:T(8,128)(2,1)S(1)} %get-tuple-element.138.refs_10_.refs_12_), channel_id=1, source_target_pairs={{0,1},{1,0},{2,3},{3,2},{4,5},{5,4},{6,7},{7,6},{8,9},{9,8},{10,11... | collective-permute-start | bytes 983048 | tf_op jit(solution)/shard_map/ppermute | solution.py:856
  78.6 20.7 %collective-permute-start.14 = (bf16[2,4,32,1280]{3,2,1,0:T(8,128)(2,1)}, bf16[2,4,32,1280]{3,2,1,0:T(8,128)(2,1)}, u32[]{:S(2)}, u32[]{:S(2)}) collective-permute-start(bf16[2,4,32,1280]{3,2,1,0:T(8,128)(2,1)} %copy-done.45), channel_id=1, source_target_pairs={{0,1},{1,0},{2,3},{3,2},{4,5},{5,4},{6,7},{7,6},{8,9},{9,8},{10,11... | collective-permute-start | bytes 1966088 | tf_op jit(solution)/shard_map/ppermute | solution.py:856
  78.8 24.2 %collective-permute-start.15 = (bf16[4,2,32,1280]{3,2,1,0:T(8,128)(2,1)S(1)}, bf16[4,2,32,1280]{3,2,1,0:T(8,128)(2,1)}, u32[]{:S(2)}, u32[]{:S(2)}) collective-permute-start(bf16[4,2,32,1280]{3,2,1,0:T(8,128)(2,1)S(1)} %get-tuple-element.141.refs_7_.refs_4_), channel_id=1, source_target_pairs={{0,16},{8,24},{16,0},{24,8},{1,17},{9,25},{17,1},{25,9},{2,18},{10... | collective-permute-start | bytes 1966088 | tf_op jit(solution)/shard_map/ppermute | solution.py:856
  108.5 17.1 %collective-permute-start.16 = (bf16[2,4,2,32,1280]{4,3,2,1,0:T(8,128)(2,1)S(1)}, bf16[2,4,2,32,1280]{4,3,2,1,0:T(8,128)(2,1)}, u32[]{:S(2)}, u32[]{:S(2)}) collective-permute-start(bf16[2,4,2,32,1280]{4,3,2,1,0:T(8,128)(2,1)S(1)} %get-tuple-element.148), channel_id=1, source_target_pairs={{0,8},{8,0},{16,24},{24,16},{1,9},{9,1},{17,25},{25,17},{2,10},{10... | collective-permute-start | bytes 3932168 | tf_op jit(solution)/shard_map/ppermute | solution.py:856
  109.1 16.5 %collective-permute-start.17 = (bf16[2,4,2,32,1280]{4,3,2,1,0:T(8,128)(2,1)S(1)}, bf16[2,4,2,32,1280]{4,3,2,1,0:T(8,128)(2,1)}, u32[]{:S(2)}, u32[]{:S(2)}) collective-permute-start(bf16[2,4,2,32,1280]{4,3,2,1,0:T(8,128)(2,1)S(1)} %get-tuple-element.146.refs_5_), channel_id=1, source_target_pairs={{0,8},{8,0},{16,24},{24,16},{1,9},{9,1},{17,25},{25,17},{2,10},{10... | collective-permute-start | bytes 3932168 | tf_op jit(solution)/shard_map/ppermute | solution.py:856
  109.1 25.6 %collective-permute-start.18 = (bf16[128,1024]{1,0:T(8,128)(2,1)S(1)}, bf16[128,1024]{1,0:T(8,128)(2,1)S(1)}, u32[]{:S(2)}, u32[]{:S(2)}) collective-permute-start(bf16[128,1024]{1,0:T(8,128)(2,1)S(1)} %get-tuple-element.151.refs_2_.refs_6_), channel_id=1, source_target_pairs={{0,2},{1,3},{2,4},{3,5},{4,6},{5,7},{6,0},{7,1},{8,10},{9,11},{10,... | collective-permute-start | bytes 786440 | tf_op jit(solution)/shard_map/ppermute | solution.py:856
  109.1 43.7 %collective-permute-start.19 = (bf16[128,1024]{1,0:T(8,128)(2,1)S(1)}, bf16[128,1024]{1,0:T(8,128)(2,1)S(1)}, u32[]{:S(2)}, u32[]{:S(2)}) collective-permute-start(bf16[128,1024]{1,0:T(8,128)(2,1)S(1)} %get-tuple-element.151.refs_2_.refs_6_), channel_id=1, source_target_pairs={{0,4},{1,5},{2,6},{3,7},{4,0},{5,1},{6,2},{7,3},{8,12},{9,13},{10,... | collective-permute-start | bytes 786440 | tf_op jit(solution)/shard_map/ppermute | solution.py:856
  109.4 45.7 %collective-permute-start.20 = (bf16[128,1024]{1,0:T(8,128)(2,1)S(1)}, bf16[128,1024]{1,0:T(8,128)(2,1)}, u32[]{:S(2)}, u32[]{:S(2)}) collective-permute-start(bf16[128,1024]{1,0:T(8,128)(2,1)S(1)} %get-tuple-element.151.refs_2_.refs_6_), channel_id=1, source_target_pairs={{0,6},{1,7},{2,0},{3,1},{4,2},{5,3},{6,4},{7,5},{8,14},{9,15},{10,... | collective-permute-start | bytes 786440 | tf_op jit(solution)/shard_map/ppermute | solution.py:856
  159.1 14.9 %collective-permute-start.21 = (bf16[4,128,512]{2,1,0:T(8,128)(2,1)S(1)}, bf16[4,128,512]{2,1,0:T(8,128)(2,1)S(1)}, u32[]{:S(2)}, u32[]{:S(2)}) collective-permute-start(bf16[4,128,512]{2,1,0:T(8,128)(2,1)S(1)} %get-tuple-element.155.refs_2_), channel_id=1, source_target_pairs={{0,16},{8,24},{16,0},{24,8},{1,17},{9,25},{17,1},{25,9},{2,18},{10... | collective-permute-start | bytes 1572872 | tf_op jit(solution)/shard_map/ppermute | solution.py:856
  160.2 13.8 %collective-permute-start.22 = (bf16[4,128,512]{2,1,0:T(8,128)(2,1)S(1)}, bf16[4,128,512]{2,1,0:T(8,128)(2,1)S(1)}, u32[]{:S(2)}, u32[]{:S(2)}) collective-permute-start(bf16[4,128,512]{2,1,0:T(8,128)(2,1)S(1)} %get-tuple-element.153.refs_5_.refs_4_), channel_id=1, source_target_pairs={{0,1},{1,0},{2,3},{3,2},{4,5},{5,4},{6,7},{7,6},{8,9},{9,8},{10,11... | collective-permute-start | bytes 1572872 | tf_op jit(solution)/shard_map/ppermute | solution.py:856
  176.0 31.4 %collective-permute-start.23 = (bf16[2,4,128,512]{3,2,1,0:T(8,128)(2,1)S(1)}, bf16[2,4,128,512]{3,2,1,0:T(8,128)(2,1)S(1)}, u32[]{:S(2)}, u32[]{:S(2)}) collective-permute-start(bf16[2,4,128,512]{3,2,1,0:T(8,128)(2,1)S(1)} %get-tuple-element.163.refs_2_), channel_id=1, source_target_pairs={{0,1},{1,0},{2,3},{3,2},{4,5},{5,4},{6,7},{7,6},{8,9},{9,8},{10,11... | collective-permute-start | bytes 3145736 | tf_op jit(solution)/shard_map/ppermute | solution.py:856
  176.3 31.1 %collective-permute-start.24 = (bf16[4,2,128,512]{3,2,1,0:T(8,128)(2,1)S(1)}, bf16[4,2,128,512]{3,2,1,0:T(8,128)(2,1)}, u32[]{:S(2)}, u32[]{:S(2)}) collective-permute-start(bf16[4,2,128,512]{3,2,1,0:T(8,128)(2,1)S(1)} %get-tuple-element.157.refs_7_.refs_4_), channel_id=1, source_target_pairs={{0,16},{8,24},{16,0},{24,8},{1,17},{9,25},{17,1},{25,9},{2,18},{10... | collective-permute-start | bytes 3145736 | tf_op jit(solution)/shard_map/ppermute | solution.py:856
  252.2 8.9 %collective-permute-start.27 = (bf16[2,8,256,512]{3,2,1,0:T(8,128)(2,1)}, bf16[2,8,256,512]{3,2,1,0:T(8,128)(2,1)S(1)}, u32[]{:S(2)}, u32[]{:S(2)}) collective-permute-start(bf16[2,8,256,512]{3,2,1,0:T(8,128)(2,1)} %outer_grad.2.refs_3_), channel_id=1, source_target_pairs={{0,8},{8,0},{16,24},{24,16},{1,9},{9,1},{17,25},{25,17},{2,10},{10... | collective-permute-start | bytes 12582920 | tf_op jit(solution)/shard_map/ppermute | solution.py:856
  267.2 40.1 %collective-permute-start.28 = (bf16[1,8,128,512]{3,2,1,0:T(8,128)(2,1)S(1)}, bf16[1,8,128,512]{3,2,1,0:T(8,128)(2,1)S(1)}, u32[]{:S(2)}, u32[]{:S(2)}) collective-permute-start(bf16[1,8,128,512]{3,2,1,0:T(8,128)(2,1)S(1)} %get-tuple-element.177), channel_id=1, source_target_pairs={{0,16},{8,24},{16,0},{24,8},{1,17},{9,25},{17,1},{25,9},{2,18},{10... | collective-permute-start | bytes 3145736 | tf_op jit(solution)/shard_map/ppermute | solution.py:856
  268.2 39.1 %collective-permute-start.29 = (bf16[8,1,128,512]{3,2,1,0:T(8,128)(2,1)S(1)}, bf16[8,1,128,512]{3,2,1,0:T(8,128)(2,1)S(1)}, u32[]{:S(2)}, u32[]{:S(2)}) collective-permute-start(bf16[8,1,128,512]{3,2,1,0:T(8,128)(2,1)S(1)} %get-tuple-element.178), channel_id=1, source_target_pairs={{0,1},{1,0},{2,3},{3,2},{4,5},{5,4},{6,7},{7,6},{8,9},{9,8},{10,11... | collective-permute-start | bytes 3145736 | tf_op jit(solution)/shard_map/ppermute | solution.py:856
  310.1 16.8 %collective-permute-start.30 = (bf16[2,8,128,1024]{3,2,1,0:T(8,128)(2,1)}, bf16[2,8,128,1024]{3,2,1,0:T(8,128)(2,1)}, u32[]{:S(2)}, u32[]{:S(2)}) collective-permute-start(bf16[2,8,128,1024]{3,2,1,0:T(8,128)(2,1)} %get-tuple-element.187), channel_id=1, source_target_pairs={{0,8},{8,0},{16,24},{24,16},{1,9},{9,1},{17,25},{25,17},{2,10},{10... | collective-permute-start | bytes 12582920 | tf_op jit(solution)/shard_map/ppermute | solution.py:856
  310.8 13.6 %collective-permute-start.31 = (bf16[4,1,128,512]{3,2,1,0:T(8,128)(2,1)S(1)}, bf16[4,1,128,512]{3,2,1,0:T(8,128)(2,1)S(1)}, u32[]{:S(2)}, u32[]{:S(2)}) collective-permute-start(bf16[4,1,128,512]{3,2,1,0:T(8,128)(2,1)S(1)} %get-tuple-element.189), channel_id=1, source_target_pairs={{0,1},{1,0},{2,3},{3,2},{4,5},{5,4},{6,7},{7,6},{8,9},{9,8},{10,11... | collective-permute-start | bytes 1572872 | tf_op jit(solution)/shard_map/ppermute | solution.py:856
  311.6 13.2 %collective-permute-start.32 = (bf16[1,4,128,512]{3,2,1,0:T(8,128)(2,1)S(1)}, bf16[1,4,128,512]{3,2,1,0:T(8,128)(2,1)S(1)}, u32[]{:S(2)}, u32[]{:S(2)}) collective-permute-start(bf16[1,4,128,512]{3,2,1,0:T(8,128)(2,1)S(1)} %get-tuple-element.190), channel_id=1, source_target_pairs={{0,16},{8,24},{16,0},{24,8},{1,17},{9,25},{17,1},{25,9},{2,18},{10... | collective-permute-start | bytes 1572872 | tf_op jit(solution)/shard_map/ppermute | solution.py:856
  326.8 86.3 %reduce-scatter.3.cloned.1.call-start = ((), (), s32[]{:S(2)}) async-start(), calls=%async_computation.3 | async-start | bytes 1310720 | tf_op jit(solution)/shard_map/reduce_scatter | solution.py:1014
  334.0 25.6 %collective-permute-start.33 = (bf16[1,8,128,512]{3,2,1,0:T(8,128)(2,1)S(1)}, bf16[1,8,128,512]{3,2,1,0:T(8,128)(2,1)S(1)}, u32[]{:S(2)}, u32[]{:S(2)}) collective-permute-start(bf16[1,8,128,512]{3,2,1,0:T(8,128)(2,1)S(1)} %get-tuple-element.199), channel_id=1, source_target_pairs={{0,16},{8,24},{16,0},{24,8},{1,17},{9,25},{17,1},{25,9},{2,18},{10... | collective-permute-start | bytes 3145736 | tf_op jit(solution)/shard_map/ppermute | solution.py:856
  334.4 25.1 %collective-permute-start.34 = (bf16[8,1,128,512]{3,2,1,0:T(8,128)(2,1)S(1)}, bf16[8,1,128,512]{3,2,1,0:T(8,128)(2,1)S(1)}, u32[]{:S(2)}, u32[]{:S(2)}) collective-permute-start(bf16[8,1,128,512]{3,2,1,0:T(8,128)(2,1)S(1)} %get-tuple-element.200), channel_id=1, source_target_pairs={{0,1},{1,0},{2,3},{3,2},{4,5},{5,4},{6,7},{7,6},{8,9},{9,8},{10,11... | collective-permute-start | bytes 3145736 | tf_op jit(solution)/shard_map/ppermute | solution.py:856
  364.5 19.8 %collective-permute-start.35 = (bf16[2,8,128,768]{3,2,1,0:T(8,128)(2,1)}, bf16[2,8,128,768]{3,2,1,0:T(8,128)(2,1)}, u32[]{:S(2)}, u32[]{:S(2)}) collective-permute-start(bf16[2,8,128,768]{3,2,1,0:T(8,128)(2,1)} %get-tuple-element.202), channel_id=1, source_target_pairs={{0,8},{8,0},{16,24},{24,16},{1,9},{9,1},{17,25},{25,17},{2,10},{10... | collective-permute-start | bytes 9437192 | tf_op jit(solution)/shard_map/ppermute | solution.py:856
  366.1 13.8 %collective-permute-start.36 = (bf16[4,1,128,512]{3,2,1,0:T(8,128)(2,1)}, bf16[4,1,128,512]{3,2,1,0:T(8,128)(2,1)S(1)}, u32[]{:S(2)}, u32[]{:S(2)}) collective-permute-start(bf16[4,1,128,512]{3,2,1,0:T(8,128)(2,1)} %get-tuple-element.204), channel_id=1, source_target_pairs={{0,1},{1,0},{2,3},{3,2},{4,5},{5,4},{6,7},{7,6},{8,9},{9,8},{10,11... | collective-permute-start | bytes 1572872 | tf_op jit(solution)/shard_map/ppermute | solution.py:856
  366.7 13.4 %collective-permute-start.37 = (bf16[1,4,128,512]{3,2,1,0:T(8,128)(2,1)}, bf16[1,4,128,512]{3,2,1,0:T(8,128)(2,1)S(1)}, u32[]{:S(2)}, u32[]{:S(2)}) collective-permute-start(bf16[1,4,128,512]{3,2,1,0:T(8,128)(2,1)} %get-tuple-element.206), channel_id=1, source_target_pairs={{0,16},{8,24},{16,0},{24,8},{1,17},{9,25},{17,1},{25,9},{2,18},{10... | collective-permute-start | bytes 1572872 | tf_op jit(solution)/shard_map/ppermute | solution.py:856
  382.4 73.2 %all-gather.10.cloned.1.call-start = ((), (), s32[]{:S(2)}) async-start(), calls=%async_computation.6 | async-start | bytes 1310720 | tf_op jit(solution)/shard_map/all_gather | solution.py:1020
  384.1 74.4 %all-gather.8.cloned.1.call-start = ((), (), s32[]{:S(2)}) async-start(), calls=%async_computation.5 | async-start | bytes 1310720 | tf_op jit(solution)/shard_map/all_gather | solution.py:1020
  389.3 19.2 %collective-permute-start.38 = (bf16[1,8,128,384]{3,2,1,0:T(8,128)(2,1)S(1)}, bf16[1,8,128,384]{3,2,1,0:T(8,128)(2,1)S(1)}, u32[]{:S(2)}, u32[]{:S(2)}) collective-permute-start(bf16[1,8,128,384]{3,2,1,0:T(8,128)(2,1)S(1)} %get-tuple-element.212), channel_id=1, source_target_pairs={{0,16},{8,24},{16,0},{24,8},{1,17},{9,25},{17,1},{25,9},{2,18},{10... | collective-permute-start | bytes 2359304 | tf_op jit(solution)/shard_map/ppermute | solution.py:856
  390.1 18.4 %collective-permute-start.39 = (bf16[8,1,128,256]{3,2,1,0:T(8,128)(2,1)S(1)}, bf16[8,1,128,256]{3,2,1,0:T(8,128)(2,1)S(1)}, u32[]{:S(2)}, u32[]{:S(2)}) collective-permute-start(bf16[8,1,128,256]{3,2,1,0:T(8,128)(2,1)S(1)} %get-tuple-element.213), channel_id=1, source_target_pairs={{0,1},{1,0},{2,3},{3,2},{4,5},{5,4},{6,7},{7,6},{8,9},{9,8},{10,11... | collective-permute-start | bytes 1572872 | tf_op jit(solution)/shard_map/ppermute | solution.py:856
  411.5 12.6 %collective-permute-start.42 = (bf16[2,8,144,384]{3,2,1,0:T(8,128)(2,1)}, bf16[2,8,144,384]{3,2,1,0:T(8,128)(2,1)S(1)}, u32[]{:S(2)}, u32[]{:S(2)}) collective-permute-start(bf16[2,8,144,384]{3,2,1,0:T(8,128)(2,1)} %get-tuple-element.223), channel_id=1, source_target_pairs={{0,8},{8,0},{16,24},{24,16},{1,9},{9,1},{17,25},{25,17},{2,10},{10... | collective-permute-start | bytes 5308424 | tf_op jit(solution)/shard_map/ppermute | solution.py:856
  413.2 10.9 %collective-permute-start.40 = (bf16[4,1,128,384]{3,2,0,1:T(8,128)(2,1)S(1)}, bf16[4,1,128,384]{3,2,0,1:T(8,128)(2,1)S(1)}, u32[]{:S(2)}, u32[]{:S(2)}) collective-permute-start(bf16[4,1,128,384]{3,2,0,1:T(8,128)(2,1)S(1)} %bitcast.163), channel_id=1, source_target_pairs={{0,1},{1,0},{2,3},{3,2},{4,5},{5,4},{6,7},{7,6},{8,9},{9,8},{10,11... | collective-permute-start | bytes 1179656 | tf_op jit(solution)/shard_map/ppermute | solution.py:856
  414.0 9.2 %collective-permute-start.41 = (bf16[1,4,128,256]{3,2,1,0:T(8,128)(2,1)S(1)}, bf16[1,4,128,256]{3,2,1,0:T(8,128)(2,1)S(1)}, u32[]{:S(2)}, u32[]{:S(2)}) collective-permute-start(bf16[1,4,128,256]{3,2,1,0:T(8,128)(2,1)S(1)} %get-tuple-element.222), channel_id=1, source_target_pairs={{0,16},{8,24},{16,0},{24,8},{1,17},{9,25},{17,1},{25,9},{2,18},{10... | collective-permute-start | bytes 786440 | tf_op jit(solution)/shard_map/ppermute | solution.py:856
  427.1 18.9 %collective-permute-start.46 = (bf16[1,8,144,256]{3,2,1,0:T(8,128)(2,1)S(1)}, bf16[1,8,144,256]{3,2,1,0:T(8,128)(2,1)S(1)}, u32[]{:S(2)}, u32[]{:S(2)}) collective-permute-start(bf16[1,8,144,256]{3,2,1,0:T(8,128)(2,1)S(1)} %get-tuple-element.230), channel_id=1, source_target_pairs={{0,16},{8,24},{16,0},{24,8},{1,17},{9,25},{17,1},{25,9},{2,18},{10... | collective-permute-start | bytes 1769480 | tf_op jit(solution)/shard_map/ppermute | solution.py:856
  427.8 18.3 %collective-permute-start.47 = (bf16[8,1,144,128]{3,2,1,0:T(8,128)(2,1)S(1)}, bf16[8,1,144,128]{3,2,1,0:T(8,128)(2,1)S(1)}, u32[]{:S(2)}, u32[]{:S(2)}) collective-permute-start(bf16[8,1,144,128]{3,2,1,0:T(8,128)(2,1)S(1)} %get-tuple-element.231), channel_id=1, source_target_pairs={{0,1},{1,0},{2,3},{3,2},{4,5},{5,4},{6,7},{7,6},{8,9},{9,8},{10,11... | collective-permute-start | bytes 884744 | tf_op jit(solution)/shard_map/ppermute | solution.py:856
  428.8 12.7 %collective-permute-start.44 = (bf16[128,640]{1,0:T(8,128)(2,1)S(1)}, bf16[128,640]{1,0:T(8,128)(2,1)S(1)}, u32[]{:S(2)}, u32[]{:S(2)}) collective-permute-start(bf16[128,640]{1,0:T(8,128)(2,1)S(1)} %get-tuple-element.227), channel_id=1, source_target_pairs={{0,4},{1,5},{2,6},{3,7},{4,0},{5,1},{6,2},{7,3},{8,12},{9,13},{10,... | collective-permute-start | bytes 491528 | tf_op jit(solution)/shard_map/ppermute | solution.py:856
  430.8 15.2 %collective-permute-start.45 = (bf16[128,640]{1,0:T(8,128)(2,1)S(1)}, bf16[128,640]{1,0:T(8,128)(2,1)S(1)}, u32[]{:S(2)}, u32[]{:S(2)}) collective-permute-start(bf16[128,640]{1,0:T(8,128)(2,1)S(1)} %get-tuple-element.228), channel_id=1, source_target_pairs={{0,6},{1,7},{2,0},{3,1},{4,2},{5,3},{6,4},{7,5},{8,14},{9,15},{10,... | collective-permute-start | bytes 491528 | tf_op jit(solution)/shard_map/ppermute | solution.py:856
  454.0 8.7 %collective-permute-start.50 = (bf16[144,384]{1,0:T(8,128)(2,1)S(1)}, bf16[144,384]{1,0:T(8,128)(2,1)S(1)}, u32[]{:S(2)}, u32[]{:S(2)}) collective-permute-start(bf16[144,384]{1,0:T(8,128)(2,1)S(1)} %get-tuple-element.237), channel_id=1, source_target_pairs={{0,2},{1,3},{2,4},{3,5},{4,6},{5,7},{6,0},{7,1},{8,10},{9,11},{10,... | collective-permute-start | bytes 331784 | tf_op jit(solution)/shard_map/ppermute | solution.py:856
  454.2 8.5 %collective-permute-start.51 = (bf16[144,384]{1,0:T(8,128)(2,1)S(1)}, bf16[144,384]{1,0:T(8,128)(2,1)S(1)}, u32[]{:S(2)}, u32[]{:S(2)}) collective-permute-start(bf16[144,384]{1,0:T(8,128)(2,1)S(1)} %get-tuple-element.238), channel_id=1, source_target_pairs={{0,4},{1,5},{2,6},{3,7},{4,0},{5,1},{6,2},{7,3},{8,12},{9,13},{10,... | collective-permute-start | bytes 331784 | tf_op jit(solution)/shard_map/ppermute | solution.py:856
  454.6 10.6 %collective-permute-start.52 = (bf16[144,384]{1,0:T(8,128)(2,1)S(1)}, bf16[144,384]{1,0:T(8,128)(2,1)S(1)}, u32[]{:S(2)}, u32[]{:S(2)}) collective-permute-start(bf16[144,384]{1,0:T(8,128)(2,1)S(1)} %get-tuple-element.239), channel_id=1, source_target_pairs={{0,6},{1,7},{2,0},{3,1},{4,2},{5,3},{6,4},{7,5},{8,14},{9,15},{10,... | collective-permute-start | bytes 331784 | tf_op jit(solution)/shard_map/ppermute | solution.py:856
  (97 other events, 507.1 us)
Sparse Core Ops, SparseCore 0:
  52.9 99.5 all-gather.5
  326.9 24.9 reduce-scatter.4
  382.5 25.4 reduce-scatter.2
  409.4 20.0 all-gather.9
  430.9 18.7 all-gather.7

commit v3 on v2

--- a/solution.py
+++ b/solution.py
@@ -10,48 +10,50 @@
 
 F32 = jnp.float32
 BF16 = jnp.bfloat16
-VMEM_LIMIT = 56 * 1024 * 1024
+VMEM_LIMIT = 48 * 1024 * 1024
 ANY = pl.BlockSpec(memory_space=pl.ANY)
+ALL_VMEM = 62 * 1024 * 1024
+HBM = pl.BlockSpec(memory_space=pltpu.HBM)
 BQ, BV, BOUT, GAIN1, SHIFT1, BOUTER, GAIN2, SHIFT2 = range(8)
 
 
 LAST = []
 
 
-def call(kernel, name, operands, in_specs, out_shape, out_specs, *, grid=(1,), scalars=(), after=(), carry=(), scratch=(), room=None):
+def call(kernel, name, operands, in_specs, out_shape, out_specs, *, grid=(1,), scalars=(), after=(), carry=(), into=(), scratch=(), time=0, room=10 << 20):
     single = not isinstance(out_shape, (tuple, list))
     shapes, specs = ([out_shape], [out_specs]) if single else (list(out_shape), list(out_specs))
     first, made = len(scalars) + len(operands), len(shapes)
-    unread = list(carry) + list(after) + LAST
-
-    limit = VMEM_LIMIT
-    if room is not None:
-        pairs = list(zip(specs, shapes)) + list(zip(in_specs, operands))
-        blocks = [math.prod(spec.block_shape) * array.dtype.itemsize for spec, array in pairs if spec.block_shape is not None]
-        limit = min(VMEM_LIMIT, 2 * sum(blocks) + room)
+    ends = made + len(carry)
+    unread = list(carry) + list(into) + list(after) + LAST
+
+    pairs = list(zip(specs, shapes)) + list(zip(in_specs, operands))
+    blocks = [math.prod(spec.block_shape) * array.dtype.itemsize for spec, array in pairs if spec.block_shape is not None]
+    held = [math.prod(s.shape) * jnp.dtype(s.dtype).itemsize for s in scratch if getattr(s, "dtype", None) in (BF16, F32)]
+    limit = ALL_VMEM if room is None else min(VMEM_LIMIT, 2 * sum(blocks) + sum(held) + room)
 
     def body(*refs):
         outs = first + len(unread)
-        kernel(*refs[:first], *refs[outs : outs + made], *refs[outs + made + len(carry) :])
+        kernel(*refs[:first], *refs[outs : outs + made], *refs[outs + ends + 1 :])
 
     outs = pl.pallas_call(
         body,
-        out_shape=shapes + [jax.ShapeDtypeStruct(c.shape, c.dtype) for c in carry],
+        out_shape=shapes + [jax.ShapeDtypeStruct(c.shape, c.dtype) for c in carry] + [jax.ShapeDtypeStruct((8, 128), F32)],
         grid_spec=pltpu.PrefetchScalarGridSpec(
             num_scalar_prefetch=len(scalars),
             grid=grid,
-            in_specs=list(in_specs) + [ANY] * len(unread),
-            out_specs=specs + [ANY] * len(carry),
+            in_specs=list(in_specs) + [HBM] * len(carry) + [ANY] * (len(unread) - len(carry) - len(LAST)) + [HBM] * len(LAST),
+            out_specs=specs + [HBM] * (len(carry) + 1),
             scratch_shapes=list(scratch),
         ),
-        input_output_aliases={first + i: made + i for i in range(len(carry))},
+        input_output_aliases={first + i: made + i for i in range(len(carry))} | {first + len(carry) + i: i for i in range(len(into))},
         compiler_params=pltpu.CompilerParams(dimension_semantics=("arbitrary",) * len(grid), vmem_limit_bytes=limit),
-        cost_estimate=pl.CostEstimate(flops=1, bytes_accessed=1, transcendentals=0),
+        cost_estimate=pl.CostEstimate(flops=int(1 + time * 1e9), bytes_accessed=int(1 + time * 1e6), transcendentals=0),
         name=name,
     )(*scalars, *operands, *unread)
-    LAST[:] = outs[made - 1 : made]
+    LAST[:] = outs[ends:]
     result = outs[0] if single else tuple(outs[:made])
-    return (result, outs[made:]) if carry else result
+    return (result, outs[made:ends]) if carry else result
 
 
 def like(shape, dtype=BF16):
@@ -96,7 +98,7 @@
     if vectors:
         shapes[0] = (shapes[0][0], shapes[0][1] + lanes)
     everything = list(operands) + list(vectors)
-    return call(kernel, "pack", everything, [whole(o.shape) for o in everything], [like(s) for s in shapes], [whole(s) for s in shapes], room=4 << 20)
+    return call(kernel, "pack", everything, [whole(o.shape) for o in everything], [like(s) for s in shapes], [whole(s) for s in shapes], room=None)
 
 
 def vector_places(vectors, rows):
@@ -187,7 +189,7 @@
     return [made[job * n : (job + 1) * n] for job in range(len(jobs))], carried
 
 
-def gather_sums(own, lists):
+def gather_sums(own, lists, carry=()):
     flat = [t for terms in lists for t in terms]
     n = flat[0].shape[0]
     rows = max(t.shape[1] for t in flat)
@@ -223,11 +225,12 @@
         [whole((rows, cols))] * n,
         grid=(n,),
         scalars=[own],
+        carry=carry,
         room=6 << 20,
     )
 
 
-def add_up(lists, after=()):
+def add_up(lists, carry=()):
     flat = [a for arrays in lists for a in arrays]
 
     def kernel(*refs):
@@ -244,7 +247,7 @@
             i += len(arrays)
 
     shape = (max(a.shape[0] for a in flat), sum(arrays[0].shape[1] for arrays in lists))
-    return call(kernel, "add_up", flat, [whole(a.shape) for a in flat], like(shape), whole(shape), after=after, room=12 << 20)
+    return call(kernel, "add_up", flat, [whole(a.shape) for a in flat], like(shape), whole(shape), carry=carry, room=12 << 20)
 
 
 def outer_result(got, order, runs=2):
@@ -315,6 +318,7 @@
         like((cols, rows)),
         pl.BlockSpec((cols, tile), lambda i: (0, i)),
         grid=(rows // tile,),
+        time=3,
     )
 
 
@@ -347,7 +351,7 @@
             copy.wait()
 
 
-def project(pieces, x, vec, half, after=()):
+def project(pieces, x, vec, half, carry=()):
     rows, depth = x.shape
     cols = pieces.shape[1]
     tile = cols // 3
@@ -382,15 +386,16 @@
         [x, vec] + list(pieces.buffers),
         [whole(x.shape), whole(vec.shape)] + [ANY] * count,
         (like((rows, cols)), like((depth, cols))),
-        (pl.BlockSpec((rows, tile), lambda i, *_: (0, i)), ANY),
+        (pl.BlockSpec((rows, tile), lambda i, *_: (0, i)), HBM),
         grid=(3,),
         scalars=[pieces.cores],
         scratch=pieces.scratch(),
-        after=after,
-    )
-
-
-def attend(qkv, row, col, heads=4, size=64, after=()):
+        carry=carry,
+        time=6,
+    )
+
+
+def attend(qkv, row, col, heads=4, size=64, carry=()):
     seqs, _, length = row.shape
     width = qkv.shape[1] // 3
     block = heads * size
@@ -432,11 +437,12 @@
         ),
         grid=(seqs, blocks),
         scratch=[pltpu.VMEM((length, length), F32)],
-        after=after,
-    )
-
-
-def attend_back(qkv, ot, probs, share, do, part, after=()):
+        carry=carry,
+        time=11,
+    )
+
+
+def attend_back(qkv, ot, probs, share, do, part, carry=()):
     seqs, blocks, heads, length = share.shape
     tokens, width = ot.shape[1], ot.shape[0]
     block = width // blocks
@@ -489,7 +495,8 @@
         (like((3, tokens, width)), like((seqs, 1, width), F32), like((seqs, 1, width), F32)),
         (pl.BlockSpec((3, length, block), lambda s, p: (0, s, p)), sums, sums),
         grid=(seqs, blocks),
-        after=after,
+        carry=carry,
+        time=11,
     )
 
 
@@ -539,17 +546,19 @@
         [o0, o1, x, vec] + list(pieces.buffers),
         [half, half, tok, whole(vec.shape)] + [ANY] * count,
         (like((rows, width), F32), like((rows, 1), F32), like((rows, width)), like((width, rows)), like((width, width))),
-        (tok, pl.BlockSpec((tile, 1), lambda i, *_: (i, 0)), tok, pl.BlockSpec((width, tile), lambda i, *_: (0, i)), ANY),
+        (tok, pl.BlockSpec((tile, 1), lambda i, *_: (i, 0)), tok, pl.BlockSpec((width, tile), lambda i, *_: (0, i)), HBM),
         grid=(rows // tile,),
         scalars=[pieces.cores],
         scratch=pieces.scratch(),
         after=after,
-    )
-
-
-def inner(h, rest, bias, tile=512, after=()):
+        time=7,
+    )
+
+
+def inner(h, rest, bias, run=0, runs=1, into=(), tile=512):
     rows, depth = h.shape
     cols = bias.shape[1]
+    steps = cols // tile // runs
 
     def kernel(h_ref, w_ref, b_ref, u_ref, g_ref):
         f = dot(h_ref[...], w_ref[...]) + b_ref[...]
@@ -558,16 +567,18 @@
         bell = jnp.exp2((f * f) * (-0.5 * math.log2(math.e)))
         g_ref[...] = (weight + (f * (1.0 / math.sqrt(2.0 * math.pi))) * bell).astype(BF16)
 
-    out = pl.BlockSpec((rows, tile), lambda i: (0, i))
+    at = lambda i: (0, run * steps + i)
+    out = pl.BlockSpec((rows, tile), at)
     return call(
         kernel,
         "inner",
         [h, rest, bias],
-        [whole(h.shape), pl.BlockSpec((depth, tile), lambda i: (0, i)), pl.BlockSpec((1, tile), lambda i: (0, i))],
+        [whole(h.shape), pl.BlockSpec((depth, tile), at), pl.BlockSpec((1, tile), at)],
         (like((rows, cols)), like((rows, cols))),
         (out, out),
-        grid=(cols // tile,),
-        after=after,
+        grid=(steps,),
+        into=into,
+        time=9,
     )
 
 
@@ -612,11 +623,12 @@
         [u, n1, cot, vec] + list(pieces.buffers),
         [pl.BlockSpec((tile, depth), lambda i, *_: (i, 0)), tok, tok, whole(vec.shape)] + [ANY] * count,
         (like((rows, width)), like((rows, width), F32), like((rows, width)), like((width, rows)), like((8, width), F32), like((depth, width))),
-        (tok, tok, tok, pl.BlockSpec((width, tile), lambda i, *_: (0, i)), whole((8, width)), ANY),
+        (tok, tok, tok, pl.BlockSpec((width, tile), lambda i, *_: (0, i)), whole((8, width)), HBM),
         grid=(rows // tile,),
         scalars=[pieces.cores],
         scratch=pieces.scratch(),
         after=after,
+        time=19,
     )
 
 
@@ -641,6 +653,7 @@
         grid=(groups // blocks,),
         scalars=[half],
         after=after,
+        time=6,
     )
 
 
@@ -696,6 +709,7 @@
         grid=(2 * steps,),
         scalars=[halves],
         after=after,
+        time=35,
     )
 
 
@@ -728,55 +742,63 @@
         (tok, tok, tok, whole((8, width))),
         grid=(rows // tile,),
         after=after,
-    )
-
-
-def token_weights_grad(halves, xt, d, groups, mixed=None, extra=None, after=()):
+        time=8,
+    )
+
+
+def token_weights_grad(halves, xt, d, groups, mixed=None, vectors=(), carry=()):
     width, rows = xt.shape
     part = d.shape[2] // 2
-    last = width // 4
-    mixed_at = -(-3 * part // (2 * last)) * last
-    cols = mixed_at + last if mixed else 3 * part // 2
-    more = 0 if extra is None else extra.shape[1]
+    size, last = part // 2, width // 4
     keep = width // groups
+    mixed_at = -(-3 * size // last) * last
+    cols = mixed_at + last if mixed else 3 * size
+    more = 16 if vectors else 0
+    arrays = [a for group, _ in vectors for a in group]
 
     def kernel(halves_ref, left_ref, d_ref, *refs):
-        refs, first_ref, second_ref = refs[:-2], refs[-2], refs[-1]
-
-        def fill(out_ref):
-            def store(made, start, group, blocks):
-                size = made.shape[1] // 2
-                for x in range(2):
-                    piece = made[:, x * size : (x + 1) * size].reshape(blocks, keep, size)
-                    out_ref[x, group : group + blocks, :keep, start : start + size] = piece
-
-            for which in range(3):
-                store(dot(left_ref[...], d_ref[which]).astype(BF16), which * (part // 2), 0, groups)
-            if mixed:
-                for i in range(2):
-                    store(dot(refs[i][...], refs[2][...]).astype(BF16), mixed_at, i * groups // 2, groups // 2)
-                if mixed_at > 3 * part // 2:
-                    out_ref[:, :, :, 3 * part // 2 : mixed_at] = jnp.zeros((2, groups, keep, mixed_at - 3 * part // 2), BF16)
-            if more:
-                for x in range(2):
-                    out_ref[x, :, keep:, :] = refs[-1][...]
-
-        @pl.when(pl.program_id(0) == 0)
-        def _():
-            fill(first_ref)
-
-        @pl.when(pl.program_id(0) == 1)
-        def _():
-            fill(second_ref)
-
-    operands = [xt, d]
+        def put(out_ref):
+            at, read = keep, list(refs)
+            for group, row in vectors:
+                here, read = read[: len(group)], read[len(group) :]
+                values = [jnp.sum(ref[...], axis=0) if len(ref.shape) == 3 else ref[row : row + 1] for ref in here]
+                wide = values[0].shape[1]
+                many = wide * len(group) // groups
+                for g in range(groups):
+                    for i in range(many // keep):
+                        start = g * many + i * keep
+                        piece = values[start // wide][:, start % wide : start % wide + keep].astype(BF16)
+                        for x in range(2):
+                            out_ref[x, g, at + i : at + i + 1, :keep] = piece
+                at += many // keep
+
+        def store(out_ref, made, start, group, blocks):
+            wide = made.shape[1] // 2
+            for x in range(2):
+                piece = made[:, x * wide : (x + 1) * wide].reshape(blocks, keep, wide)
+                out_ref[x, group : group + blocks, :keep, start : start + wide] = piece
+
+        for step, out_ref in enumerate(refs[-2:]):
+
+            @pl.when(pl.program_id(0) == step)
+            def _():
+                for which in range(3):
+                    store(out_ref, dot(left_ref[...], d_ref[which]).astype(BF16), which * size, 0, groups)
+                if mixed:
+                    for i in range(2):
+                        made = dot(refs[i][...], refs[2][...]).astype(BF16)
+                        store(out_ref, made, mixed_at, i * groups // 2, groups // 2)
+                    if mixed_at > 3 * size:
+                        out_ref[:, :, :, 3 * size : mixed_at] = jnp.zeros((2, groups, keep, mixed_at - 3 * size), BF16)
+                if more:
+                    out_ref[:, :, keep:, :] = jnp.zeros((2, groups, more, cols), BF16)
+                    put(out_ref)
+
+    operands = [xt, d] + list(mixed or ()) + arrays
     specs = [whole(xt.shape), pl.BlockSpec((3, rows, part), lambda i, halves: (0, 0, halves[i]))]
     if mixed:
-        operands += mixed
         specs += [whole(mixed[0].shape), whole(mixed[1].shape), pl.BlockSpec((rows, width // 2), lambda i, halves: (0, halves[i]))]
-    if more:
-        operands.append(extra)
-        specs.append(whole(extra.shape))
+    specs += [whole(a.shape) for a in arrays]
     shape = (2, groups, keep + more, cols)
     return call(
         kernel,
@@ -787,7 +809,8 @@
         (whole(shape), whole(shape)),
         grid=(2,),
         scalars=[halves],
-        after=after,
+        carry=carry,
+        time=8,
     )
 
 
@@ -811,6 +834,7 @@
         tok,
         grid=(rows // tile,),
         after=after,
+        time=6,
     )
 
 
@@ -965,13 +989,15 @@
         [w_query, w_key, w_value, w_out, w_outer, w_inner],
         [[(0, half, half), (1, half, half), (2, half, half), (3, 0, width)], [(4, 0, width)], [(5, 0, hidden)]],
     )
+    whole_winner = lax.all_gather(inner_rows, ("replica", "group"), axis=0, tiled=True)
+    a, b, second = move(a, b, carry=[second])
     second = Chain(layout, second, zxy)
-    (va, vb, vc, vd), (inner_rows,) = stack([a.job(), b.job(), second.job(0, wide), second.job(wide, wide)], carry=[inner_rows])
-    a, b, c, d = a.after(va), b.after(vb), second.after(vc), second.after(vd, zyx)
-    whole_winner = lax.all_gather(inner_rows, ("replica", "group"), axis=0, tiled=True)
-    while a.order:
-        a, b, c, d = move(a, b, c, d)
+    while a.order[1:]:
+        a, b = move(a, b)
+    va, vb, c, d = stack([a.job(), b.job(), second.job(0, wide), second.job(wide, wide)])
+    a, b = a.after(va), b.after(vb)
     pieces0 = layout.pieces([(a, cut), (b, cut)], (width, 3 * half))
+    c, d = second.after(c), second.after(d, zyx)
     spots = vector_places(vectors, high)
     used = max(r for r, _ in spots) + 1
     both = [v.reshape(-1, groups, high, v.shape[-1])[:, :, :used, cut:].astype(F32) for v in pieces0.buffers[-2:]]
@@ -981,22 +1007,24 @@
     whole_binner = small[:, r, l : l + b_inner.shape[0]].reshape(1, -1)
     row, col = segment_ids.reshape(seqs, 1, length), segment_ids.reshape(seqs, length, 1)
 
-    qkv0, wqkv0 = project(pieces0, tokens, vec, 0)
-    while c.order:
-        c, d, last = move(c, d, carry=[last])
+    (qkv0, wqkv0), (last,) = project(pieces0, tokens, vec, 0, carry=[last])
+    last = Chain(layout, last, zxy)
+    while c.order[1:]:
+        c, d = move(c, d)
+    o0, ot0, probs0, share0 = attend(qkv0, row, col)
+    c_value, d_value, e, f = stack([c.job(), d.job(), last.job(0, half), last.job(half, half)])
+    c, d = c.after(c_value), d.after(d_value)
     pieces1 = layout.pieces([(c, wide), (d, wide)], (width, 3 * half + width))
-    last = Chain(layout, last, zxy)
-    o0, ot0, probs0, share0 = attend(qkv0, row, col)
+    e, f = last.after(e), last.after(f, zyx)
     qkv1, wqkv1 = project(pieces1.part(0, 3 * half), tokens, vec, 1)
-    e, f = stack([last.job(0, half), last.job(half, half)])
-    e, f = last.after(e), last.after(f, zyx)
     o1, ot1, probs1, share1 = attend(qkv1, row, col)
     while len(e.order) > 1:
         e, f = move(e, f)
     n1, rstd1, h, ht, whole_wout = join(pieces1.part(3 * half, width), o0, o1, tokens, vec)
-    u, slope = inner(h, whole_winner, whole_binner)
+    made = inner(h, whole_winner, whole_binner, 0, 2)
     e, f = move(e, f)
     pieces2 = layout.pieces([(e, half), (f, half)], (w_outer.shape[0] * devices, width))
+    u, slope = inner(h, whole_winner, whole_binner, 1, 2, made)
     out, dz2, dm, dmt, sums2, whole_wouter = outer(pieces2, u, n1, cotangent, vec)
 
     def reduction(other, own, *orders, by_rows=False, runs=None):
@@ -1009,58 +1037,56 @@
             parts = [((0, start // size), (rows, size)) for start, size in runs]
         return [Reduction(layout, [(own,) + part, (came,) + part], order) for part, order in zip(parts, orders)]
 
-    def along_z(reductions):
-        sums = add_up([[t.reshape(-1, t.shape[-1]) for t in r.last()] for r in reductions])
-        return lax.psum_scatter(sums, ("replica", "group"), scatter_dimension=0, axis_index_groups=layout.along(z_digit[0]), tiled=True)
-
-    def across_z(reductions):
-        made = gather_sums(layout.place(z_digit[0]).astype(jnp.int32).reshape(1), [r.last() for r in reductions])
-        return [made[-1]] + [layout.send(s, z_digit[0], k + 1) for k, s in enumerate(made[:-1])]
+    def along_z(reductions, carry=()):
+        sums = add_up([[t.reshape(-1, t.shape[-1]) for t in r.last()] for r in reductions], carry)
+        sums, carry = sums if carry else (sums, ())
+        sums = lax.psum_scatter(sums, ("replica", "group"), scatter_dimension=0, axis_index_groups=layout.along(z_digit[0]), tiled=True)
+        return [sums] + list(carry)
+
+    def across_z(reductions, carry=()):
+        made = gather_sums(layout.place(z_digit[0]).astype(jnp.int32).reshape(1), [r.last() for r in reductions], carry)
+        made, carry = made if carry else (made, ())
+        return [[made[-1]] + [layout.send(s, z_digit[0], k + 1) for k, s in enumerate(made[:-1])]] + list(carry)
 
     spread = lambda block: lax.all_gather(block, "replica", axis=0, tiled=False)
+    middle = range(len(xyz) - 2)
+    cols = 3 * half // 4
     other = outer_grad(theirs, dmt, u, groups)
     own = outer_grad(mine, dmt, u, groups)
     outers = reduction(other, own, xyz, yxz, by_rows=True)
     step(*outers)
     other, own, dh, sum_inner = inner_back(halves, dm, whole_wouter, slope, ht, whole_winner, groups)
-    for _ in range(len(xyz) - 2):
+    for _ in middle:
         (other,) = step(*outers, carry=[other])
     inners = reduction(other, own, xyz, yxz)
     dz1, da, do, sums1 = join_back(dz2, dh, n1, rstd1, vec, whole_wout)
-    got_wouter = along_z(outers)
+    (got_wouter,) = along_z(outers)
     step(*inners)
     d0, sq0, sv0 = attend_back(qkv0, ot0, probs0, share0, do, 0)
-    other, own = token_weights_grad(halves, xt, d0, groups, mixed=[ot0, ot1, da])
-    for _ in range(len(xyz) - 2):
+    other, own = token_weights_grad(halves, xt, d0, groups, mixed=(ot0, ot1, da))
+    for _ in middle:
         (other,) = step(*inners, carry=[other])
-    runs = ((0, 3 * half // 4), (other.shape[3] - width // 4, width // 4))
-    firsts = reduction(other, own, xyz, yxz, runs=runs)
+    firsts = reduction(other, own, xyz, yxz, runs=((0, cols), (other.shape[3] - width // 4, width // 4)))
     d1, sq1, sv1 = attend_back(qkv1, ot1, probs1, share1, do, 1)
-    bq = jnp.concatenate([jnp.sum(s, axis=0) for s in (sq0, sq1)], axis=1)
-    bv = jnp.concatenate([jnp.sum(s, axis=0) for s in (sv0, sv1)], axis=1)
-    sums = jnp.concatenate([bq, bv, sums1[:3], sums2[:3]], axis=0)
-    sums = sums.reshape(8, groups, -1).transpose(1, 0, 2).reshape(groups, -1)
-    sums = jnp.concatenate([sums, sum_inner.reshape(groups, -1)], axis=1)
-    used, cols = sums.shape[1], 3 * half // 4
-    extra = jnp.pad(sums.astype(BF16), ((0, 0), (0, 16 * cols - used))).reshape(groups, 16, cols)
-    got_winner = along_z(inners)
+    (got_winner,) = along_z(inners)
     step(*firsts)
     partial = token_grad(dz1, d0, wqkv0, F32)
-    other, own = token_weights_grad(halves, xt, d1, groups, extra=extra)
-    for _ in range(len(xyz) - 2):
+    vectors = [((sq0, sq1), 0), ((sv0, sv1), 0)] + [((sums,), i) for sums in (sums1, sums2) for i in range(3)] + [((sum_inner,), 0)]
+    (other, own), (got_wouter,) = token_weights_grad(halves, xt, d1, groups, vectors=vectors, carry=[got_wouter])
+    got_wouter = spread(got_wouter)
+    for _ in middle:
         (other,) = step(*firsts, carry=[other])
     seconds = reduction(other, own, xyz, yxz, runs=((0, 2 * cols // 3), (2 * cols // 3, cols // 3)))
-    grad_tokens = token_grad(partial, d1, wqkv1, BF16)
-    step(*seconds, after=[t for r in firsts for t in r.came()])
-    first_sums = across_z(firsts)
-    for _ in range(len(xyz) - 2):
-        step(*seconds, after=first_sums[1:])
-    second_sums = across_z(seconds)
-    got_wouter, got_winner = spread(got_wouter), spread(got_winner)
     cores = layout.core[2]
     order = [r % cores * (layout.replicas // cores) + r // cores for r in range(layout.replicas)]
+    step(*seconds)
+    (first_sums,) = across_z(firsts)
+    grad_tokens = token_grad(partial, d1, wqkv1, BF16)
+    for _ in middle:
+        (got_winner,) = step(*seconds, carry=[got_winner])
+    got_winner = spread(got_winner)
+    (second_sums,) = across_z(seconds)
     grad_wouter = outer_result(got_wouter, order)
-    grad_winner = inner_result(got_winner, order)
     got = [add_up([first_sums, second_sums])]
     places = jnp.zeros((1,), jnp.int32)
     weight = 1
@@ -1069,11 +1095,11 @@
         places = jnp.concatenate([places + own * weight, places + (1 - own) * weight])
         got = got + [layout.send(g, digit) for g in got]
         weight *= digit[2]
+    grad_winner = inner_result(got_winner, order)
     keep = width // groups
     wq, wk, wv, grad_wout, sums = token_weights_result(got, places, keep, half // 4, width // 4)
-    sums = sums.reshape(-1)[:used]
-    bq, bv, bout, gain1, shift1, bouter, gain2, shift2 = (sums[i * keep : (i + 1) * keep] for i in range(8))
-    binner = sums[8 * keep :]
+    bq, bv, bout, gain1, shift1, bouter, gain2, shift2 = (sums[i, :keep] for i in range(8))
+    binner = sums[8 : 8 + hidden // width, :keep].reshape(-1)
     return (out, grad_tokens, wq, bq, wk, wv, bv, grad_wout, bout, gain1, shift1, grad_winner, binner, grad_wouter, bouter, gain2, shift2)
 
 

time: 496 us -> 447 us (0.901)
  Pallas kernels: 254 us -> 199 us
  local copies, waits for them, and re-layouts: 63.8 us -> 92.3 us
  waiting for transfers between devices: 104 us -> 90.6 us
    pallas_call x43 -> x44, Pallas kernels: 254 us -> 199 us  [call(): pl.pallas_call(body, out_shape=shapes + [jax.ShapeDtypeStruct(c.shape, c....]
    unnamed x171 -> x184, local copies, waits for them, and re-layouts: 56.8 us -> 90.2 us
    ppermute x56, waiting for transfers between devices: 104 us -> 90.5 us  [send(): return lax.ppermute(value, axis, pairs)]
  transfers between devices with their start and end apart: 61 -> 61, of which waited for: 27 -> 27; matrix products, arithmetic and copies ran while one was open for 2% -> 1% of each run, Pallas kernels for 44% -> 36%
where the time goes in v3:
time: 447 us; the launch traced here: 441 us
  Pallas kernels  199 us (45%)
  local copies, waits for them, and re-layouts  92.3 us (21%)
  waiting for transfers between devices  90.6 us (20%)
  starting transfers between devices  43.1 us (10%)
  between operations  14.8 us (3%)
    pallas_call x44, Pallas kernels, call(): pl.pallas_call(body, out_shape=shapes + [jax.ShapeDtypeStruct(c.shape, c....  199 us
    ppermute x56, waiting for transfers between devices, send(): return lax.ppermute(value, axis, pairs)  90.5 us
    unnamed x184, local copies, waits for them, and re-layouts  90.2 us
    ppermute x56, starting transfers between devices, send(): return lax.ppermute(value, axis, pairs)  42.9 us
  transfers between devices with their start and end apart: 61, of which 27 were waited for; matrix products, arithmetic and copies ran while one was open for 1% of the time, Pallas kernels for 36%

profile of v3, /device:TPU:9, one launch (start us, length us, event | category | flops | bytes accessed | tf_op | source)
XLA Modules:
  0.0 441.3 jit_solution(1833607035756666445)
XLA Ops:
  19.0 2.7 collective-permute-done.2.refs_5_.refs_9_
  22.5 2.0 pack.3
  27.2 4.4 %collective-permute-done.3.refs_3_ = bf16[4,32,768]{2,1,0:T(8,128)(2,1)S(1)} collective-permute-done((bf16[4,32,768]{2,1,0:T(8,128)(2,1)S(1)}, bf16[4,32,768]{2,1,0:T(8,128)(2,1)S(1)}, u32[]{:S(2)}, u32[]{:S(2)}) %collective-permute-start.3) | collective-permute-done | bytes 196640 | tf_op jit(solution)/shard_map/ppermute | solution.py:880
  38.3 4.8 %collective-permute-done.7.refs_9_.refs_13_ = bf16[32,2560]{1,0:T(8,128)(2,1)S(1)} collective-permute-done((bf16[32,2560]{1,0:T(8,128)(2,1)S(1)}, bf16[32,2560]{1,0:T(8,128)(2,1)S(1)}, u32[]{:S(2)}, u32[]{:S(2)}) %collective-permute-start.7) | collective-permute-done | bytes 163872 | tf_op jit(solution)/shard_map/ppermute | solution.py:880
  43.2 9.8 %collective-permute-done.8.refs_10_.refs_14_ = bf16[32,2560]{1,0:T(8,128)(2,1)S(1)} collective-permute-done((bf16[32,2560]{1,0:T(8,128)(2,1)S(1)}, bf16[32,2560]{1,0:T(8,128)(2,1)S(1)}, u32[]{:S(2)}, u32[]{:S(2)}) %collective-permute-start.8) | collective-permute-done | bytes 163872 | tf_op jit(solution)/shard_map/ppermute | solution.py:880
  53.0 3.9 collective-permute-done.9.refs_11_.refs_15_
  66.3 6.5 %project.2 = (bf16[1024,1536]{1,0:T(8,128)(2,1)S(1)}, bf16[1024,1536]{1,0:T(8,128)(2,1)S(1)}, bf16[128,1024]{1,0:T(8,128)(2,1)S(1)}, f32[8,128]{1,0:T(8,128)S(1)}) custom-call(s32[2]{0:T(128)S(1)} %pad_add_fusion.refs_0_, bf16[1024,1024]{1,0:T(8,128)(2,1)S(1)} %copy-done.33, f32[8,1024]{1,0:T(8,128)S(1)} %stack.40.refs_2_.refs_4_, ...), custom_call_target="tpu_custom_call", output_to_operand_aliasing={{2}: (7, {})} | custom-call | flops 6000000000 | bytes 6000001 | tf_op jit(solution)/shard_map/project/pallas_call | solution.py:39
  79.4 10.3 %attend.2 = (bf16[1024,512]{1,0:T(8,128)(2,1)S(1)}, bf16[512,1024]{1,0:T(8,128)(2,1)S(1)}, bf16[2,8,512,512]{3,2,1,0:T(8,128)(2,1)S(1)}, f32[2,2,4,512]{3,2,1,0:T(4,128)S(1)}, f32[8,128]{1,0:T(8,128)S(1)}) custom-call(bf16[1024,1536]{1,0:T(8,128)(2,1)S(1)} %get-tuple-element.205.refs_0_.refs_1_.refs_2_, ...), custom_call_target="tpu_custom_call" | custom-call | flops 11000000512 | bytes 11000001 | tf_op jit(solution)/shard_map/attend/pallas_call | solution.py:39
  89.8 3.3 copy-done.63
  95.6 9.7 %collective-permute-done.17.refs_10_.refs_14_ = bf16[128,1024]{1,0:T(8,128)(2,1)S(1)} collective-permute-done((bf16[128,1024]{1,0:T(8,128)(2,1)S(1)}, bf16[128,1024]{1,0:T(8,128)(2,1)S(1)}, u32[]{:S(2)}, u32[]{:S(2)}) %collective-permute-start.17) | collective-permute-done | bytes 262176 | tf_op jit(solution)/shard_map/ppermute | solution.py:880
  105.3 4.6 %collective-permute-done.18.refs_11_.refs_15_ = bf16[128,1024]{1,0:T(8,128)(2,1)S(1)} collective-permute-done((bf16[128,1024]{1,0:T(8,128)(2,1)S(1)}, bf16[128,1024]{1,0:T(8,128)(2,1)S(1)}, u32[]{:S(2)}, u32[]{:S(2)}) %collective-permute-start.18) | collective-permute-done | bytes 262176 | tf_op jit(solution)/shard_map/ppermute | solution.py:880
  115.9 5.1 %project.3 = (bf16[1024,1536]{1,0:T(8,128)(2,1)S(1)}, bf16[1024,1536]{1,0:T(8,128)(2,1)S(1)}, f32[8,128]{1,0:T(8,128)S(1)}) custom-call(s32[2]{0:T(128)S(1)} %pad_add_fusion.refs_0_, bf16[1024,1024]{1,0:T(8,128)(2,1)S(1)} %copy-done.34, f32[8,1024]{1,0:T(8,128)S(1)} %stack.40.refs_2_.refs_4_, bf16[2,256,1280]{2,1,0:T(8,128)(2,1)S(1)} %bitcast.173, ...), custom_call_target="tpu_custom_call" | custom-call | flops 6000000000 | bytes 6000001 | tf_op jit(solution)/shard_map/project/pallas_call | solution.py:39
  122.8 10.3 %attend.3 = (bf16[1024,512]{1,0:T(8,128)(2,1)S(1)}, bf16[512,1024]{1,0:T(8,128)(2,1)S(1)}, bf16[2,8,512,512]{3,2,1,0:T(8,128)(2,1)S(1)}, f32[2,2,4,512]{3,2,1,0:T(4,128)S(1)}, f32[8,128]{1,0:T(8,128)S(1)}) custom-call(bf16[1024,1536]{1,0:T(8,128)(2,1)S(1)} %get-tuple-element.218.refs_0_.refs_1_.refs_2_, ...), custom_call_target="tpu_custom_call" | custom-call | flops 11000000512 | bytes 11000001 | tf_op jit(solution)/shard_map/attend/pallas_call | solution.py:39
  133.1 3.3 copy-done.65
  138.0 5.7 %join.1 = (f32[1024,1024]{1,0:T(8,128)S(1)}, f32[1024,1]{1,0:T(8,128)S(1)}, bf16[1024,1024]{1,0:T(8,128)(2,1)S(1)}, bf16[1024,1024]{1,0:T(8,128)(2,1)S(1)}, bf16...) custom-call(s32[2]{0:T(128)S(1)} %pad_add_fusion.refs_0_, bf16[1024,512]{1,0:T(8,128)(2,1)S(1)} %get-tuple-element.210.refs_1_, ...), custom_call_target="tpu_custom_call" | custom-call | flops 7000000000 | bytes 7000001 | tf_op jit(solution)/shard_map/join/pallas_call | solution.py:39
  150.4 3.4 copy-done.31
  155.4 8.5 %inner.2 = (bf16[1024,4096]{1,0:T(8,128)(2,1)S(1)}, bf16[1024,4096]{1,0:T(8,128)(2,1)S(1)}, f32[8,128]{1,0:T(8,128)S(1)}) custom-call(bf16[1024,1024]{1,0:T(8,128)(2,1)S(1)} %copy-done.46, bf16[1024,4096]{1,0:T(8,128)(2,1)S(1)} %copy-done.31, f32[1,4096]{1,0:T(1,128)S(1)} %bitcast.161, f32[8,128]{1,0:T(8,128)S(1)} %get-tuple-element.227.refs_3_), custom_call_target="tpu_custom_call" | custom-call | flops 9000000512 | bytes 9000001 | tf_op jit(solution)/shard_map/inner/pallas_call | solution.py:39
  166.1 8.7 %inner.3 = (bf16[1024,4096]{1,0:T(8,128)(2,1)S(1)}, bf16[1024,4096]{1,0:T(8,128)(2,1)S(1)}, f32[8,128]{1,0:T(8,128)S(1)}) custom-call(bf16[1024,1024]{1,0:T(8,128)(2,1)S(1)} %copy-done.46, bf16[1024,4096]{1,0:T(8,128)(2,1)S(1)} %copy-done.31, f32[1,4096]{1,0:T(1,128)S(1)} %bitcast.162, ...), custom_call_target="tpu_custom_call", output_to_operand_aliasing={{0}: (3, {}), {1}: (4, {})} | custom-call | flops 9000000512 | bytes 9000001 | tf_op jit(solution)/shard_map/inner/pallas_call | solution.py:39
  174.8 3.3 copy-done.41
  178.1 3.2 copy-done.44
  181.3 2.2 copy-done.68
  183.5 17.2 %outer.1 = (bf16[1024,1024]{1,0:T(8,128)(2,1)}, f32[1024,1024]{1,0:T(8,128)S(1)}, bf16[1024,1024]{1,0:T(8,128)(2,1)S(1)}, bf16[1024,1024]{1,0:T(8,128)(2,1)S(1)}...) custom-call(s32[2]{0:T(128)S(1)} %pad_add_fusion.refs_0_, ...), custom_call_target="tpu_custom_call" | custom-call | flops 19000000512 | bytes 19000000 | tf_op jit(solution)/shard_map/outer/pallas_call | solution.py:39
  202.7 4.1 copy-done.42
  206.9 5.5 %outer_grad.2 = (bf16[2,8,256,512]{3,2,1,0:T(8,128)(2,1)S(1)}, f32[8,128]{1,0:T(8,128)S(1)}) custom-call(s32[1]{0:T(128)} %bitcast.1.refs_0_, bf16[1024,1024]{1,0:T(8,128)(2,1)S(1)} %get-tuple-element.245.refs_1_, bf16[1024,4096]{1,0:T(8,128)(2,1)S(1)} %copy-done.42, f32[8,128]{1,0:T(8,128)S(1)} %get-tuple-element.246.refs_3_), custom_call_target="tpu_custom_call" | custom-call | flops 6000000000 | bytes 6000001 | tf_op jit(solution)/shard_map/outer_grad/pallas_call | solution.py:39
  212.9 5.5 %outer_grad.3 = (bf16[2,8,256,512]{3,2,1,0:T(8,128)(2,1)S(1)}, f32[8,128]{1,0:T(8,128)S(1)}) custom-call(s32[1]{0:T(128)} %bitcast.refs_0_, bf16[1024,1024]{1,0:T(8,128)(2,1)S(1)} %get-tuple-element.245.refs_1_, bf16[1024,4096]{1,0:T(8,128)(2,1)S(1)} %copy-done.43, f32[8,128]{1,0:T(8,128)S(1)} %get-tuple-element.247.refs_3_), custom_call_target="tpu_custom_call" | custom-call | flops 6000000000 | bytes 6000001 | tf_op jit(solution)/shard_map/outer_grad/pallas_call | solution.py:39
  219.7 2.9 combine.8
  224.5 35.0 %inner_back.1 = (bf16[2,8,128,1024]{3,2,1,0:T(8,128)(2,1)S(1)}, bf16[2,8,128,1024]{3,2,1,0:T(8,128)(2,1)S(1)}, f32[1024,1024]{1,0:T(8,128)S(1)}, f32[1,4096]{1,0:T(1,128)S(1)}, f32[8,128]{1,0:T(8,128)S(1)}) custom-call(s32[2]{0:T(128)S(1)} %pad_add_fusion.1.refs_0_, bf16[1024,1024]{1,0:T(8,128)(2,1)S(1)} %copy-done.90, ...), custom_call_target="tpu_custom_call" | custom-call | flops 35000000512 | bytes 35000000 | tf_op jit(solution)/shard_map/inner_back/pallas_call | solution.py:39
  263.2 2.2 copy-done.71
  267.0 5.1 %join_back.1 = (f32[1024,1024]{1,0:T(8,128)S(1)}, bf16[1024,1024]{1,0:T(8,128)(2,1)S(1)}, bf16[1024,1024]{1,0:T(8,128)(2,1)S(1)}, f32[8,1024]{1,0:T(8,128)S(1)}, f32[8,128]{1,0:T(8,128)S(1)}) custom-call(f32[1024,1024]{1,0:T(8,128)S(1)} %copy-done.71, f32[1024,1024]{1,0:T(8,128)S(1)} %get-tuple-element.252.refs_1_, f32[1024,1024]{1,0:T(8,128)S(1)} %copy-done.69, ...), custom_call_target="tpu_custom_call" | custom-call | flops 8000000000 | bytes 8000001 | tf_op jit(solution)/shard_map/join_back/pallas_call | solution.py:39
  277.6 2.9 combine.10
  281.0 3.4 copy-done.64
  284.3 9.4 %attend_back.2 = (bf16[3,1024,512]{2,1,0:T(8,128)(2,1)S(1)}, f32[2,1,512]{2,1,0:T(1,128)S(1)}, f32[2,1,512]{2,1,0:T(1,128)S(1)}, f32[8,128]{1,0:T(8,128)S(1)}) custom-call(bf16[1024,1536]{1,0:T(8,128)(2,1)S(1)} %copy-done.75, bf16[1024,1536]{1,0:T(8,128)(2,1)S(1)} %copy-done.75, bf16[1024,1536]{1,0:T(8,128)(2,1)S(1)} %copy-done.75, ...), custom_call_target="tpu_custom_call" | custom-call | flops 11000000512 | bytes 11000001 | tf_op jit(solution)/shard_map/attend_back/pallas_call | solution.py:39
  293.8 8.9 %token_weights_grad.2 = (bf16[2,8,128,768]{3,2,1,0:T(8,128)(2,1)}, bf16[2,8,128,768]{3,2,1,0:T(8,128)(2,1)S(1)}, f32[8,128]{1,0:T(8,128)S(1)}) custom-call(s32[2]{0:T(128)S(1)} %pad_add_fusion.1.refs_0_, bf16[1024,1024]{1,0:T(8,128)(2,1)S(1)} %copy-done.52, bf16[3,1024,512]{2,1,0:T(8,128)(2,1)S(1)} %get-tuple-element.276.refs_2_.refs_1_, ...), custom_call_target="tpu_custom_call" | custom-call | flops 8000000000 | bytes 8000001 | tf_op jit(solution)/shard_map/token_weights_grad/pallas_call | solution.py:39
  308.7 2.1 collective-permute-start.35
  312.5 3.5 copy-done.66
  320.7 9.4 %attend_back.3 = (bf16[3,1024,512]{2,1,0:T(8,128)(2,1)S(1)}, f32[2,1,512]{2,1,0:T(1,128)S(1)}, f32[2,1,512]{2,1,0:T(1,128)S(1)}, f32[8,128]{1,0:T(8,128)S(1)}) custom-call(bf16[1024,1536]{1,0:T(8,128)(2,1)S(1)} %copy-done.73, bf16[1024,1536]{1,0:T(8,128)(2,1)S(1)} %copy-done.73, bf16[1024,1536]{1,0:T(8,128)(2,1)S(1)} %copy-done.73, ...), custom_call_target="tpu_custom_call" | custom-call | flops 11000000512 | bytes 11000001 | tf_op jit(solution)/shard_map/attend_back/pallas_call | solution.py:39
  333.3 4.1 combine.12
  340.5 4.3 token_grad.2
  351.3 5.7 %token_weights_grad.3 = (bf16[2,8,144,384]{3,2,1,0:T(8,128)(2,1)}, bf16[2,8,144,384]{3,2,1,0:T(8,128)(2,1)S(1)}, bf16[128,1024]{1,0:T(8,128)(2,1)S(1)}, f32[8,128]{1,0:T(8,128)S(1)}) custom-call(s32[2]{0:T(128)S(1)} %pad_add_fusion.1.refs_0_, bf16[1024,1024]{1,0:T(8,128)(2,1)S(1)} %copy-done.53, ...), custom_call_target="tpu_custom_call", output_to_operand_aliasing={{2}: (14, {})} | custom-call | flops 8000000000 | bytes 8000001 | tf_op jit(solution)/shard_map/token_weights_grad/pallas_call | solution.py:39
  366.6 2.3 combine.14
  376.4 5.1 %token_grad.3 = (bf16[1024,1024]{1,0:T(8,128)(2,1)}, f32[8,128]{1,0:T(8,128)S(1)}) custom-call(f32[1024,1024]{1,0:T(8,128)S(1)} %copy-done.50, bf16[3,1024,512]{2,1,0:T(8,128)(2,1)S(1)} %copy-done.60, bf16[1024,1536]{1,0:T(8,128)(2,1)S(1)} %copy-done.55, f32[8,128]{1,0:T(8,128)S(1)} %get-tuple-element.326.refs_3_), custom_call_target="tpu_custom_call" | custom-call | flops 6000000000 | bytes 6000001 | tf_op jit(solution)/shard_map/token_grad/pallas_call | solution.py:39
  381.5 9.0 %collective-permute-done.46 = bf16[1,8,144,256]{3,2,1,0:T(8,128)(2,1)S(1)} collective-permute-done((bf16[1,8,144,256]{3,2,1,0:T(8,128)(2,1)}, bf16[1,8,144,256]{3,2,1,0:T(8,128)(2,1)S(1)}, u32[]{:S(2)}, u32[]{:S(2)}) %collective-permute-start.46) | collective-permute-done | bytes 589856 | tf_op jit(solution)/shard_map/ppermute | solution.py:880
  395.7 2.1 collective-permute-done.49
  397.8 2.5 collective-permute-done.48
  405.6 8.4 %collective-permute-done.45.refs_3_ = bf16[128,640]{1,0:T(8,128)(2,1)S(1)} collective-permute-done((bf16[128,640]{1,0:T(8,128)(2,1)S(1)}, bf16[128,640]{1,0:T(8,128)(2,1)S(1)}, u32[]{:S(2)}, u32[]{:S(2)}) %collective-permute-start.45) | collective-permute-done | bytes 163872 | tf_op jit(solution)/shard_map/ppermute | solution.py:880
  415.8 3.0 collective-permute-done.52.refs_7_
  419.9 7.2 %collective-permute-done.53.refs_2_ = bf16[144,1024]{1,0:T(8,128)(2,1)S(1)} collective-permute-done((bf16[144,1024]{1,0:T(8,128)(2,1)S(1)}, bf16[144,1024]{1,0:T(8,128)(2,1)S(1)}, u32[]{:S(2)}, u32[]{:S(2)}) %collective-permute-start.53) | collective-permute-done | bytes 294944 | tf_op jit(solution)/shard_map/ppermute | solution.py:880
  431.4 2.1 token_weights_result.1
  (330 shorter events, 137.7 us)
Async XLA Ops:
  7.2 143.2 %all-gather.6.cloned.1.call-start = ((), (), s32[]{:S(2)}) async-start(), calls=%async_computation.2 | async-start | bytes 8650752 | tf_op jit(solution)/shard_map/all_gather | solution.py:992
  8.9 8.5 %collective-permute-start = (bf16[32,1664]{1,0:T(8,128)(2,1)}, bf16[32,1664]{1,0:T(8,128)(2,1)S(1)}, u32[]{:S(2)}, u32[]{:S(2)}) collective-permute-start(bf16[32,1664]{1,0:T(8,128)(2,1)} %get-tuple-element.189.refs_2_.refs_6_), channel_id=1, source_target_pairs={{0,2},{1,3},{2,4},{3,5},{4,6},{5,7},{6,0},{7,1},{8,10},{9,11},{10,... | collective-permute-start | bytes 319496 | tf_op jit(solution)/shard_map/ppermute | solution.py:880
  10.2 8.8 %collective-permute-start.1 = (bf16[32,1664]{1,0:T(8,128)(2,1)}, bf16[32,1664]{1,0:T(8,128)(2,1)S(1)}, u32[]{:S(2)}, u32[]{:S(2)}) collective-permute-start(bf16[32,1664]{1,0:T(8,128)(2,1)} %get-tuple-element.189.refs_2_.refs_6_), channel_id=1, source_target_pairs={{0,4},{1,5},{2,6},{3,7},{4,0},{5,1},{6,2},{7,3},{8,12},{9,13},{10,... | collective-permute-start | bytes 319496 | tf_op jit(solution)/shard_map/ppermute | solution.py:880
  11.2 10.5 %collective-permute-start.2 = (bf16[32,1664]{1,0:T(8,128)(2,1)}, bf16[32,1664]{1,0:T(8,128)(2,1)S(1)}, u32[]{:S(2)}, u32[]{:S(2)}) collective-permute-start(bf16[32,1664]{1,0:T(8,128)(2,1)} %get-tuple-element.189.refs_2_.refs_6_), channel_id=1, source_target_pairs={{0,6},{1,7},{2,0},{3,1},{4,2},{5,3},{6,4},{7,5},{8,14},{9,15},{10,... | collective-permute-start | bytes 319496 | tf_op jit(solution)/shard_map/ppermute | solution.py:880
  24.6 322.2 %reduce-scatter.3.cloned.1.call-start = ((), (), s32[]{:S(2)}) async-start(), calls=%async_computation.3 | async-start | bytes 1310720 | tf_op jit(solution)/shard_map/reduce_scatter | solution.py:1043
  33.9 23.0 %collective-permute-start.6 = (bf16[4,2,32,896]{3,2,1,0:T(8,128)(2,1)S(1)}, bf16[4,2,32,896]{3,2,1,0:T(8,128)(2,1)S(1)}, u32[]{:S(2)}, u32[]{:S(2)}) collective-permute-start(bf16[4,2,32,896]{3,2,1,0:T(8,128)(2,1)S(1)} %get-tuple-element.198.refs_6_), channel_id=1, source_target_pairs={{0,16},{8,24},{16,0},{24,8},{1,17},{9,25},{17,1},{25,9},{2,18},{10... | collective-permute-start | bytes 1376264 | tf_op jit(solution)/shard_map/ppermute | solution.py:880
  35.2 21.7 %collective-permute-start.5 = (bf16[2,4,32,768]{3,2,1,0:T(8,128)(2,1)S(1)}, bf16[2,4,32,768]{3,2,1,0:T(8,128)(2,1)S(1)}, u32[]{:S(2)}, u32[]{:S(2)}) collective-permute-start(bf16[2,4,32,768]{3,2,1,0:T(8,128)(2,1)S(1)} %get-tuple-element.197.refs_4_), channel_id=1, source_target_pairs={{0,1},{1,0},{2,3},{3,2},{4,5},{5,4},{6,7},{7,6},{8,9},{9,8},{10,11... | collective-permute-start | bytes 1179656 | tf_op jit(solution)/shard_map/ppermute | solution.py:880
  36.2 16.8 %collective-permute-start.8 = (bf16[32,2560]{1,0:T(8,128)(2,1)S(1)}, bf16[32,2560]{1,0:T(8,128)(2,1)S(1)}, u32[]{:S(2)}, u32[]{:S(2)}) collective-permute-start(bf16[32,2560]{1,0:T(8,128)(2,1)S(1)} %get-tuple-element.199.refs_8_.refs_12_), channel_id=1, source_target_pairs={{0,4},{1,5},{2,6},{3,7},{4,0},{5,1},{6,2},{7,3},{8,12},{9,13},{10,... | collective-permute-start | bytes 491528 | tf_op jit(solution)/shard_map/ppermute | solution.py:880
  37.1 19.8 %collective-permute-start.9 = (bf16[32,2560]{1,0:T(8,128)(2,1)S(1)}, bf16[32,2560]{1,0:T(8,128)(2,1)S(1)}, u32[]{:S(2)}, u32[]{:S(2)}) collective-permute-start(bf16[32,2560]{1,0:T(8,128)(2,1)S(1)} %get-tuple-element.199.refs_8_.refs_12_), channel_id=1, source_target_pairs={{0,6},{1,7},{2,0},{3,1},{4,2},{5,3},{6,4},{7,5},{8,14},{9,15},{10,... | collective-permute-start | bytes 491528 | tf_op jit(solution)/shard_map/ppermute | solution.py:880
  60.7 16.3 %collective-permute-start.12 = (bf16[4,32,1280]{2,1,0:T(8,128)(2,1)S(1)}, bf16[4,32,1280]{2,1,0:T(8,128)(2,1)S(1)}, u32[]{:S(2)}, u32[]{:S(2)}) collective-permute-start(bf16[4,32,1280]{2,1,0:T(8,128)(2,1)S(1)} %get-tuple-element.206.refs_2_), channel_id=1, source_target_pairs={{0,16},{8,24},{16,0},{24,8},{1,17},{9,25},{17,1},{25,9},{2,18},{10... | collective-permute-start | bytes 983048 | tf_op jit(solution)/shard_map/ppermute | solution.py:880
  61.4 15.6 %collective-permute-start.13 = (bf16[4,32,1280]{2,1,0:T(8,128)(2,1)S(1)}, bf16[4,32,1280]{2,1,0:T(8,128)(2,1)S(1)}, u32[]{:S(2)}, u32[]{:S(2)}) collective-permute-start(bf16[4,32,1280]{2,1,0:T(8,128)(2,1)S(1)} %get-tuple-element.207.refs_4_), channel_id=1, source_target_pairs={{0,1},{1,0},{2,3},{3,2},{4,5},{5,4},{6,7},{7,6},{8,9},{9,8},{10,11... | collective-permute-start | bytes 983048 | tf_op jit(solution)/shard_map/ppermute | solution.py:880
  74.5 21.2 %collective-permute-start.16 = (bf16[128,1024]{1,0:T(8,128)(2,1)S(1)}, bf16[128,1024]{1,0:T(8,128)(2,1)S(1)}, u32[]{:S(2)}, u32[]{:S(2)}) collective-permute-start(bf16[128,1024]{1,0:T(8,128)(2,1)S(1)} %get-tuple-element.213.refs_8_.refs_12_), channel_id=1, source_target_pairs={{0,2},{1,3},{2,4},{3,5},{4,6},{5,7},{6,0},{7,1},{8,10},{9,11},{10,... | collective-permute-start | bytes 786440 | tf_op jit(solution)/shard_map/ppermute | solution.py:880
  74.5 30.9 %collective-permute-start.17 = (bf16[128,1024]{1,0:T(8,128)(2,1)S(1)}, bf16[128,1024]{1,0:T(8,128)(2,1)S(1)}, u32[]{:S(2)}, u32[]{:S(2)}) collective-permute-start(bf16[128,1024]{1,0:T(8,128)(2,1)S(1)} %get-tuple-element.213.refs_8_.refs_12_), channel_id=1, source_target_pairs={{0,4},{1,5},{2,6},{3,7},{4,0},{5,1},{6,2},{7,3},{8,12},{9,13},{10,... | collective-permute-start | bytes 786440 | tf_op jit(solution)/shard_map/ppermute | solution.py:880
  75.0 34.9 %collective-permute-start.18 = (bf16[128,1024]{1,0:T(8,128)(2,1)S(1)}, bf16[128,1024]{1,0:T(8,128)(2,1)S(1)}, u32[]{:S(2)}, u32[]{:S(2)}) collective-permute-start(bf16[128,1024]{1,0:T(8,128)(2,1)S(1)} %get-tuple-element.213.refs_8_.refs_12_), channel_id=1, source_target_pairs={{0,6},{1,7},{2,0},{3,1},{4,2},{5,3},{6,4},{7,5},{8,14},{9,15},{10,... | collective-permute-start | bytes 786440 | tf_op jit(solution)/shard_map/ppermute | solution.py:880
  77.3 32.6 %collective-permute-start.14 = (bf16[2,4,32,1280]{3,2,1,0:T(8,128)(2,1)S(1)}, bf16[2,4,32,1280]{3,2,1,0:T(8,128)(2,1)S(1)}, u32[]{:S(2)}, u32[]{:S(2)}) collective-permute-start(bf16[2,4,32,1280]{3,2,1,0:T(8,128)(2,1)S(1)} %get-tuple-element.211.refs_4_), channel_id=1, source_target_pairs={{0,1},{1,0},{2,3},{3,2},{4,5},{5,4},{6,7},{7,6},{8,9},{9,8},{10,11... | collective-permute-start | bytes 1966088 | tf_op jit(solution)/shard_map/ppermute | solution.py:880
  78.2 31.7 %collective-permute-start.15 = (bf16[4,2,32,1280]{3,2,1,0:T(8,128)(2,1)S(1)}, bf16[4,2,32,1280]{3,2,1,0:T(8,128)(2,1)S(1)}, u32[]{:S(2)}, u32[]{:S(2)}) collective-permute-start(bf16[4,2,32,1280]{3,2,1,0:T(8,128)(2,1)S(1)} %get-tuple-element.212.refs_6_), channel_id=1, source_target_pairs={{0,16},{8,24},{16,0},{24,8},{1,17},{9,25},{17,1},{25,9},{2,18},{10... | collective-permute-start | bytes 1966088 | tf_op jit(solution)/shard_map/ppermute | solution.py:880
  111.4 25.0 %collective-permute-start.21 = (bf16[4,128,512]{2,1,0:T(8,128)(2,1)S(1)}, bf16[4,128,512]{2,1,0:T(8,128)(2,1)S(1)}, u32[]{:S(2)}, u32[]{:S(2)}) collective-permute-start(bf16[4,128,512]{2,1,0:T(8,128)(2,1)S(1)} %get-tuple-element.221.refs_2_), channel_id=1, source_target_pairs={{0,16},{8,24},{16,0},{24,8},{1,17},{9,25},{17,1},{25,9},{2,18},{10... | collective-permute-start | bytes 1572872 | tf_op jit(solution)/shard_map/ppermute | solution.py:880
  111.4 25.0 %collective-permute-start.22 = (bf16[4,128,512]{2,1,0:T(8,128)(2,1)S(1)}, bf16[4,128,512]{2,1,0:T(8,128)(2,1)S(1)}, u32[]{:S(2)}, u32[]{:S(2)}) collective-permute-start(bf16[4,128,512]{2,1,0:T(8,128)(2,1)S(1)} %get-tuple-element.222.refs_4_), channel_id=1, source_target_pairs={{0,1},{1,0},{2,3},{3,2},{4,5},{5,4},{6,7},{7,6},{8,9},{9,8},{10,11... | collective-permute-start | bytes 1572872 | tf_op jit(solution)/shard_map/ppermute | solution.py:880
  136.6 27.3 %collective-permute-start.23 = (bf16[2,4,128,512]{3,2,1,0:T(8,128)(2,1)S(1)}, bf16[2,4,128,512]{3,2,1,0:T(8,128)(2,1)S(1)}, u32[]{:S(2)}, u32[]{:S(2)}) collective-permute-start(bf16[2,4,128,512]{3,2,1,0:T(8,128)(2,1)S(1)} %get-tuple-element.230.refs_2_), channel_id=1, source_target_pairs={{0,1},{1,0},{2,3},{3,2},{4,5},{5,4},{6,7},{7,6},{8,9},{9,8},{10,11... | collective-permute-start | bytes 3145736 | tf_op jit(solution)/shard_map/ppermute | solution.py:880
  138.0 25.9 %collective-permute-start.24 = (bf16[4,2,128,512]{3,2,1,0:T(8,128)(2,1)S(1)}, bf16[4,2,128,512]{3,2,1,0:T(8,128)(2,1)}, u32[]{:S(2)}, u32[]{:S(2)}) collective-permute-start(bf16[4,2,128,512]{3,2,1,0:T(8,128)(2,1)S(1)} %get-tuple-element.231.refs_4_), channel_id=1, source_target_pairs={{0,16},{8,24},{16,0},{24,8},{1,17},{9,25},{17,1},{25,9},{2,18},{10... | collective-permute-start | bytes 3145736 | tf_op jit(solution)/shard_map/ppermute | solution.py:880
  165.4 15.9 %collective-permute-start.25 = (bf16[2,4,2,128,512]{4,3,2,1,0:T(8,128)(2,1)S(1)}, bf16[2,4,2,128,512]{4,3,2,1,0:T(8,128)(2,1)S(1)}, u32[]{:S(2)}, u32[]{:S(2)}) collective-permute-start(bf16[2,4,2,128,512]{4,3,2,1,0:T(8,128)(2,1)S(1)} %get-tuple-element.236), channel_id=1, source_target_pairs={{0,8},{8,0},{16,24},{24,16},{1,9},{9,1},{17,25},{25,17},{2,10},{10... | collective-permute-start | bytes 6291464 | tf_op jit(solution)/shard_map/ppermute | solution.py:880
  166.0 15.3 %collective-permute-start.26 = (bf16[2,4,2,128,512]{4,3,2,1,0:T(8,128)(2,1)S(1)}, bf16[2,4,2,128,512]{4,3,2,1,0:T(8,128)(2,1)S(1)}, u32[]{:S(2)}, u32[]{:S(2)}) collective-permute-start(bf16[2,4,2,128,512]{4,3,2,1,0:T(8,128)(2,1)S(1)} %get-tuple-element.237), channel_id=1, source_target_pairs={{0,8},{8,0},{16,24},{24,16},{1,9},{9,1},{17,25},{25,17},{2,10},{10... | collective-permute-start | bytes 6291464 | tf_op jit(solution)/shard_map/ppermute | solution.py:880
  222.6 37.0 %collective-permute-start.28 = (bf16[1,8,128,512]{3,2,1,0:T(8,128)(2,1)S(1)}, bf16[1,8,128,512]{3,2,1,0:T(8,128)(2,1)S(1)}, u32[]{:S(2)}, u32[]{:S(2)}) collective-permute-start(bf16[1,8,128,512]{3,2,1,0:T(8,128)(2,1)S(1)} %get-tuple-element.256), channel_id=1, source_target_pairs={{0,16},{8,24},{16,0},{24,8},{1,17},{9,25},{17,1},{25,9},{2,18},{10... | collective-permute-start | bytes 3145736 | tf_op jit(solution)/shard_map/ppermute | solution.py:880
  224.4 35.2 %collective-permute-start.29 = (bf16[8,1,128,512]{3,2,1,0:T(8,128)(2,1)S(1)}, bf16[8,1,128,512]{3,2,1,0:T(8,128)(2,1)S(1)}, u32[]{:S(2)}, u32[]{:S(2)}) collective-permute-start(bf16[8,1,128,512]{3,2,1,0:T(8,128)(2,1)S(1)} %get-tuple-element.258), channel_id=1, source_target_pairs={{0,1},{1,0},{2,3},{3,2},{4,5},{5,4},{6,7},{7,6},{8,9},{9,8},{10,11... | collective-permute-start | bytes 3145736 | tf_op jit(solution)/shard_map/ppermute | solution.py:880
  260.9 16.7 %collective-permute-start.30 = (bf16[2,8,128,1024]{3,2,1,0:T(8,128)(2,1)S(1)}, bf16[2,8,128,1024]{3,2,1,0:T(8,128)(2,1)S(1)}, u32[]{:S(2)}, u32[]{:S(2)}) collective-permute-start(bf16[2,8,128,1024]{3,2,1,0:T(8,128)(2,1)S(1)} %get-tuple-element.268), channel_id=1, source_target_pairs={{0,8},{8,0},{16,24},{24,16},{1,9},{9,1},{17,25},{25,17},{2,10},{10... | collective-permute-start | bytes 12582920 | tf_op jit(solution)/shard_map/ppermute | solution.py:880
  261.9 13.5 %collective-permute-start.31 = (bf16[4,1,128,512]{3,2,1,0:T(8,128)(2,1)S(1)}, bf16[4,1,128,512]{3,2,1,0:T(8,128)(2,1)S(1)}, u32[]{:S(2)}, u32[]{:S(2)}) collective-permute-start(bf16[4,1,128,512]{3,2,1,0:T(8,128)(2,1)S(1)} %get-tuple-element.270), channel_id=1, source_target_pairs={{0,1},{1,0},{2,3},{3,2},{4,5},{5,4},{6,7},{7,6},{8,9},{9,8},{10,11... | collective-permute-start | bytes 1572872 | tf_op jit(solution)/shard_map/ppermute | solution.py:880
  263.2 13.2 %collective-permute-start.32 = (bf16[1,4,128,512]{3,2,1,0:T(8,128)(2,1)S(1)}, bf16[1,4,128,512]{3,2,1,0:T(8,128)(2,1)S(1)}, u32[]{:S(2)}, u32[]{:S(2)}) collective-permute-start(bf16[1,4,128,512]{3,2,1,0:T(8,128)(2,1)S(1)} %get-tuple-element.272), channel_id=1, source_target_pairs={{0,16},{8,24},{16,0},{24,8},{1,17},{9,25},{17,1},{25,9},{2,18},{10... | collective-permute-start | bytes 1572872 | tf_op jit(solution)/shard_map/ppermute | solution.py:880
  280.5 23.5 %collective-permute-start.33 = (bf16[1,8,128,512]{3,2,1,0:T(8,128)(2,1)S(1)}, bf16[1,8,128,512]{3,2,1,0:T(8,128)(2,1)S(1)}, u32[]{:S(2)}, u32[]{:S(2)}) collective-permute-start(bf16[1,8,128,512]{3,2,1,0:T(8,128)(2,1)S(1)} %get-tuple-element.284), channel_id=1, source_target_pairs={{0,16},{8,24},{16,0},{24,8},{1,17},{9,25},{17,1},{25,9},{2,18},{10... | collective-permute-start | bytes 3145736 | tf_op jit(solution)/shard_map/ppermute | solution.py:880
  280.8 23.4 %collective-permute-start.34 = (bf16[8,1,128,512]{3,2,1,0:T(8,128)(2,1)S(1)}, bf16[8,1,128,512]{3,2,1,0:T(8,128)(2,1)S(1)}, u32[]{:S(2)}, u32[]{:S(2)}) collective-permute-start(bf16[8,1,128,512]{3,2,1,0:T(8,128)(2,1)S(1)} %get-tuple-element.286), channel_id=1, source_target_pairs={{0,1},{1,0},{2,3},{3,2},{4,5},{5,4},{6,7},{7,6},{8,9},{9,8},{10,11... | collective-permute-start | bytes 3145736 | tf_op jit(solution)/shard_map/ppermute | solution.py:880
  308.7 24.5 %collective-permute-start.35 = (bf16[2,8,128,768]{3,2,1,0:T(8,128)(2,1)}, bf16[2,8,128,768]{3,2,1,0:T(8,128)(2,1)}, u32[]{:S(2)}, u32[]{:S(2)}) collective-permute-start(bf16[2,8,128,768]{3,2,1,0:T(8,128)(2,1)} %get-tuple-element.289), channel_id=1, source_target_pairs={{0,8},{8,0},{16,24},{24,16},{1,9},{9,1},{17,25},{25,17},{2,10},{10... | collective-permute-start | bytes 9437192 | tf_op jit(solution)/shard_map/ppermute | solution.py:880
  310.9 70.6 %reduce-scatter.5.cloned.1.call-start = ((), (), s32[]{:S(2)}) async-start(), calls=%async_computation.4 | async-start | bytes 1310720 | tf_op jit(solution)/shard_map/reduce_scatter | solution.py:1043
  310.9 21.0 %collective-permute-start.36 = (bf16[4,1,128,512]{3,2,1,0:T(8,128)(2,1)}, bf16[4,1,128,512]{3,2,1,0:T(8,128)(2,1)S(1)}, u32[]{:S(2)}, u32[]{:S(2)}) collective-permute-start(bf16[4,1,128,512]{3,2,1,0:T(8,128)(2,1)} %copy-done.37), channel_id=1, source_target_pairs={{0,1},{1,0},{2,3},{3,2},{4,5},{5,4},{6,7},{7,6},{8,9},{9,8},{10,11... | collective-permute-start | bytes 1572872 | tf_op jit(solution)/shard_map/ppermute | solution.py:880
  311.1 20.8 %collective-permute-start.37 = (bf16[1,4,128,512]{3,2,1,0:T(8,128)(2,1)}, bf16[1,4,128,512]{3,2,1,0:T(8,128)(2,1)S(1)}, u32[]{:S(2)}, u32[]{:S(2)}) collective-permute-start(bf16[1,4,128,512]{3,2,1,0:T(8,128)(2,1)} %copy-done.36), channel_id=1, source_target_pairs={{0,16},{8,24},{16,0},{24,8},{1,17},{9,25},{17,1},{25,9},{2,18},{10... | collective-permute-start | bytes 1572872 | tf_op jit(solution)/shard_map/ppermute | solution.py:880
  333.2 69.5 %all-gather.8.cloned.1.call-start = ((), (), s32[]{:S(2)}) async-start(), calls=%async_computation.5 | async-start | bytes 1310720 | tf_op jit(solution)/shard_map/all_gather | solution.py:1051
  339.1 18.8 %collective-permute-start.38 = (bf16[1,8,128,384]{3,2,1,0:T(8,128)(2,1)}, bf16[1,8,128,384]{3,2,1,0:T(8,128)(2,1)S(1)}, u32[]{:S(2)}, u32[]{:S(2)}) collective-permute-start(bf16[1,8,128,384]{3,2,1,0:T(8,128)(2,1)} %get-tuple-element.304), channel_id=1, source_target_pairs={{0,16},{8,24},{16,0},{24,8},{1,17},{9,25},{17,1},{25,9},{2,18},{10... | collective-permute-start | bytes 2359304 | tf_op jit(solution)/shard_map/ppermute | solution.py:880
  339.2 17.8 %collective-permute-start.39 = (bf16[8,1,128,256]{3,2,1,0:T(8,128)(2,1)}, bf16[8,1,128,256]{3,2,1,0:T(8,128)(2,1)S(1)}, u32[]{:S(2)}, u32[]{:S(2)}) collective-permute-start(bf16[8,1,128,256]{3,2,1,0:T(8,128)(2,1)} %get-tuple-element.306), channel_id=1, source_target_pairs={{0,1},{1,0},{2,3},{3,2},{4,5},{5,4},{6,7},{7,6},{8,9},{9,8},{10,11... | collective-permute-start | bytes 1572872 | tf_op jit(solution)/shard_map/ppermute | solution.py:880
  363.0 65.6 %all-gather.10.cloned.1.call-start = ((), (), s32[]{:S(2)}) async-start(), calls=%async_computation.6 | async-start | bytes 1310720 | tf_op jit(solution)/shard_map/all_gather | solution.py:1051
  363.1 11.0 %collective-permute-start.40 = (bf16[4,1,128,384]{3,2,0,1:T(8,128)(2,1)}, bf16[4,1,128,384]{3,2,0,1:T(8,128)(2,1)S(1)}, u32[]{:S(2)}, u32[]{:S(2)}) collective-permute-start(bf16[4,1,128,384]{3,2,0,1:T(8,128)(2,1)} %bitcast.175), channel_id=1, source_target_pairs={{0,1},{1,0},{2,3},{3,2},{4,5},{5,4},{6,7},{7,6},{8,9},{9,8},{10,11... | collective-permute-start | bytes 1179656 | tf_op jit(solution)/shard_map/ppermute | solution.py:880
  369.7 20.8 %collective-permute-start.46 = (bf16[1,8,144,256]{3,2,1,0:T(8,128)(2,1)}, bf16[1,8,144,256]{3,2,1,0:T(8,128)(2,1)S(1)}, u32[]{:S(2)}, u32[]{:S(2)}) collective-permute-start(bf16[1,8,144,256]{3,2,1,0:T(8,128)(2,1)} %get-tuple-element.333), channel_id=1, source_target_pairs={{0,16},{8,24},{16,0},{24,8},{1,17},{9,25},{17,1},{25,9},{2,18},{10... | collective-permute-start | bytes 1769480 | tf_op jit(solution)/shard_map/ppermute | solution.py:880
  369.9 11.6 %collective-permute-start.47 = (bf16[8,1,144,128]{3,2,1,0:T(8,128)(2,1)}, bf16[8,1,144,128]{3,2,1,0:T(8,128)(2,1)S(1)}, u32[]{:S(2)}, u32[]{:S(2)}) collective-permute-start(bf16[8,1,144,128]{3,2,1,0:T(8,128)(2,1)} %get-tuple-element.335), channel_id=1, source_target_pairs={{0,1},{1,0},{2,3},{3,2},{4,5},{5,4},{6,7},{7,6},{8,9},{9,8},{10,11... | collective-permute-start | bytes 884744 | tf_op jit(solution)/shard_map/ppermute | solution.py:880
  393.5 8.2 %collective-permute-start.43 = (bf16[128,640]{1,0:T(8,128)(2,1)S(1)}, bf16[128,640]{1,0:T(8,128)(2,1)S(1)}, u32[]{:S(2)}, u32[]{:S(2)}) collective-permute-start(bf16[128,640]{1,0:T(8,128)(2,1)S(1)} %get-tuple-element.329), channel_id=1, source_target_pairs={{0,2},{1,3},{2,4},{3,5},{4,6},{5,7},{6,0},{7,1},{8,10},{9,11},{10,... | collective-permute-start | bytes 491528 | tf_op jit(solution)/shard_map/ppermute | solution.py:880
  393.8 11.9 %collective-permute-start.44 = (bf16[128,640]{1,0:T(8,128)(2,1)S(1)}, bf16[128,640]{1,0:T(8,128)(2,1)S(1)}, u32[]{:S(2)}, u32[]{:S(2)}) collective-permute-start(bf16[128,640]{1,0:T(8,128)(2,1)S(1)} %get-tuple-element.330), channel_id=1, source_target_pairs={{0,4},{1,5},{2,6},{3,7},{4,0},{5,1},{6,2},{7,3},{8,12},{9,13},{10,... | collective-permute-start | bytes 491528 | tf_op jit(solution)/shard_map/ppermute | solution.py:880
  394.2 19.9 %collective-permute-start.45 = (bf16[128,640]{1,0:T(8,128)(2,1)S(1)}, bf16[128,640]{1,0:T(8,128)(2,1)S(1)}, u32[]{:S(2)}, u32[]{:S(2)}) collective-permute-start(bf16[128,640]{1,0:T(8,128)(2,1)S(1)} %get-tuple-element.331), channel_id=1, source_target_pairs={{0,6},{1,7},{2,0},{3,1},{4,2},{5,3},{6,4},{7,5},{8,14},{9,15},{10,... | collective-permute-start | bytes 491528 | tf_op jit(solution)/shard_map/ppermute | solution.py:880
  400.5 13.5 %collective-permute-start.50 = (bf16[144,384]{1,0:T(8,128)(2,1)S(1)}, bf16[144,384]{1,0:T(8,128)(2,1)S(1)}, u32[]{:S(2)}, u32[]{:S(2)}) collective-permute-start(bf16[144,384]{1,0:T(8,128)(2,1)S(1)} %get-tuple-element.344), channel_id=1, source_target_pairs={{0,2},{1,3},{2,4},{3,5},{4,6},{5,7},{6,0},{7,1},{8,10},{9,11},{10,... | collective-permute-start | bytes 331784 | tf_op jit(solution)/shard_map/ppermute | solution.py:880
  400.6 15.2 %collective-permute-start.51 = (bf16[144,384]{1,0:T(8,128)(2,1)S(1)}, bf16[144,384]{1,0:T(8,128)(2,1)S(1)}, u32[]{:S(2)}, u32[]{:S(2)}) collective-permute-start(bf16[144,384]{1,0:T(8,128)(2,1)S(1)} %get-tuple-element.345), channel_id=1, source_target_pairs={{0,4},{1,5},{2,6},{3,7},{4,0},{5,1},{6,2},{7,3},{8,12},{9,13},{10,... | collective-permute-start | bytes 331784 | tf_op jit(solution)/shard_map/ppermute | solution.py:880
  401.7 17.1 %collective-permute-start.52 = (bf16[144,384]{1,0:T(8,128)(2,1)S(1)}, bf16[144,384]{1,0:T(8,128)(2,1)S(1)}, u32[]{:S(2)}, u32[]{:S(2)}) collective-permute-start(bf16[144,384]{1,0:T(8,128)(2,1)S(1)} %get-tuple-element.346), channel_id=1, source_target_pairs={{0,6},{1,7},{2,0},{3,1},{4,2},{5,3},{6,4},{7,5},{8,14},{9,15},{10,... | collective-permute-start | bytes 331784 | tf_op jit(solution)/shard_map/ppermute | solution.py:880
  419.0 8.2 %collective-permute-start.53 = (bf16[144,1024]{1,0:T(8,128)(2,1)S(1)}, bf16[144,1024]{1,0:T(8,128)(2,1)S(1)}, u32[]{:S(2)}, u32[]{:S(2)}) collective-permute-start(bf16[144,1024]{1,0:T(8,128)(2,1)S(1)} %get-tuple-element.350.refs_1_), channel_id=1, source_target_pairs={{0,16},{8,24},{16,0},{24,8},{1,17},{9,25},{17,1},{25,9},{2,18},{10... | collective-permute-start | bytes 884744 | tf_op jit(solution)/shard_map/ppermute | solution.py:880
  419.0 12.3 %collective-permute-start.54 = (bf16[144,1024]{1,0:T(8,128)(2,1)S(1)}, bf16[144,1024]{1,0:T(8,128)(2,1)S(1)}, u32[]{:S(2)}, u32[]{:S(2)}) collective-permute-start(bf16[144,1024]{1,0:T(8,128)(2,1)S(1)} %get-tuple-element.350.refs_1_), channel_id=1, source_target_pairs={{0,8},{8,0},{16,24},{24,16},{1,9},{9,1},{17,25},{25,17},{2,10},{10... | collective-permute-start | bytes 884744 | tf_op jit(solution)/shard_map/ppermute | solution.py:880
  (105 other events, 487.4 us)
Sparse Core Ops, SparseCore 0:
  24.7 112.7 all-gather.5
  311.0 23.0 reduce-scatter.2
  336.5 25.7 reduce-scatter.4
  363.8 23.3 all-gather.7
  392.8 15.6 all-gather.9

commit v4 on v3

--- a/solution.py
+++ b/solution.py
@@ -10,7 +10,7 @@
 
 F32 = jnp.float32
 BF16 = jnp.bfloat16
-VMEM_LIMIT = 48 * 1024 * 1024
+VMEM_LIMIT = 46 * 1024 * 1024
 ANY = pl.BlockSpec(memory_space=pl.ANY)
 ALL_VMEM = 62 * 1024 * 1024
 HBM = pl.BlockSpec(memory_space=pltpu.HBM)
@@ -20,17 +20,18 @@
 LAST = []
 
 
-def call(kernel, name, operands, in_specs, out_shape, out_specs, *, grid=(1,), scalars=(), after=(), carry=(), into=(), scratch=(), time=0, room=10 << 20):
+def call(kernel, name, operands, in_specs, out_shape, out_specs, *, grid=(1,), scalars=(), after=(), carry=(), into=(), scratch=(), time=0, room=None):
     single = not isinstance(out_shape, (tuple, list))
     shapes, specs = ([out_shape], [out_specs]) if single else (list(out_shape), list(out_specs))
     first, made = len(scalars) + len(operands), len(shapes)
     ends = made + len(carry)
     unread = list(carry) + list(into) + list(after) + LAST
 
-    pairs = list(zip(specs, shapes)) + list(zip(in_specs, operands))
-    blocks = [math.prod(spec.block_shape) * array.dtype.itemsize for spec, array in pairs if spec.block_shape is not None]
-    held = [math.prod(s.shape) * jnp.dtype(s.dtype).itemsize for s in scratch if getattr(s, "dtype", None) in (BF16, F32)]
-    limit = ALL_VMEM if room is None else min(VMEM_LIMIT, 2 * sum(blocks) + sum(held) + room)
+    limit = VMEM_LIMIT
+    if room is not None:
+        pairs = list(zip(specs, shapes)) + list(zip(in_specs, operands))
+        blocks = [math.prod(spec.block_shape) * array.dtype.itemsize for spec, array in pairs if spec.block_shape is not None]
+        limit = ALL_VMEM if room < 0 else min(VMEM_LIMIT, 2 * sum(blocks) + room)
 
     def body(*refs):
         outs = first + len(unread)
@@ -98,7 +99,7 @@
     if vectors:
         shapes[0] = (shapes[0][0], shapes[0][1] + lanes)
     everything = list(operands) + list(vectors)
-    return call(kernel, "pack", everything, [whole(o.shape) for o in everything], [like(s) for s in shapes], [whole(s) for s in shapes], room=None)
+    return call(kernel, "pack", everything, [whole(o.shape) for o in everything], [like(s) for s in shapes], [whole(s) for s in shapes], room=-1)
 
 
 def vector_places(vectors, rows):
@@ -1072,10 +1073,10 @@
     step(*firsts)
     partial = token_grad(dz1, d0, wqkv0, F32)
     vectors = [((sq0, sq1), 0), ((sv0, sv1), 0)] + [((sums,), i) for sums in (sums1, sums2) for i in range(3)] + [((sum_inner,), 0)]
-    (other, own), (got_wouter,) = token_weights_grad(halves, xt, d1, groups, vectors=vectors, carry=[got_wouter])
+    other, own = token_weights_grad(halves, xt, d1, groups, vectors=vectors)
+    for _ in middle:
+        other, got_wouter = step(*firsts, carry=[other, got_wouter])
     got_wouter = spread(got_wouter)
-    for _ in middle:
-        (other,) = step(*firsts, carry=[other])
     seconds = reduction(other, own, xyz, yxz, runs=((0, 2 * cols // 3), (2 * cols // 3, cols // 3)))
     cores = layout.core[2]
     order = [r % cores * (layout.replicas // cores) + r // cores for r in range(layout.replicas)]
@@ -1083,7 +1084,7 @@
     (first_sums,) = across_z(firsts)
     grad_tokens = token_grad(partial, d1, wqkv1, BF16)
     for _ in middle:
-        (got_winner,) = step(*seconds, carry=[got_winner])
+        (got_winner,) = step(*seconds, after=first_sums[1:], carry=[got_winner])
     got_winner = spread(got_winner)
     (second_sums,) = across_z(seconds)
     grad_wouter = outer_result(got_wouter, order)

time: 447 us -> 436 us (0.975)
  local copies, waits for them, and re-layouts: 92.3 us -> 46 us
  Pallas kernels: 199 us -> 233 us
    unnamed x184 -> x170, local copies, waits for them, and re-layouts: 90.2 us -> 43.9 us
    pallas_call x44, Pallas kernels: 199 us -> 233 us  [call(): pl.pallas_call(body, out_shape=shapes + [jax.ShapeDtypeStruct(c.shape, c....]
  transfers between devices with their start and end apart: 61 -> 61, of which waited for: 27 -> 27; matrix products, arithmetic and copies ran while one was open for 1% -> 1% of each run, Pallas kernels for 36% -> 44%
where the time goes in v4:
time: 436 us; the launch traced here: 431 us
  Pallas kernels  233 us (53%)
  waiting for transfers between devices  88.5 us (20%)
  starting transfers between devices  46.7 us (11%)
  local copies, waits for them, and re-layouts  46 us (11%)
  between operations  15.1 us (3%)
    pallas_call x44, Pallas kernels, call(): pl.pallas_call(body, out_shape=shapes + [jax.ShapeDtypeStruct(c.shape, c....  233 us
    ppermute x56, waiting for transfers between devices, send(): return lax.ppermute(value, axis, pairs)  88.3 us
    ppermute x56, starting transfers between devices, send(): return lax.ppermute(value, axis, pairs)  46.5 us
    unnamed x170, local copies, waits for them, and re-layouts  43.9 us
  transfers between devices with their start and end apart: 61, of which 27 were waited for; matrix products, arithmetic and copies ran while one was open for 1% of the time, Pallas kernels for 44%

profile of v4, /device:TPU:9, one launch (start us, length us, event | category | flops | bytes accessed | tf_op | source)
XLA Modules:
  0.0 430.6 jit_solution(5053382486963702615)
XLA Ops:
  19.0 2.7 collective-permute-done.2.refs_5_.refs_9_
  22.5 2.0 pack.3
  27.2 4.4 %collective-permute-done.3.refs_3_ = bf16[4,32,768]{2,1,0:T(8,128)(2,1)S(1)} collective-permute-done((bf16[4,32,768]{2,1,0:T(8,128)(2,1)S(1)}, bf16[4,32,768]{2,1,0:T(8,128)(2,1)S(1)}, u32[]{:S(2)}, u32[]{:S(2)}) %collective-permute-start.3) | collective-permute-done | bytes 196640 | tf_op jit(solution)/shard_map/ppermute | solution.py:881
  38.3 4.8 %collective-permute-done.7.refs_9_.refs_13_ = bf16[32,2560]{1,0:T(8,128)(2,1)S(1)} collective-permute-done((bf16[32,2560]{1,0:T(8,128)(2,1)S(1)}, bf16[32,2560]{1,0:T(8,128)(2,1)S(1)}, u32[]{:S(2)}, u32[]{:S(2)}) %collective-permute-start.7) | collective-permute-done | bytes 163872 | tf_op jit(solution)/shard_map/ppermute | solution.py:881
  43.2 9.8 %collective-permute-done.8.refs_10_.refs_14_ = bf16[32,2560]{1,0:T(8,128)(2,1)S(1)} collective-permute-done((bf16[32,2560]{1,0:T(8,128)(2,1)S(1)}, bf16[32,2560]{1,0:T(8,128)(2,1)S(1)}, u32[]{:S(2)}, u32[]{:S(2)}) %collective-permute-start.8) | collective-permute-done | bytes 163872 | tf_op jit(solution)/shard_map/ppermute | solution.py:881
  53.0 3.9 collective-permute-done.9.refs_11_.refs_15_
  57.8 1.9 stack.43
  66.3 7.1 %project.2 = (bf16[1024,1536]{1,0:T(8,128)(2,1)}, bf16[1024,1536]{1,0:T(8,128)(2,1)}, bf16[128,1024]{1,0:T(8,128)(2,1)S(1)}, f32[8,128]{1,0:T(8,128)S(1)}) custom-call(s32[2]{0:T(128)S(1)} %pad_add_fusion.refs_0_, bf16[1024,1024]{1,0:T(8,128)(2,1)S(1)} %copy-done.34, f32[8,1024]{1,0:T(8,128)S(1)} %stack.40.refs_2_.refs_4_, ...), custom_call_target="tpu_custom_call", output_to_operand_aliasing={{2}: (7, {})} | custom-call | flops 6000000000 | bytes 6000001 | tf_op jit(solution)/shard_map/project/pallas_call | solution.py:40
  74.2 1.8 collective-permute-start.18
  78.5 1.9 copy-done.56
  80.3 11.6 %attend.2 = (bf16[1024,512]{1,0:T(8,128)(2,1)S(1)}, bf16[512,1024]{1,0:T(8,128)(2,1)S(1)}, bf16[2,8,512,512]{3,2,1,0:T(8,128)(2,1)}, f32[2,2,4,512]{3,2,1,0:T(4,128)S(1)}, f32[8,128]{1,0:T(8,128)S(1)}) custom-call(bf16[1024,1536]{1,0:T(8,128)(2,1)S(1)} %copy-done.56, bf16[1024,1536]{1,0:T(8,128)(2,1)S(1)} %copy-done.56, bf16[1024,1536]{1,0:T(8,128)(2,1)S(1)} %copy-done.56, ...), custom_call_target="tpu_custom_call" | custom-call | flops 11000000512 | bytes 11000001 | tf_op jit(solution)/shard_map/attend/pallas_call | solution.py:40
  92.0 14.4 %collective-permute-done.17.refs_10_.refs_14_ = bf16[128,1024]{1,0:T(8,128)(2,1)S(1)} collective-permute-done((bf16[128,1024]{1,0:T(8,128)(2,1)S(1)}, bf16[128,1024]{1,0:T(8,128)(2,1)S(1)}, u32[]{:S(2)}, u32[]{:S(2)}) %collective-permute-start.17) | collective-permute-done | bytes 262176 | tf_op jit(solution)/shard_map/ppermute | solution.py:881
  106.4 4.4 %collective-permute-done.18.refs_11_.refs_15_ = bf16[128,1024]{1,0:T(8,128)(2,1)S(1)} collective-permute-done((bf16[128,1024]{1,0:T(8,128)(2,1)S(1)}, bf16[128,1024]{1,0:T(8,128)(2,1)S(1)}, u32[]{:S(2)}, u32[]{:S(2)}) %collective-permute-start.18) | collective-permute-done | bytes 262176 | tf_op jit(solution)/shard_map/ppermute | solution.py:881
  112.3 2.5 collective-permute-done.19
  114.8 1.9 collective-permute-done.20
  116.7 5.7 %project.3 = (bf16[1024,1536]{1,0:T(8,128)(2,1)}, bf16[1024,1536]{1,0:T(8,128)(2,1)}, f32[8,128]{1,0:T(8,128)S(1)}) custom-call(s32[2]{0:T(128)S(1)} %pad_add_fusion.refs_0_, bf16[1024,1024]{1,0:T(8,128)(2,1)S(1)} %copy-done.35, f32[8,1024]{1,0:T(8,128)S(1)} %stack.40.refs_2_.refs_4_, bf16[2,256,1280]{2,1,0:T(8,128)(2,1)S(1)} %bitcast.169, ...), custom_call_target="tpu_custom_call" | custom-call | flops 6000000000 | bytes 6000001 | tf_op jit(solution)/shard_map/project/pallas_call | solution.py:40
  122.4 1.9 copy-done.55
  124.3 11.6 %attend.3 = (bf16[1024,512]{1,0:T(8,128)(2,1)S(1)}, bf16[512,1024]{1,0:T(8,128)(2,1)S(1)}, bf16[2,8,512,512]{3,2,1,0:T(8,128)(2,1)}, f32[2,2,4,512]{3,2,1,0:T(4,128)S(1)}, f32[8,128]{1,0:T(8,128)S(1)}) custom-call(bf16[1024,1536]{1,0:T(8,128)(2,1)S(1)} %copy-done.55, bf16[1024,1536]{1,0:T(8,128)(2,1)S(1)} %copy-done.55, bf16[1024,1536]{1,0:T(8,128)(2,1)S(1)} %copy-done.55, ...), custom_call_target="tpu_custom_call" | custom-call | flops 11000000512 | bytes 11000001 | tf_op jit(solution)/shard_map/attend/pallas_call | solution.py:40
  136.9 7.8 %join.1 = (f32[1024,1024]{1,0:T(8,128)}, f32[1024,1]{1,0:T(8,128)S(1)}, bf16[1024,1024]{1,0:T(8,128)(2,1)S(1)}, bf16[1024,1024]{1,0:T(8,128)(2,1)}, bf16[1024,1024]{1,0:T(8,128)(2,1)}, /*index=5*/f32[8,128]{1,0:T(8,128)S(1)}) custom-call(s32[2]{0:T(128)S(1)} %pad_add_fusion.refs_0_, bf16[1024,512]{1,0:T(8,128)(2,1)S(1)} %get-tuple-element.210.refs_1_, ...), custom_call_target="tpu_custom_call" | custom-call | flops 7000000000 | bytes 7000001 | tf_op jit(solution)/shard_map/join/pallas_call | solution.py:40
  148.4 10.2 %inner.2 = (bf16[1024,4096]{1,0:T(8,128)(2,1)}, bf16[1024,4096]{1,0:T(8,128)(2,1)}, f32[8,128]{1,0:T(8,128)S(1)}) custom-call(bf16[1024,1024]{1,0:T(8,128)(2,1)S(1)} %copy-done.45, bf16[1024,4096]{1,0:T(8,128)(2,1)} %all-gather.6.cloned.1.call-done.refs_1_.refs_5_, f32[1,4096]{1,0:T(1,128)S(1)} %bitcast.159, f32[8,128]{1,0:T(8,128)S(1)} %get-tuple-element.227.refs_3_), custom_call_target="tpu_custom_call" | custom-call | flops 9000000512 | bytes 9000001 | tf_op jit(solution)/shard_map/inner/pallas_call | solution.py:40
  158.6 2.0 collective-permute-done.23.refs_3_
  163.6 10.4 %inner.3 = (bf16[1024,4096]{1,0:T(8,128)(2,1)}, bf16[1024,4096]{1,0:T(8,128)(2,1)}, f32[8,128]{1,0:T(8,128)S(1)}) custom-call(bf16[1024,1024]{1,0:T(8,128)(2,1)S(1)} %copy-done.45, bf16[1024,4096]{1,0:T(8,128)(2,1)} %all-gather.6.cloned.1.call-done.refs_1_.refs_5_, f32[1,4096]{1,0:T(1,128)S(1)} %bitcast.160, ...), custom_call_target="tpu_custom_call", output_to_operand_aliasing={{0}: (3, {}), {1}: (4, {})} | custom-call | flops 9000000512 | bytes 9000001 | tf_op jit(solution)/shard_map/inner/pallas_call | solution.py:40
  176.0 20.5 %outer.1 = (bf16[1024,1024]{1,0:T(8,128)(2,1)}, f32[1024,1024]{1,0:T(8,128)}, bf16[1024,1024]{1,0:T(8,128)(2,1)S(1)}, bf16[1024,1024]{1,0:T(8,128)(2,1)S(1)}, f3...) custom-call(s32[2]{0:T(128)S(1)} %pad_add_fusion.refs_0_, ...), custom_call_target="tpu_custom_call" | custom-call | flops 19000000512 | bytes 19000000 | tf_op jit(solution)/shard_map/outer/pallas_call | solution.py:40
  197.9 7.2 %outer_grad.2 = (bf16[2,8,256,512]{3,2,1,0:T(8,128)(2,1)S(1)}, f32[8,128]{1,0:T(8,128)S(1)}) custom-call(s32[1]{0:T(128)} %bitcast.1.refs_0_, bf16[1024,1024]{1,0:T(8,128)(2,1)S(1)} %get-tuple-element.245.refs_1_, bf16[1024,4096]{1,0:T(8,128)(2,1)} %get-tuple-element.234.refs_1_.refs_2_, f32[8,128]{1,0:T(8,128)S(1)} %get-tuple-element.246.refs_3_), custom_call_target="tpu_custom_call" | custom-call | flops 6000000000 | bytes 6000001 | tf_op jit(solution)/shard_map/outer_grad/pallas_call | solution.py:40
  206.4 7.1 %outer_grad.3 = (bf16[2,8,256,512]{3,2,1,0:T(8,128)(2,1)S(1)}, f32[8,128]{1,0:T(8,128)S(1)}) custom-call(s32[1]{0:T(128)} %bitcast.refs_0_, bf16[1024,1024]{1,0:T(8,128)(2,1)S(1)} %get-tuple-element.245.refs_1_, bf16[1024,4096]{1,0:T(8,128)(2,1)} %get-tuple-element.234.refs_1_.refs_2_, f32[8,128]{1,0:T(8,128)S(1)} %get-tuple-element.247.refs_3_), custom_call_target="tpu_custom_call" | custom-call | flops 6000000000 | bytes 6000001 | tf_op jit(solution)/shard_map/outer_grad/pallas_call | solution.py:40
  213.6 2.9 combine.8
  218.1 35.9 %inner_back.1 = (bf16[2,8,128,1024]{3,2,1,0:T(8,128)(2,1)}, bf16[2,8,128,1024]{3,2,1,0:T(8,128)(2,1)}, f32[1024,1024]{1,0:T(8,128)}, f32[1,4096]{1,0:T(1,128)S(1)}, f32[8,128]{1,0:T(8,128)S(1)}) custom-call(s32[2]{0:T(128)S(1)} %pad_add_fusion.1.refs_0_, bf16[1024,1024]{1,0:T(8,128)(2,1)S(1)} %copy-done.71, bf16[4096,1024]{1,0:T(8,128)(2,1)} %get-tuple-element.242.refs_2_, ...), custom_call_target="tpu_custom_call" | custom-call | flops 35000000512 | bytes 35000000 | tf_op jit(solution)/shard_map/inner_back/pallas_call | solution.py:40
  254.0 2.3 combine.9
  260.0 8.7 %join_back.1 = (f32[1024,1024]{1,0:T(8,128)}, bf16[1024,1024]{1,0:T(8,128)(2,1)S(1)}, bf16[1024,1024]{1,0:T(8,128)(2,1)S(1)}, f32[8,1024]{1,0:T(8,128)S(1)}, f32[8,128]{1,0:T(8,128)S(1)}) custom-call(f32[1024,1024]{1,0:T(8,128)} %get-tuple-element.240.refs_0_, f32[1024,1024]{1,0:T(8,128)} %get-tuple-element.252.refs_1_, ...), custom_call_target="tpu_custom_call" | custom-call | flops 8000000000 | bytes 8000001 | tf_op jit(solution)/shard_map/join_back/pallas_call | solution.py:40
  271.8 2.9 combine.10
  277.2 11.1 %attend_back.2 = (bf16[3,1024,512]{2,1,0:T(8,128)(2,1)S(1)}, f32[2,1,512]{2,1,0:T(1,128)S(1)}, f32[2,1,512]{2,1,0:T(1,128)S(1)}, f32[8,128]{1,0:T(8,128)S(1)}) custom-call(bf16[1024,1536]{1,0:T(8,128)(2,1)} %get-tuple-element.205.refs_0_.refs_1_.refs_2_, bf16[1024,1536]{1,0:T(8,128)(2,1)} %get-tuple-element.205.refs_0_.refs_1_.refs_2_, ...), custom_call_target="tpu_custom_call" | custom-call | flops 11000000512 | bytes 11000001 | tf_op jit(solution)/shard_map/attend_back/pallas_call | solution.py:40
  290.1 10.4 %token_weights_grad.2 = (bf16[2,8,128,768]{3,2,1,0:T(8,128)(2,1)}, bf16[2,8,128,768]{3,2,1,0:T(8,128)(2,1)}, f32[8,128]{1,0:T(8,128)S(1)}) custom-call(s32[2]{0:T(128)S(1)} %pad_add_fusion.1.refs_0_, bf16[1024,1024]{1,0:T(8,128)(2,1)S(1)} %copy-done.47, bf16[3,1024,512]{2,1,0:T(8,128)(2,1)} %copy-done.53, bf16[512,1024]{1,0:T(8,128)(2,1)S(1)} %copy-done.64, ...), custom_call_target="tpu_custom_call" | custom-call | flops 8000000000 | bytes 8000001 | tf_op jit(solution)/shard_map/token_weights_grad/pallas_call | solution.py:40
  300.5 2.3 combine.11
  307.1 11.3 %attend_back.3 = (bf16[3,1024,512]{2,1,0:T(8,128)(2,1)S(1)}, f32[2,1,512]{2,1,0:T(1,128)S(1)}, f32[2,1,512]{2,1,0:T(1,128)S(1)}, f32[8,128]{1,0:T(8,128)S(1)}) custom-call(bf16[1024,1536]{1,0:T(8,128)(2,1)} %get-tuple-element.218.refs_0_.refs_1_.refs_2_, bf16[1024,1536]{1,0:T(8,128)(2,1)} %get-tuple-element.218.refs_0_.refs_1_.refs_2_, ...), custom_call_target="tpu_custom_call" | custom-call | flops 11000000512 | bytes 11000001 | tf_op jit(solution)/shard_map/attend_back/pallas_call | solution.py:40
  322.4 3.9 combine.12
  330.1 7.2 %token_grad.2 = (f32[1024,1024]{1,0:T(8,128)}, f32[8,128]{1,0:T(8,128)S(1)}) custom-call(f32[1024,1024]{1,0:T(8,128)} %get-tuple-element.262.refs_0_, bf16[3,1024,512]{2,1,0:T(8,128)(2,1)S(1)} %copy-done.54, bf16[1024,1536]{1,0:T(8,128)(2,1)S(1)} %copy-done.50, f32[8,128]{1,0:T(8,128)S(1)} %get-tuple-element.299.refs_3_), custom_call_target="tpu_custom_call" | custom-call | flops 6000000000 | bytes 6000001 | tf_op jit(solution)/shard_map/token_grad/pallas_call | solution.py:40
  337.3 5.8 %token_weights_grad.3 = (bf16[2,8,144,384]{3,2,1,0:T(8,128)(2,1)S(1)}, bf16[2,8,144,384]{3,2,1,0:T(8,128)(2,1)S(1)}, f32[8,128]{1,0:T(8,128)S(1)}) custom-call(s32[2]{0:T(128)S(1)} %pad_add_fusion.1.refs_0_, bf16[1024,1024]{1,0:T(8,128)(2,1)S(1)} %copy-done.48, bf16[3,1024,512]{2,1,0:T(8,128)(2,1)} %copy-done.51, ...), custom_call_target="tpu_custom_call" | custom-call | flops 8000000000 | bytes 8000001 | tf_op jit(solution)/shard_map/token_weights_grad/pallas_call | solution.py:40
  343.1 3.9 collective-permute-done.38
  361.4 2.3 combine.14
  366.5 2.4 collective-permute-done.40
  373.0 6.7 %token_grad.3 = (bf16[1024,1024]{1,0:T(8,128)(2,1)}, f32[8,128]{1,0:T(8,128)S(1)}) custom-call(f32[1024,1024]{1,0:T(8,128)} %get-tuple-element.300.refs_0_, bf16[3,1024,512]{2,1,0:T(8,128)(2,1)S(1)} %copy-done.52, bf16[1024,1536]{1,0:T(8,128)(2,1)S(1)} %copy-done.49, f32[8,128]{1,0:T(8,128)S(1)} %get-tuple-element.326.refs_3_), custom_call_target="tpu_custom_call" | custom-call | flops 6000000000 | bytes 6000001 | tf_op jit(solution)/shard_map/token_grad/pallas_call | solution.py:40
  379.7 3.2 collective-permute-done.44.refs_8_.refs_2_
  383.0 3.0 collective-permute-done.45.refs_9_.refs_3_
  390.2 3.5 collective-permute-done.49
  393.7 2.7 collective-permute-done.48
  402.0 5.9 %collective-permute-done.52.refs_7_ = bf16[144,384]{1,0:T(8,128)(2,1)S(1)} collective-permute-done((bf16[144,384]{1,0:T(8,128)(2,1)S(1)}, bf16[144,384]{1,0:T(8,128)(2,1)S(1)}, u32[]{:S(2)}, u32[]{:S(2)}) %collective-permute-start.52) | collective-permute-done | bytes 110624 | tf_op jit(solution)/shard_map/ppermute | solution.py:881
  410.4 5.7 %collective-permute-done.53.refs_2_ = bf16[144,1024]{1,0:T(8,128)(2,1)S(1)} collective-permute-done((bf16[144,1024]{1,0:T(8,128)(2,1)S(1)}, bf16[144,1024]{1,0:T(8,128)(2,1)S(1)}, u32[]{:S(2)}, u32[]{:S(2)}) %collective-permute-start.53) | collective-permute-done | bytes 294944 | tf_op jit(solution)/shard_map/ppermute | solution.py:881
  420.5 2.1 token_weights_result.1
  (316 shorter events, 109.8 us)
Async XLA Ops:
  7.2 139.6 %all-gather.6.cloned.1.call-start = ((), (), s32[]{:S(2)}) async-start(), calls=%async_computation.2 | async-start | bytes 8650752 | tf_op jit(solution)/shard_map/all_gather | solution.py:993
  8.9 8.6 %collective-permute-start = (bf16[32,1664]{1,0:T(8,128)(2,1)}, bf16[32,1664]{1,0:T(8,128)(2,1)S(1)}, u32[]{:S(2)}, u32[]{:S(2)}) collective-permute-start(bf16[32,1664]{1,0:T(8,128)(2,1)} %get-tuple-element.189.refs_2_.refs_6_), channel_id=1, source_target_pairs={{0,2},{1,3},{2,4},{3,5},{4,6},{5,7},{6,0},{7,1},{8,10},{9,11},{10,... | collective-permute-start | bytes 319496 | tf_op jit(solution)/shard_map/ppermute | solution.py:881
  10.2 8.8 %collective-permute-start.1 = (bf16[32,1664]{1,0:T(8,128)(2,1)}, bf16[32,1664]{1,0:T(8,128)(2,1)S(1)}, u32[]{:S(2)}, u32[]{:S(2)}) collective-permute-start(bf16[32,1664]{1,0:T(8,128)(2,1)} %get-tuple-element.189.refs_2_.refs_6_), channel_id=1, source_target_pairs={{0,4},{1,5},{2,6},{3,7},{4,0},{5,1},{6,2},{7,3},{8,12},{9,13},{10,... | collective-permute-start | bytes 319496 | tf_op jit(solution)/shard_map/ppermute | solution.py:881
  11.2 10.5 %collective-permute-start.2 = (bf16[32,1664]{1,0:T(8,128)(2,1)}, bf16[32,1664]{1,0:T(8,128)(2,1)S(1)}, u32[]{:S(2)}, u32[]{:S(2)}) collective-permute-start(bf16[32,1664]{1,0:T(8,128)(2,1)} %get-tuple-element.189.refs_2_.refs_6_), channel_id=1, source_target_pairs={{0,6},{1,7},{2,0},{3,1},{4,2},{5,3},{6,4},{7,5},{8,14},{9,15},{10,... | collective-permute-start | bytes 319496 | tf_op jit(solution)/shard_map/ppermute | solution.py:881
  24.6 318.5 %reduce-scatter.3.cloned.1.call-start = ((), (), s32[]{:S(2)}) async-start(), calls=%async_computation.3 | async-start | bytes 1310720 | tf_op jit(solution)/shard_map/reduce_scatter | solution.py:1044
  33.9 23.0 %collective-permute-start.6 = (bf16[4,2,32,896]{3,2,1,0:T(8,128)(2,1)S(1)}, bf16[4,2,32,896]{3,2,1,0:T(8,128)(2,1)S(1)}, u32[]{:S(2)}, u32[]{:S(2)}) collective-permute-start(bf16[4,2,32,896]{3,2,1,0:T(8,128)(2,1)S(1)} %get-tuple-element.198.refs_6_), channel_id=1, source_target_pairs={{0,16},{8,24},{16,0},{24,8},{1,17},{9,25},{17,1},{25,9},{2,18},{10... | collective-permute-start | bytes 1376264 | tf_op jit(solution)/shard_map/ppermute | solution.py:881
  35.2 21.7 %collective-permute-start.5 = (bf16[2,4,32,768]{3,2,1,0:T(8,128)(2,1)S(1)}, bf16[2,4,32,768]{3,2,1,0:T(8,128)(2,1)S(1)}, u32[]{:S(2)}, u32[]{:S(2)}) collective-permute-start(bf16[2,4,32,768]{3,2,1,0:T(8,128)(2,1)S(1)} %get-tuple-element.197.refs_4_), channel_id=1, source_target_pairs={{0,1},{1,0},{2,3},{3,2},{4,5},{5,4},{6,7},{7,6},{8,9},{9,8},{10,11... | collective-permute-start | bytes 1179656 | tf_op jit(solution)/shard_map/ppermute | solution.py:881
  36.2 16.8 %collective-permute-start.8 = (bf16[32,2560]{1,0:T(8,128)(2,1)S(1)}, bf16[32,2560]{1,0:T(8,128)(2,1)S(1)}, u32[]{:S(2)}, u32[]{:S(2)}) collective-permute-start(bf16[32,2560]{1,0:T(8,128)(2,1)S(1)} %get-tuple-element.199.refs_8_.refs_12_), channel_id=1, source_target_pairs={{0,4},{1,5},{2,6},{3,7},{4,0},{5,1},{6,2},{7,3},{8,12},{9,13},{10,... | collective-permute-start | bytes 491528 | tf_op jit(solution)/shard_map/ppermute | solution.py:881
  37.1 19.8 %collective-permute-start.9 = (bf16[32,2560]{1,0:T(8,128)(2,1)S(1)}, bf16[32,2560]{1,0:T(8,128)(2,1)S(1)}, u32[]{:S(2)}, u32[]{:S(2)}) collective-permute-start(bf16[32,2560]{1,0:T(8,128)(2,1)S(1)} %get-tuple-element.199.refs_8_.refs_12_), channel_id=1, source_target_pairs={{0,6},{1,7},{2,0},{3,1},{4,2},{5,3},{6,4},{7,5},{8,14},{9,15},{10,... | collective-permute-start | bytes 491528 | tf_op jit(solution)/shard_map/ppermute | solution.py:881
  60.7 15.3 %collective-permute-start.12 = (bf16[4,32,1280]{2,1,0:T(8,128)(2,1)S(1)}, bf16[4,32,1280]{2,1,0:T(8,128)(2,1)S(1)}, u32[]{:S(2)}, u32[]{:S(2)}) collective-permute-start(bf16[4,32,1280]{2,1,0:T(8,128)(2,1)S(1)} %get-tuple-element.206.refs_2_), channel_id=1, source_target_pairs={{0,16},{8,24},{16,0},{24,8},{1,17},{9,25},{17,1},{25,9},{2,18},{10... | collective-permute-start | bytes 983048 | tf_op jit(solution)/shard_map/ppermute | solution.py:881
  61.4 14.6 %collective-permute-start.13 = (bf16[4,32,1280]{2,1,0:T(8,128)(2,1)S(1)}, bf16[4,32,1280]{2,1,0:T(8,128)(2,1)S(1)}, u32[]{:S(2)}, u32[]{:S(2)}) collective-permute-start(bf16[4,32,1280]{2,1,0:T(8,128)(2,1)S(1)} %get-tuple-element.207.refs_4_), channel_id=1, source_target_pairs={{0,1},{1,0},{2,3},{3,2},{4,5},{5,4},{6,7},{7,6},{8,9},{9,8},{10,11... | collective-permute-start | bytes 983048 | tf_op jit(solution)/shard_map/ppermute | solution.py:881
  73.5 18.5 %collective-permute-start.16 = (bf16[128,1024]{1,0:T(8,128)(2,1)S(1)}, bf16[128,1024]{1,0:T(8,128)(2,1)S(1)}, u32[]{:S(2)}, u32[]{:S(2)}) collective-permute-start(bf16[128,1024]{1,0:T(8,128)(2,1)S(1)} %get-tuple-element.213.refs_8_.refs_12_), channel_id=1, source_target_pairs={{0,2},{1,3},{2,4},{3,5},{4,6},{5,7},{6,0},{7,1},{8,10},{9,11},{10,... | collective-permute-start | bytes 786440 | tf_op jit(solution)/shard_map/ppermute | solution.py:881
  73.5 32.8 %collective-permute-start.17 = (bf16[128,1024]{1,0:T(8,128)(2,1)S(1)}, bf16[128,1024]{1,0:T(8,128)(2,1)S(1)}, u32[]{:S(2)}, u32[]{:S(2)}) collective-permute-start(bf16[128,1024]{1,0:T(8,128)(2,1)S(1)} %get-tuple-element.213.refs_8_.refs_12_), channel_id=1, source_target_pairs={{0,4},{1,5},{2,6},{3,7},{4,0},{5,1},{6,2},{7,3},{8,12},{9,13},{10,... | collective-permute-start | bytes 786440 | tf_op jit(solution)/shard_map/ppermute | solution.py:881
  74.2 36.6 %collective-permute-start.18 = (bf16[128,1024]{1,0:T(8,128)(2,1)S(1)}, bf16[128,1024]{1,0:T(8,128)(2,1)S(1)}, u32[]{:S(2)}, u32[]{:S(2)}) collective-permute-start(bf16[128,1024]{1,0:T(8,128)(2,1)S(1)} %get-tuple-element.213.refs_8_.refs_12_), channel_id=1, source_target_pairs={{0,6},{1,7},{2,0},{3,1},{4,2},{5,3},{6,4},{7,5},{8,14},{9,15},{10,... | collective-permute-start | bytes 786440 | tf_op jit(solution)/shard_map/ppermute | solution.py:881
  76.4 34.4 %collective-permute-start.14 = (bf16[2,4,32,1280]{3,2,1,0:T(8,128)(2,1)S(1)}, bf16[2,4,32,1280]{3,2,1,0:T(8,128)(2,1)S(1)}, u32[]{:S(2)}, u32[]{:S(2)}) collective-permute-start(bf16[2,4,32,1280]{3,2,1,0:T(8,128)(2,1)S(1)} %get-tuple-element.211.refs_4_), channel_id=1, source_target_pairs={{0,1},{1,0},{2,3},{3,2},{4,5},{5,4},{6,7},{7,6},{8,9},{9,8},{10,11... | collective-permute-start | bytes 1966088 | tf_op jit(solution)/shard_map/ppermute | solution.py:881
  77.3 33.5 %collective-permute-start.15 = (bf16[4,2,32,1280]{3,2,1,0:T(8,128)(2,1)S(1)}, bf16[4,2,32,1280]{3,2,1,0:T(8,128)(2,1)S(1)}, u32[]{:S(2)}, u32[]{:S(2)}) collective-permute-start(bf16[4,2,32,1280]{3,2,1,0:T(8,128)(2,1)S(1)} %get-tuple-element.212.refs_6_), channel_id=1, source_target_pairs={{0,16},{8,24},{16,0},{24,8},{1,17},{9,25},{17,1},{25,9},{2,18},{10... | collective-permute-start | bytes 1966088 | tf_op jit(solution)/shard_map/ppermute | solution.py:881
  112.3 23.7 %collective-permute-start.21 = (bf16[4,128,512]{2,1,0:T(8,128)(2,1)S(1)}, bf16[4,128,512]{2,1,0:T(8,128)(2,1)S(1)}, u32[]{:S(2)}, u32[]{:S(2)}) collective-permute-start(bf16[4,128,512]{2,1,0:T(8,128)(2,1)S(1)} %get-tuple-element.221.refs_2_), channel_id=1, source_target_pairs={{0,16},{8,24},{16,0},{24,8},{1,17},{9,25},{17,1},{25,9},{2,18},{10... | collective-permute-start | bytes 1572872 | tf_op jit(solution)/shard_map/ppermute | solution.py:881
  112.3 23.7 %collective-permute-start.22 = (bf16[4,128,512]{2,1,0:T(8,128)(2,1)S(1)}, bf16[4,128,512]{2,1,0:T(8,128)(2,1)S(1)}, u32[]{:S(2)}, u32[]{:S(2)}) collective-permute-start(bf16[4,128,512]{2,1,0:T(8,128)(2,1)S(1)} %get-tuple-element.222.refs_4_), channel_id=1, source_target_pairs={{0,1},{1,0},{2,3},{3,2},{4,5},{5,4},{6,7},{7,6},{8,9},{9,8},{10,11... | collective-permute-start | bytes 1572872 | tf_op jit(solution)/shard_map/ppermute | solution.py:881
  136.1 24.6 %collective-permute-start.23 = (bf16[2,4,128,512]{3,2,1,0:T(8,128)(2,1)S(1)}, bf16[2,4,128,512]{3,2,1,0:T(8,128)(2,1)S(1)}, u32[]{:S(2)}, u32[]{:S(2)}) collective-permute-start(bf16[2,4,128,512]{3,2,1,0:T(8,128)(2,1)S(1)} %get-tuple-element.230.refs_2_), channel_id=1, source_target_pairs={{0,1},{1,0},{2,3},{3,2},{4,5},{5,4},{6,7},{7,6},{8,9},{9,8},{10,11... | collective-permute-start | bytes 3145736 | tf_op jit(solution)/shard_map/ppermute | solution.py:881
  136.2 24.6 %collective-permute-start.24 = (bf16[4,2,128,512]{3,2,1,0:T(8,128)(2,1)S(1)}, bf16[4,2,128,512]{3,2,1,0:T(8,128)(2,1)}, u32[]{:S(2)}, u32[]{:S(2)}) collective-permute-start(bf16[4,2,128,512]{3,2,1,0:T(8,128)(2,1)S(1)} %get-tuple-element.231.refs_4_), channel_id=1, source_target_pairs={{0,16},{8,24},{16,0},{24,8},{1,17},{9,25},{17,1},{25,9},{2,18},{10... | collective-permute-start | bytes 3145736 | tf_op jit(solution)/shard_map/ppermute | solution.py:881
  162.3 11.8 %collective-permute-start.25 = (bf16[2,4,2,128,512]{4,3,2,1,0:T(8,128)(2,1)S(1)}, bf16[2,4,2,128,512]{4,3,2,1,0:T(8,128)(2,1)S(1)}, u32[]{:S(2)}, u32[]{:S(2)}) collective-permute-start(bf16[2,4,2,128,512]{4,3,2,1,0:T(8,128)(2,1)S(1)} %get-tuple-element.236), channel_id=1, source_target_pairs={{0,8},{8,0},{16,24},{24,16},{1,9},{9,1},{17,25},{25,17},{2,10},{10... | collective-permute-start | bytes 6291464 | tf_op jit(solution)/shard_map/ppermute | solution.py:881
  163.5 10.5 %collective-permute-start.26 = (bf16[2,4,2,128,512]{4,3,2,1,0:T(8,128)(2,1)S(1)}, bf16[2,4,2,128,512]{4,3,2,1,0:T(8,128)(2,1)S(1)}, u32[]{:S(2)}, u32[]{:S(2)}) collective-permute-start(bf16[2,4,2,128,512]{4,3,2,1,0:T(8,128)(2,1)S(1)} %get-tuple-element.237), channel_id=1, source_target_pairs={{0,8},{8,0},{16,24},{24,16},{1,9},{9,1},{17,25},{25,17},{2,10},{10... | collective-permute-start | bytes 6291464 | tf_op jit(solution)/shard_map/ppermute | solution.py:881
  205.0 8.5 %collective-permute-start.27 = (bf16[2,8,256,512]{3,2,1,0:T(8,128)(2,1)S(1)}, bf16[2,8,256,512]{3,2,1,0:T(8,128)(2,1)S(1)}, u32[]{:S(2)}, u32[]{:S(2)}) collective-permute-start(bf16[2,8,256,512]{3,2,1,0:T(8,128)(2,1)S(1)} %get-tuple-element.249), channel_id=1, source_target_pairs={{0,8},{8,0},{16,24},{24,16},{1,9},{9,1},{17,25},{25,17},{2,10},{10... | collective-permute-start | bytes 12582920 | tf_op jit(solution)/shard_map/ppermute | solution.py:881
  216.5 37.4 %collective-permute-start.28 = (bf16[1,8,128,512]{3,2,1,0:T(8,128)(2,1)S(1)}, bf16[1,8,128,512]{3,2,1,0:T(8,128)(2,1)S(1)}, u32[]{:S(2)}, u32[]{:S(2)}) collective-permute-start(bf16[1,8,128,512]{3,2,1,0:T(8,128)(2,1)S(1)} %get-tuple-element.256), channel_id=1, source_target_pairs={{0,16},{8,24},{16,0},{24,8},{1,17},{9,25},{17,1},{25,9},{2,18},{10... | collective-permute-start | bytes 3145736 | tf_op jit(solution)/shard_map/ppermute | solution.py:881
  216.6 37.4 %collective-permute-start.29 = (bf16[8,1,128,512]{3,2,1,0:T(8,128)(2,1)S(1)}, bf16[8,1,128,512]{3,2,1,0:T(8,128)(2,1)S(1)}, u32[]{:S(2)}, u32[]{:S(2)}) collective-permute-start(bf16[8,1,128,512]{3,2,1,0:T(8,128)(2,1)S(1)} %get-tuple-element.258), channel_id=1, source_target_pairs={{0,1},{1,0},{2,3},{3,2},{4,5},{5,4},{6,7},{7,6},{8,9},{9,8},{10,11... | collective-permute-start | bytes 3145736 | tf_op jit(solution)/shard_map/ppermute | solution.py:881
  256.3 15.5 %collective-permute-start.30 = (bf16[2,8,128,1024]{3,2,1,0:T(8,128)(2,1)}, bf16[2,8,128,1024]{3,2,1,0:T(8,128)(2,1)S(1)}, u32[]{:S(2)}, u32[]{:S(2)}) collective-permute-start(bf16[2,8,128,1024]{3,2,1,0:T(8,128)(2,1)} %get-tuple-element.268), channel_id=1, source_target_pairs={{0,8},{8,0},{16,24},{24,16},{1,9},{9,1},{17,25},{25,17},{2,10},{10... | collective-permute-start | bytes 12582920 | tf_op jit(solution)/shard_map/ppermute | solution.py:881
  256.9 13.7 %collective-permute-start.31 = (bf16[4,1,128,512]{3,2,1,0:T(8,128)(2,1)}, bf16[4,1,128,512]{3,2,1,0:T(8,128)(2,1)S(1)}, u32[]{:S(2)}, u32[]{:S(2)}) collective-permute-start(bf16[4,1,128,512]{3,2,1,0:T(8,128)(2,1)} %get-tuple-element.270), channel_id=1, source_target_pairs={{0,1},{1,0},{2,3},{3,2},{4,5},{5,4},{6,7},{7,6},{8,9},{9,8},{10,11... | collective-permute-start | bytes 1572872 | tf_op jit(solution)/shard_map/ppermute | solution.py:881
  256.9 13.6 %collective-permute-start.32 = (bf16[1,4,128,512]{3,2,1,0:T(8,128)(2,1)S(1)}, bf16[1,4,128,512]{3,2,1,0:T(8,128)(2,1)S(1)}, u32[]{:S(2)}, u32[]{:S(2)}) collective-permute-start(bf16[1,4,128,512]{3,2,1,0:T(8,128)(2,1)S(1)} %get-tuple-element.272), channel_id=1, source_target_pairs={{0,16},{8,24},{16,0},{24,8},{1,17},{9,25},{17,1},{25,9},{2,18},{10... | collective-permute-start | bytes 1572872 | tf_op jit(solution)/shard_map/ppermute | solution.py:881
  274.8 25.7 %collective-permute-start.33 = (bf16[1,8,128,512]{3,2,1,0:T(8,128)(2,1)S(1)}, bf16[1,8,128,512]{3,2,1,0:T(8,128)(2,1)S(1)}, u32[]{:S(2)}, u32[]{:S(2)}) collective-permute-start(bf16[1,8,128,512]{3,2,1,0:T(8,128)(2,1)S(1)} %get-tuple-element.284), channel_id=1, source_target_pairs={{0,16},{8,24},{16,0},{24,8},{1,17},{9,25},{17,1},{25,9},{2,18},{10... | collective-permute-start | bytes 3145736 | tf_op jit(solution)/shard_map/ppermute | solution.py:881
  276.3 24.2 %collective-permute-start.34 = (bf16[8,1,128,512]{3,2,1,0:T(8,128)(2,1)S(1)}, bf16[8,1,128,512]{3,2,1,0:T(8,128)(2,1)S(1)}, u32[]{:S(2)}, u32[]{:S(2)}) collective-permute-start(bf16[8,1,128,512]{3,2,1,0:T(8,128)(2,1)S(1)} %get-tuple-element.286), channel_id=1, source_target_pairs={{0,1},{1,0},{2,3},{3,2},{4,5},{5,4},{6,7},{7,6},{8,9},{9,8},{10,11... | collective-permute-start | bytes 3145736 | tf_op jit(solution)/shard_map/ppermute | solution.py:881
  304.4 17.2 %collective-permute-start.35 = (bf16[2,8,128,768]{3,2,1,0:T(8,128)(2,1)}, bf16[2,8,128,768]{3,2,1,0:T(8,128)(2,1)}, u32[]{:S(2)}, u32[]{:S(2)}) collective-permute-start(bf16[2,8,128,768]{3,2,1,0:T(8,128)(2,1)} %get-tuple-element.289), channel_id=1, source_target_pairs={{0,8},{8,0},{16,24},{24,16},{1,9},{9,1},{17,25},{25,17},{2,10},{10... | collective-permute-start | bytes 9437192 | tf_op jit(solution)/shard_map/ppermute | solution.py:881
  306.1 73.6 %reduce-scatter.5.cloned.1.call-start = ((), (), s32[]{:S(2)}) async-start(), calls=%async_computation.4 | async-start | bytes 1310720 | tf_op jit(solution)/shard_map/reduce_scatter | solution.py:1044
  306.2 13.9 %collective-permute-start.36 = (bf16[4,1,128,512]{3,2,1,0:T(8,128)(2,1)}, bf16[4,1,128,512]{3,2,1,0:T(8,128)(2,1)S(1)}, u32[]{:S(2)}, u32[]{:S(2)}) collective-permute-start(bf16[4,1,128,512]{3,2,1,0:T(8,128)(2,1)} %get-tuple-element.291), channel_id=1, source_target_pairs={{0,1},{1,0},{2,3},{3,2},{4,5},{5,4},{6,7},{7,6},{8,9},{9,8},{10,11... | collective-permute-start | bytes 1572872 | tf_op jit(solution)/shard_map/ppermute | solution.py:881
  306.7 13.6 %collective-permute-start.37 = (bf16[1,4,128,512]{3,2,1,0:T(8,128)(2,1)}, bf16[1,4,128,512]{3,2,1,0:T(8,128)(2,1)S(1)}, u32[]{:S(2)}, u32[]{:S(2)}) collective-permute-start(bf16[1,4,128,512]{3,2,1,0:T(8,128)(2,1)} %get-tuple-element.293), channel_id=1, source_target_pairs={{0,16},{8,24},{16,0},{24,8},{1,17},{9,25},{17,1},{25,9},{2,18},{10... | collective-permute-start | bytes 1572872 | tf_op jit(solution)/shard_map/ppermute | solution.py:881
  321.5 76.6 %all-gather.8.cloned.1.call-start = ((), (), s32[]{:S(2)}) async-start(), calls=%async_computation.5 | async-start | bytes 1310720 | tf_op jit(solution)/shard_map/all_gather | solution.py:1052
  327.9 19.1 %collective-permute-start.38 = (bf16[1,8,128,384]{3,2,1,0:T(8,128)(2,1)}, bf16[1,8,128,384]{3,2,1,0:T(8,128)(2,1)}, u32[]{:S(2)}, u32[]{:S(2)}) collective-permute-start(bf16[1,8,128,384]{3,2,1,0:T(8,128)(2,1)} %get-tuple-element.304), channel_id=1, source_target_pairs={{0,16},{8,24},{16,0},{24,8},{1,17},{9,25},{17,1},{25,9},{2,18},{10... | collective-permute-start | bytes 2359304 | tf_op jit(solution)/shard_map/ppermute | solution.py:881
  329.1 14.0 %collective-permute-start.39 = (bf16[8,1,128,256]{3,2,1,0:T(8,128)(2,1)}, bf16[8,1,128,256]{3,2,1,0:T(8,128)(2,1)}, u32[]{:S(2)}, u32[]{:S(2)}) collective-permute-start(bf16[8,1,128,256]{3,2,1,0:T(8,128)(2,1)} %get-tuple-element.306), channel_id=1, source_target_pairs={{0,1},{1,0},{2,3},{3,2},{4,5},{5,4},{6,7},{7,6},{8,9},{9,8},{10,11... | collective-permute-start | bytes 1572872 | tf_op jit(solution)/shard_map/ppermute | solution.py:881
  357.9 59.9 %all-gather.10.cloned.1.call-start = ((), (), s32[]{:S(2)}) async-start(), calls=%async_computation.6 | async-start | bytes 1310720 | tf_op jit(solution)/shard_map/all_gather | solution.py:1052
  357.9 11.0 %collective-permute-start.40 = (bf16[4,1,128,384]{3,2,0,1:T(8,128)(2,1)}, bf16[4,1,128,384]{3,2,0,1:T(8,128)(2,1)S(1)}, u32[]{:S(2)}, u32[]{:S(2)}) collective-permute-start(bf16[4,1,128,384]{3,2,0,1:T(8,128)(2,1)} %bitcast.171), channel_id=1, source_target_pairs={{0,1},{1,0},{2,3},{3,2},{4,5},{5,4},{6,7},{7,6},{8,9},{9,8},{10,11... | collective-permute-start | bytes 1179656 | tf_op jit(solution)/shard_map/ppermute | solution.py:881
  363.7 22.2 %collective-permute-start.46 = (bf16[1,8,144,256]{3,2,1,0:T(8,128)(2,1)}, bf16[1,8,144,256]{3,2,1,0:T(8,128)(2,1)S(1)}, u32[]{:S(2)}, u32[]{:S(2)}) collective-permute-start(bf16[1,8,144,256]{3,2,1,0:T(8,128)(2,1)} %get-tuple-element.333), channel_id=1, source_target_pairs={{0,16},{8,24},{16,0},{24,8},{1,17},{9,25},{17,1},{25,9},{2,18},{10... | collective-permute-start | bytes 1769480 | tf_op jit(solution)/shard_map/ppermute | solution.py:881
  369.3 10.4 %collective-permute-start.43 = (bf16[128,640]{1,0:T(8,128)(2,1)S(1)}, bf16[128,640]{1,0:T(8,128)(2,1)S(1)}, u32[]{:S(2)}, u32[]{:S(2)}) collective-permute-start(bf16[128,640]{1,0:T(8,128)(2,1)S(1)} %get-tuple-element.329), channel_id=1, source_target_pairs={{0,2},{1,3},{2,4},{3,5},{4,6},{5,7},{6,0},{7,1},{8,10},{9,11},{10,... | collective-permute-start | bytes 491528 | tf_op jit(solution)/shard_map/ppermute | solution.py:881
  369.4 13.6 %collective-permute-start.44 = (bf16[128,640]{1,0:T(8,128)(2,1)S(1)}, bf16[128,640]{1,0:T(8,128)(2,1)S(1)}, u32[]{:S(2)}, u32[]{:S(2)}) collective-permute-start(bf16[128,640]{1,0:T(8,128)(2,1)S(1)} %get-tuple-element.330), channel_id=1, source_target_pairs={{0,4},{1,5},{2,6},{3,7},{4,0},{5,1},{6,2},{7,3},{8,12},{9,13},{10,... | collective-permute-start | bytes 491528 | tf_op jit(solution)/shard_map/ppermute | solution.py:881
  370.8 15.1 %collective-permute-start.45 = (bf16[128,640]{1,0:T(8,128)(2,1)S(1)}, bf16[128,640]{1,0:T(8,128)(2,1)S(1)}, u32[]{:S(2)}, u32[]{:S(2)}) collective-permute-start(bf16[128,640]{1,0:T(8,128)(2,1)S(1)} %get-tuple-element.331), channel_id=1, source_target_pairs={{0,6},{1,7},{2,0},{3,1},{4,2},{5,3},{6,4},{7,5},{8,14},{9,15},{10,... | collective-permute-start | bytes 491528 | tf_op jit(solution)/shard_map/ppermute | solution.py:881
  372.2 13.7 %collective-permute-start.47 = (bf16[8,1,144,128]{3,2,1,0:T(8,128)(2,1)}, bf16[8,1,144,128]{3,2,1,0:T(8,128)(2,1)S(1)}, u32[]{:S(2)}, u32[]{:S(2)}) collective-permute-start(bf16[8,1,144,128]{3,2,1,0:T(8,128)(2,1)} %get-tuple-element.335), channel_id=1, source_target_pairs={{0,1},{1,0},{2,3},{3,2},{4,5},{5,4},{6,7},{7,6},{8,9},{9,8},{10,11... | collective-permute-start | bytes 884744 | tf_op jit(solution)/shard_map/ppermute | solution.py:881
  388.2 8.2 %collective-permute-start.48 = (bf16[4,1,144,256]{3,2,0,1:T(8,128)(2,1)S(1)}, bf16[4,1,144,256]{3,2,0,1:T(8,128)(2,1)S(1)}, u32[]{:S(2)}, u32[]{:S(2)}) collective-permute-start(bf16[4,1,144,256]{3,2,0,1:T(8,128)(2,1)S(1)} %bitcast.172), channel_id=1, source_target_pairs={{0,1},{1,0},{2,3},{3,2},{4,5},{5,4},{6,7},{7,6},{8,9},{9,8},{10,11... | collective-permute-start | bytes 884744 | tf_op jit(solution)/shard_map/ppermute | solution.py:881
  396.8 11.1 %collective-permute-start.52 = (bf16[144,384]{1,0:T(8,128)(2,1)S(1)}, bf16[144,384]{1,0:T(8,128)(2,1)S(1)}, u32[]{:S(2)}, u32[]{:S(2)}) collective-permute-start(bf16[144,384]{1,0:T(8,128)(2,1)S(1)} %get-tuple-element.346), channel_id=1, source_target_pairs={{0,6},{1,7},{2,0},{3,1},{4,2},{5,3},{6,4},{7,5},{8,14},{9,15},{10,... | collective-permute-start | bytes 331784 | tf_op jit(solution)/shard_map/ppermute | solution.py:881
  408.1 8.0 %collective-permute-start.53 = (bf16[144,1024]{1,0:T(8,128)(2,1)S(1)}, bf16[144,1024]{1,0:T(8,128)(2,1)S(1)}, u32[]{:S(2)}, u32[]{:S(2)}) collective-permute-start(bf16[144,1024]{1,0:T(8,128)(2,1)S(1)} %get-tuple-element.350.refs_1_), channel_id=1, source_target_pairs={{0,16},{8,24},{16,0},{24,8},{1,17},{9,25},{17,1},{25,9},{2,18},{10... | collective-permute-start | bytes 884744 | tf_op jit(solution)/shard_map/ppermute | solution.py:881
  409.4 11.1 %collective-permute-start.54 = (bf16[144,1024]{1,0:T(8,128)(2,1)S(1)}, bf16[144,1024]{1,0:T(8,128)(2,1)S(1)}, u32[]{:S(2)}, u32[]{:S(2)}) collective-permute-start(bf16[144,1024]{1,0:T(8,128)(2,1)S(1)} %get-tuple-element.350.refs_1_), channel_id=1, source_target_pairs={{0,8},{8,0},{16,24},{24,16},{1,9},{9,1},{17,25},{25,17},{2,10},{10... | collective-permute-start | bytes 884744 | tf_op jit(solution)/shard_map/ppermute | solution.py:881
  (98 other events, 579.3 us)
Sparse Core Ops, SparseCore 0:
  24.7 111.8 all-gather.5
  306.2 23.4 reduce-scatter.2
  332.7 25.8 reduce-scatter.4
  360.0 23.4 all-gather.7
  388.3 16.4 all-gather.9

commit v5 on v4

--- a/solution.py
+++ b/solution.py
@@ -61,6 +61,10 @@
     return jax.ShapeDtypeStruct(shape, dtype)
 
 
+def far(shape, dtype=BF16):
+    return pltpu.HBM(shape, dtype)
+
+
 def dot(left, right):
     return lax.dot_general(left, right, (((1,), (0,)), ((), ())), preferred_element_type=F32)
 
@@ -178,7 +182,7 @@
         "combine",
         [t[0] for t in flat],
         [at(job, t[1]) for job, (_, terms) in enumerate(jobs) for t in terms],
-        [like(size) for size in sizes for _ in range(n)],
+        [far(size) for size in sizes for _ in range(n)],
         [whole(size) for size in sizes for _ in range(n)],
         grid=(n,),
         scalars=[own for own, _ in jobs],
@@ -276,6 +280,21 @@
     return call(kernel, "inner_result", [got], [whole(got.shape)], like(shape, F32), whole(shape), room=8 << 20)
 
 
+def wide_results(got, order, runs=2):
+    count, rows, cols = got.shape
+    high, wide = cols // 2 // runs, cols // 2
+
+    def kernel(got_ref, first_ref, second_ref):
+        for i, j in enumerate(order):
+            for run in range(runs):
+                at = (j * runs + run) * rows
+                first_ref[:, at : at + rows] = got_ref[i, :, run * high : (run + 1) * high].astype(F32).T
+            second_ref[:, j * wide : (j + 1) * wide] = got_ref[i, :, wide:].astype(F32)
+
+    shapes = [(high, count * runs * rows), (rows, count * wide)]
+    return call(kernel, "wide_results", [got], [whole(got.shape)], [like(s, F32) for s in shapes], [whole(s) for s in shapes], room=8 << 20)
+
+
 def token_weights_result(pieces, places, keep, size, last):
     count = len(pieces)
     rows = pieces[0].shape[0]
@@ -316,7 +335,7 @@
         "transposed",
         [x],
         [pl.BlockSpec((tile, cols), lambda i: (i, 0))],
-        like((cols, rows)),
+        far((cols, rows)),
         pl.BlockSpec((cols, tile), lambda i: (0, i)),
         grid=(rows // tile,),
         time=3,
@@ -493,7 +512,7 @@
             pl.BlockSpec((1, 1, heads, length), lambda s, p: (s, p, 0, 0)),
             spec(part),
         ],
-        (like((3, tokens, width)), like((seqs, 1, width), F32), like((seqs, 1, width), F32)),
+        (far((3, tokens, width)), like((seqs, 1, width), F32), like((seqs, 1, width), F32)),
         (pl.BlockSpec((3, length, block), lambda s, p: (0, s, p)), sums, sums),
         grid=(seqs, blocks),
         carry=carry,
@@ -546,7 +565,7 @@
         "join",
         [o0, o1, x, vec] + list(pieces.buffers),
         [half, half, tok, whole(vec.shape)] + [ANY] * count,
-        (like((rows, width), F32), like((rows, 1), F32), like((rows, width)), like((width, rows)), like((width, width))),
+        (far((rows, width), F32), far((rows, 1), F32), like((rows, width)), far((width, rows)), like((width, width))),
         (tok, pl.BlockSpec((tile, 1), lambda i, *_: (i, 0)), tok, pl.BlockSpec((width, tile), lambda i, *_: (0, i)), HBM),
         grid=(rows // tile,),
         scalars=[pieces.cores],
@@ -623,7 +642,7 @@
         "outer",
         [u, n1, cot, vec] + list(pieces.buffers),
         [pl.BlockSpec((tile, depth), lambda i, *_: (i, 0)), tok, tok, whole(vec.shape)] + [ANY] * count,
-        (like((rows, width)), like((rows, width), F32), like((rows, width)), like((width, rows)), like((8, width), F32), like((depth, width))),
+        (far((rows, width)), far((rows, width), F32), far((rows, width)), like((width, rows)), like((8, width), F32), like((depth, width))),
         (tok, tok, tok, pl.BlockSpec((width, tile), lambda i, *_: (0, i)), whole((8, width)), HBM),
         grid=(rows // tile,),
         scalars=[pieces.cores],
@@ -739,7 +758,7 @@
         "join_back",
         [dz2, dh, n1, rstd, vec, w],
         [tok, tok, tok, pl.BlockSpec((tile, 1), lambda i: (i, 0)), whole(vec.shape), whole(w.shape)],
-        (like((rows, width), F32), like((rows, width)), like((rows, width)), like((8, width), F32)),
+        (far((rows, width), F32), far((rows, width)), far((rows, width)), like((8, width), F32)),
         (tok, tok, tok, whole((8, width))),
         grid=(rows // tile,),
         after=after,
@@ -1075,19 +1094,26 @@
     vectors = [((sq0, sq1), 0), ((sv0, sv1), 0)] + [((sums,), i) for sums in (sums1, sums2) for i in range(3)] + [((sum_inner,), 0)]
     other, own = token_weights_grad(halves, xt, d1, groups, vectors=vectors)
     for _ in middle:
-        other, got_wouter = step(*firsts, carry=[other, got_wouter])
-    got_wouter = spread(got_wouter)
+        (other,) = step(*firsts, carry=[other])
     seconds = reduction(other, own, xyz, yxz, runs=((0, 2 * cols // 3), (2 * cols // 3, cols // 3)))
     cores = layout.core[2]
     order = [r % cores * (layout.replicas // cores) + r // cores for r in range(layout.replicas)]
     step(*seconds)
     (first_sums,) = across_z(firsts)
+    together = got_wouter.shape[0] == got_winner.shape[0]
+    if together:
+        (got,) = pack([got_wouter, got_winner], [[(0, 0, got_wouter.shape[1]), (1, 0, got_winner.shape[1])]])
+        got = spread(got)
+    else:
+        got_wouter, got_winner = spread(got_wouter), spread(got_winner)
     grad_tokens = token_grad(partial, d1, wqkv1, BF16)
     for _ in middle:
-        (got_winner,) = step(*seconds, after=first_sums[1:], carry=[got_winner])
-    got_winner = spread(got_winner)
+        step(*seconds, after=first_sums[1:])
     (second_sums,) = across_z(seconds)
-    grad_wouter = outer_result(got_wouter, order)
+    if together:
+        grad_wouter, grad_winner = wide_results(got, order)
+    else:
+        grad_wouter, grad_winner = outer_result(got_wouter, order), inner_result(got_winner, order)
     got = [add_up([first_sums, second_sums])]
     places = jnp.zeros((1,), jnp.int32)
     weight = 1
@@ -1096,7 +1122,6 @@
         places = jnp.concatenate([places + own * weight, places + (1 - own) * weight])
         got = got + [layout.send(g, digit) for g in got]
         weight *= digit[2]
-    grad_winner = inner_result(got_winner, order)
     keep = width // groups
     wq, wk, wv, grad_wout, sums = token_weights_result(got, places, keep, half // 4, width // 4)
     bq, bv, bout, gain1, shift1, bouter, gain2, shift2 = (sums[i, :keep] for i in range(8))

time: 436 us -> 434 us (level)
  Pallas kernels: 233 us -> 244 us
  local copies, waits for them, and re-layouts: 46 us -> 35.3 us
  waiting for transfers between devices: 88.5 us -> 82.8 us
    pallas_call x44, Pallas kernels: 233 us -> 244 us  [call(): pl.pallas_call(body, out_shape=shapes + [jax.ShapeDtypeStruct(c.shape, c....]
    unnamed x170 -> x132, local copies, waits for them, and re-layouts: 43.9 us -> 33.1 us
    ppermute x56, waiting for transfers between devices: 88.3 us -> 82.7 us  [send(): return lax.ppermute(value, axis, pairs)]
  transfers between devices with their start and end apart: 61 -> 60, of which waited for: 27 -> 25; matrix products, arithmetic and copies ran while one was open for 1% -> 1% of each run, Pallas kernels for 44% -> 45%
where the time goes in v5:
time: 434 us; the launch traced here: 428 us
  Pallas kernels  244 us (56%)
  waiting for transfers between devices  82.8 us (19%)
  starting transfers between devices  49.9 us (11%)
  local copies, waits for them, and re-layouts  35.3 us (8%)
  between operations  14.9 us (3%)
    pallas_call x44, Pallas kernels, call(): pl.pallas_call(body, out_shape=shapes + [jax.ShapeDtypeStruct(c.shape, c....  244 us
    ppermute x56, waiting for transfers between devices, send(): return lax.ppermute(value, axis, pairs)  82.7 us
    ppermute x56, starting transfers between devices, send(): return lax.ppermute(value, axis, pairs)  49.8 us
    unnamed x132, local copies, waits for them, and re-layouts  33.1 us
  transfers between devices with their start and end apart: 60, of which 25 were waited for; matrix products, arithmetic and copies ran while one was open for 1% of the time, Pallas kernels for 45%

profile of v5, /device:TPU:9, one launch (start us, length us, event | category | flops | bytes accessed | tf_op | source)
XLA Modules:
  0.0 428.0 jit_solution(16422024766955441887)
XLA Ops:
  14.9 2.2 transposed.1
  19.0 2.7 collective-permute-done.2.refs_5_.refs_9_
  27.2 4.4 %collective-permute-done.3.refs_3_ = bf16[4,32,768]{2,1,0:T(8,128)(2,1)S(1)} collective-permute-done((bf16[4,32,768]{2,1,0:T(8,128)(2,1)S(1)}, bf16[4,32,768]{2,1,0:T(8,128)(2,1)S(1)}, u32[]{:S(2)}, u32[]{:S(2)}) %collective-permute-start.3) | collective-permute-done | bytes 196640 | tf_op jit(solution)/shard_map/ppermute | solution.py:900
  38.3 4.8 %collective-permute-done.7.refs_9_.refs_13_ = bf16[32,2560]{1,0:T(8,128)(2,1)S(1)} collective-permute-done((bf16[32,2560]{1,0:T(8,128)(2,1)S(1)}, bf16[32,2560]{1,0:T(8,128)(2,1)S(1)}, u32[]{:S(2)}, u32[]{:S(2)}) %collective-permute-start.7) | collective-permute-done | bytes 163872 | tf_op jit(solution)/shard_map/ppermute | solution.py:900
  43.2 9.8 %collective-permute-done.8.refs_10_.refs_14_ = bf16[32,2560]{1,0:T(8,128)(2,1)S(1)} collective-permute-done((bf16[32,2560]{1,0:T(8,128)(2,1)S(1)}, bf16[32,2560]{1,0:T(8,128)(2,1)S(1)}, u32[]{:S(2)}, u32[]{:S(2)}) %collective-permute-start.8) | collective-permute-done | bytes 163872 | tf_op jit(solution)/shard_map/ppermute | solution.py:900
  53.0 3.9 collective-permute-done.9.refs_11_.refs_15_
  66.3 7.1 %project.2 = (bf16[1024,1536]{1,0:T(8,128)(2,1)}, bf16[1024,1536]{1,0:T(8,128)(2,1)}, bf16[128,1024]{1,0:T(8,128)(2,1)S(1)}, f32[8,128]{1,0:T(8,128)S(1)}) custom-call(s32[2]{0:T(128)S(1)} %pad_add_fusion.refs_0_, bf16[1024,1024]{1,0:T(8,128)(2,1)S(1)} %copy-done.29, f32[8,1024]{1,0:T(8,128)S(1)} %stack.40.refs_2_.refs_4_, ...), custom_call_target="tpu_custom_call", output_to_operand_aliasing={{2}: (7, {})} | custom-call | flops 6000000000 | bytes 6000001 | tf_op jit(solution)/shard_map/project/pallas_call | solution.py:40
  80.3 11.6 %attend.2 = (bf16[1024,512]{1,0:T(8,128)(2,1)S(1)}, bf16[512,1024]{1,0:T(8,128)(2,1)S(1)}, bf16[2,8,512,512]{3,2,1,0:T(8,128)(2,1)}, f32[2,2,4,512]{3,2,1,0:T(4,128)S(1)}, f32[8,128]{1,0:T(8,128)S(1)}) custom-call(bf16[1024,1536]{1,0:T(8,128)(2,1)S(1)} %copy-done.48, bf16[1024,1536]{1,0:T(8,128)(2,1)S(1)} %copy-done.48, bf16[1024,1536]{1,0:T(8,128)(2,1)S(1)} %copy-done.48, ...), custom_call_target="tpu_custom_call" | custom-call | flops 11000000512 | bytes 11000001 | tf_op jit(solution)/shard_map/attend/pallas_call | solution.py:40
  91.9 14.4 %collective-permute-done.17.refs_10_.refs_14_ = bf16[128,1024]{1,0:T(8,128)(2,1)S(1)} collective-permute-done((bf16[128,1024]{1,0:T(8,128)(2,1)S(1)}, bf16[128,1024]{1,0:T(8,128)(2,1)S(1)}, u32[]{:S(2)}, u32[]{:S(2)}) %collective-permute-start.17) | collective-permute-done | bytes 262176 | tf_op jit(solution)/shard_map/ppermute | solution.py:900
  106.3 4.4 %collective-permute-done.18.refs_11_.refs_15_ = bf16[128,1024]{1,0:T(8,128)(2,1)S(1)} collective-permute-done((bf16[128,1024]{1,0:T(8,128)(2,1)S(1)}, bf16[128,1024]{1,0:T(8,128)(2,1)S(1)}, u32[]{:S(2)}, u32[]{:S(2)}) %collective-permute-start.18) | collective-permute-done | bytes 262176 | tf_op jit(solution)/shard_map/ppermute | solution.py:900
  112.2 2.5 collective-permute-done.19
  116.6 5.7 %project.3 = (bf16[1024,1536]{1,0:T(8,128)(2,1)}, bf16[1024,1536]{1,0:T(8,128)(2,1)}, f32[8,128]{1,0:T(8,128)S(1)}) custom-call(s32[2]{0:T(128)S(1)} %pad_add_fusion.refs_0_, bf16[1024,1024]{1,0:T(8,128)(2,1)S(1)} %copy-done.30, f32[8,1024]{1,0:T(8,128)S(1)} %stack.40.refs_2_.refs_4_, bf16[2,256,1280]{2,1,0:T(8,128)(2,1)S(1)} %bitcast.169, ...), custom_call_target="tpu_custom_call" | custom-call | flops 6000000000 | bytes 6000001 | tf_op jit(solution)/shard_map/project/pallas_call | solution.py:40
  124.3 11.6 %attend.3 = (bf16[1024,512]{1,0:T(8,128)(2,1)S(1)}, bf16[512,1024]{1,0:T(8,128)(2,1)S(1)}, bf16[2,8,512,512]{3,2,1,0:T(8,128)(2,1)}, f32[2,2,4,512]{3,2,1,0:T(4,128)S(1)}, f32[8,128]{1,0:T(8,128)S(1)}) custom-call(bf16[1024,1536]{1,0:T(8,128)(2,1)S(1)} %copy-done.46, bf16[1024,1536]{1,0:T(8,128)(2,1)S(1)} %copy-done.46, bf16[1024,1536]{1,0:T(8,128)(2,1)S(1)} %copy-done.46, ...), custom_call_target="tpu_custom_call" | custom-call | flops 11000000512 | bytes 11000001 | tf_op jit(solution)/shard_map/attend/pallas_call | solution.py:40
  136.8 7.9 %join.1 = (f32[1024,1024]{1,0:T(8,128)}, f32[1024,1]{1,0:T(8,128)}, bf16[1024,1024]{1,0:T(8,128)(2,1)S(1)}, bf16[1024,1024]{1,0:T(8,128)(2,1)}, bf16[1024,1024]{1,0:T(8,128)(2,1)}, /*index=5*/f32[8,128]{1,0:T(8,128)S(1)}) custom-call(s32[2]{0:T(128)S(1)} %pad_add_fusion.refs_0_, bf16[1024,512]{1,0:T(8,128)(2,1)S(1)} %get-tuple-element.209.refs_1_, ...), custom_call_target="tpu_custom_call" | custom-call | flops 7000000000 | bytes 7000001 | tf_op jit(solution)/shard_map/join/pallas_call | solution.py:40
  147.6 10.3 %inner.2 = (bf16[1024,4096]{1,0:T(8,128)(2,1)}, bf16[1024,4096]{1,0:T(8,128)(2,1)}, f32[8,128]{1,0:T(8,128)S(1)}) custom-call(bf16[1024,1024]{1,0:T(8,128)(2,1)S(1)} %copy-done.38, bf16[1024,4096]{1,0:T(8,128)(2,1)} %all-gather.4.cloned.1.call-done.refs_1_.refs_5_, f32[1,4096]{1,0:T(1,128)S(1)} %bitcast.159, f32[8,128]{1,0:T(8,128)S(1)} %get-tuple-element.226.refs_3_), custom_call_target="tpu_custom_call" | custom-call | flops 9000000512 | bytes 9000001 | tf_op jit(solution)/shard_map/inner/pallas_call | solution.py:40
  157.9 2.7 collective-permute-done.23.refs_3_
  163.6 10.4 %inner.3 = (bf16[1024,4096]{1,0:T(8,128)(2,1)}, bf16[1024,4096]{1,0:T(8,128)(2,1)}, f32[8,128]{1,0:T(8,128)S(1)}) custom-call(bf16[1024,1024]{1,0:T(8,128)(2,1)S(1)} %copy-done.38, bf16[1024,4096]{1,0:T(8,128)(2,1)} %all-gather.4.cloned.1.call-done.refs_1_.refs_5_, f32[1,4096]{1,0:T(1,128)S(1)} %bitcast.160, ...), custom_call_target="tpu_custom_call", output_to_operand_aliasing={{0}: (3, {}), {1}: (4, {})} | custom-call | flops 9000000512 | bytes 9000001 | tf_op jit(solution)/shard_map/inner/pallas_call | solution.py:40
  176.1 20.3 %outer.1 = (bf16[1024,1024]{1,0:T(8,128)(2,1)}, f32[1024,1024]{1,0:T(8,128)}, bf16[1024,1024]{1,0:T(8,128)(2,1)}, bf16[1024,1024]{1,0:T(8,128)(2,1)S(1)}, f32[8,...) custom-call(s32[2]{0:T(128)S(1)} %pad_add_fusion.refs_0_, ...), custom_call_target="tpu_custom_call" | custom-call | flops 19000000512 | bytes 19000000 | tf_op jit(solution)/shard_map/outer/pallas_call | solution.py:40
  196.4 7.2 %outer_grad.2 = (bf16[2,8,256,512]{3,2,1,0:T(8,128)(2,1)S(1)}, f32[8,128]{1,0:T(8,128)S(1)}) custom-call(s32[1]{0:T(128)} %bitcast.1.refs_0_, bf16[1024,1024]{1,0:T(8,128)(2,1)S(1)} %get-tuple-element.244.refs_1_, bf16[1024,4096]{1,0:T(8,128)(2,1)} %get-tuple-element.233.refs_1_.refs_2_, f32[8,128]{1,0:T(8,128)S(1)} %get-tuple-element.245.refs_3_), custom_call_target="tpu_custom_call" | custom-call | flops 6000000000 | bytes 6000001 | tf_op jit(solution)/shard_map/outer_grad/pallas_call | solution.py:40
  204.2 7.1 %outer_grad.3 = (bf16[2,8,256,512]{3,2,1,0:T(8,128)(2,1)S(1)}, f32[8,128]{1,0:T(8,128)S(1)}) custom-call(s32[1]{0:T(128)} %bitcast.refs_0_, bf16[1024,1024]{1,0:T(8,128)(2,1)S(1)} %get-tuple-element.244.refs_1_, bf16[1024,4096]{1,0:T(8,128)(2,1)} %get-tuple-element.233.refs_1_.refs_2_, f32[8,128]{1,0:T(8,128)S(1)} %get-tuple-element.246.refs_3_), custom_call_target="tpu_custom_call" | custom-call | flops 6000000000 | bytes 6000001 | tf_op jit(solution)/shard_map/outer_grad/pallas_call | solution.py:40
  211.4 5.1 %combine.8 = (bf16[1,8,128,512]{3,2,1,0:T(8,128)(2,1)}, bf16[1,8,128,512]{3,2,1,0:T(8,128)(2,1)}, bf16[8,1,128,512]{3,2,1,0:T(8,128)(2,1)}, bf16[8,1,128,512]{3,2,1,0:T(8,128)(2,1)}, f32[8,128]{1,0:T(8,128)S(1)}) custom-call(s32[1]{0:T(128)} %bitcast.3.refs_0_.refs_1_, s32[1]{0:T(128)} %bitcast.2.refs_1_.refs_0_, bf16[1,2,8,256,512]{4,3,2,1,0:T(8,128)(2,1)S(1)} %bitcast.118, ...), custom_call_target="tpu_custom_call" | custom-call | flops 1 | bytes 1 | tf_op jit(solution)/shard_map/combine/pallas_call | solution.py:40
  217.8 35.9 %inner_back.1 = (bf16[2,8,128,1024]{3,2,1,0:T(8,128)(2,1)}, bf16[2,8,128,1024]{3,2,1,0:T(8,128)(2,1)}, f32[1024,1024]{1,0:T(8,128)}, f32[1,4096]{1,0:T(1,128)S(1)}, f32[8,128]{1,0:T(8,128)S(1)}) custom-call(s32[2]{0:T(128)S(1)} %pad_add_fusion.1.refs_0_, bf16[1024,1024]{1,0:T(8,128)(2,1)S(1)} %copy-done.62, bf16[4096,1024]{1,0:T(8,128)(2,1)} %get-tuple-element.241.refs_2_, ...), custom_call_target="tpu_custom_call" | custom-call | flops 35000000512 | bytes 35000000 | tf_op jit(solution)/shard_map/inner_back/pallas_call | solution.py:40
  253.8 2.8 combine.9
  258.9 2.2 copy-done.45
  261.1 9.2 %join_back.1 = (f32[1024,1024]{1,0:T(8,128)}, bf16[1024,1024]{1,0:T(8,128)(2,1)}, bf16[1024,1024]{1,0:T(8,128)(2,1)}, f32[8,1024]{1,0:T(8,128)S(1)}, f32[8,128]{1,0:T(8,128)S(1)}) custom-call(f32[1024,1024]{1,0:T(8,128)S(1)} %copy-done.45, f32[1024,1024]{1,0:T(8,128)} %get-tuple-element.251.refs_1_, f32[1024,1024]{1,0:T(8,128)} %get-tuple-element.234.refs_2_, ...), custom_call_target="tpu_custom_call" | custom-call | flops 8000000000 | bytes 8000001 | tf_op jit(solution)/shard_map/join_back/pallas_call | solution.py:40
  272.4 4.9 %combine.10 = (bf16[1,8,128,512]{3,2,1,0:T(8,128)(2,1)}, bf16[1,8,128,512]{3,2,1,0:T(8,128)(2,1)}, bf16[8,1,128,512]{3,2,1,0:T(8,128)(2,1)}, bf16[8,1,128,512]{3,2,1,0:T(8,128)(2,1)}, f32[8,128]{1,0:T(8,128)S(1)}) custom-call(s32[1]{0:T(128)} %bitcast.3.refs_0_.refs_1_, s32[1]{0:T(128)} %bitcast.2.refs_1_.refs_0_, ...), custom_call_target="tpu_custom_call" | custom-call | flops 1 | bytes 1 | tf_op jit(solution)/shard_map/combine/pallas_call | solution.py:40
  279.9 11.8 %attend_back.2 = (bf16[3,1024,512]{2,1,0:T(8,128)(2,1)}, f32[2,1,512]{2,1,0:T(1,128)S(1)}, f32[2,1,512]{2,1,0:T(1,128)S(1)}, f32[8,128]{1,0:T(8,128)S(1)}) custom-call(bf16[1024,1536]{1,0:T(8,128)(2,1)S(1)} %copy-done.49, bf16[1024,1536]{1,0:T(8,128)(2,1)S(1)} %copy-done.49, bf16[1024,1536]{1,0:T(8,128)(2,1)S(1)} %copy-done.49, ...), custom_call_target="tpu_custom_call" | custom-call | flops 11000000512 | bytes 11000001 | tf_op jit(solution)/shard_map/attend_back/pallas_call | solution.py:40
  291.8 10.5 %token_weights_grad.2 = (bf16[2,8,128,768]{3,2,1,0:T(8,128)(2,1)}, bf16[2,8,128,768]{3,2,1,0:T(8,128)(2,1)}, f32[8,128]{1,0:T(8,128)S(1)}) custom-call(s32[2]{0:T(128)S(1)} %pad_add_fusion.1.refs_0_, bf16[1024,1024]{1,0:T(8,128)(2,1)S(1)} %copy-done.39, bf16[3,1024,512]{2,1,0:T(8,128)(2,1)} %get-tuple-element.275.refs_2_.refs_1_, ...), custom_call_target="tpu_custom_call" | custom-call | flops 8000000000 | bytes 8000001 | tf_op jit(solution)/shard_map/token_weights_grad/pallas_call | solution.py:40
  302.4 2.6 combine.11
  305.0 2.1 collective-permute-start.35
  311.3 12.0 %attend_back.3 = (bf16[3,1024,512]{2,1,0:T(8,128)(2,1)}, f32[2,1,512]{2,1,0:T(1,128)S(1)}, f32[2,1,512]{2,1,0:T(1,128)S(1)}, f32[8,128]{1,0:T(8,128)S(1)}) custom-call(bf16[1024,1536]{1,0:T(8,128)(2,1)S(1)} %copy-done.47, bf16[1024,1536]{1,0:T(8,128)(2,1)S(1)} %copy-done.47, bf16[1024,1536]{1,0:T(8,128)(2,1)S(1)} %copy-done.47, ...), custom_call_target="tpu_custom_call" | custom-call | flops 11000000512 | bytes 11000001 | tf_op jit(solution)/shard_map/attend_back/pallas_call | solution.py:40
  325.5 4.3 %combine.12 = (bf16[1,8,128,384]{3,2,1,0:T(8,128)(2,1)}, bf16[1,8,128,384]{3,2,1,0:T(8,128)(2,1)}, bf16[8,1,128,256]{3,2,1,0:T(8,128)(2,1)}, bf16[8,1,128,256]{3,2,1,0:T(8,128)(2,1)}, f32[8,128]{1,0:T(8,128)S(1)}) custom-call(s32[1]{0:T(128)} %bitcast.3.refs_0_.refs_1_, s32[1]{0:T(128)} %bitcast.2.refs_1_.refs_0_, ...), custom_call_target="tpu_custom_call" | custom-call | flops 1 | bytes 1 | tf_op jit(solution)/shard_map/combine/pallas_call | solution.py:40
  331.6 7.1 %token_grad.2 = (f32[1024,1024]{1,0:T(8,128)}, f32[8,128]{1,0:T(8,128)S(1)}) custom-call(f32[1024,1024]{1,0:T(8,128)} %get-tuple-element.261.refs_0_, bf16[3,1024,512]{2,1,0:T(8,128)(2,1)S(1)} %copy-done.44, bf16[1024,1536]{1,0:T(8,128)(2,1)S(1)} %copy-done.42, f32[8,128]{1,0:T(8,128)S(1)} %get-tuple-element.298.refs_3_), custom_call_target="tpu_custom_call" | custom-call | flops 6000000000 | bytes 6000001 | tf_op jit(solution)/shard_map/token_grad/pallas_call | solution.py:40
  338.7 5.8 %token_weights_grad.3 = (bf16[2,8,144,384]{3,2,1,0:T(8,128)(2,1)S(1)}, bf16[2,8,144,384]{3,2,1,0:T(8,128)(2,1)S(1)}, f32[8,128]{1,0:T(8,128)S(1)}) custom-call(s32[2]{0:T(128)S(1)} %pad_add_fusion.1.refs_0_, bf16[1024,1024]{1,0:T(8,128)(2,1)S(1)} %copy-done.40, bf16[3,1024,512]{2,1,0:T(8,128)(2,1)} %get-tuple-element.300.refs_2_.refs_1_, ...), custom_call_target="tpu_custom_call" | custom-call | flops 8000000000 | bytes 8000001 | tf_op jit(solution)/shard_map/token_weights_grad/pallas_call | solution.py:40
  344.5 4.3 %collective-permute-done.38 = bf16[1,8,128,384]{3,2,1,0:T(8,128)(2,1)S(1)} collective-permute-done((bf16[1,8,128,384]{3,2,1,0:T(8,128)(2,1)}, bf16[1,8,128,384]{3,2,1,0:T(8,128)(2,1)S(1)}, u32[]{:S(2)}, u32[]{:S(2)}) %collective-permute-start.38) | collective-permute-done | bytes 786464 | tf_op jit(solution)/shard_map/ppermute | solution.py:900
  355.2 2.6 combine.14
  357.8 2.1 collective-permute-done.41
  360.0 2.9 collective-permute-done.40
  371.4 2.1 copy-done.41
  373.5 2.2 copy-done.43
  375.7 6.7 %token_grad.3 = (bf16[1024,1024]{1,0:T(8,128)(2,1)}, f32[8,128]{1,0:T(8,128)S(1)}) custom-call(f32[1024,1024]{1,0:T(8,128)} %get-tuple-element.299.refs_0_, bf16[3,1024,512]{2,1,0:T(8,128)(2,1)S(1)} %copy-done.43, bf16[1024,1536]{1,0:T(8,128)(2,1)S(1)} %copy-done.41, f32[8,128]{1,0:T(8,128)S(1)} %copy-done.35), custom_call_target="tpu_custom_call" | custom-call | flops 6000000000 | bytes 6000001 | tf_op jit(solution)/shard_map/token_grad/pallas_call | solution.py:40
  388.1 6.2 %collective-permute-done.49 = bf16[1,4,144,128]{3,2,1,0:T(8,128)(2,1)S(1)} collective-permute-done((bf16[1,4,144,128]{3,2,1,0:T(8,128)(2,1)}, bf16[1,4,144,128]{3,2,1,0:T(8,128)(2,1)S(1)}, u32[]{:S(2)}, u32[]{:S(2)}) %collective-permute-start.49) | collective-permute-done | bytes 147488 | tf_op jit(solution)/shard_map/ppermute | solution.py:900
  400.5 2.4 wide_results.1
  402.9 4.0 collective-permute-done.52.refs_7_
  408.0 2.7 collective-permute-start.54
  410.7 3.0 collective-permute-done.53.refs_2_
  413.7 2.8 collective-permute-start.55
  417.8 2.1 token_weights_result.1
  (275 shorter events, 99.5 us)
Async XLA Ops:
  7.2 138.9 %all-gather.4.cloned.1.call-start = ((), (), s32[]{:S(2)}) async-start(), calls=%async_computation.2 | async-start | bytes 8650752 | tf_op jit(solution)/shard_map/all_gather | solution.py:1012
  8.9 8.2 %collective-permute-start = (bf16[32,1664]{1,0:T(8,128)(2,1)}, bf16[32,1664]{1,0:T(8,128)(2,1)S(1)}, u32[]{:S(2)}, u32[]{:S(2)}) collective-permute-start(bf16[32,1664]{1,0:T(8,128)(2,1)} %get-tuple-element.188.refs_2_.refs_6_), channel_id=1, source_target_pairs={{0,2},{1,3},{2,4},{3,5},{4,6},{5,7},{6,0},{7,1},{8,10},{9,11},{10,... | collective-permute-start | bytes 319496 | tf_op jit(solution)/shard_map/ppermute | solution.py:900
  10.2 8.8 %collective-permute-start.1 = (bf16[32,1664]{1,0:T(8,128)(2,1)}, bf16[32,1664]{1,0:T(8,128)(2,1)S(1)}, u32[]{:S(2)}, u32[]{:S(2)}) collective-permute-start(bf16[32,1664]{1,0:T(8,128)(2,1)} %get-tuple-element.188.refs_2_.refs_6_), channel_id=1, source_target_pairs={{0,4},{1,5},{2,6},{3,7},{4,0},{5,1},{6,2},{7,3},{8,12},{9,13},{10,... | collective-permute-start | bytes 319496 | tf_op jit(solution)/shard_map/ppermute | solution.py:900
  11.2 10.5 %collective-permute-start.2 = (bf16[32,1664]{1,0:T(8,128)(2,1)}, bf16[32,1664]{1,0:T(8,128)(2,1)S(1)}, u32[]{:S(2)}, u32[]{:S(2)}) collective-permute-start(bf16[32,1664]{1,0:T(8,128)(2,1)} %get-tuple-element.188.refs_2_.refs_6_), channel_id=1, source_target_pairs={{0,6},{1,7},{2,0},{3,1},{4,2},{5,3},{6,4},{7,5},{8,14},{9,15},{10,... | collective-permute-start | bytes 319496 | tf_op jit(solution)/shard_map/ppermute | solution.py:900
  24.6 339.2 %reduce-scatter.3.cloned.1.call-start = ((), (), s32[]{:S(2)}) async-start(), calls=%async_computation.3 | async-start | bytes 1310720 | tf_op jit(solution)/shard_map/reduce_scatter | solution.py:1063
  33.9 23.0 %collective-permute-start.6 = (bf16[4,2,32,896]{3,2,1,0:T(8,128)(2,1)S(1)}, bf16[4,2,32,896]{3,2,1,0:T(8,128)(2,1)S(1)}, u32[]{:S(2)}, u32[]{:S(2)}) collective-permute-start(bf16[4,2,32,896]{3,2,1,0:T(8,128)(2,1)S(1)} %get-tuple-element.197.refs_6_), channel_id=1, source_target_pairs={{0,16},{8,24},{16,0},{24,8},{1,17},{9,25},{17,1},{25,9},{2,18},{10... | collective-permute-start | bytes 1376264 | tf_op jit(solution)/shard_map/ppermute | solution.py:900
  35.2 21.7 %collective-permute-start.5 = (bf16[2,4,32,768]{3,2,1,0:T(8,128)(2,1)S(1)}, bf16[2,4,32,768]{3,2,1,0:T(8,128)(2,1)S(1)}, u32[]{:S(2)}, u32[]{:S(2)}) collective-permute-start(bf16[2,4,32,768]{3,2,1,0:T(8,128)(2,1)S(1)} %get-tuple-element.196.refs_4_), channel_id=1, source_target_pairs={{0,1},{1,0},{2,3},{3,2},{4,5},{5,4},{6,7},{7,6},{8,9},{9,8},{10,11... | collective-permute-start | bytes 1179656 | tf_op jit(solution)/shard_map/ppermute | solution.py:900
  36.2 16.8 %collective-permute-start.8 = (bf16[32,2560]{1,0:T(8,128)(2,1)S(1)}, bf16[32,2560]{1,0:T(8,128)(2,1)S(1)}, u32[]{:S(2)}, u32[]{:S(2)}) collective-permute-start(bf16[32,2560]{1,0:T(8,128)(2,1)S(1)} %get-tuple-element.198.refs_8_.refs_12_), channel_id=1, source_target_pairs={{0,4},{1,5},{2,6},{3,7},{4,0},{5,1},{6,2},{7,3},{8,12},{9,13},{10,... | collective-permute-start | bytes 491528 | tf_op jit(solution)/shard_map/ppermute | solution.py:900
  37.1 19.8 %collective-permute-start.9 = (bf16[32,2560]{1,0:T(8,128)(2,1)S(1)}, bf16[32,2560]{1,0:T(8,128)(2,1)S(1)}, u32[]{:S(2)}, u32[]{:S(2)}) collective-permute-start(bf16[32,2560]{1,0:T(8,128)(2,1)S(1)} %get-tuple-element.198.refs_8_.refs_12_), channel_id=1, source_target_pairs={{0,6},{1,7},{2,0},{3,1},{4,2},{5,3},{6,4},{7,5},{8,14},{9,15},{10,... | collective-permute-start | bytes 491528 | tf_op jit(solution)/shard_map/ppermute | solution.py:900
  60.7 15.3 %collective-permute-start.12 = (bf16[4,32,1280]{2,1,0:T(8,128)(2,1)S(1)}, bf16[4,32,1280]{2,1,0:T(8,128)(2,1)S(1)}, u32[]{:S(2)}, u32[]{:S(2)}) collective-permute-start(bf16[4,32,1280]{2,1,0:T(8,128)(2,1)S(1)} %get-tuple-element.205.refs_2_), channel_id=1, source_target_pairs={{0,16},{8,24},{16,0},{24,8},{1,17},{9,25},{17,1},{25,9},{2,18},{10... | collective-permute-start | bytes 983048 | tf_op jit(solution)/shard_map/ppermute | solution.py:900
  61.4 14.6 %collective-permute-start.13 = (bf16[4,32,1280]{2,1,0:T(8,128)(2,1)S(1)}, bf16[4,32,1280]{2,1,0:T(8,128)(2,1)S(1)}, u32[]{:S(2)}, u32[]{:S(2)}) collective-permute-start(bf16[4,32,1280]{2,1,0:T(8,128)(2,1)S(1)} %get-tuple-element.206.refs_4_), channel_id=1, source_target_pairs={{0,1},{1,0},{2,3},{3,2},{4,5},{5,4},{6,7},{7,6},{8,9},{9,8},{10,11... | collective-permute-start | bytes 983048 | tf_op jit(solution)/shard_map/ppermute | solution.py:900
  73.4 18.5 %collective-permute-start.16 = (bf16[128,1024]{1,0:T(8,128)(2,1)S(1)}, bf16[128,1024]{1,0:T(8,128)(2,1)S(1)}, u32[]{:S(2)}, u32[]{:S(2)}) collective-permute-start(bf16[128,1024]{1,0:T(8,128)(2,1)S(1)} %get-tuple-element.212.refs_8_.refs_12_), channel_id=1, source_target_pairs={{0,2},{1,3},{2,4},{3,5},{4,6},{5,7},{6,0},{7,1},{8,10},{9,11},{10,... | collective-permute-start | bytes 786440 | tf_op jit(solution)/shard_map/ppermute | solution.py:900
  73.5 32.8 %collective-permute-start.17 = (bf16[128,1024]{1,0:T(8,128)(2,1)S(1)}, bf16[128,1024]{1,0:T(8,128)(2,1)S(1)}, u32[]{:S(2)}, u32[]{:S(2)}) collective-permute-start(bf16[128,1024]{1,0:T(8,128)(2,1)S(1)} %get-tuple-element.212.refs_8_.refs_12_), channel_id=1, source_target_pairs={{0,4},{1,5},{2,6},{3,7},{4,0},{5,1},{6,2},{7,3},{8,12},{9,13},{10,... | collective-permute-start | bytes 786440 | tf_op jit(solution)/shard_map/ppermute | solution.py:900
  74.2 36.6 %collective-permute-start.18 = (bf16[128,1024]{1,0:T(8,128)(2,1)S(1)}, bf16[128,1024]{1,0:T(8,128)(2,1)S(1)}, u32[]{:S(2)}, u32[]{:S(2)}) collective-permute-start(bf16[128,1024]{1,0:T(8,128)(2,1)S(1)} %get-tuple-element.212.refs_8_.refs_12_), channel_id=1, source_target_pairs={{0,6},{1,7},{2,0},{3,1},{4,2},{5,3},{6,4},{7,5},{8,14},{9,15},{10,... | collective-permute-start | bytes 786440 | tf_op jit(solution)/shard_map/ppermute | solution.py:900
  76.3 34.4 %collective-permute-start.14 = (bf16[2,4,32,1280]{3,2,1,0:T(8,128)(2,1)S(1)}, bf16[2,4,32,1280]{3,2,1,0:T(8,128)(2,1)S(1)}, u32[]{:S(2)}, u32[]{:S(2)}) collective-permute-start(bf16[2,4,32,1280]{3,2,1,0:T(8,128)(2,1)S(1)} %get-tuple-element.210.refs_4_), channel_id=1, source_target_pairs={{0,1},{1,0},{2,3},{3,2},{4,5},{5,4},{6,7},{7,6},{8,9},{9,8},{10,11... | collective-permute-start | bytes 1966088 | tf_op jit(solution)/shard_map/ppermute | solution.py:900
  77.2 33.5 %collective-permute-start.15 = (bf16[4,2,32,1280]{3,2,1,0:T(8,128)(2,1)S(1)}, bf16[4,2,32,1280]{3,2,1,0:T(8,128)(2,1)S(1)}, u32[]{:S(2)}, u32[]{:S(2)}) collective-permute-start(bf16[4,2,32,1280]{3,2,1,0:T(8,128)(2,1)S(1)} %get-tuple-element.211.refs_6_), channel_id=1, source_target_pairs={{0,16},{8,24},{16,0},{24,8},{1,17},{9,25},{17,1},{25,9},{2,18},{10... | collective-permute-start | bytes 1966088 | tf_op jit(solution)/shard_map/ppermute | solution.py:900
  112.2 23.7 %collective-permute-start.21 = (bf16[4,128,512]{2,1,0:T(8,128)(2,1)S(1)}, bf16[4,128,512]{2,1,0:T(8,128)(2,1)S(1)}, u32[]{:S(2)}, u32[]{:S(2)}) collective-permute-start(bf16[4,128,512]{2,1,0:T(8,128)(2,1)S(1)} %get-tuple-element.220.refs_2_), channel_id=1, source_target_pairs={{0,16},{8,24},{16,0},{24,8},{1,17},{9,25},{17,1},{25,9},{2,18},{10... | collective-permute-start | bytes 1572872 | tf_op jit(solution)/shard_map/ppermute | solution.py:900
  112.2 23.7 %collective-permute-start.22 = (bf16[4,128,512]{2,1,0:T(8,128)(2,1)S(1)}, bf16[4,128,512]{2,1,0:T(8,128)(2,1)S(1)}, u32[]{:S(2)}, u32[]{:S(2)}) collective-permute-start(bf16[4,128,512]{2,1,0:T(8,128)(2,1)S(1)} %get-tuple-element.221.refs_4_), channel_id=1, source_target_pairs={{0,1},{1,0},{2,3},{3,2},{4,5},{5,4},{6,7},{7,6},{8,9},{9,8},{10,11... | collective-permute-start | bytes 1572872 | tf_op jit(solution)/shard_map/ppermute | solution.py:900
  136.1 24.6 %collective-permute-start.23 = (bf16[2,4,128,512]{3,2,1,0:T(8,128)(2,1)S(1)}, bf16[2,4,128,512]{3,2,1,0:T(8,128)(2,1)S(1)}, u32[]{:S(2)}, u32[]{:S(2)}) collective-permute-start(bf16[2,4,128,512]{3,2,1,0:T(8,128)(2,1)S(1)} %get-tuple-element.229.refs_2_), channel_id=1, source_target_pairs={{0,1},{1,0},{2,3},{3,2},{4,5},{5,4},{6,7},{7,6},{8,9},{9,8},{10,11... | collective-permute-start | bytes 3145736 | tf_op jit(solution)/shard_map/ppermute | solution.py:900
  136.2 24.6 %collective-permute-start.24 = (bf16[4,2,128,512]{3,2,1,0:T(8,128)(2,1)S(1)}, bf16[4,2,128,512]{3,2,1,0:T(8,128)(2,1)}, u32[]{:S(2)}, u32[]{:S(2)}) collective-permute-start(bf16[4,2,128,512]{3,2,1,0:T(8,128)(2,1)S(1)} %get-tuple-element.230.refs_4_), channel_id=1, source_target_pairs={{0,16},{8,24},{16,0},{24,8},{1,17},{9,25},{17,1},{25,9},{2,18},{10... | collective-permute-start | bytes 3145736 | tf_op jit(solution)/shard_map/ppermute | solution.py:900
  162.2 11.7 %collective-permute-start.25 = (bf16[2,4,2,128,512]{4,3,2,1,0:T(8,128)(2,1)S(1)}, bf16[2,4,2,128,512]{4,3,2,1,0:T(8,128)(2,1)S(1)}, u32[]{:S(2)}, u32[]{:S(2)}) collective-permute-start(bf16[2,4,2,128,512]{4,3,2,1,0:T(8,128)(2,1)S(1)} %get-tuple-element.235), channel_id=1, source_target_pairs={{0,8},{8,0},{16,24},{24,16},{1,9},{9,1},{17,25},{25,17},{2,10},{10... | collective-permute-start | bytes 6291464 | tf_op jit(solution)/shard_map/ppermute | solution.py:900
  163.5 10.5 %collective-permute-start.26 = (bf16[2,4,2,128,512]{4,3,2,1,0:T(8,128)(2,1)S(1)}, bf16[2,4,2,128,512]{4,3,2,1,0:T(8,128)(2,1)S(1)}, u32[]{:S(2)}, u32[]{:S(2)}) collective-permute-start(bf16[2,4,2,128,512]{4,3,2,1,0:T(8,128)(2,1)S(1)} %get-tuple-element.236), channel_id=1, source_target_pairs={{0,8},{8,0},{16,24},{24,16},{1,9},{9,1},{17,25},{25,17},{2,10},{10... | collective-permute-start | bytes 6291464 | tf_op jit(solution)/shard_map/ppermute | solution.py:900
  203.6 7.8 %collective-permute-start.27 = (bf16[2,8,256,512]{3,2,1,0:T(8,128)(2,1)S(1)}, bf16[2,8,256,512]{3,2,1,0:T(8,128)(2,1)S(1)}, u32[]{:S(2)}, u32[]{:S(2)}) collective-permute-start(bf16[2,8,256,512]{3,2,1,0:T(8,128)(2,1)S(1)} %get-tuple-element.248), channel_id=1, source_target_pairs={{0,8},{8,0},{16,24},{24,16},{1,9},{9,1},{17,25},{25,17},{2,10},{10... | collective-permute-start | bytes 12582920 | tf_op jit(solution)/shard_map/ppermute | solution.py:900
  216.4 37.3 %collective-permute-start.28 = (bf16[1,8,128,512]{3,2,1,0:T(8,128)(2,1)}, bf16[1,8,128,512]{3,2,1,0:T(8,128)(2,1)S(1)}, u32[]{:S(2)}, u32[]{:S(2)}) collective-permute-start(bf16[1,8,128,512]{3,2,1,0:T(8,128)(2,1)} %get-tuple-element.255), channel_id=1, source_target_pairs={{0,16},{8,24},{16,0},{24,8},{1,17},{9,25},{17,1},{25,9},{2,18},{10... | collective-permute-start | bytes 3145736 | tf_op jit(solution)/shard_map/ppermute | solution.py:900
  216.4 37.3 %collective-permute-start.29 = (bf16[8,1,128,512]{3,2,1,0:T(8,128)(2,1)}, bf16[8,1,128,512]{3,2,1,0:T(8,128)(2,1)S(1)}, u32[]{:S(2)}, u32[]{:S(2)}) collective-permute-start(bf16[8,1,128,512]{3,2,1,0:T(8,128)(2,1)} %get-tuple-element.257), channel_id=1, source_target_pairs={{0,1},{1,0},{2,3},{3,2},{4,5},{5,4},{6,7},{7,6},{8,9},{9,8},{10,11... | collective-permute-start | bytes 3145736 | tf_op jit(solution)/shard_map/ppermute | solution.py:900
  256.7 15.7 %collective-permute-start.30 = (bf16[2,8,128,1024]{3,2,1,0:T(8,128)(2,1)}, bf16[2,8,128,1024]{3,2,1,0:T(8,128)(2,1)S(1)}, u32[]{:S(2)}, u32[]{:S(2)}) collective-permute-start(bf16[2,8,128,1024]{3,2,1,0:T(8,128)(2,1)} %get-tuple-element.267), channel_id=1, source_target_pairs={{0,8},{8,0},{16,24},{24,16},{1,9},{9,1},{17,25},{25,17},{2,10},{10... | collective-permute-start | bytes 12582920 | tf_op jit(solution)/shard_map/ppermute | solution.py:900
  257.3 13.7 %collective-permute-start.31 = (bf16[4,1,128,512]{3,2,1,0:T(8,128)(2,1)}, bf16[4,1,128,512]{3,2,1,0:T(8,128)(2,1)S(1)}, u32[]{:S(2)}, u32[]{:S(2)}) collective-permute-start(bf16[4,1,128,512]{3,2,1,0:T(8,128)(2,1)} %get-tuple-element.269), channel_id=1, source_target_pairs={{0,1},{1,0},{2,3},{3,2},{4,5},{5,4},{6,7},{7,6},{8,9},{9,8},{10,11... | collective-permute-start | bytes 1572872 | tf_op jit(solution)/shard_map/ppermute | solution.py:900
  257.5 13.6 %collective-permute-start.32 = (bf16[1,4,128,512]{3,2,1,0:T(8,128)(2,1)}, bf16[1,4,128,512]{3,2,1,0:T(8,128)(2,1)S(1)}, u32[]{:S(2)}, u32[]{:S(2)}) collective-permute-start(bf16[1,4,128,512]{3,2,1,0:T(8,128)(2,1)} %get-tuple-element.271), channel_id=1, source_target_pairs={{0,16},{8,24},{16,0},{24,8},{1,17},{9,25},{17,1},{25,9},{2,18},{10... | collective-permute-start | bytes 1572872 | tf_op jit(solution)/shard_map/ppermute | solution.py:900
  277.3 25.0 %collective-permute-start.33 = (bf16[1,8,128,512]{3,2,1,0:T(8,128)(2,1)}, bf16[1,8,128,512]{3,2,1,0:T(8,128)(2,1)S(1)}, u32[]{:S(2)}, u32[]{:S(2)}) collective-permute-start(bf16[1,8,128,512]{3,2,1,0:T(8,128)(2,1)} %get-tuple-element.283), channel_id=1, source_target_pairs={{0,16},{8,24},{16,0},{24,8},{1,17},{9,25},{17,1},{25,9},{2,18},{10... | collective-permute-start | bytes 3145736 | tf_op jit(solution)/shard_map/ppermute | solution.py:900
  278.7 23.7 %collective-permute-start.34 = (bf16[8,1,128,512]{3,2,1,0:T(8,128)(2,1)}, bf16[8,1,128,512]{3,2,1,0:T(8,128)(2,1)S(1)}, u32[]{:S(2)}, u32[]{:S(2)}) collective-permute-start(bf16[8,1,128,512]{3,2,1,0:T(8,128)(2,1)} %get-tuple-element.285), channel_id=1, source_target_pairs={{0,1},{1,0},{2,3},{3,2},{4,5},{5,4},{6,7},{7,6},{8,9},{9,8},{10,11... | collective-permute-start | bytes 3145736 | tf_op jit(solution)/shard_map/ppermute | solution.py:900
  305.0 19.6 %collective-permute-start.35 = (bf16[2,8,128,768]{3,2,1,0:T(8,128)(2,1)}, bf16[2,8,128,768]{3,2,1,0:T(8,128)(2,1)}, u32[]{:S(2)}, u32[]{:S(2)}) collective-permute-start(bf16[2,8,128,768]{3,2,1,0:T(8,128)(2,1)} %get-tuple-element.288), channel_id=1, source_target_pairs={{0,8},{8,0},{16,24},{24,16},{1,9},{9,1},{17,25},{25,17},{2,10},{10... | collective-permute-start | bytes 9437192 | tf_op jit(solution)/shard_map/ppermute | solution.py:900
  307.2 56.7 %reduce-scatter.5.cloned.1.call-start = ((), (), s32[]{:S(2)}) async-start(), calls=%async_computation.4 | async-start | bytes 1310720 | tf_op jit(solution)/shard_map/reduce_scatter | solution.py:1063
  307.2 16.1 %collective-permute-start.36 = (bf16[4,1,128,512]{3,2,1,0:T(8,128)(2,1)}, bf16[4,1,128,512]{3,2,1,0:T(8,128)(2,1)S(1)}, u32[]{:S(2)}, u32[]{:S(2)}) collective-permute-start(bf16[4,1,128,512]{3,2,1,0:T(8,128)(2,1)} %get-tuple-element.290), channel_id=1, source_target_pairs={{0,1},{1,0},{2,3},{3,2},{4,5},{5,4},{6,7},{7,6},{8,9},{9,8},{10,11... | collective-permute-start | bytes 1572872 | tf_op jit(solution)/shard_map/ppermute | solution.py:900
  308.4 14.9 %collective-permute-start.37 = (bf16[1,4,128,512]{3,2,1,0:T(8,128)(2,1)}, bf16[1,4,128,512]{3,2,1,0:T(8,128)(2,1)S(1)}, u32[]{:S(2)}, u32[]{:S(2)}) collective-permute-start(bf16[1,4,128,512]{3,2,1,0:T(8,128)(2,1)} %get-tuple-element.292), channel_id=1, source_target_pairs={{0,16},{8,24},{16,0},{24,8},{1,17},{9,25},{17,1},{25,9},{2,18},{10... | collective-permute-start | bytes 1572872 | tf_op jit(solution)/shard_map/ppermute | solution.py:900
  324.5 74.4 %all-gather.6.cloned.1.call-start = ((), (), s32[]{:S(2)}) async-start(), calls=%async_computation.5 | async-start | bytes 2621440 | tf_op jit(solution)/shard_map/all_gather | solution.py:1071
  329.9 18.9 %collective-permute-start.38 = (bf16[1,8,128,384]{3,2,1,0:T(8,128)(2,1)}, bf16[1,8,128,384]{3,2,1,0:T(8,128)(2,1)S(1)}, u32[]{:S(2)}, u32[]{:S(2)}) collective-permute-start(bf16[1,8,128,384]{3,2,1,0:T(8,128)(2,1)} %get-tuple-element.305), channel_id=1, source_target_pairs={{0,16},{8,24},{16,0},{24,8},{1,17},{9,25},{17,1},{25,9},{2,18},{10... | collective-permute-start | bytes 2359304 | tf_op jit(solution)/shard_map/ppermute | solution.py:900
  331.3 13.2 %collective-permute-start.39 = (bf16[8,1,128,256]{3,2,1,0:T(8,128)(2,1)}, bf16[8,1,128,256]{3,2,1,0:T(8,128)(2,1)S(1)}, u32[]{:S(2)}, u32[]{:S(2)}) collective-permute-start(bf16[8,1,128,256]{3,2,1,0:T(8,128)(2,1)} %get-tuple-element.307), channel_id=1, source_target_pairs={{0,1},{1,0},{2,3},{3,2},{4,5},{5,4},{6,7},{7,6},{8,9},{9,8},{10,11... | collective-permute-start | bytes 1572872 | tf_op jit(solution)/shard_map/ppermute | solution.py:900
  351.9 11.0 %collective-permute-start.40 = (bf16[4,1,128,384]{3,2,0,1:T(8,128)(2,1)}, bf16[4,1,128,384]{3,2,0,1:T(8,128)(2,1)S(1)}, u32[]{:S(2)}, u32[]{:S(2)}) collective-permute-start(bf16[4,1,128,384]{3,2,0,1:T(8,128)(2,1)} %bitcast.176), channel_id=1, source_target_pairs={{0,1},{1,0},{2,3},{3,2},{4,5},{5,4},{6,7},{7,6},{8,9},{9,8},{10,11... | collective-permute-start | bytes 1179656 | tf_op jit(solution)/shard_map/ppermute | solution.py:900
  352.1 7.8 %collective-permute-start.41 = (bf16[1,4,128,256]{3,2,1,0:T(8,128)(2,1)}, bf16[1,4,128,256]{3,2,1,0:T(8,128)(2,1)S(1)}, u32[]{:S(2)}, u32[]{:S(2)}) collective-permute-start(bf16[1,4,128,256]{3,2,1,0:T(8,128)(2,1)} %get-tuple-element.321), channel_id=1, source_target_pairs={{0,16},{8,24},{16,0},{24,8},{1,17},{9,25},{17,1},{25,9},{2,18},{10... | collective-permute-start | bytes 786440 | tf_op jit(solution)/shard_map/ppermute | solution.py:900
  365.7 18.8 %collective-permute-start.46 = (bf16[1,8,144,256]{3,2,1,0:T(8,128)(2,1)}, bf16[1,8,144,256]{3,2,1,0:T(8,128)(2,1)S(1)}, u32[]{:S(2)}, u32[]{:S(2)}) collective-permute-start(bf16[1,8,144,256]{3,2,1,0:T(8,128)(2,1)} %get-tuple-element.334), channel_id=1, source_target_pairs={{0,16},{8,24},{16,0},{24,8},{1,17},{9,25},{17,1},{25,9},{2,18},{10... | collective-permute-start | bytes 1769480 | tf_op jit(solution)/shard_map/ppermute | solution.py:900
  367.2 15.3 %collective-permute-start.43 = (bf16[128,640]{1,0:T(8,128)(2,1)S(1)}, bf16[128,640]{1,0:T(8,128)(2,1)S(1)}, u32[]{:S(2)}, u32[]{:S(2)}) collective-permute-start(bf16[128,640]{1,0:T(8,128)(2,1)S(1)} %get-tuple-element.330), channel_id=1, source_target_pairs={{0,2},{1,3},{2,4},{3,5},{4,6},{5,7},{6,0},{7,1},{8,10},{9,11},{10,... | collective-permute-start | bytes 491528 | tf_op jit(solution)/shard_map/ppermute | solution.py:900
  367.2 15.3 %collective-permute-start.44 = (bf16[128,640]{1,0:T(8,128)(2,1)S(1)}, bf16[128,640]{1,0:T(8,128)(2,1)S(1)}, u32[]{:S(2)}, u32[]{:S(2)}) collective-permute-start(bf16[128,640]{1,0:T(8,128)(2,1)S(1)} %get-tuple-element.331), channel_id=1, source_target_pairs={{0,4},{1,5},{2,6},{3,7},{4,0},{5,1},{6,2},{7,3},{8,12},{9,13},{10,... | collective-permute-start | bytes 491528 | tf_op jit(solution)/shard_map/ppermute | solution.py:900
  368.2 15.3 %collective-permute-start.45 = (bf16[128,640]{1,0:T(8,128)(2,1)S(1)}, bf16[128,640]{1,0:T(8,128)(2,1)S(1)}, u32[]{:S(2)}, u32[]{:S(2)}) collective-permute-start(bf16[128,640]{1,0:T(8,128)(2,1)S(1)} %get-tuple-element.332), channel_id=1, source_target_pairs={{0,6},{1,7},{2,0},{3,1},{4,2},{5,3},{6,4},{7,5},{8,14},{9,15},{10,... | collective-permute-start | bytes 491528 | tf_op jit(solution)/shard_map/ppermute | solution.py:900
  369.6 13.8 %collective-permute-start.47 = (bf16[8,1,144,128]{3,2,1,0:T(8,128)(2,1)}, bf16[8,1,144,128]{3,2,1,0:T(8,128)(2,1)S(1)}, u32[]{:S(2)}, u32[]{:S(2)}) collective-permute-start(bf16[8,1,144,128]{3,2,1,0:T(8,128)(2,1)} %get-tuple-element.336), channel_id=1, source_target_pairs={{0,1},{1,0},{2,3},{3,2},{4,5},{5,4},{6,7},{7,6},{8,9},{9,8},{10,11... | collective-permute-start | bytes 884744 | tf_op jit(solution)/shard_map/ppermute | solution.py:900
  385.9 8.4 %collective-permute-start.48 = (bf16[4,1,144,256]{3,2,0,1:T(8,128)(2,1)}, bf16[4,1,144,256]{3,2,0,1:T(8,128)(2,1)S(1)}, u32[]{:S(2)}, u32[]{:S(2)}) collective-permute-start(bf16[4,1,144,256]{3,2,0,1:T(8,128)(2,1)} %bitcast.177), channel_id=1, source_target_pairs={{0,1},{1,0},{2,3},{3,2},{4,5},{5,4},{6,7},{7,6},{8,9},{9,8},{10,11... | collective-permute-start | bytes 884744 | tf_op jit(solution)/shard_map/ppermute | solution.py:900
  386.1 8.2 %collective-permute-start.49 = (bf16[1,4,144,128]{3,2,1,0:T(8,128)(2,1)}, bf16[1,4,144,128]{3,2,1,0:T(8,128)(2,1)S(1)}, u32[]{:S(2)}, u32[]{:S(2)}) collective-permute-start(bf16[1,4,144,128]{3,2,1,0:T(8,128)(2,1)} %get-tuple-element.341), channel_id=1, source_target_pairs={{0,16},{8,24},{16,0},{24,8},{1,17},{9,25},{17,1},{25,9},{2,18},{10... | collective-permute-start | bytes 442376 | tf_op jit(solution)/shard_map/ppermute | solution.py:900
  397.5 9.4 %collective-permute-start.52 = (bf16[144,384]{1,0:T(8,128)(2,1)S(1)}, bf16[144,384]{1,0:T(8,128)(2,1)S(1)}, u32[]{:S(2)}, u32[]{:S(2)}) collective-permute-start(bf16[144,384]{1,0:T(8,128)(2,1)S(1)} %get-tuple-element.346), channel_id=1, source_target_pairs={{0,6},{1,7},{2,0},{3,1},{4,2},{5,3},{6,4},{7,5},{8,14},{9,15},{10,... | collective-permute-start | bytes 331784 | tf_op jit(solution)/shard_map/ppermute | solution.py:900
  408.0 8.8 %collective-permute-start.54 = (bf16[144,1024]{1,0:T(8,128)(2,1)S(1)}, bf16[144,1024]{1,0:T(8,128)(2,1)S(1)}, u32[]{:S(2)}, u32[]{:S(2)}) collective-permute-start(bf16[144,1024]{1,0:T(8,128)(2,1)S(1)} %get-tuple-element.350.refs_1_), channel_id=1, source_target_pairs={{0,8},{8,0},{16,24},{24,16},{1,9},{9,1},{17,25},{25,17},{2,10},{10... | collective-permute-start | bytes 884744 | tf_op jit(solution)/shard_map/ppermute | solution.py:900
  (78 other events, 598.4 us)
Sparse Core Ops, SparseCore 0:
  24.7 111.8 all-gather.3
  307.3 23.5 reduce-scatter.2
  333.9 25.7 reduce-scatter.4
  365.8 29.9 all-gather.5

commit v6 on v5

--- a/solution.py
+++ b/solution.py
@@ -149,17 +149,24 @@
     )
 
 
-def combine(jobs, carry=(), after=()):
+def combine(jobs, carry=(), after=(), also=()):
     n = jobs[0][1][0][0].shape[1]
     sizes = []
     for _, terms in jobs:
         before, _, behind, _, _ = terms[0][0].shape
         sizes.append((before, behind) + terms[0][2])
     flat = [t for _, terms in jobs for t in terms]
+    done = [a for arrays in also for a in arrays]
 
     def kernel(*refs):
         refs = refs[len(jobs) :]
-        outs = refs[len(flat) :]
+        outs = refs[len(flat) + len(done) :]
+        if also:
+
+            @pl.when(pl.program_id(0) == 0)
+            def _():
+                add_side_by_side(also, refs[len(flat) : len(flat) + len(done)], outs[-1])
+
         i = 0
         for job, (_, terms) in enumerate(jobs):
             total = refs[i][:, 0].astype(F32)
@@ -177,13 +184,14 @@
         before, behind, rows, cols = sizes[job]
         return pl.BlockSpec((before, 1, behind, rows, cols), lambda i, *own: (0, lax.rem(own[job][0] + i + 1, n), 0) + block)
 
+    joined = [(done[0].shape[0], sum(arrays[0].shape[1] for arrays in also))] if also else []
     made = call(
         kernel,
         "combine",
-        [t[0] for t in flat],
-        [at(job, t[1]) for job, (_, terms) in enumerate(jobs) for t in terms],
-        [far(size) for size in sizes for _ in range(n)],
-        [whole(size) for size in sizes for _ in range(n)],
+        [t[0] for t in flat] + done,
+        [at(job, t[1]) for job, (_, terms) in enumerate(jobs) for t in terms] + [whole(a.shape) for a in done],
+        [far(size) for size in sizes for _ in range(n)] + [like(shape) for shape in joined],
+        [whole(size) for size in sizes for _ in range(n)] + [whole(shape) for shape in joined],
         grid=(n,),
         scalars=[own for own, _ in jobs],
         carry=carry,
@@ -191,7 +199,18 @@
         room=12 << 20,
     )
     made, carried = made if carry else (made, ())
-    return [made[job * n : (job + 1) * n] for job in range(len(jobs))], carried
+    return [made[job * n : (job + 1) * n] for job in range(len(jobs))], carried, made[-1]
+
+
+def add_side_by_side(lists, refs, out_ref):
+    at, i = 0, 0
+    for arrays in lists:
+        total = refs[i][...].astype(F32)
+        for ref in refs[i + 1 : i + len(arrays)]:
+            total = total + ref[...].astype(F32)
+        out_ref[:, at : at + total.shape[1]] = total.astype(BF16)
+        at += total.shape[1]
+        i += len(arrays)
 
 
 def gather_sums(own, lists, carry=()):
@@ -968,18 +987,18 @@
         return [t.reshape((-1,) + t.shape[-2:]) for t, _, _ in self.terms]
 
 
-def step(*reductions, carry=(), after=()):
+def step(*reductions, carry=(), after=(), also=()):
     jobs = [r.job() for r in reductions]
     if len({r.digit[2] for r in reductions}) == 1:
-        made, carry = combine(jobs, carry, after)
+        made, carry, total = combine(jobs, carry, after, also)
     else:
-        made = []
+        made, total = [], add_up(also) if also else None
         for job in jobs:
-            one, carry = combine([job], carry, after)
+            one, carry, _ = combine([job], carry, after)
             made += one
     for reduction, one in zip(reductions, made):
         reduction.take(one)
-    return carry
+    return total if also else carry
 
 
 def local(layout, tokens, segment_ids, w_query, b_query, w_key, w_value, b_value, w_out, b_out, gain_first, shift_first, w_inner, b_inner, w_outer, b_outer, gain_second, shift_second, cotangent):
@@ -1057,11 +1076,11 @@
             parts = [((0, start // size), (rows, size)) for start, size in runs]
         return [Reduction(layout, [(own,) + part, (came,) + part], order) for part, order in zip(parts, orders)]
 
-    def along_z(reductions, carry=()):
-        sums = add_up([[t.reshape(-1, t.shape[-1]) for t in r.last()] for r in reductions], carry)
-        sums, carry = sums if carry else (sums, ())
-        sums = lax.psum_scatter(sums, ("replica", "group"), scatter_dimension=0, axis_index_groups=layout.along(z_digit[0]), tiled=True)
-        return [sums] + list(carry)
+    def flat(reductions):
+        return [[t.reshape(-1, t.shape[-1]) for t in r.last()] for r in reductions]
+
+    def along_z(sums):
+        return lax.psum_scatter(sums, ("replica", "group"), scatter_dimension=0, axis_index_groups=layout.along(z_digit[0]), tiled=True)
 
     def across_z(reductions, carry=()):
         made = gather_sums(layout.place(z_digit[0]).astype(jnp.int32).reshape(1), [r.last() for r in reductions], carry)
@@ -1080,16 +1099,14 @@
         (other,) = step(*outers, carry=[other])
     inners = reduction(other, own, xyz, yxz)
     dz1, da, do, sums1 = join_back(dz2, dh, n1, rstd1, vec, whole_wout)
-    (got_wouter,) = along_z(outers)
-    step(*inners)
+    got_wouter = along_z(step(*inners, also=flat(outers)))
     d0, sq0, sv0 = attend_back(qkv0, ot0, probs0, share0, do, 0)
     other, own = token_weights_grad(halves, xt, d0, groups, mixed=(ot0, ot1, da))
     for _ in middle:
         (other,) = step(*inners, carry=[other])
     firsts = reduction(other, own, xyz, yxz, runs=((0, cols), (other.shape[3] - width // 4, width // 4)))
     d1, sq1, sv1 = attend_back(qkv1, ot1, probs1, share1, do, 1)
-    (got_winner,) = along_z(inners)
-    step(*firsts)
+    got_winner = along_z(step(*firsts, also=flat(inners)))
     partial = token_grad(dz1, d0, wqkv0, F32)
     vectors = [((sq0, sq1), 0), ((sv0, sv1), 0)] + [((sums,), i) for sums in (sums1, sums2) for i in range(3)] + [((sum_inner,), 0)]
     other, own = token_weights_grad(halves, xt, d1, groups, vectors=vectors)

time: 434 us -> 435 us (level)
  local copies, waits for them, and re-layouts: 35.3 us -> 42.9 us
  waiting for transfers between devices: 82.8 us -> 76.9 us
    unnamed x132, local copies, waits for them, and re-layouts: 33.1 us -> 40.8 us
    ppermute x56, waiting for transfers between devices: 82.7 us -> 76.9 us  [send(): return lax.ppermute(value, axis, pairs)]
    pallas_call x44 -> x42, Pallas kernels: 244 us -> 242 us  [call(): pl.pallas_call(body, out_shape=shapes + [jax.ShapeDtypeStruct(c.shape, c....]
  transfers between devices with their start and end apart: 60 -> 60, of which waited for: 25 -> 23; matrix products, arithmetic and copies ran while one was open for 1% -> 1% of each run, Pallas kernels for 45% -> 44%
where the time goes in v6:
time: 435 us; the launch traced here: 429 us
  Pallas kernels  242 us (56%)
  waiting for transfers between devices  76.9 us (18%)
  starting transfers between devices  50.7 us (12%)
  local copies, waits for them, and re-layouts  42.9 us (10%)
  between operations  14.9 us (3%)
    pallas_call x42, Pallas kernels, call(): pl.pallas_call(body, out_shape=shapes + [jax.ShapeDtypeStruct(c.shape, c....  242 us
    ppermute x56, waiting for transfers between devices, send(): return lax.ppermute(value, axis, pairs)  76.9 us
    ppermute x56, starting transfers between devices, send(): return lax.ppermute(value, axis, pairs)  50.5 us
    unnamed x132, local copies, waits for them, and re-layouts  40.8 us
  transfers between devices with their start and end apart: 60, of which 23 were waited for; matrix products, arithmetic and copies ran while one was open for 1% of the time, Pallas kernels for 44%

profile of v6, /device:TPU:9, one launch (start us, length us, event | category | flops | bytes accessed | tf_op | source)
XLA Modules:
  0.0 428.8 jit_solution(4433704475231968736)
XLA Ops:
  14.9 2.2 transposed.1
  19.0 2.7 collective-permute-done.2.refs_5_.refs_9_
  27.2 4.4 %collective-permute-done.3.refs_3_ = bf16[4,32,768]{2,1,0:T(8,128)(2,1)S(1)} collective-permute-done((bf16[4,32,768]{2,1,0:T(8,128)(2,1)S(1)}, bf16[4,32,768]{2,1,0:T(8,128)(2,1)S(1)}, u32[]{:S(2)}, u32[]{:S(2)}) %collective-permute-start.3) | collective-permute-done | bytes 196640 | tf_op jit(solution)/shard_map/ppermute | solution.py:919
  38.3 4.8 %collective-permute-done.7.refs_9_.refs_13_ = bf16[32,2560]{1,0:T(8,128)(2,1)S(1)} collective-permute-done((bf16[32,2560]{1,0:T(8,128)(2,1)S(1)}, bf16[32,2560]{1,0:T(8,128)(2,1)S(1)}, u32[]{:S(2)}, u32[]{:S(2)}) %collective-permute-start.7) | collective-permute-done | bytes 163872 | tf_op jit(solution)/shard_map/ppermute | solution.py:919
  43.2 9.8 %collective-permute-done.8.refs_10_.refs_14_ = bf16[32,2560]{1,0:T(8,128)(2,1)S(1)} collective-permute-done((bf16[32,2560]{1,0:T(8,128)(2,1)S(1)}, bf16[32,2560]{1,0:T(8,128)(2,1)S(1)}, u32[]{:S(2)}, u32[]{:S(2)}) %collective-permute-start.8) | collective-permute-done | bytes 163872 | tf_op jit(solution)/shard_map/ppermute | solution.py:919
  53.0 3.9 collective-permute-done.9.refs_11_.refs_15_
  66.3 7.1 %project.2 = (bf16[1024,1536]{1,0:T(8,128)(2,1)}, bf16[1024,1536]{1,0:T(8,128)(2,1)}, bf16[128,1024]{1,0:T(8,128)(2,1)S(1)}, f32[8,128]{1,0:T(8,128)S(1)}) custom-call(s32[2]{0:T(128)S(1)} %pad_add_fusion.refs_0_, bf16[1024,1024]{1,0:T(8,128)(2,1)S(1)} %copy-done.30, f32[8,1024]{1,0:T(8,128)S(1)} %stack.40.refs_2_.refs_4_, ...), custom_call_target="tpu_custom_call", output_to_operand_aliasing={{2}: (7, {})} | custom-call | flops 6000000000 | bytes 6000001 | tf_op jit(solution)/shard_map/project/pallas_call | solution.py:40
  80.4 11.7 %attend.2 = (bf16[1024,512]{1,0:T(8,128)(2,1)S(1)}, bf16[512,1024]{1,0:T(8,128)(2,1)S(1)}, bf16[2,8,512,512]{3,2,1,0:T(8,128)(2,1)}, f32[2,2,4,512]{3,2,1,0:T(4,128)S(1)}, f32[8,128]{1,0:T(8,128)S(1)}) custom-call(bf16[1024,1536]{1,0:T(8,128)(2,1)S(1)} %copy-done.49, bf16[1024,1536]{1,0:T(8,128)(2,1)S(1)} %copy-done.49, bf16[1024,1536]{1,0:T(8,128)(2,1)S(1)} %copy-done.49, ...), custom_call_target="tpu_custom_call" | custom-call | flops 11000000512 | bytes 11000001 | tf_op jit(solution)/shard_map/attend/pallas_call | solution.py:40
  92.0 14.4 %collective-permute-done.17.refs_10_.refs_14_ = bf16[128,1024]{1,0:T(8,128)(2,1)S(1)} collective-permute-done((bf16[128,1024]{1,0:T(8,128)(2,1)S(1)}, bf16[128,1024]{1,0:T(8,128)(2,1)S(1)}, u32[]{:S(2)}, u32[]{:S(2)}) %collective-permute-start.17) | collective-permute-done | bytes 262176 | tf_op jit(solution)/shard_map/ppermute | solution.py:919
  106.4 4.4 %collective-permute-done.18.refs_11_.refs_15_ = bf16[128,1024]{1,0:T(8,128)(2,1)S(1)} collective-permute-done((bf16[128,1024]{1,0:T(8,128)(2,1)S(1)}, bf16[128,1024]{1,0:T(8,128)(2,1)S(1)}, u32[]{:S(2)}, u32[]{:S(2)}) %collective-permute-start.18) | collective-permute-done | bytes 262176 | tf_op jit(solution)/shard_map/ppermute | solution.py:919
  112.3 2.5 collective-permute-done.19
  116.7 5.8 %project.3 = (bf16[1024,1536]{1,0:T(8,128)(2,1)}, bf16[1024,1536]{1,0:T(8,128)(2,1)}, f32[8,128]{1,0:T(8,128)S(1)}) custom-call(s32[2]{0:T(128)S(1)} %pad_add_fusion.refs_0_, bf16[1024,1024]{1,0:T(8,128)(2,1)S(1)} %copy-done.31, f32[8,1024]{1,0:T(8,128)S(1)} %stack.40.refs_2_.refs_4_, bf16[2,256,1280]{2,1,0:T(8,128)(2,1)S(1)} %bitcast.171, ...), custom_call_target="tpu_custom_call" | custom-call | flops 6000000000 | bytes 6000001 | tf_op jit(solution)/shard_map/project/pallas_call | solution.py:40
  124.4 11.6 %attend.3 = (bf16[1024,512]{1,0:T(8,128)(2,1)S(1)}, bf16[512,1024]{1,0:T(8,128)(2,1)S(1)}, bf16[2,8,512,512]{3,2,1,0:T(8,128)(2,1)}, f32[2,2,4,512]{3,2,1,0:T(4,128)S(1)}, f32[8,128]{1,0:T(8,128)S(1)}) custom-call(bf16[1024,1536]{1,0:T(8,128)(2,1)S(1)} %copy-done.47, bf16[1024,1536]{1,0:T(8,128)(2,1)S(1)} %copy-done.47, bf16[1024,1536]{1,0:T(8,128)(2,1)S(1)} %copy-done.47, ...), custom_call_target="tpu_custom_call" | custom-call | flops 11000000512 | bytes 11000001 | tf_op jit(solution)/shard_map/attend/pallas_call | solution.py:40
  137.0 7.9 %join.1 = (f32[1024,1024]{1,0:T(8,128)}, f32[1024,1]{1,0:T(8,128)}, bf16[1024,1024]{1,0:T(8,128)(2,1)S(1)}, bf16[1024,1024]{1,0:T(8,128)(2,1)}, bf16[1024,1024]{1,0:T(8,128)(2,1)}, /*index=5*/f32[8,128]{1,0:T(8,128)S(1)}) custom-call(s32[2]{0:T(128)S(1)} %pad_add_fusion.refs_0_, bf16[1024,512]{1,0:T(8,128)(2,1)S(1)} %get-tuple-element.207.refs_1_, ...), custom_call_target="tpu_custom_call" | custom-call | flops 7000000000 | bytes 7000001 | tf_op jit(solution)/shard_map/join/pallas_call | solution.py:40
  147.8 10.3 %inner.2 = (bf16[1024,4096]{1,0:T(8,128)(2,1)}, bf16[1024,4096]{1,0:T(8,128)(2,1)}, f32[8,128]{1,0:T(8,128)S(1)}) custom-call(bf16[1024,1024]{1,0:T(8,128)(2,1)S(1)} %copy-done.39, bf16[1024,4096]{1,0:T(8,128)(2,1)} %all-gather.4.cloned.1.call-done.refs_1_.refs_5_, f32[1,4096]{1,0:T(1,128)S(1)} %bitcast.161, f32[8,128]{1,0:T(8,128)S(1)} %get-tuple-element.224.refs_3_), custom_call_target="tpu_custom_call" | custom-call | flops 9000000512 | bytes 9000001 | tf_op jit(solution)/shard_map/inner/pallas_call | solution.py:40
  158.0 2.8 collective-permute-done.23.refs_3_
  163.7 10.4 %inner.3 = (bf16[1024,4096]{1,0:T(8,128)(2,1)}, bf16[1024,4096]{1,0:T(8,128)(2,1)}, f32[8,128]{1,0:T(8,128)S(1)}) custom-call(bf16[1024,1024]{1,0:T(8,128)(2,1)S(1)} %copy-done.39, bf16[1024,4096]{1,0:T(8,128)(2,1)} %all-gather.4.cloned.1.call-done.refs_1_.refs_5_, f32[1,4096]{1,0:T(1,128)S(1)} %bitcast.162, ...), custom_call_target="tpu_custom_call", output_to_operand_aliasing={{0}: (3, {}), {1}: (4, {})} | custom-call | flops 9000000512 | bytes 9000001 | tf_op jit(solution)/shard_map/inner/pallas_call | solution.py:40
  176.3 20.3 %outer.1 = (bf16[1024,1024]{1,0:T(8,128)(2,1)}, f32[1024,1024]{1,0:T(8,128)}, bf16[1024,1024]{1,0:T(8,128)(2,1)}, bf16[1024,1024]{1,0:T(8,128)(2,1)S(1)}, f32[8,...) custom-call(s32[2]{0:T(128)S(1)} %pad_add_fusion.refs_0_, ...), custom_call_target="tpu_custom_call" | custom-call | flops 19000000512 | bytes 19000000 | tf_op jit(solution)/shard_map/outer/pallas_call | solution.py:40
  196.6 7.2 %outer_grad.2 = (bf16[2,8,256,512]{3,2,1,0:T(8,128)(2,1)S(1)}, f32[8,128]{1,0:T(8,128)S(1)}) custom-call(s32[1]{0:T(128)} %bitcast.1.refs_0_, bf16[1024,1024]{1,0:T(8,128)(2,1)S(1)} %get-tuple-element.242.refs_1_, bf16[1024,4096]{1,0:T(8,128)(2,1)} %get-tuple-element.231.refs_1_.refs_2_, f32[8,128]{1,0:T(8,128)S(1)} %get-tuple-element.243.refs_3_), custom_call_target="tpu_custom_call" | custom-call | flops 6000000000 | bytes 6000001 | tf_op jit(solution)/shard_map/outer_grad/pallas_call | solution.py:40
  204.3 7.1 %outer_grad.3 = (bf16[2,8,256,512]{3,2,1,0:T(8,128)(2,1)S(1)}, f32[8,128]{1,0:T(8,128)S(1)}) custom-call(s32[1]{0:T(128)} %bitcast.refs_0_, bf16[1024,1024]{1,0:T(8,128)(2,1)S(1)} %get-tuple-element.242.refs_1_, bf16[1024,4096]{1,0:T(8,128)(2,1)} %get-tuple-element.231.refs_1_.refs_2_, f32[8,128]{1,0:T(8,128)S(1)} %get-tuple-element.244.refs_3_), custom_call_target="tpu_custom_call" | custom-call | flops 6000000000 | bytes 6000001 | tf_op jit(solution)/shard_map/outer_grad/pallas_call | solution.py:40
  211.5 5.0 %combine.8 = (bf16[1,8,128,512]{3,2,1,0:T(8,128)(2,1)}, bf16[1,8,128,512]{3,2,1,0:T(8,128)(2,1)}, bf16[8,1,128,512]{3,2,1,0:T(8,128)(2,1)}, bf16[8,1,128,512]{3,2,1,0:T(8,128)(2,1)}, f32[8,128]{1,0:T(8,128)S(1)}) custom-call(s32[1]{0:T(128)} %bitcast.3.refs_0_.refs_1_, s32[1]{0:T(128)} %bitcast.2.refs_1_.refs_0_, bf16[1,2,8,256,512]{4,3,2,1,0:T(8,128)(2,1)S(1)} %bitcast.114, ...), custom_call_target="tpu_custom_call" | custom-call | flops 1 | bytes 1 | tf_op jit(solution)/shard_map/combine/pallas_call | solution.py:40
  218.0 35.9 %inner_back.1 = (bf16[2,8,128,1024]{3,2,1,0:T(8,128)(2,1)}, bf16[2,8,128,1024]{3,2,1,0:T(8,128)(2,1)}, f32[1024,1024]{1,0:T(8,128)}, f32[1,4096]{1,0:T(1,128)S(1)}, f32[8,128]{1,0:T(8,128)S(1)}) custom-call(s32[2]{0:T(128)S(1)} %pad_add_fusion.1.refs_0_, bf16[1024,1024]{1,0:T(8,128)(2,1)S(1)} %copy-done.62, bf16[4096,1024]{1,0:T(8,128)(2,1)} %get-tuple-element.239.refs_2_, ...), custom_call_target="tpu_custom_call" | custom-call | flops 35000000512 | bytes 35000000 | tf_op jit(solution)/shard_map/inner_back/pallas_call | solution.py:40
  253.9 2.8 combine.9
  259.0 2.2 copy-done.46
  261.2 9.2 %join_back.1 = (f32[1024,1024]{1,0:T(8,128)}, bf16[1024,1024]{1,0:T(8,128)(2,1)}, bf16[1024,1024]{1,0:T(8,128)(2,1)}, f32[8,1024]{1,0:T(8,128)S(1)}, f32[8,128]{1,0:T(8,128)S(1)}) custom-call(f32[1024,1024]{1,0:T(8,128)S(1)} %copy-done.46, f32[1024,1024]{1,0:T(8,128)} %get-tuple-element.249.refs_1_, f32[1024,1024]{1,0:T(8,128)} %get-tuple-element.232.refs_2_, ...), custom_call_target="tpu_custom_call" | custom-call | flops 8000000000 | bytes 8000001 | tf_op jit(solution)/shard_map/join_back/pallas_call | solution.py:40
  271.2 5.2 %combine.10 = (bf16[1,8,128,512]{3,2,1,0:T(8,128)(2,1)}, bf16[1,8,128,512]{3,2,1,0:T(8,128)(2,1)}, bf16[8,1,128,512]{3,2,1,0:T(8,128)(2,1)}, bf16[8,1,128,512]{3...) custom-call(s32[1]{0:T(128)} %bitcast.3.refs_0_.refs_1_, s32[1]{0:T(128)} %bitcast.2.refs_1_.refs_0_, ...), custom_call_target="tpu_custom_call" | custom-call | flops 1 | bytes 1 | tf_op jit(solution)/shard_map/combine/pallas_call | solution.py:40
  281.9 11.7 %attend_back.2 = (bf16[3,1024,512]{2,1,0:T(8,128)(2,1)}, f32[2,1,512]{2,1,0:T(1,128)S(1)}, f32[2,1,512]{2,1,0:T(1,128)S(1)}, f32[8,128]{1,0:T(8,128)S(1)}) custom-call(bf16[1024,1536]{1,0:T(8,128)(2,1)S(1)} %copy-done.50, bf16[1024,1536]{1,0:T(8,128)(2,1)S(1)} %copy-done.50, bf16[1024,1536]{1,0:T(8,128)(2,1)S(1)} %copy-done.50, ...), custom_call_target="tpu_custom_call" | custom-call | flops 11000000512 | bytes 11000001 | tf_op jit(solution)/shard_map/attend_back/pallas_call | solution.py:40
  293.7 10.4 %token_weights_grad.2 = (bf16[2,8,128,768]{3,2,1,0:T(8,128)(2,1)}, bf16[2,8,128,768]{3,2,1,0:T(8,128)(2,1)}, f32[8,128]{1,0:T(8,128)S(1)}) custom-call(s32[2]{0:T(128)S(1)} %pad_add_fusion.1.refs_0_, bf16[1024,1024]{1,0:T(8,128)(2,1)S(1)} %copy-done.40, bf16[3,1024,512]{2,1,0:T(8,128)(2,1)} %get-tuple-element.272.refs_2_.refs_1_, ...), custom_call_target="tpu_custom_call" | custom-call | flops 8000000000 | bytes 8000001 | tf_op jit(solution)/shard_map/token_weights_grad/pallas_call | solution.py:40
  304.2 2.6 combine.11
  313.5 12.1 %attend_back.3 = (bf16[3,1024,512]{2,1,0:T(8,128)(2,1)}, f32[2,1,512]{2,1,0:T(1,128)S(1)}, f32[2,1,512]{2,1,0:T(1,128)S(1)}, f32[8,128]{1,0:T(8,128)S(1)}) custom-call(bf16[1024,1536]{1,0:T(8,128)(2,1)S(1)} %copy-done.48, bf16[1024,1536]{1,0:T(8,128)(2,1)S(1)} %copy-done.48, bf16[1024,1536]{1,0:T(8,128)(2,1)S(1)} %copy-done.48, ...), custom_call_target="tpu_custom_call" | custom-call | flops 11000000512 | bytes 11000001 | tf_op jit(solution)/shard_map/attend_back/pallas_call | solution.py:40
  325.6 3.6 combine.12
  336.9 7.1 %token_grad.2 = (f32[1024,1024]{1,0:T(8,128)}, f32[8,128]{1,0:T(8,128)S(1)}) custom-call(f32[1024,1024]{1,0:T(8,128)} %get-tuple-element.259.refs_0_, bf16[3,1024,512]{2,1,0:T(8,128)(2,1)S(1)} %copy-done.45, bf16[1024,1536]{1,0:T(8,128)(2,1)S(1)} %copy-done.43, f32[8,128]{1,0:T(8,128)S(1)} %get-tuple-element.294.refs_3_), custom_call_target="tpu_custom_call" | custom-call | flops 6000000000 | bytes 6000001 | tf_op jit(solution)/shard_map/token_grad/pallas_call | solution.py:40
  344.1 5.8 %token_weights_grad.3 = (bf16[2,8,144,384]{3,2,1,0:T(8,128)(2,1)S(1)}, bf16[2,8,144,384]{3,2,1,0:T(8,128)(2,1)S(1)}, f32[8,128]{1,0:T(8,128)S(1)}) custom-call(s32[2]{0:T(128)S(1)} %pad_add_fusion.1.refs_0_, bf16[1024,1024]{1,0:T(8,128)(2,1)S(1)} %copy-done.41, bf16[3,1024,512]{2,1,0:T(8,128)(2,1)} %get-tuple-element.296.refs_2_.refs_1_, ...), custom_call_target="tpu_custom_call" | custom-call | flops 8000000000 | bytes 8000001 | tf_op jit(solution)/shard_map/token_weights_grad/pallas_call | solution.py:40
  356.3 2.6 combine.14
  358.9 2.6 collective-permute-done.41
  361.5 2.5 collective-permute-done.40
  367.5 2.1 collective-permute-start.44
  372.2 2.1 copy-done.42
  374.3 2.2 copy-done.44
  376.5 6.7 %token_grad.3 = (bf16[1024,1024]{1,0:T(8,128)(2,1)}, f32[8,128]{1,0:T(8,128)S(1)}) custom-call(f32[1024,1024]{1,0:T(8,128)} %get-tuple-element.295.refs_0_, bf16[3,1024,512]{2,1,0:T(8,128)(2,1)S(1)} %copy-done.44, bf16[1024,1536]{1,0:T(8,128)(2,1)S(1)} %copy-done.42, f32[8,128]{1,0:T(8,128)S(1)} %copy-done.36), custom_call_target="tpu_custom_call" | custom-call | flops 6000000000 | bytes 6000001 | tf_op jit(solution)/shard_map/token_grad/pallas_call | solution.py:40
  387.5 2.2 collective-permute-start.49
  389.7 5.5 %collective-permute-done.49 = bf16[1,4,144,128]{3,2,1,0:T(8,128)(2,1)S(1)} collective-permute-done((bf16[1,4,144,128]{3,2,1,0:T(8,128)(2,1)}, bf16[1,4,144,128]{3,2,1,0:T(8,128)(2,1)S(1)}, u32[]{:S(2)}, u32[]{:S(2)}) %collective-permute-start.49) | collective-permute-done | bytes 147488 | tf_op jit(solution)/shard_map/ppermute | solution.py:919
  401.6 2.4 wide_results.1
  404.1 3.7 collective-permute-done.52.refs_7_
  409.3 2.3 collective-permute-start.54
  411.6 2.8 collective-permute-done.53.refs_2_
  414.4 3.0 collective-permute-start.55
  418.6 2.1 token_weights_result.1
  (273 shorter events, 104.2 us)
Async XLA Ops:
  7.2 139.0 %all-gather.4.cloned.1.call-start = ((), (), s32[]{:S(2)}) async-start(), calls=%async_computation.2 | async-start | bytes 8650752 | tf_op jit(solution)/shard_map/all_gather | solution.py:1031
  8.9 8.2 %collective-permute-start = (bf16[32,1664]{1,0:T(8,128)(2,1)}, bf16[32,1664]{1,0:T(8,128)(2,1)S(1)}, u32[]{:S(2)}, u32[]{:S(2)}) collective-permute-start(bf16[32,1664]{1,0:T(8,128)(2,1)} %get-tuple-element.186.refs_2_.refs_6_), channel_id=1, source_target_pairs={{0,2},{1,3},{2,4},{3,5},{4,6},{5,7},{6,0},{7,1},{8,10},{9,11},{10,... | collective-permute-start | bytes 319496 | tf_op jit(solution)/shard_map/ppermute | solution.py:919
  10.2 8.8 %collective-permute-start.1 = (bf16[32,1664]{1,0:T(8,128)(2,1)}, bf16[32,1664]{1,0:T(8,128)(2,1)S(1)}, u32[]{:S(2)}, u32[]{:S(2)}) collective-permute-start(bf16[32,1664]{1,0:T(8,128)(2,1)} %get-tuple-element.186.refs_2_.refs_6_), channel_id=1, source_target_pairs={{0,4},{1,5},{2,6},{3,7},{4,0},{5,1},{6,2},{7,3},{8,12},{9,13},{10,... | collective-permute-start | bytes 319496 | tf_op jit(solution)/shard_map/ppermute | solution.py:919
  11.2 10.5 %collective-permute-start.2 = (bf16[32,1664]{1,0:T(8,128)(2,1)}, bf16[32,1664]{1,0:T(8,128)(2,1)S(1)}, u32[]{:S(2)}, u32[]{:S(2)}) collective-permute-start(bf16[32,1664]{1,0:T(8,128)(2,1)} %get-tuple-element.186.refs_2_.refs_6_), channel_id=1, source_target_pairs={{0,6},{1,7},{2,0},{3,1},{4,2},{5,3},{6,4},{7,5},{8,14},{9,15},{10,... | collective-permute-start | bytes 319496 | tf_op jit(solution)/shard_map/ppermute | solution.py:919
  24.6 340.3 %reduce-scatter.3.cloned.1.call-start = ((), (), s32[]{:S(2)}) async-start(), calls=%async_computation.3 | async-start | bytes 1310720 | tf_op jit(solution)/shard_map/reduce_scatter | solution.py:1083
  33.9 23.0 %collective-permute-start.6 = (bf16[4,2,32,896]{3,2,1,0:T(8,128)(2,1)S(1)}, bf16[4,2,32,896]{3,2,1,0:T(8,128)(2,1)S(1)}, u32[]{:S(2)}, u32[]{:S(2)}) collective-permute-start(bf16[4,2,32,896]{3,2,1,0:T(8,128)(2,1)S(1)} %get-tuple-element.195.refs_6_), channel_id=1, source_target_pairs={{0,16},{8,24},{16,0},{24,8},{1,17},{9,25},{17,1},{25,9},{2,18},{10... | collective-permute-start | bytes 1376264 | tf_op jit(solution)/shard_map/ppermute | solution.py:919
  35.2 21.7 %collective-permute-start.5 = (bf16[2,4,32,768]{3,2,1,0:T(8,128)(2,1)S(1)}, bf16[2,4,32,768]{3,2,1,0:T(8,128)(2,1)S(1)}, u32[]{:S(2)}, u32[]{:S(2)}) collective-permute-start(bf16[2,4,32,768]{3,2,1,0:T(8,128)(2,1)S(1)} %get-tuple-element.194.refs_4_), channel_id=1, source_target_pairs={{0,1},{1,0},{2,3},{3,2},{4,5},{5,4},{6,7},{7,6},{8,9},{9,8},{10,11... | collective-permute-start | bytes 1179656 | tf_op jit(solution)/shard_map/ppermute | solution.py:919
  36.2 16.8 %collective-permute-start.8 = (bf16[32,2560]{1,0:T(8,128)(2,1)S(1)}, bf16[32,2560]{1,0:T(8,128)(2,1)S(1)}, u32[]{:S(2)}, u32[]{:S(2)}) collective-permute-start(bf16[32,2560]{1,0:T(8,128)(2,1)S(1)} %get-tuple-element.196.refs_8_.refs_12_), channel_id=1, source_target_pairs={{0,4},{1,5},{2,6},{3,7},{4,0},{5,1},{6,2},{7,3},{8,12},{9,13},{10,... | collective-permute-start | bytes 491528 | tf_op jit(solution)/shard_map/ppermute | solution.py:919
  37.1 19.8 %collective-permute-start.9 = (bf16[32,2560]{1,0:T(8,128)(2,1)S(1)}, bf16[32,2560]{1,0:T(8,128)(2,1)S(1)}, u32[]{:S(2)}, u32[]{:S(2)}) collective-permute-start(bf16[32,2560]{1,0:T(8,128)(2,1)S(1)} %get-tuple-element.196.refs_8_.refs_12_), channel_id=1, source_target_pairs={{0,6},{1,7},{2,0},{3,1},{4,2},{5,3},{6,4},{7,5},{8,14},{9,15},{10,... | collective-permute-start | bytes 491528 | tf_op jit(solution)/shard_map/ppermute | solution.py:919
  60.7 15.4 %collective-permute-start.12 = (bf16[4,32,1280]{2,1,0:T(8,128)(2,1)S(1)}, bf16[4,32,1280]{2,1,0:T(8,128)(2,1)S(1)}, u32[]{:S(2)}, u32[]{:S(2)}) collective-permute-start(bf16[4,32,1280]{2,1,0:T(8,128)(2,1)S(1)} %get-tuple-element.203.refs_2_), channel_id=1, source_target_pairs={{0,16},{8,24},{16,0},{24,8},{1,17},{9,25},{17,1},{25,9},{2,18},{10... | collective-permute-start | bytes 983048 | tf_op jit(solution)/shard_map/ppermute | solution.py:919
  61.4 14.6 %collective-permute-start.13 = (bf16[4,32,1280]{2,1,0:T(8,128)(2,1)S(1)}, bf16[4,32,1280]{2,1,0:T(8,128)(2,1)S(1)}, u32[]{:S(2)}, u32[]{:S(2)}) collective-permute-start(bf16[4,32,1280]{2,1,0:T(8,128)(2,1)S(1)} %get-tuple-element.204.refs_4_), channel_id=1, source_target_pairs={{0,1},{1,0},{2,3},{3,2},{4,5},{5,4},{6,7},{7,6},{8,9},{9,8},{10,11... | collective-permute-start | bytes 983048 | tf_op jit(solution)/shard_map/ppermute | solution.py:919
  73.5 18.5 %collective-permute-start.16 = (bf16[128,1024]{1,0:T(8,128)(2,1)S(1)}, bf16[128,1024]{1,0:T(8,128)(2,1)S(1)}, u32[]{:S(2)}, u32[]{:S(2)}) collective-permute-start(bf16[128,1024]{1,0:T(8,128)(2,1)S(1)} %get-tuple-element.210.refs_8_.refs_12_), channel_id=1, source_target_pairs={{0,2},{1,3},{2,4},{3,5},{4,6},{5,7},{6,0},{7,1},{8,10},{9,11},{10,... | collective-permute-start | bytes 786440 | tf_op jit(solution)/shard_map/ppermute | solution.py:919
  73.6 32.8 %collective-permute-start.17 = (bf16[128,1024]{1,0:T(8,128)(2,1)S(1)}, bf16[128,1024]{1,0:T(8,128)(2,1)S(1)}, u32[]{:S(2)}, u32[]{:S(2)}) collective-permute-start(bf16[128,1024]{1,0:T(8,128)(2,1)S(1)} %get-tuple-element.210.refs_8_.refs_12_), channel_id=1, source_target_pairs={{0,4},{1,5},{2,6},{3,7},{4,0},{5,1},{6,2},{7,3},{8,12},{9,13},{10,... | collective-permute-start | bytes 786440 | tf_op jit(solution)/shard_map/ppermute | solution.py:919
  74.2 36.6 %collective-permute-start.18 = (bf16[128,1024]{1,0:T(8,128)(2,1)S(1)}, bf16[128,1024]{1,0:T(8,128)(2,1)S(1)}, u32[]{:S(2)}, u32[]{:S(2)}) collective-permute-start(bf16[128,1024]{1,0:T(8,128)(2,1)S(1)} %get-tuple-element.210.refs_8_.refs_12_), channel_id=1, source_target_pairs={{0,6},{1,7},{2,0},{3,1},{4,2},{5,3},{6,4},{7,5},{8,14},{9,15},{10,... | collective-permute-start | bytes 786440 | tf_op jit(solution)/shard_map/ppermute | solution.py:919
  76.4 34.4 %collective-permute-start.14 = (bf16[2,4,32,1280]{3,2,1,0:T(8,128)(2,1)S(1)}, bf16[2,4,32,1280]{3,2,1,0:T(8,128)(2,1)S(1)}, u32[]{:S(2)}, u32[]{:S(2)}) collective-permute-start(bf16[2,4,32,1280]{3,2,1,0:T(8,128)(2,1)S(1)} %get-tuple-element.208.refs_4_), channel_id=1, source_target_pairs={{0,1},{1,0},{2,3},{3,2},{4,5},{5,4},{6,7},{7,6},{8,9},{9,8},{10,11... | collective-permute-start | bytes 1966088 | tf_op jit(solution)/shard_map/ppermute | solution.py:919
  77.3 33.5 %collective-permute-start.15 = (bf16[4,2,32,1280]{3,2,1,0:T(8,128)(2,1)S(1)}, bf16[4,2,32,1280]{3,2,1,0:T(8,128)(2,1)S(1)}, u32[]{:S(2)}, u32[]{:S(2)}) collective-permute-start(bf16[4,2,32,1280]{3,2,1,0:T(8,128)(2,1)S(1)} %get-tuple-element.209.refs_6_), channel_id=1, source_target_pairs={{0,16},{8,24},{16,0},{24,8},{1,17},{9,25},{17,1},{25,9},{2,18},{10... | collective-permute-start | bytes 1966088 | tf_op jit(solution)/shard_map/ppermute | solution.py:919
  112.3 23.7 %collective-permute-start.21 = (bf16[4,128,512]{2,1,0:T(8,128)(2,1)S(1)}, bf16[4,128,512]{2,1,0:T(8,128)(2,1)S(1)}, u32[]{:S(2)}, u32[]{:S(2)}) collective-permute-start(bf16[4,128,512]{2,1,0:T(8,128)(2,1)S(1)} %get-tuple-element.218.refs_2_), channel_id=1, source_target_pairs={{0,16},{8,24},{16,0},{24,8},{1,17},{9,25},{17,1},{25,9},{2,18},{10... | collective-permute-start | bytes 1572872 | tf_op jit(solution)/shard_map/ppermute | solution.py:919
  112.3 23.7 %collective-permute-start.22 = (bf16[4,128,512]{2,1,0:T(8,128)(2,1)S(1)}, bf16[4,128,512]{2,1,0:T(8,128)(2,1)S(1)}, u32[]{:S(2)}, u32[]{:S(2)}) collective-permute-start(bf16[4,128,512]{2,1,0:T(8,128)(2,1)S(1)} %get-tuple-element.219.refs_4_), channel_id=1, source_target_pairs={{0,1},{1,0},{2,3},{3,2},{4,5},{5,4},{6,7},{7,6},{8,9},{9,8},{10,11... | collective-permute-start | bytes 1572872 | tf_op jit(solution)/shard_map/ppermute | solution.py:919
  136.2 24.6 %collective-permute-start.23 = (bf16[2,4,128,512]{3,2,1,0:T(8,128)(2,1)S(1)}, bf16[2,4,128,512]{3,2,1,0:T(8,128)(2,1)S(1)}, u32[]{:S(2)}, u32[]{:S(2)}) collective-permute-start(bf16[2,4,128,512]{3,2,1,0:T(8,128)(2,1)S(1)} %get-tuple-element.227.refs_2_), channel_id=1, source_target_pairs={{0,1},{1,0},{2,3},{3,2},{4,5},{5,4},{6,7},{7,6},{8,9},{9,8},{10,11... | collective-permute-start | bytes 3145736 | tf_op jit(solution)/shard_map/ppermute | solution.py:919
  136.3 24.6 %collective-permute-start.24 = (bf16[4,2,128,512]{3,2,1,0:T(8,128)(2,1)S(1)}, bf16[4,2,128,512]{3,2,1,0:T(8,128)(2,1)}, u32[]{:S(2)}, u32[]{:S(2)}) collective-permute-start(bf16[4,2,128,512]{3,2,1,0:T(8,128)(2,1)S(1)} %get-tuple-element.228.refs_4_), channel_id=1, source_target_pairs={{0,16},{8,24},{16,0},{24,8},{1,17},{9,25},{17,1},{25,9},{2,18},{10... | collective-permute-start | bytes 3145736 | tf_op jit(solution)/shard_map/ppermute | solution.py:919
  162.4 11.7 %collective-permute-start.25 = (bf16[2,4,2,128,512]{4,3,2,1,0:T(8,128)(2,1)S(1)}, bf16[2,4,2,128,512]{4,3,2,1,0:T(8,128)(2,1)S(1)}, u32[]{:S(2)}, u32[]{:S(2)}) collective-permute-start(bf16[2,4,2,128,512]{4,3,2,1,0:T(8,128)(2,1)S(1)} %get-tuple-element.233), channel_id=1, source_target_pairs={{0,8},{8,0},{16,24},{24,16},{1,9},{9,1},{17,25},{25,17},{2,10},{10... | collective-permute-start | bytes 6291464 | tf_op jit(solution)/shard_map/ppermute | solution.py:919
  163.6 10.5 %collective-permute-start.26 = (bf16[2,4,2,128,512]{4,3,2,1,0:T(8,128)(2,1)S(1)}, bf16[2,4,2,128,512]{4,3,2,1,0:T(8,128)(2,1)S(1)}, u32[]{:S(2)}, u32[]{:S(2)}) collective-permute-start(bf16[2,4,2,128,512]{4,3,2,1,0:T(8,128)(2,1)S(1)} %get-tuple-element.234), channel_id=1, source_target_pairs={{0,8},{8,0},{16,24},{24,16},{1,9},{9,1},{17,25},{25,17},{2,10},{10... | collective-permute-start | bytes 6291464 | tf_op jit(solution)/shard_map/ppermute | solution.py:919
  203.7 7.8 %collective-permute-start.27 = (bf16[2,8,256,512]{3,2,1,0:T(8,128)(2,1)S(1)}, bf16[2,8,256,512]{3,2,1,0:T(8,128)(2,1)S(1)}, u32[]{:S(2)}, u32[]{:S(2)}) collective-permute-start(bf16[2,8,256,512]{3,2,1,0:T(8,128)(2,1)S(1)} %get-tuple-element.246), channel_id=1, source_target_pairs={{0,8},{8,0},{16,24},{24,16},{1,9},{9,1},{17,25},{25,17},{2,10},{10... | collective-permute-start | bytes 12582920 | tf_op jit(solution)/shard_map/ppermute | solution.py:919
  216.6 37.3 %collective-permute-start.28 = (bf16[1,8,128,512]{3,2,1,0:T(8,128)(2,1)}, bf16[1,8,128,512]{3,2,1,0:T(8,128)(2,1)S(1)}, u32[]{:S(2)}, u32[]{:S(2)}) collective-permute-start(bf16[1,8,128,512]{3,2,1,0:T(8,128)(2,1)} %get-tuple-element.253), channel_id=1, source_target_pairs={{0,16},{8,24},{16,0},{24,8},{1,17},{9,25},{17,1},{25,9},{2,18},{10... | collective-permute-start | bytes 3145736 | tf_op jit(solution)/shard_map/ppermute | solution.py:919
  216.6 37.3 %collective-permute-start.29 = (bf16[8,1,128,512]{3,2,1,0:T(8,128)(2,1)}, bf16[8,1,128,512]{3,2,1,0:T(8,128)(2,1)S(1)}, u32[]{:S(2)}, u32[]{:S(2)}) collective-permute-start(bf16[8,1,128,512]{3,2,1,0:T(8,128)(2,1)} %get-tuple-element.255), channel_id=1, source_target_pairs={{0,1},{1,0},{2,3},{3,2},{4,5},{5,4},{6,7},{7,6},{8,9},{9,8},{10,11... | collective-permute-start | bytes 3145736 | tf_op jit(solution)/shard_map/ppermute | solution.py:919
  256.8 14.4 %collective-permute-start.30 = (bf16[2,8,128,1024]{3,2,1,0:T(8,128)(2,1)}, bf16[2,8,128,1024]{3,2,1,0:T(8,128)(2,1)S(1)}, u32[]{:S(2)}, u32[]{:S(2)}) collective-permute-start(bf16[2,8,128,1024]{3,2,1,0:T(8,128)(2,1)} %get-tuple-element.265), channel_id=1, source_target_pairs={{0,8},{8,0},{16,24},{24,16},{1,9},{9,1},{17,25},{25,17},{2,10},{10... | collective-permute-start | bytes 12582920 | tf_op jit(solution)/shard_map/ppermute | solution.py:919
  257.4 13.7 %collective-permute-start.31 = (bf16[4,1,128,512]{3,2,1,0:T(8,128)(2,1)}, bf16[4,1,128,512]{3,2,1,0:T(8,128)(2,1)S(1)}, u32[]{:S(2)}, u32[]{:S(2)}) collective-permute-start(bf16[4,1,128,512]{3,2,1,0:T(8,128)(2,1)} %get-tuple-element.267), channel_id=1, source_target_pairs={{0,1},{1,0},{2,3},{3,2},{4,5},{5,4},{6,7},{7,6},{8,9},{9,8},{10,11... | collective-permute-start | bytes 1572872 | tf_op jit(solution)/shard_map/ppermute | solution.py:919
  257.5 13.6 %collective-permute-start.32 = (bf16[1,4,128,512]{3,2,1,0:T(8,128)(2,1)}, bf16[1,4,128,512]{3,2,1,0:T(8,128)(2,1)S(1)}, u32[]{:S(2)}, u32[]{:S(2)}) collective-permute-start(bf16[1,4,128,512]{3,2,1,0:T(8,128)(2,1)} %get-tuple-element.269), channel_id=1, source_target_pairs={{0,16},{8,24},{16,0},{24,8},{1,17},{9,25},{17,1},{25,9},{2,18},{10... | collective-permute-start | bytes 1572872 | tf_op jit(solution)/shard_map/ppermute | solution.py:919
  277.4 26.7 %collective-permute-start.33 = (bf16[1,8,128,512]{3,2,1,0:T(8,128)(2,1)}, bf16[1,8,128,512]{3,2,1,0:T(8,128)(2,1)S(1)}, u32[]{:S(2)}, u32[]{:S(2)}) collective-permute-start(bf16[1,8,128,512]{3,2,1,0:T(8,128)(2,1)} %get-tuple-element.280), channel_id=1, source_target_pairs={{0,16},{8,24},{16,0},{24,8},{1,17},{9,25},{17,1},{25,9},{2,18},{10... | collective-permute-start | bytes 3145736 | tf_op jit(solution)/shard_map/ppermute | solution.py:919
  278.9 25.3 %collective-permute-start.34 = (bf16[8,1,128,512]{3,2,1,0:T(8,128)(2,1)}, bf16[8,1,128,512]{3,2,1,0:T(8,128)(2,1)S(1)}, u32[]{:S(2)}, u32[]{:S(2)}) collective-permute-start(bf16[8,1,128,512]{3,2,1,0:T(8,128)(2,1)} %get-tuple-element.282), channel_id=1, source_target_pairs={{0,1},{1,0},{2,3},{3,2},{4,5},{5,4},{6,7},{7,6},{8,9},{9,8},{10,11... | collective-permute-start | bytes 3145736 | tf_op jit(solution)/shard_map/ppermute | solution.py:919
  306.8 18.8 %collective-permute-start.35 = (bf16[2,8,128,768]{3,2,1,0:T(8,128)(2,1)}, bf16[2,8,128,768]{3,2,1,0:T(8,128)(2,1)S(1)}, u32[]{:S(2)}, u32[]{:S(2)}) collective-permute-start(bf16[2,8,128,768]{3,2,1,0:T(8,128)(2,1)} %get-tuple-element.285), channel_id=1, source_target_pairs={{0,8},{8,0},{16,24},{24,16},{1,9},{9,1},{17,25},{25,17},{2,10},{10... | collective-permute-start | bytes 9437192 | tf_op jit(solution)/shard_map/ppermute | solution.py:919
  308.5 56.4 %reduce-scatter.5.cloned.1.call-start = ((), (), s32[]{:S(2)}) async-start(), calls=%async_computation.4 | async-start | bytes 1310720 | tf_op jit(solution)/shard_map/reduce_scatter | solution.py:1083
  308.6 16.9 %collective-permute-start.36 = (bf16[4,1,128,512]{3,2,1,0:T(8,128)(2,1)}, bf16[4,1,128,512]{3,2,1,0:T(8,128)(2,1)S(1)}, u32[]{:S(2)}, u32[]{:S(2)}) collective-permute-start(bf16[4,1,128,512]{3,2,1,0:T(8,128)(2,1)} %get-tuple-element.287), channel_id=1, source_target_pairs={{0,1},{1,0},{2,3},{3,2},{4,5},{5,4},{6,7},{7,6},{8,9},{9,8},{10,11... | collective-permute-start | bytes 1572872 | tf_op jit(solution)/shard_map/ppermute | solution.py:919
  308.7 16.8 %collective-permute-start.37 = (bf16[1,4,128,512]{3,2,1,0:T(8,128)(2,1)}, bf16[1,4,128,512]{3,2,1,0:T(8,128)(2,1)S(1)}, u32[]{:S(2)}, u32[]{:S(2)}) collective-permute-start(bf16[1,4,128,512]{3,2,1,0:T(8,128)(2,1)} %get-tuple-element.289), channel_id=1, source_target_pairs={{0,16},{8,24},{16,0},{24,8},{1,17},{9,25},{17,1},{25,9},{2,18},{10... | collective-permute-start | bytes 1572872 | tf_op jit(solution)/shard_map/ppermute | solution.py:919
  330.1 19.7 %collective-permute-start.38 = (bf16[1,8,128,384]{3,2,1,0:T(8,128)(2,1)}, bf16[1,8,128,384]{3,2,1,0:T(8,128)(2,1)S(1)}, u32[]{:S(2)}, u32[]{:S(2)}) collective-permute-start(bf16[1,8,128,384]{3,2,1,0:T(8,128)(2,1)} %get-tuple-element.301), channel_id=1, source_target_pairs={{0,16},{8,24},{16,0},{24,8},{1,17},{9,25},{17,1},{25,9},{2,18},{10... | collective-permute-start | bytes 2359304 | tf_op jit(solution)/shard_map/ppermute | solution.py:919
  331.6 18.3 %collective-permute-start.39 = (bf16[8,1,128,256]{3,2,1,0:T(8,128)(2,1)}, bf16[8,1,128,256]{3,2,1,0:T(8,128)(2,1)S(1)}, u32[]{:S(2)}, u32[]{:S(2)}) collective-permute-start(bf16[8,1,128,256]{3,2,1,0:T(8,128)(2,1)} %get-tuple-element.303), channel_id=1, source_target_pairs={{0,1},{1,0},{2,3},{3,2},{4,5},{5,4},{6,7},{7,6},{8,9},{9,8},{10,11... | collective-permute-start | bytes 1572872 | tf_op jit(solution)/shard_map/ppermute | solution.py:919
  333.1 67.0 %all-gather.6.cloned.1.call-start = ((), (), s32[]{:S(2)}) async-start(), calls=%async_computation.5 | async-start | bytes 2621440 | tf_op jit(solution)/shard_map/all_gather | solution.py:1090
  353.0 11.0 %collective-permute-start.40 = (bf16[4,1,128,384]{3,2,0,1:T(8,128)(2,1)}, bf16[4,1,128,384]{3,2,0,1:T(8,128)(2,1)S(1)}, u32[]{:S(2)}, u32[]{:S(2)}) collective-permute-start(bf16[4,1,128,384]{3,2,0,1:T(8,128)(2,1)} %bitcast.178), channel_id=1, source_target_pairs={{0,1},{1,0},{2,3},{3,2},{4,5},{5,4},{6,7},{7,6},{8,9},{9,8},{10,11... | collective-permute-start | bytes 1179656 | tf_op jit(solution)/shard_map/ppermute | solution.py:919
  353.6 7.8 %collective-permute-start.41 = (bf16[1,4,128,256]{3,2,1,0:T(8,128)(2,1)}, bf16[1,4,128,256]{3,2,1,0:T(8,128)(2,1)S(1)}, u32[]{:S(2)}, u32[]{:S(2)}) collective-permute-start(bf16[1,4,128,256]{3,2,1,0:T(8,128)(2,1)} %get-tuple-element.317), channel_id=1, source_target_pairs={{0,16},{8,24},{16,0},{24,8},{1,17},{9,25},{17,1},{25,9},{2,18},{10... | collective-permute-start | bytes 786440 | tf_op jit(solution)/shard_map/ppermute | solution.py:919
  366.8 18.7 %collective-permute-start.46 = (bf16[1,8,144,256]{3,2,1,0:T(8,128)(2,1)}, bf16[1,8,144,256]{3,2,1,0:T(8,128)(2,1)S(1)}, u32[]{:S(2)}, u32[]{:S(2)}) collective-permute-start(bf16[1,8,144,256]{3,2,1,0:T(8,128)(2,1)} %get-tuple-element.330), channel_id=1, source_target_pairs={{0,16},{8,24},{16,0},{24,8},{1,17},{9,25},{17,1},{25,9},{2,18},{10... | collective-permute-start | bytes 1769480 | tf_op jit(solution)/shard_map/ppermute | solution.py:919
  367.5 15.7 %collective-permute-start.43 = (bf16[128,640]{1,0:T(8,128)(2,1)S(1)}, bf16[128,640]{1,0:T(8,128)(2,1)S(1)}, u32[]{:S(2)}, u32[]{:S(2)}) collective-permute-start(bf16[128,640]{1,0:T(8,128)(2,1)S(1)} %get-tuple-element.326), channel_id=1, source_target_pairs={{0,2},{1,3},{2,4},{3,5},{4,6},{5,7},{6,0},{7,1},{8,10},{9,11},{10,... | collective-permute-start | bytes 491528 | tf_op jit(solution)/shard_map/ppermute | solution.py:919
  367.5 15.7 %collective-permute-start.44 = (bf16[128,640]{1,0:T(8,128)(2,1)S(1)}, bf16[128,640]{1,0:T(8,128)(2,1)S(1)}, u32[]{:S(2)}, u32[]{:S(2)}) collective-permute-start(bf16[128,640]{1,0:T(8,128)(2,1)S(1)} %get-tuple-element.327), channel_id=1, source_target_pairs={{0,4},{1,5},{2,6},{3,7},{4,0},{5,1},{6,2},{7,3},{8,12},{9,13},{10,... | collective-permute-start | bytes 491528 | tf_op jit(solution)/shard_map/ppermute | solution.py:919
  369.6 15.3 %collective-permute-start.45 = (bf16[128,640]{1,0:T(8,128)(2,1)S(1)}, bf16[128,640]{1,0:T(8,128)(2,1)S(1)}, u32[]{:S(2)}, u32[]{:S(2)}) collective-permute-start(bf16[128,640]{1,0:T(8,128)(2,1)S(1)} %get-tuple-element.328), channel_id=1, source_target_pairs={{0,6},{1,7},{2,0},{3,1},{4,2},{5,3},{6,4},{7,5},{8,14},{9,15},{10,... | collective-permute-start | bytes 491528 | tf_op jit(solution)/shard_map/ppermute | solution.py:919
  371.0 13.8 %collective-permute-start.47 = (bf16[8,1,144,128]{3,2,1,0:T(8,128)(2,1)}, bf16[8,1,144,128]{3,2,1,0:T(8,128)(2,1)S(1)}, u32[]{:S(2)}, u32[]{:S(2)}) collective-permute-start(bf16[8,1,144,128]{3,2,1,0:T(8,128)(2,1)} %get-tuple-element.332), channel_id=1, source_target_pairs={{0,1},{1,0},{2,3},{3,2},{4,5},{5,4},{6,7},{7,6},{8,9},{9,8},{10,11... | collective-permute-start | bytes 884744 | tf_op jit(solution)/shard_map/ppermute | solution.py:919
  387.0 8.2 %collective-permute-start.48 = (bf16[4,1,144,256]{3,2,0,1:T(8,128)(2,1)}, bf16[4,1,144,256]{3,2,0,1:T(8,128)(2,1)S(1)}, u32[]{:S(2)}, u32[]{:S(2)}) collective-permute-start(bf16[4,1,144,256]{3,2,0,1:T(8,128)(2,1)} %bitcast.179), channel_id=1, source_target_pairs={{0,1},{1,0},{2,3},{3,2},{4,5},{5,4},{6,7},{7,6},{8,9},{9,8},{10,11... | collective-permute-start | bytes 884744 | tf_op jit(solution)/shard_map/ppermute | solution.py:919
  387.5 7.7 %collective-permute-start.49 = (bf16[1,4,144,128]{3,2,1,0:T(8,128)(2,1)}, bf16[1,4,144,128]{3,2,1,0:T(8,128)(2,1)S(1)}, u32[]{:S(2)}, u32[]{:S(2)}) collective-permute-start(bf16[1,4,144,128]{3,2,1,0:T(8,128)(2,1)} %get-tuple-element.337), channel_id=1, source_target_pairs={{0,16},{8,24},{16,0},{24,8},{1,17},{9,25},{17,1},{25,9},{2,18},{10... | collective-permute-start | bytes 442376 | tf_op jit(solution)/shard_map/ppermute | solution.py:919
  398.7 9.1 %collective-permute-start.52 = (bf16[144,384]{1,0:T(8,128)(2,1)S(1)}, bf16[144,384]{1,0:T(8,128)(2,1)S(1)}, u32[]{:S(2)}, u32[]{:S(2)}) collective-permute-start(bf16[144,384]{1,0:T(8,128)(2,1)S(1)} %get-tuple-element.342), channel_id=1, source_target_pairs={{0,6},{1,7},{2,0},{3,1},{4,2},{5,3},{6,4},{7,5},{8,14},{9,15},{10,... | collective-permute-start | bytes 331784 | tf_op jit(solution)/shard_map/ppermute | solution.py:919
  409.3 8.3 %collective-permute-start.54 = (bf16[144,1024]{1,0:T(8,128)(2,1)S(1)}, bf16[144,1024]{1,0:T(8,128)(2,1)S(1)}, u32[]{:S(2)}, u32[]{:S(2)}) collective-permute-start(bf16[144,1024]{1,0:T(8,128)(2,1)S(1)} %get-tuple-element.346.refs_1_), channel_id=1, source_target_pairs={{0,8},{8,0},{16,24},{24,16},{1,9},{9,1},{17,25},{25,17},{2,10},{10... | collective-permute-start | bytes 884744 | tf_op jit(solution)/shard_map/ppermute | solution.py:919
  (78 other events, 572.7 us)
Sparse Core Ops, SparseCore 0:
  24.7 111.9 all-gather.3
  308.7 23.4 reduce-scatter.2
  335.1 25.7 reduce-scatter.4
  366.9 29.5 all-gather.5
